TPU v7x, 32 devices: a whole 2x2x4 slice. The times are simulated.
32 devices in a mesh: scene: 2 (over x), pulse: 16 (over z, y, core).
Axes of the slice: x: 2, y: 2, z: 4, core: 2. Of those that a mesh axis runs over, the one named last changes fastest.
Arguments:
- beams: bfloat16 [2, 2048, 4096], P(None, ('scene', 'pulse')), parts along dimension 1, may hold values from -6 to 6
- ukern: bfloat16 [2, 32], replicated, may hold values from -1 to 1
- rkern: float32 [16, 4], replicated, may hold values from -3 to 3
- angles: float32 [4, 2, 128], replicated, may hold values from -3.140625 to 3.140625
- taps: int32 [4, 2048], P(None, ('scene', 'pulse')), parts along dimension 1, may hold values from 0 to 15
- shifts: int32 [4, 16], replicated, may hold values from -48 to 48
- half_table: int32 [4, 16], replicated, may hold values from 0 to 1, as said below
Outputs:
- merged: bfloat16 [2, 2048, 4096], P(None, ('scene', 'pulse')), parts along dimension 1
There are 2 independent parts, one for each index of `scene`. A program takes and returns all parts, laid end to end along the dimension named above; an argument that names none is the same for every part. Nothing has to cross between parts.
Inputs may be any that keep to these rules, and one draw needn't show every extreme that they name: half_table[l, s] + half_table[l, s XOR 2**l] == 1 for every level l and block s.
All inputs are finite; a program needn't handle non-finite values.
Results may differ from a plain program's by a relative error of at most 0.0074.
Values may be sent and summed in bfloat16 or wider, within the bound.
No kernel may reach another device: no remote copies, remote signals or barrier semaphores. Data moves between devices by JAX's collectives and lax.ppermute only.
A program may use at most 64 MiB of HBM per device.

v0:
```python
import jax
import jax.numpy as jnp
from jax import lax
from jax.sharding import PartitionSpec as P

SHIFT = 48


def from_partner(value, axis, bit):
    mask = 2**bit
    pairs = [(source, source ^ mask) for source in range(lax.axis_size(axis))]
    return lax.ppermute(value, axis, pairs)


def band_matrix(ukern, half, count, utaps):
    width = count // 2 + utaps
    local = jnp.arange(count, dtype=jnp.int32)
    rows = half * count + local
    cols = half * (count // 2) + jnp.arange(width, dtype=jnp.int32)
    offset = cols[None, :] - rows[:, None] // 2 - 1
    kernel = jnp.where(
        (local % 2 == 0)[:, None],
        ukern[0].astype(jnp.float32)[None, :],
        ukern[1].astype(jnp.float32)[None, :],
    )
    picks = (offset[:, :, None] == jnp.arange(utaps, dtype=jnp.int32)[None, None, :]).astype(
        jnp.float32
    )
    return jnp.sum(picks * kernel[:, None, :], axis=2).astype(jnp.bfloat16)


def tap_weights(tap_row, rkern):
    onehot = (tap_row[:, None] == jnp.arange(rkern.shape[0], dtype=jnp.int32)[None, :]).astype(
        jnp.float32
    )
    return jnp.dot(
        onehot, rkern, precision=lax.Precision.HIGHEST, preferred_element_type=jnp.float32
    )


def child_term(range_band, sample_window, weights, shift, segment):
    blended_beam = jnp.einsum(
        "dp,upe->ude", range_band, sample_window, preferred_element_type=jnp.float32
    )
    length = blended_beam.shape[2]
    margin = SHIFT + weights.shape[1]
    padded = jnp.pad(blended_beam, ((0, 0), (0, 0), (margin, margin)))
    shifted = jnp.zeros(blended_beam.shape, jnp.float32)
    for tap in range(weights.shape[1]):
        piece = lax.dynamic_slice_in_dim(padded, margin + shift + tap - 1, length, 2)
        shifted = shifted + weights[None, :, tap, None] * piece
    cosine = jnp.cos(segment)[:, None]
    sine = jnp.sin(segment)[:, None]
    real_part = cosine * shifted[0] - sine * shifted[1]
    imag_part = sine * shifted[0] + cosine * shifted[1]
    return jnp.stack([real_part, imag_part])


def on_device(beams, ukern, rkern, angles, taps, shifts, half_table):
    count = beams.shape[1]
    utaps = ukern.shape[1]
    width = count // 2 + utaps
    myself = lax.axis_index("pulse")
    current = beams
    for level in range(half_table.shape[0]):
        partner = jnp.bitwise_xor(myself, 1 << level)
        half = half_table[level, myself]
        range_band = band_matrix(ukern, half, count, utaps)
        own_pad = jnp.pad(current, ((0, 0), (utaps // 2, utaps // 2), (0, 0)))
        own_window = lax.dynamic_slice_in_dim(own_pad, half * (count // 2), width, 1)
        outbound_rows = lax.dynamic_slice_in_dim(own_pad, (1 - half) * (count // 2), width, 1)
        far_window = from_partner(outbound_rows, "pulse", level)
        weights = tap_weights(taps[level], rkern)
        own_bit = jnp.bitwise_and(jnp.right_shift(myself, level), 1)
        own_row = jnp.where(own_bit == 0, angles[level, 0], angles[level, 1])
        distant_row = jnp.where(own_bit == 0, angles[level, 1], angles[level, 0])
        own_seg = lax.dynamic_slice_in_dim(own_row, half * count, count, 0)
        far_seg = lax.dynamic_slice_in_dim(distant_row, half * count, count, 0)
        own_term = child_term(range_band, own_window, weights, shifts[level, myself], own_seg)
        far_term = child_term(range_band, far_window, weights, shifts[level, partner], far_seg)
        current = (0.70710678 * (own_term + far_term)).astype(jnp.bfloat16)
    return current


def solution(mesh):
    in_specs = (
        P(None, ("scene", "pulse"), None),
        P(),
        P(),
        P(),
        P(None, ("scene", "pulse")),
        P(),
        P(),
    )
    out_specs = P(None, ("scene", "pulse"), None)
    return jax.shard_map(
        on_device, mesh=mesh, in_specs=in_specs, out_specs=out_specs, check_vma=False
    )
```

profile of v0, /device:TPU:0, one launch (start us, length us, event | category | flops | bytes accessed | tf_op | source)
XLA Modules:
  0.0 147.3 jit_solution(9022183245340307306)
XLA Ops:
  0.0 1.5 %constant_dynamic-slice_fusion.7 = (s32[1,1]{1,0:T(1,128)}, s32[1,1]{1,0:T(1,128)}, s32[1,1]{1,0:T(1,128)}, s32[1,1]{1,0:T(1,128)}) fusion(s32[4,16]{1,0:T(4,128)} %param.13, s32[]{:T(128)S(6)} %select_n.272), kind=kLoop, calls=%fused_computation.96 | loop fusion | bytes 36 | tf_op jit(solution)/shard_map/dynamic_slice | solution.py:67
  2.2 1.3 pad_dynamic-slice_fusion.6
  3.4 0.5 collective-permute-start
  8.9 0.7 constant_dynamic-slice_fusion.17
  20.7 0.1 subtract_add_fusion.2
  20.7 0.1 subtract_add_fusion.3
  20.9 1.3 select_reduce_fusion
  22.3 0.1 cosine_bitcast_fusion.3
  22.5 0.2 fusion.11
  22.7 0.4 convolution_bitcast_fusion.7
  23.1 0.4 convolution_bitcast_fusion.6
  23.6 4.5 %multiply_add_fusion.6 = (f32[2,64,4096]{2,1,0:T(8,128)S(1)}, f32[2,64,4096]{2,1,0:T(8,128)S(1)}) fusion(s32[]{:T(128)S(6)} %select_n.297, s32[]{:T(128)S(6)} %select_n.296, s32[]{:T(128)S(6)} %select_n.295, s32[]{:T(128)S(6)} %select_n.294, f32[2,64,4096]{2,1,0:T(8,128)S(1)} %convolution_bitcast_fusion.6, f32[64]{0:T(128)S(1)} %get-tuple-element.65, ...), kind=kLoop, calls=%fused_computation.26 | loop fusion | flops 7340032 | bytes 8389664 | tf_op jit(solution)/shard_map/add | solution.py:51
  28.0 0.3 multiply_subtract_fusion.6
  28.4 0.3 multiply_subtract_fusion.7
  28.7 0.3 fusion.1
  29.0 0.1 pad_dynamic-slice_fusion.4
  29.1 2.6 %collective-permute-start.1 = (bf16[2,64,4096]{2,1,0:T(8,128)(2,1)S(1)}, bf16[2,64,4096]{2,1,0:T(8,128)(2,1)S(1)}, u32[]{:S(2)}, u32[]{:S(2)}) collective-permute-start(bf16[2,64,4096]{2,1,0:T(8,128)(2,1)S(1)} %pad_dynamic-slice_fusion.4), channel_id=1, source_target_pairs={{0,2},{1,3},{2,0},{3,1},{4,6},{5,7},{6,4},{7,5},{8,10},{9,11},{10,... | collective-permute-start | bytes 3145736 | tf_op jit(solution)/shard_map/ppermute | solution.py:12
  42.3 0.1 cosine_bitcast_fusion.2
  42.4 0.2 fusion.10
  42.6 0.5 convolution_bitcast_fusion.5
  43.1 12.5 %collective-permute-done.1 = bf16[2,64,4096]{2,1,0:T(8,128)(2,1)S(1)} collective-permute-done((bf16[2,64,4096]{2,1,0:T(8,128)(2,1)S(1)}, bf16[2,64,4096]{2,1,0:T(8,128)(2,1)S(1)}, u32[]{:S(2)}, u32[]{:S(2)}) %collective-permute-start.1) | collective-permute-done | bytes 1048608 | tf_op jit(solution)/shard_map/ppermute | solution.py:12
  55.5 0.4 convolution_bitcast_fusion.4
  55.9 4.6 %multiply_add_fusion.4 = (f32[2,64,4096]{2,1,0:T(8,128)S(1)}, f32[2,64,4096]{2,1,0:T(8,128)S(1)}) fusion(s32[]{:T(128)S(6)} %select_n.310, s32[]{:T(128)S(6)} %select_n.309, s32[]{:T(128)S(6)} %select_n.308, s32[]{:T(128)S(6)} %select_n.307, f32[2,64,4096]{2,1,0:T(8,128)S(1)} %convolution_bitcast_fusion.4, f32[64]{0:T(128)S(1)} %get-tuple-element.59, ...), kind=kLoop, calls=%fused_computation.24 | loop fusion | flops 7340032 | bytes 8389664 | tf_op jit(solution)/shard_map/add | solution.py:51
  60.6 0.3 multiply_subtract_fusion.4
  60.9 0.3 multiply_subtract_fusion.5
  61.3 0.3 fusion.3
  61.5 0.1 pad_dynamic-slice_fusion.2
  61.7 1.9 %collective-permute-start.2 = (bf16[2,64,4096]{2,1,0:T(8,128)(2,1)S(1)}, bf16[2,64,4096]{2,1,0:T(8,128)(2,1)S(1)}, u32[]{:S(2)}, u32[]{:S(2)}) collective-permute-start(bf16[2,64,4096]{2,1,0:T(8,128)(2,1)S(1)} %pad_dynamic-slice_fusion.2), channel_id=1, source_target_pairs={{0,4},{1,5},{2,6},{3,7},{4,0},{5,1},{6,2},{7,3},{8,12},{9,13},{10,... | collective-permute-start | bytes 3145736 | tf_op jit(solution)/shard_map/ppermute | solution.py:12
  84.6 0.1 cosine_bitcast_fusion.1
  84.8 0.2 fusion.9
  85.0 0.5 convolution_bitcast_fusion.3
  85.4 1.3 collective-permute-done.2
  86.8 0.4 convolution_bitcast_fusion.2
  87.2 4.7 %multiply_add_fusion.2 = (f32[2,64,4096]{2,1,0:T(8,128)S(1)}, f32[2,64,4096]{2,1,0:T(8,128)S(1)}) fusion(s32[]{:T(128)S(6)} %select_n.323, s32[]{:T(128)S(6)} %select_n.322, s32[]{:T(128)S(6)} %select_n.321, s32[]{:T(128)S(6)} %select_n.320, f32[2,64,4096]{2,1,0:T(8,128)S(1)} %convolution_bitcast_fusion.2, f32[64]{0:T(128)S(1)} %get-tuple-element.53, ...), kind=kLoop, calls=%fused_computation.22 | loop fusion | flops 7340032 | bytes 8389664 | tf_op jit(solution)/shard_map/add | solution.py:51
  91.9 0.3 multiply_subtract_fusion.2
  92.2 0.3 multiply_subtract_fusion.3
  92.6 0.3 fusion.5
  92.8 0.1 pad_dynamic-slice_fusion
  93.0 2.5 %collective-permute-start.3 = (bf16[2,64,4096]{2,1,0:T(8,128)(2,1)S(1)}, bf16[2,64,4096]{2,1,0:T(8,128)(2,1)S(1)}, u32[]{:S(2)}, u32[]{:S(2)}) collective-permute-start(bf16[2,64,4096]{2,1,0:T(8,128)(2,1)S(1)} %pad_dynamic-slice_fusion), channel_id=1, source_target_pairs={{0,8},{1,9},{2,10},{3,11},{4,12},{5,13},{6,14},{7,15},{8,0},{9,1},... | collective-permute-start | bytes 3145736 | tf_op jit(solution)/shard_map/ppermute | solution.py:12
  95.5 0.1 cosine_bitcast_fusion
  95.6 0.2 fusion.8
  95.8 0.5 convolution_bitcast_fusion.1
  96.3 44.0 %collective-permute-done.3 = bf16[2,64,4096]{2,1,0:T(8,128)(2,1)S(1)} collective-permute-done((bf16[2,64,4096]{2,1,0:T(8,128)(2,1)S(1)}, bf16[2,64,4096]{2,1,0:T(8,128)(2,1)S(1)}, u32[]{:S(2)}, u32[]{:S(2)}) %collective-permute-start.3) | collective-permute-done | bytes 1048608 | tf_op jit(solution)/shard_map/ppermute | solution.py:12
  140.3 0.4 convolution_bitcast_fusion
  140.7 4.7 %multiply_add_fusion = (f32[2,64,4096]{2,1,0:T(8,128)S(1)}, f32[2,64,4096]{2,1,0:T(8,128)S(1)}) fusion(s32[]{:T(128)S(6)} %select_n.336, s32[]{:T(128)S(6)} %select_n.335, s32[]{:T(128)S(6)} %select_n.334, s32[]{:T(128)S(6)} %select_n.333, f32[2,64,4096]{2,1,0:T(8,128)S(1)} %convolution_bitcast_fusion, f32[64]{0:T(128)S(1)} %get-tuple-element.43, ...), kind=kLoop, calls=%fused_computation.20 | loop fusion | flops 7340032 | bytes 8389664 | tf_op jit(solution)/shard_map/add | solution.py:51
  145.4 0.3 multiply_subtract_fusion
  145.8 0.3 multiply_subtract_fusion.1
  146.1 1.2 fusion.7
  (31 shorter events, 0.4 us)
Async XLA Ops:
  0.0 22.4 %copy-start = (f32[16,4]{0,1:T(4,128)S(1)}, f32[16,4]{0,1:T(4,128)}, u32[]{:S(2)}) copy-start(f32[16,4]{0,1:T(4,128)} %param.9) | copy-start | bytes 772
  0.0 22.7 %copy-start.1 = (bf16[2,64,4096]{2,1,0:T(8,128)(2,1)S(1)}, bf16[2,64,4096]{2,1,0:T(8,128)(2,1)}, u32[]{:S(2)}) copy-start(bf16[2,64,4096]{2,1,0:T(8,128)(2,1)} %param.7) | copy-start | bytes 3145732
  0.0 8.9 %copy-start.2 = (s32[4,16]{1,0:T(4,128)S(1)}, s32[4,16]{1,0:T(4,128)}, u32[]{:S(2)}) copy-start(s32[4,16]{1,0:T(4,128)} %param.12) | copy-start | bytes 772
  0.0 20.4 %copy-start.5 = (bf16[2,32]{1,0:T(2,128)(2,1)S(1)}, bf16[2,32]{1,0:T(2,128)(2,1)}, u32[]{:S(2)}) copy-start(bf16[2,32]{1,0:T(2,128)(2,1)} %param.8) | copy-start | bytes 388
  0.0 22.3 %copy-start.3 = (f32[4,2,128]{2,1,0:T(2,128)S(1)}, f32[4,2,128]{2,1,0:T(2,128)}, u32[]{:S(2)}) copy-start(f32[4,2,128]{2,1,0:T(2,128)} %param.10) | copy-start | bytes 12292
  0.0 22.4 %copy-start.4 = (s32[4,64]{1,0:T(4,128)S(1)}, s32[4,64]{1,0:T(4,128)}, u32[]{:S(2)}) copy-start(s32[4,64]{1,0:T(4,128)} %param.11) | copy-start | bytes 3076
  3.4 19.7 %collective-permute-start = (bf16[2,64,4096]{2,1,0:T(8,128)(2,1)S(1)}, bf16[2,64,4096]{2,1,0:T(8,128)(2,1)S(1)}, u32[]{:S(2)}, u32[]{:S(2)}) collective-permute-start(bf16[2,64,4096]{2,1,0:T(8,128)(2,1)S(1)} %pad_dynamic-slice_fusion.6), channel_id=1, source_target_pairs={{0,1},{1,0},{2,3},{3,2},{4,5},{5,4},{6,7},{7,6},{8,9},{9,8},{10,11... | collective-permute-start | bytes 3145736 | tf_op jit(solution)/shard_map/ppermute | solution.py:12
  29.1 26.4 %collective-permute-start.1 = (bf16[2,64,4096]{2,1,0:T(8,128)(2,1)S(1)}, bf16[2,64,4096]{2,1,0:T(8,128)(2,1)S(1)}, u32[]{:S(2)}, u32[]{:S(2)}) collective-permute-start(bf16[2,64,4096]{2,1,0:T(8,128)(2,1)S(1)} %pad_dynamic-slice_fusion.4), channel_id=1, source_target_pairs={{0,2},{1,3},{2,0},{3,1},{4,6},{5,7},{6,4},{7,5},{8,10},{9,11},{10,... | collective-permute-start | bytes 3145736 | tf_op jit(solution)/shard_map/ppermute | solution.py:12
  61.7 25.1 %collective-permute-start.2 = (bf16[2,64,4096]{2,1,0:T(8,128)(2,1)S(1)}, bf16[2,64,4096]{2,1,0:T(8,128)(2,1)S(1)}, u32[]{:S(2)}, u32[]{:S(2)}) collective-permute-start(bf16[2,64,4096]{2,1,0:T(8,128)(2,1)S(1)} %pad_dynamic-slice_fusion.2), channel_id=1, source_target_pairs={{0,4},{1,5},{2,6},{3,7},{4,0},{5,1},{6,2},{7,3},{8,12},{9,13},{10,... | collective-permute-start | bytes 3145736 | tf_op jit(solution)/shard_map/ppermute | solution.py:12
  93.0 47.3 %collective-permute-start.3 = (bf16[2,64,4096]{2,1,0:T(8,128)(2,1)S(1)}, bf16[2,64,4096]{2,1,0:T(8,128)(2,1)S(1)}, u32[]{:S(2)}, u32[]{:S(2)}) collective-permute-start(bf16[2,64,4096]{2,1,0:T(8,128)(2,1)S(1)} %pad_dynamic-slice_fusion), channel_id=1, source_target_pairs={{0,8},{1,9},{2,10},{3,11},{4,12},{5,13},{6,14},{7,15},{8,0},{9,1},... | collective-permute-start | bytes 3145736 | tf_op jit(solution)/shard_map/ppermute | solution.py:12
where the time goes:
time: 148 us; the launch traced here: 147 us
  waiting for transfers between devices  57.8 us (39%)
  between operations  48.4 us (33%)
  other arithmetic  25 us (17%)
  starting transfers between devices  7.49 us (5%)
  local copies, waits for them, and re-layouts  4.43 us (3%)
  matrix products  4.23 us (3%)
    ppermute x4, waiting for transfers between devices, from_partner(): return lax.ppermute(value, axis, pairs)  57.8 us
    add x4, other arithmetic, child_term(): shifted = shifted + weights[None, :, tap, None] * piece  18.5 us
    ppermute x4, starting transfers between devices, from_partner(): return lax.ppermute(value, axis, pairs)  7.49 us
    dot_general x8, matrix products, child_term(): jnp.einsum('dp,upe->ude', range_band, sample_window, preferred_element_ty...  3.49 us
  transfers between devices with their start and end apart: 4, of which 3 were waited for; matrix products, arithmetic and copies ran while one was open for 4% of the time, Pallas kernels for 0%

commit v1 on v0

v1 whole, which is shorter than its diff:
```python
import functools

import jax
import jax.numpy as jnp
from jax import lax
from jax.experimental import pallas as pl
from jax.experimental.pallas import tpu as pltpu
from jax.sharding import PartitionSpec as P

LANES = 128
TILE = 256
CHUNKS = 4
SCALE = 0.70710678


def prep_kernel(levels, beams, utaps, half_ref, rkern_ref, angles_ref, taps_ref, ukern_ref,
                mix_ref, band_ref, flat_ref):
    window = beams // 2 + utaps // 2
    phases, rtaps = rkern_ref.shape
    myself = lax.axis_index("pulse")
    lane = lax.broadcasted_iota(jnp.int32, (1, 2 * beams), 1)
    first = lane < beams
    beam = jnp.where(first, lane, lane - beams)
    depth = beams // 2 + utaps
    row = lax.broadcasted_iota(jnp.int32, (depth, 2 * beams), 0)
    offset = row - beam // 2 - 1
    band = jnp.zeros((depth, 2 * beams), jnp.float32)
    even = beam % 2 == 0
    for k in range(utaps):
        value = jnp.where(even, ukern_ref[0, k], ukern_ref[1, k])
        band = jnp.where(offset == k, value, band)
    band_ref[...] = band

    def one_level(level, carry):
        half = half_ref[level, myself]
        bit = lax.rem(lax.shift_right_logical(myself, level), 2)
        start = pl.multiple_of((1 - half) * (utaps // 2), 8)
        near = band_ref[pl.ds(start, window), :]
        chosen = taps_ref[pl.ds(level, 1), :]
        weights = []
        for tap in range(rtaps):
            weight = jnp.zeros((1, 2 * beams), jnp.float32)
            for phase in range(phases):
                weight = jnp.where(chosen == phase, rkern_ref[phase, tap], weight)
            weights.append(weight)
        for child in range(2):
            side = bit if child == 0 else 1 - bit
            angle = angles_ref[pl.ds(2 * level + side, 1), :]
            turned = pltpu.roll(angle, beams, 1)
            angle = jnp.where(first == (half == 0), angle, turned)
            cosine = SCALE * jnp.cos(angle)
            sine = SCALE * jnp.sin(angle)
            factors = (jnp.where(first, cosine, sine), jnp.where(first, -sine, cosine))
            for tap in range(rtaps):
                for part in range(2):
                    place = ((child * rtaps + tap) * 2 + part) * window
                    flat_ref[place:place + window, :] = near * (factors[part] * weights[tap])
        for block in range(flat_ref.shape[0] // LANES):
            mixed = flat_ref[block * LANES:(block + 1) * LANES, :].T
            high = mixed.astype(jnp.bfloat16)
            low = (mixed - high.astype(jnp.float32)).astype(jnp.bfloat16)
            columns = pl.ds(block * LANES, LANES)
            mix_ref[level, 0:2 * beams, columns] = high
            mix_ref[level, 2 * beams:4 * beams, columns] = low
        return carry

    lax.fori_loop(0, levels, one_level, 0)


def mixing(ukern, rkern, angles, taps, half_table):
    levels = half_table.shape[0]
    beams = taps.shape[1]
    utaps = ukern.shape[1]
    window = beams // 2 + utaps // 2
    depth = 2 * rkern.shape[1] * 2 * window
    smem = pl.BlockSpec(memory_space=pltpu.SMEM)
    vmem = pl.BlockSpec(memory_space=pltpu.VMEM)
    return pl.pallas_call(
        functools.partial(prep_kernel, levels, beams, utaps),
        out_shape=jax.ShapeDtypeStruct((levels, 4 * beams, depth), jnp.bfloat16),
        in_specs=[smem, smem, vmem, vmem, smem],
        out_specs=vmem,
        scratch_shapes=[
            pltpu.VMEM((beams // 2 + utaps, 2 * beams), jnp.float32),
            pltpu.VMEM((depth, 2 * beams), jnp.float32),
        ],
        compiler_params=pltpu.CompilerParams(vmem_limit_bytes=24 * 2**20),
        name="mixing",
    )(
        half_table,
        rkern,
        angles.reshape(2 * levels, 2 * beams),
        jnp.concatenate([taps, taps], axis=1),
        ukern.astype(jnp.float32),
    )


def merge_kernel(level, plan, start, stop, length, beams, window, rtaps, last, *refs):
    half_ref, shift_ref, mix_ref = refs[:3]
    count = len(plan)
    own_refs, far_refs = refs[3:3 + count], refs[3 + count:3 + 2 * count]
    outs = refs[4 + 2 * count:]
    out_ref = outs[0]
    send_ref = None if last else outs[1]
    wide_ref, stack_ref, sem = outs[1 if last else 2:]
    myself = lax.axis_index("pulse")
    half = half_ref[level, myself]
    rows = pl.ds(pl.multiple_of(half * (beams - window), 16), window)
    base = start - LANES
    copies = []
    for number, (piece, source, target, width) in enumerate(plan):
        for child, ref in ((0, own_refs[number]), (1, far_refs[number])):
            for part in range(2):
                taken = rows if child == 0 else pl.ds(0, window)
                copy = pltpu.make_async_copy(
                    ref.at[part, taken, pl.ds(source, width)],
                    wide_ref.at[child, part, :, pl.ds(target - base, width)],
                    sem.at[child, number, part],
                )
                copy.start()
                copies.append(copy)
    if base < 0:
        wide_ref[:, :, :, 0:LANES] = jnp.zeros((2, 2, window, LANES), jnp.bfloat16)
    if stop + LANES > length:
        wide_ref[:, :, :, stop - base:stop - base + LANES] = jnp.zeros(
            (2, 2, window, LANES), jnp.bfloat16
        )
    shifts = (shift_ref[level, myself], shift_ref[level, jnp.bitwise_xor(myself, 1 << level)])
    for copy in copies:
        copy.wait()
    span = stop - start
    tile = min(TILE, span)
    reach = tile + LANES

    def one_tile(step, carry):
        column = pl.multiple_of(jnp.minimum(step * tile, span - tile), LANES)
        for child in range(2):
            for tap in range(rtaps):
                shift = shifts[child] + (tap - 1 + LANES)
                whole = pl.multiple_of(column + shift // LANES * LANES, LANES)
                turn = lax.rem(reach - lax.rem(shift, LANES), reach)
                piece = wide_ref[child, :, :, pl.ds(whole, reach)].reshape(2 * window, reach)
                piece = pltpu.roll(piece, turn, 1)[:, :tile]
                place = (child * rtaps + tap) * 2 * window
                stack_ref[place:place + 2 * window, :] = piece
        both = jnp.dot(mix_ref[0], stack_ref[...], preferred_element_type=jnp.float32)
        total = (both[:2 * beams] + both[2 * beams:]).astype(jnp.bfloat16)
        out_ref[:, :, pl.ds(column, tile)] = total.reshape(2, beams, tile)
        return carry

    lax.fori_loop(0, pl.cdiv(span, tile), one_tile, 0)
    if not last:
        following = half_ref[level + 1, myself]
        other = pl.ds(pl.multiple_of((1 - following) * (beams - window), 16), window)
        send_ref[...] = out_ref[:, other, :]


def pieces_of(bounds, start, stop):
    found = []
    for chunk in range(len(bounds) - 1):
        low, high = max(bounds[chunk], start), min(bounds[chunk + 1], stop)
        if low < high:
            found.append((chunk, low - bounds[chunk], low, high - low))
    return found


def merge(level, levels, half_table, shifts, mix, own, far, bounds, start, stop, sizes, before):
    beams, window, rtaps, length = sizes
    last = level == levels - 1
    plan = pieces_of(bounds, max(start - LANES, 0), min(stop + LANES, length))
    span = stop - start
    smem = pl.BlockSpec(memory_space=pltpu.SMEM)
    vmem = pl.BlockSpec(memory_space=pltpu.VMEM)
    anywhere = pl.BlockSpec(memory_space=pl.ANY)
    depth = mix.shape[2]
    out_shape = [jax.ShapeDtypeStruct((2, beams, span), jnp.bfloat16)]
    if not last:
        out_shape.append(jax.ShapeDtypeStruct((2, window, span), jnp.bfloat16))
    return pl.pallas_call(
        functools.partial(
            merge_kernel, level, plan, start, stop, length, beams, window, rtaps, last
        ),
        grid=(1,),
        out_shape=out_shape,
        in_specs=[smem, smem, pl.BlockSpec((1, 4 * beams, depth), lambda i: (level, 0, 0))]
        + [anywhere] * (2 * len(plan) + 1),
        out_specs=[vmem] * len(out_shape),
        scratch_shapes=[
            pltpu.VMEM((2, 2, window, span + 2 * LANES), jnp.bfloat16),
            pltpu.VMEM((depth, min(TILE, span)), jnp.bfloat16),
            pltpu.SemaphoreType.DMA((2, len(plan), 2)),
        ],
        compiler_params=pltpu.CompilerParams(vmem_limit_bytes=24 * 2**20),
        cost_estimate=pl.CostEstimate(
            flops=2 * 4 * beams * depth * span,
            bytes_accessed=8 * beams * span * 2,
            transcendentals=0,
        ),
        name=f"merge_{level}",
    )(
        half_table,
        shifts,
        mix,
        *[own[piece[0]] for piece in plan],
        *[far[piece[0]] for piece in plan],
        before,
    )


def merge_order(levels, bounds):
    sending = [8.0] + [18.0] * (levels - 2) + [36.0]
    working, fixed = 3.0, 1.0
    length = bounds[0][-1]
    ready = {}
    clock = 3.0
    link = [clock] * levels
    for chunk in range(CHUNKS):
        link[0] += sending[0] * (bounds[0][chunk + 1] - bounds[0][chunk]) / length
        ready[0, chunk] = link[0]
    order = []
    following = [0] * levels
    while len(order) < levels * CHUNKS:
        choices = [
            (ready[level, following[level]], -level, level)
            for level in range(levels)
            if (level, following[level]) in ready
        ]
        now = [choice for choice in choices if choice[0] <= clock]
        level = max(choice[2] for choice in now) if now else min(choices)[2]
        chunk = following[level]
        following[level] += 1
        order.append((level, chunk))
        width = (bounds[level + 1][chunk + 1] - bounds[level + 1][chunk]) / length
        clock = max(clock, ready[level, chunk]) + fixed + working * width
        if level < levels - 1:
            link[level + 1] = max(link[level + 1], clock) + sending[level + 1] * width
            ready[level + 1, chunk] = link[level + 1]
    return order


def from_partner(value, bit):
    mask = 1 << bit
    pairs = [(source, source ^ mask) for source in range(lax.axis_size("pulse"))]
    return lax.ppermute(value, "pulse", pairs)


def on_device(beams_in, ukern, rkern, angles, taps, shifts, half_table):
    beams, length = beams_in.shape[1:]
    utaps, rtaps = ukern.shape[1], rkern.shape[1]
    window = beams // 2 + utaps // 2
    levels = half_table.shape[0]
    sizes = (beams, window, rtaps, length)
    step = length // CHUNKS
    ends = [min((chunk + 1) * step, length) for chunk in range(CHUNKS)]
    bounds = [
        [0] + [min(end + (levels - level) * LANES, length) for end in ends]
        for level in range(levels + 1)
    ]
    half = half_table[0, lax.axis_index("pulse")]
    own = [beams_in[:, :, low:high] for low, high in zip(bounds[0][:-1], bounds[0][1:])]
    gap = beams - window
    send = [
        jnp.where(half == 0, piece[:, gap:gap + window], piece[:, :window]) for piece in own
    ]
    far = [from_partner(piece, 0) for piece in send]
    mix = mixing(ukern, rkern, angles, taps, half_table)
    owns = [own] + [[None] * CHUNKS for _ in range(levels)]
    fars = [far] + [[None] * CHUNKS for _ in range(levels - 1)]
    before = mix
    for level, chunk in merge_order(levels, bounds):
        start, stop = bounds[level + 1][chunk], bounds[level + 1][chunk + 1]
        done = merge(
            level, levels, half_table, shifts, mix, owns[level], fars[level], bounds[level],
            start, stop, sizes, before,
        )
        before = owns[level + 1][chunk] = done[0]
        if level < levels - 1:
            fars[level + 1][chunk] = from_partner(done[1], level + 1)
    return jnp.concatenate(owns[levels], axis=2)


def solution(mesh):
    in_specs = (
        P(None, ("scene", "pulse"), None),
        P(),
        P(),
        P(),
        P(None, ("scene", "pulse")),
        P(),
        P(),
    )
    out_specs = P(None, ("scene", "pulse"), None)
    return jax.shard_map(
        on_device, mesh=mesh, in_specs=in_specs, out_specs=out_specs, check_vma=False
    )
```

time: 148 us -> 83.6 us (0.56)
  between operations: 48.4 us -> 0.29 us
  Pallas kernels: 0 us -> 44.1 us
  waiting for transfers between devices: 57.8 us -> 14.5 us
  other arithmetic: 25 us -> 6.58 us
  starting transfers between devices: 7.49 us -> 17.7 us
  local copies, waits for them, and re-layouts: 4.43 us -> 0.19 us
  matrix products: 4.23 us -> 0 us
    pallas_call x0 -> x17, Pallas kernels: none -> 44.1 us  [the longest x16 42.1 us: merge(): pl.pallas_call(functools.partial(merge_kernel, level, plan, start, stop,...]
    ppermute x4 -> x16, waiting for transfers between devices: 57.8 us -> 14.5 us  [from_partner(): return lax.ppermute(value, 'pulse', pairs)]
    add x8 -> x0, other arithmetic: 18.5 us -> none  [the longest x4 18.5 us: child_term(): shifted = shifted + weights[None, :, tap, None] * piece]
    ppermute x4 -> x16, starting transfers between devices: 7.49 us -> 17.7 us  [from_partner(): return lax.ppermute(value, 'pulse', pairs)]
    dot_general x12 -> x0, matrix products: 4.23 us -> none  [the longest x8 3.49 us: child_term(): jnp.einsum('dp,upe->ude', range_band, sample_window, preferred_element_ty...]
    select_n x5 -> x3, other arithmetic: 0.11 us -> 4.1 us  [on_device(): jnp.where(half == 0, piece[:, gap:gap + window], piece[:, :window])]
    dynamic_slice x6 -> x0, local copies, waits for them, and re-layouts: 3.88 us -> none  [the longest x4 1.7 us: on_device(): lax.dynamic_slice_in_dim(own_pad, (1 - half) * (count // 2), width, 1)]
    sub x12 -> x0, other arithmetic: 3 us -> none  [the longest x8 2.7 us: child_term(): real_part = cosine * shifted[0] - sine * shifted[1]]
  transfers between devices with their start and end apart: 4 -> 16, of which waited for: 3 -> 5; matrix products, arithmetic and copies ran while one was open for 4% -> 3% of each run, Pallas kernels for 0% -> 46%
where the time goes in v1:
time: 83.6 us; the launch traced here: 83.4 us
  Pallas kernels  44.1 us (53%)
  starting transfers between devices  17.7 us (21%)
  waiting for transfers between devices  14.5 us (17%)
  other arithmetic  6.58 us (8%)
    pallas_call x16, Pallas kernels, merge(): pl.pallas_call(functools.partial(merge_kernel, level, plan, start, stop,...  42.1 us
    ppermute x16, starting transfers between devices, from_partner(): return lax.ppermute(value, 'pulse', pairs)  17.7 us
    ppermute x16, waiting for transfers between devices, from_partner(): return lax.ppermute(value, 'pulse', pairs)  14.5 us
    select_n x3, other arithmetic, on_device(): jnp.where(half == 0, piece[:, gap:gap + window], piece[:, :window])  4.1 us
    pallas_call x1, Pallas kernels, mixing(): pl.pallas_call(functools.partial(prep_kernel, levels, beams, utaps), out_...  1.97 us
  transfers between devices with their start and end apart: 16, of which 5 were waited for; matrix products, arithmetic and copies ran while one was open for 3% of the time, Pallas kernels for 46%

profile of v1, /device:TPU:0, one launch (start us, length us, event | category | flops | bytes accessed | tf_op | source)
XLA Modules:
  0.0 83.4 jit_solution(3420286428681738809)
XLA Ops:
  0.0 1.4 %fusion.1 = pred[1,1]{1,0:T(4,128)(4,1)} fusion(s32[4,16]{1,0:T(4,128)} %refs_0_.31, s32[]{:T(128)S(6)} %select_n.31), kind=kLoop, calls=%fused_computation.8 | loop fusion | flops 1 | bytes 9 | tf_op jit(solution)/shard_map/eq | solution.py:263
  1.4 0.0 copy-start.2
  1.4 1.7 %slice_select_fusion.3 = bf16[2,48,512]{2,1,0:T(8,128)(2,1)S(1)} fusion(bf16[2,64,4096]{2,1,0:T(8,128)(2,1)} %param.7, pred[]{:T(512)} %bitcast.1), kind=kLoop, calls=%fused_computation.4 | loop fusion | flops 49152 | bytes 294913 | tf_op jit(solution)/shard_map/jit(_where)/select_n | solution.py:263
  3.1 0.5 collective-permute-start.3
  3.6 1.7 %slice_select_fusion = bf16[2,48,1536]{2,1,0:T(8,128)(2,1)S(1)} fusion(bf16[2,64,4096]{2,1,0:T(8,128)(2,1)} %param.7, pred[]{:T(512)} %bitcast.1), kind=kLoop, calls=%fused_computation.1 | loop fusion | flops 147456 | bytes 884737 | tf_op jit(solution)/shard_map/jit(_where)/select_n | solution.py:263
  5.3 0.0 copy-start.1
  5.3 0.1 collective-permute-start
  5.5 0.7 slice_select_fusion.2
  6.2 0.5 collective-permute-start.2
  6.7 0.1 collective-permute-start.4
  6.8 0.1 copy.8.rkern_ref
  6.9 0.1 pad_add_fusion.taps_ref
  7.0 2.0 %mixing.1.refs_2_.refs_5_ = bf16[4,256,768]{2,1,0:T(8,128)(2,1)S(1)} custom-call(s32[4,16]{1,0:T(4,128)S(1)} %copy-done, f32[16,4]{1,0:T(8,128)S(1)} %copy.8.rkern_ref, f32[8,128]{1,0:T(8,128)S(1)} %bitcast.2, s32[4,128]{1,0:T(4,128)S(1)} %pad_add_fusion.taps_ref, f32[2,32]{1,0:T(2,128)S(1)} %convert_element_type.3.ukern_ref), custom_call_target="tpu_custom_call" | custom-call | tf_op jit(solution)/shard_map/mixing/pallas_call | solution.py:78
  9.0 0.0 collective-permute-done.refs_4_.refs_5_
  9.0 3.5 %merge_0.4 = (bf16[2,64,1408]{2,1,0:T(8,128)(2,1)S(1)}, bf16[2,48,1408]{2,1,0:T(8,128)(2,1)S(1)}) custom-call(s32[4,16]{1,0:T(4,128)S(1)} %copy-done, s32[4,16]{1,0:T(4,128)S(1)} %copy-done.1, bf16[4,256,768]{2,1,0:T(8,128)(2,1)S(1)} %mixing.1.refs_2_.refs_5_, bf16[2,64,1536]{2,1,0:T(8,128)(2,1)S(1)} %slice.44.refs_3_, ...), custom_call_target="tpu_custom_call" | custom-call | flops 553648128 | bytes 1441792 | tf_op jit(solution)/shard_map/merge_0/pallas_call | solution.py:179
  12.5 3.0 %collective-permute-start.1 = (bf16[2,48,1408]{2,1,0:T(8,128)(2,1)S(1)}, bf16[2,48,1408]{2,1,0:T(8,128)(2,1)S(1)}, u32[]{:S(2)}, u32[]{:S(2)}) collective-permute-start(bf16[2,48,1408]{2,1,0:T(8,128)(2,1)S(1)} %get-tuple-element.30), channel_id=1, source_target_pairs={{0,2},{1,3},{2,0},{3,1},{4,6},{5,7},{6,4},{7,5},{8,10},{9,11},{10,... | collective-permute-start | bytes 811016 | tf_op jit(solution)/shard_map/ppermute | solution.py:244
  15.5 2.6 %merge_0.5 = (bf16[2,64,1024]{2,1,0:T(8,128)(2,1)S(1)}, bf16[2,48,1024]{2,1,0:T(8,128)(2,1)S(1)}) custom-call(s32[4,16]{1,0:T(4,128)S(1)} %copy-done, s32[4,16]{1,0:T(4,128)S(1)} %copy-done.1, bf16[4,256,768]{2,1,0:T(8,128)(2,1)S(1)} %mixing.1.refs_2_.refs_5_, bf16[2,64,1536]{2,1,0:T(8,128)(2,1)S(1)} %slice.44.refs_3_, ...), custom_call_target="tpu_custom_call" | custom-call | flops 402653184 | bytes 1048576 | tf_op jit(solution)/shard_map/merge_0/pallas_call | solution.py:179
  18.1 2.6 %merge_0.6 = (bf16[2,64,1024]{2,1,0:T(8,128)(2,1)S(1)}, bf16[2,48,1024]{2,1,0:T(8,128)(2,1)S(1)}) custom-call(s32[4,16]{1,0:T(4,128)S(1)} %copy-done, s32[4,16]{1,0:T(4,128)S(1)} %copy-done.1, bf16[4,256,768]{2,1,0:T(8,128)(2,1)S(1)} %mixing.1.refs_2_.refs_5_, bf16[2,64,1024]{2,1,0:T(8,128)(2,1)S(1)} %get-tuple-element.56.refs_4_.refs_3_, ...), custom_call_target="tpu_custom_call" | custom-call | flops 402653184 | bytes 1048576 | tf_op jit(solution)/shard_map/merge_0/pallas_call | solution.py:179
  20.8 2.1 %merge_0.7 = (bf16[2,64,640]{2,1,0:T(8,128)(2,1)S(1)}, bf16[2,48,640]{2,1,0:T(8,128)(2,1)S(1)}) custom-call(s32[4,16]{1,0:T(4,128)S(1)} %copy-done, s32[4,16]{1,0:T(4,128)S(1)} %copy-done.1, bf16[4,256,768]{2,1,0:T(8,128)(2,1)S(1)} %mixing.1.refs_2_.refs_5_, bf16[2,64,1024]{2,1,0:T(8,128)(2,1)S(1)} %get-tuple-element.55.refs_4_.refs_3_, ...), custom_call_target="tpu_custom_call" | custom-call | flops 251658240 | bytes 655360 | tf_op jit(solution)/shard_map/merge_0/pallas_call | solution.py:179
  22.9 3.0 %merge_1.4 = (bf16[2,64,1280]{2,1,0:T(8,128)(2,1)S(1)}, bf16[2,48,1280]{2,1,0:T(8,128)(2,1)S(1)}) custom-call(s32[4,16]{1,0:T(4,128)S(1)} %copy-done, s32[4,16]{1,0:T(4,128)S(1)} %copy-done.1, bf16[4,256,768]{2,1,0:T(8,128)(2,1)S(1)} %mixing.1.refs_2_.refs_5_, bf16[2,64,1408]{2,1,0:T(8,128)(2,1)S(1)} %get-tuple-element.29.refs_7_.refs_3_, ...), custom_call_target="tpu_custom_call" | custom-call | flops 503316480 | bytes 1310720 | tf_op jit(solution)/shard_map/merge_1/pallas_call | solution.py:179
  25.9 1.6 %collective-permute-start.5 = (bf16[2,48,1280]{2,1,0:T(8,128)(2,1)S(1)}, bf16[2,48,1280]{2,1,0:T(8,128)(2,1)S(1)}, u32[]{:S(2)}, u32[]{:S(2)}) collective-permute-start(bf16[2,48,1280]{2,1,0:T(8,128)(2,1)S(1)} %get-tuple-element.35), channel_id=1, source_target_pairs={{0,4},{1,5},{2,6},{3,7},{4,0},{5,1},{6,2},{7,3},{8,12},{9,13},{10,... | collective-permute-start | bytes 737288 | tf_op jit(solution)/shard_map/ppermute | solution.py:244
  27.6 1.0 %collective-permute-start.6 = (bf16[2,48,1024]{2,1,0:T(8,128)(2,1)S(1)}, bf16[2,48,1024]{2,1,0:T(8,128)(2,1)S(1)}, u32[]{:S(2)}, u32[]{:S(2)}) collective-permute-start(bf16[2,48,1024]{2,1,0:T(8,128)(2,1)S(1)} %get-tuple-element.36), channel_id=1, source_target_pairs={{0,2},{1,3},{2,0},{3,1},{4,6},{5,7},{6,4},{7,5},{8,10},{9,11},{10,... | collective-permute-start | bytes 589832 | tf_op jit(solution)/shard_map/ppermute | solution.py:244
  28.6 1.0 %collective-permute-start.8 = (bf16[2,48,1024]{2,1,0:T(8,128)(2,1)S(1)}, bf16[2,48,1024]{2,1,0:T(8,128)(2,1)S(1)}, u32[]{:S(2)}, u32[]{:S(2)}) collective-permute-start(bf16[2,48,1024]{2,1,0:T(8,128)(2,1)S(1)} %get-tuple-element.40), channel_id=1, source_target_pairs={{0,2},{1,3},{2,0},{3,1},{4,6},{5,7},{6,4},{7,5},{8,10},{9,11},{10,... | collective-permute-start | bytes 589832 | tf_op jit(solution)/shard_map/ppermute | solution.py:244
  29.6 1.0 %collective-permute-start.11 = (bf16[2,48,640]{2,1,0:T(8,128)(2,1)S(1)}, bf16[2,48,640]{2,1,0:T(8,128)(2,1)S(1)}, u32[]{:S(2)}, u32[]{:S(2)}) collective-permute-start(bf16[2,48,640]{2,1,0:T(8,128)(2,1)S(1)} %get-tuple-element.44), channel_id=1, source_target_pairs={{0,2},{1,3},{2,0},{3,1},{4,6},{5,7},{6,4},{7,5},{8,10},{9,11},{10,... | collective-permute-start | bytes 368648 | tf_op jit(solution)/shard_map/ppermute | solution.py:244
  30.6 4.8 %collective-permute-done.6.refs_6_.refs_5_ = bf16[2,48,1024]{2,1,0:T(8,128)(2,1)S(1)} collective-permute-done((bf16[2,48,1024]{2,1,0:T(8,128)(2,1)S(1)}, bf16[2,48,1024]{2,1,0:T(8,128)(2,1)S(1)}, u32[]{:S(2)}, u32[]{:S(2)}) %collective-permute-start.6) | collective-permute-done | bytes 196640 | tf_op jit(solution)/shard_map/ppermute | solution.py:244
  35.4 2.6 %merge_1.5 = (bf16[2,64,1024]{2,1,0:T(8,128)(2,1)S(1)}, bf16[2,48,1024]{2,1,0:T(8,128)(2,1)S(1)}) custom-call(s32[4,16]{1,0:T(4,128)S(1)} %copy-done, s32[4,16]{1,0:T(4,128)S(1)} %copy-done.1, bf16[4,256,768]{2,1,0:T(8,128)(2,1)S(1)} %mixing.1.refs_2_.refs_5_, bf16[2,64,1408]{2,1,0:T(8,128)(2,1)S(1)} %get-tuple-element.29.refs_7_.refs_3_, ...), custom_call_target="tpu_custom_call" | custom-call | flops 402653184 | bytes 1048576 | tf_op jit(solution)/shard_map/merge_1/pallas_call | solution.py:179
  38.0 0.5 collective-permute-start.9
  38.5 3.0 %merge_2.4 = (bf16[2,64,1152]{2,1,0:T(8,128)(2,1)S(1)}, bf16[2,48,1152]{2,1,0:T(8,128)(2,1)S(1)}) custom-call(s32[4,16]{1,0:T(4,128)S(1)} %copy-done, s32[4,16]{1,0:T(4,128)S(1)} %copy-done.1, bf16[4,256,768]{2,1,0:T(8,128)(2,1)S(1)} %mixing.1.refs_2_.refs_5_, bf16[2,64,1280]{2,1,0:T(8,128)(2,1)S(1)} %get-tuple-element.34.refs_7_.refs_3_, ...), custom_call_target="tpu_custom_call" | custom-call | flops 452984832 | bytes 1179648 | tf_op jit(solution)/shard_map/merge_2/pallas_call | solution.py:179
  41.5 2.6 %merge_1.6 = (bf16[2,64,1024]{2,1,0:T(8,128)(2,1)S(1)}, bf16[2,48,1024]{2,1,0:T(8,128)(2,1)S(1)}) custom-call(s32[4,16]{1,0:T(4,128)S(1)} %copy-done, s32[4,16]{1,0:T(4,128)S(1)} %copy-done.1, bf16[4,256,768]{2,1,0:T(8,128)(2,1)S(1)} %mixing.1.refs_2_.refs_5_, bf16[2,64,1024]{2,1,0:T(8,128)(2,1)S(1)} %get-tuple-element.31.refs_7_.refs_4_.refs_3_, ...), custom_call_target="tpu_custom_call" | custom-call | flops 402653184 | bytes 1048576 | tf_op jit(solution)/shard_map/merge_1/pallas_call | solution.py:179
  44.2 1.6 %collective-permute-start.10 = (bf16[2,48,1024]{2,1,0:T(8,128)(2,1)S(1)}, bf16[2,48,1024]{2,1,0:T(8,128)(2,1)S(1)}, u32[]{:S(2)}, u32[]{:S(2)}) collective-permute-start(bf16[2,48,1024]{2,1,0:T(8,128)(2,1)S(1)} %get-tuple-element.43), channel_id=1, source_target_pairs={{0,4},{1,5},{2,6},{3,7},{4,0},{5,1},{6,2},{7,3},{8,12},{9,13},{10,... | collective-permute-start | bytes 589832 | tf_op jit(solution)/shard_map/ppermute | solution.py:244
  45.8 2.6 %collective-permute-start.7 = (bf16[2,48,1152]{2,1,0:T(8,128)(2,1)S(1)}, bf16[2,48,1152]{2,1,0:T(8,128)(2,1)S(1)}, u32[]{:S(2)}, u32[]{:S(2)}) collective-permute-start(bf16[2,48,1152]{2,1,0:T(8,128)(2,1)S(1)} %get-tuple-element.39), channel_id=1, source_target_pairs={{0,8},{1,9},{2,10},{3,11},{4,12},{5,13},{6,14},{7,15},{8,0},{9,1},... | collective-permute-start | bytes 663560 | tf_op jit(solution)/shard_map/ppermute | solution.py:244
  48.4 2.1 %merge_1.7 = (bf16[2,64,768]{2,1,0:T(8,128)(2,1)S(1)}, bf16[2,48,768]{2,1,0:T(8,128)(2,1)S(1)}) custom-call(s32[4,16]{1,0:T(4,128)S(1)} %copy-done, s32[4,16]{1,0:T(4,128)S(1)} %copy-done.1, bf16[4,256,768]{2,1,0:T(8,128)(2,1)S(1)} %mixing.1.refs_2_.refs_5_, bf16[2,64,1024]{2,1,0:T(8,128)(2,1)S(1)} %get-tuple-element.32.refs_7_.refs_4_.refs_3_, ...), custom_call_target="tpu_custom_call" | custom-call | flops 301989888 | bytes 786432 | tf_op jit(solution)/shard_map/merge_1/pallas_call | solution.py:179
  50.5 0.5 collective-permute-start.13
  51.0 2.6 %merge_2.5 = (bf16[2,64,1024]{2,1,0:T(8,128)(2,1)S(1)}, bf16[2,48,1024]{2,1,0:T(8,128)(2,1)S(1)}) custom-call(s32[4,16]{1,0:T(4,128)S(1)} %copy-done, s32[4,16]{1,0:T(4,128)S(1)} %copy-done.1, bf16[4,256,768]{2,1,0:T(8,128)(2,1)S(1)} %mixing.1.refs_2_.refs_5_, bf16[2,64,1280]{2,1,0:T(8,128)(2,1)S(1)} %get-tuple-element.34.refs_7_.refs_3_, ...), custom_call_target="tpu_custom_call" | custom-call | flops 402653184 | bytes 1048576 | tf_op jit(solution)/shard_map/merge_2/pallas_call | solution.py:179
  53.6 0.4 collective-permute-start.12
  54.0 0.1 collective-permute-done.10.refs_6_.refs_5_
  54.2 2.6 %merge_2.6 = (bf16[2,64,1024]{2,1,0:T(8,128)(2,1)S(1)}, bf16[2,48,1024]{2,1,0:T(8,128)(2,1)S(1)}) custom-call(s32[4,16]{1,0:T(4,128)S(1)} %copy-done, s32[4,16]{1,0:T(4,128)S(1)} %copy-done.1, bf16[4,256,768]{2,1,0:T(8,128)(2,1)S(1)} %mixing.1.refs_2_.refs_5_, bf16[2,64,1024]{2,1,0:T(8,128)(2,1)S(1)} %get-tuple-element.37.refs_5_.refs_4_.refs_3_, ...), custom_call_target="tpu_custom_call" | custom-call | flops 402653184 | bytes 1048576 | tf_op jit(solution)/shard_map/merge_2/pallas_call | solution.py:179
  56.8 2.5 %collective-permute-start.14 = (bf16[2,48,1024]{2,1,0:T(8,128)(2,1)S(1)}, bf16[2,48,1024]{2,1,0:T(8,128)(2,1)S(1)}, u32[]{:S(2)}, u32[]{:S(2)}) collective-permute-start(bf16[2,48,1024]{2,1,0:T(8,128)(2,1)S(1)} %get-tuple-element.51), channel_id=1, source_target_pairs={{0,8},{1,9},{2,10},{3,11},{4,12},{5,13},{6,14},{7,15},{8,0},{9,1},... | collective-permute-start | bytes 589832 | tf_op jit(solution)/shard_map/ppermute | solution.py:244
  59.3 2.5 %merge_3.4.refs_7_ = bf16[2,64,1024]{2,1,0:T(8,128)(2,1)S(1)} custom-call(s32[4,16]{1,0:T(4,128)S(1)} %copy-done, s32[4,16]{1,0:T(4,128)S(1)} %copy-done.1, bf16[4,256,768]{2,1,0:T(8,128)(2,1)S(1)} %mixing.1.refs_2_.refs_5_, bf16[2,64,1152]{2,1,0:T(8,128)(2,1)S(1)} %get-tuple-element.38.refs_7_.refs_3_, ...), custom_call_target="tpu_custom_call" | custom-call | flops 402653184 | bytes 1048576 | tf_op jit(solution)/shard_map/merge_3/pallas_call | solution.py:179
  61.8 2.6 %merge_2.7 = (bf16[2,64,896]{2,1,0:T(8,128)(2,1)S(1)}, bf16[2,48,896]{2,1,0:T(8,128)(2,1)S(1)}) custom-call(s32[4,16]{1,0:T(4,128)S(1)} %copy-done, s32[4,16]{1,0:T(4,128)S(1)} %copy-done.1, bf16[4,256,768]{2,1,0:T(8,128)(2,1)S(1)} %mixing.1.refs_2_.refs_5_, bf16[2,64,1024]{2,1,0:T(8,128)(2,1)S(1)} %get-tuple-element.41.refs_7_.refs_4_.refs_3_, ...), custom_call_target="tpu_custom_call" | custom-call | flops 352321536 | bytes 917504 | tf_op jit(solution)/shard_map/merge_2/pallas_call | solution.py:179
  64.4 0.5 collective-permute-start.15
  65.0 7.8 %collective-permute-done.12.refs_6_.refs_5_ = bf16[2,48,1024]{2,1,0:T(8,128)(2,1)S(1)} collective-permute-done((bf16[2,48,1024]{2,1,0:T(8,128)(2,1)S(1)}, bf16[2,48,1024]{2,1,0:T(8,128)(2,1)S(1)}, u32[]{:S(2)}, u32[]{:S(2)}) %collective-permute-start.12) | collective-permute-done | bytes 196640 | tf_op jit(solution)/shard_map/ppermute | solution.py:244
  72.8 2.6 %merge_3.5.refs_7_ = bf16[2,64,1024]{2,1,0:T(8,128)(2,1)S(1)} custom-call(s32[4,16]{1,0:T(4,128)S(1)} %copy-done, s32[4,16]{1,0:T(4,128)S(1)} %copy-done.1, bf16[4,256,768]{2,1,0:T(8,128)(2,1)S(1)} %mixing.1.refs_2_.refs_5_, bf16[2,64,1152]{2,1,0:T(8,128)(2,1)S(1)} %get-tuple-element.38.refs_7_.refs_3_, ...), custom_call_target="tpu_custom_call" | custom-call | flops 402653184 | bytes 1048576 | tf_op jit(solution)/shard_map/merge_3/pallas_call | solution.py:179
  75.4 1.6 %collective-permute-done.14.refs_6_.refs_5_ = bf16[2,48,1024]{2,1,0:T(8,128)(2,1)S(1)} collective-permute-done((bf16[2,48,1024]{2,1,0:T(8,128)(2,1)S(1)}, bf16[2,48,1024]{2,1,0:T(8,128)(2,1)S(1)}, u32[]{:S(2)}, u32[]{:S(2)}) %collective-permute-start.14) | collective-permute-done | bytes 196640 | tf_op jit(solution)/shard_map/ppermute | solution.py:244
  77.0 2.6 %merge_3.6.refs_7_ = bf16[2,64,1024]{2,1,0:T(8,128)(2,1)S(1)} custom-call(s32[4,16]{1,0:T(4,128)S(1)} %copy-done, s32[4,16]{1,0:T(4,128)S(1)} %copy-done.1, bf16[4,256,768]{2,1,0:T(8,128)(2,1)S(1)} %mixing.1.refs_2_.refs_5_, bf16[2,64,1024]{2,1,0:T(8,128)(2,1)S(1)} %get-tuple-element.46.refs_7_.refs_4_.refs_3_, ...), custom_call_target="tpu_custom_call" | custom-call | flops 402653184 | bytes 1048576 | tf_op jit(solution)/shard_map/merge_3/pallas_call | solution.py:179
  79.6 0.1 collective-permute-done.15.refs_6_
  79.8 2.6 %merge_3.7 = bf16[2,64,1024]{2,1,0:T(8,128)(2,1)S(1)} custom-call(s32[4,16]{1,0:T(4,128)S(1)} %copy-done, s32[4,16]{1,0:T(4,128)S(1)} %copy-done.1, bf16[4,256,768]{2,1,0:T(8,128)(2,1)S(1)} %mixing.1.refs_2_.refs_5_, bf16[2,64,1024]{2,1,0:T(8,128)(2,1)S(1)} %get-tuple-element.47.refs_5_.refs_4_.refs_3_, ...), custom_call_target="tpu_custom_call" | custom-call | flops 402653184 | bytes 1048576 | tf_op jit(solution)/shard_map/merge_3/pallas_call | solution.py:179
  82.3 1.0 %pad_maximum_fusion = bf16[2,64,4096]{2,1,0:T(8,128)(2,1)} fusion(bf16[2,64,1024]{2,1,0:T(8,128)(2,1)S(1)} %merge_3.7, bf16[2,64,1024]{2,1,0:T(8,128)(2,1)S(1)} %merge_3.6.refs_7_, bf16[2,64,1024]{2,1,0:T(8,128)(2,1)S(1)} %merge_3.5.refs_7_, bf16[2,64,1024]{2,1,0:T(8,128)(2,1)S(1)} %merge_3.4.refs_7_), kind=kLoop, calls=%fused_computation | loop fusion | flops 4194304 | bytes 2097152 | tf_op jit(solution)/shard_map/concatenate | solution.py:279
  (26 shorter events, 0.1 us)
Async XLA Ops:
  0.0 5.5 %copy-start.3 = (bf16[2,64,4096]{2,1,0:T(8,128)(2,1)S(1)}, bf16[2,64,4096]{2,1,0:T(8,128)(2,1)}, u32[]{:S(2)}) copy-start(bf16[2,64,4096]{2,1,0:T(8,128)(2,1)} %param.7) | copy-start | bytes 3145732
  1.4 5.4 %copy-start.6 = (bf16[2,32]{1,0:T(2,128)(2,1)S(1)}, bf16[2,32]{1,0:T(2,128)(2,1)}, u32[]{:S(2)}) copy-start(bf16[2,32]{1,0:T(2,128)(2,1)} %param.8) | copy-start | bytes 388
  1.4 5.4 %copy-start.4 = (f32[16,4]{0,1:T(4,128)S(1)}, f32[16,4]{0,1:T(4,128)}, u32[]{:S(2)}) copy-start(f32[16,4]{0,1:T(4,128)} %param.9) | copy-start | bytes 772
  1.4 5.5 %copy-start.5 = (s32[4,64]{1,0:T(4,128)S(1)}, s32[4,64]{1,0:T(4,128)}, u32[]{:S(2)}) copy-start(s32[4,64]{1,0:T(4,128)} %param.11) | copy-start | bytes 3076
  1.4 5.6 %copy-start = (s32[4,16]{1,0:T(4,128)S(1)}, s32[4,16]{1,0:T(4,128)}, u32[]{:S(2)}) copy-start(s32[4,16]{1,0:T(4,128)} %refs_0_.31) | copy-start | bytes 772
  1.4 5.6 %copy-start.2 = (f32[4,2,128]{2,1,0:T(2,128)S(1)}, f32[4,2,128]{2,1,0:T(2,128)}, u32[]{:S(2)}) copy-start(f32[4,2,128]{2,1,0:T(2,128)} %param.10) | copy-start | bytes 12292
  3.1 17.7 %collective-permute-start.3 = (bf16[2,48,512]{2,1,0:T(8,128)(2,1)S(1)}, bf16[2,48,512]{2,1,0:T(8,128)(2,1)S(1)}, u32[]{:S(2)}, u32[]{:S(2)}) collective-permute-start(bf16[2,48,512]{2,1,0:T(8,128)(2,1)S(1)} %slice_select_fusion.3), channel_id=1, source_target_pairs={{0,1},{1,0},{2,3},{3,2},{4,5},{5,4},{6,7},{7,6},{8,9},{9,8},{10,11... | collective-permute-start | bytes 294920 | tf_op jit(solution)/shard_map/ppermute | solution.py:244
  5.3 3.6 %copy-start.1 = (s32[4,16]{1,0:T(4,128)S(1)}, s32[4,16]{1,0:T(4,128)}, u32[]{:S(2)}) copy-start(s32[4,16]{1,0:T(4,128)} %refs_1_.31) | copy-start | bytes 772
  5.3 3.6 %collective-permute-start = (bf16[2,48,1536]{2,1,0:T(8,128)(2,1)S(1)}, bf16[2,48,1536]{2,1,0:T(8,128)(2,1)S(1)}, u32[]{:S(2)}, u32[]{:S(2)}) collective-permute-start(bf16[2,48,1536]{2,1,0:T(8,128)(2,1)S(1)} %slice_select_fusion), channel_id=1, source_target_pairs={{0,1},{1,0},{2,3},{3,2},{4,5},{5,4},{6,7},{7,6},{8,9},{9,8},{10,11... | collective-permute-start | bytes 884744 | tf_op jit(solution)/shard_map/ppermute | solution.py:244
  6.2 12.0 %collective-permute-start.2 = (bf16[2,48,1024]{2,1,0:T(8,128)(2,1)S(1)}, bf16[2,48,1024]{2,1,0:T(8,128)(2,1)S(1)}, u32[]{:S(2)}, u32[]{:S(2)}) collective-permute-start(bf16[2,48,1024]{2,1,0:T(8,128)(2,1)S(1)} %get-tuple-element.53), channel_id=1, source_target_pairs={{0,1},{1,0},{2,3},{3,2},{4,5},{5,4},{6,7},{7,6},{8,9},{9,8},{10,11... | collective-permute-start | bytes 589832 | tf_op jit(solution)/shard_map/ppermute | solution.py:244
  6.7 8.9 %collective-permute-start.4 = (bf16[2,48,1024]{2,1,0:T(8,128)(2,1)S(1)}, bf16[2,48,1024]{2,1,0:T(8,128)(2,1)S(1)}, u32[]{:S(2)}, u32[]{:S(2)}) collective-permute-start(bf16[2,48,1024]{2,1,0:T(8,128)(2,1)S(1)} %get-tuple-element.54), channel_id=1, source_target_pairs={{0,1},{1,0},{2,3},{3,2},{4,5},{5,4},{6,7},{7,6},{8,9},{9,8},{10,11... | collective-permute-start | bytes 589832 | tf_op jit(solution)/shard_map/ppermute | solution.py:244
  12.5 10.4 %collective-permute-start.1 = (bf16[2,48,1408]{2,1,0:T(8,128)(2,1)S(1)}, bf16[2,48,1408]{2,1,0:T(8,128)(2,1)S(1)}, u32[]{:S(2)}, u32[]{:S(2)}) collective-permute-start(bf16[2,48,1408]{2,1,0:T(8,128)(2,1)S(1)} %get-tuple-element.30), channel_id=1, source_target_pairs={{0,2},{1,3},{2,0},{3,1},{4,6},{5,7},{6,4},{7,5},{8,10},{9,11},{10,... | collective-permute-start | bytes 811016 | tf_op jit(solution)/shard_map/ppermute | solution.py:244
  25.9 12.6 %collective-permute-start.5 = (bf16[2,48,1280]{2,1,0:T(8,128)(2,1)S(1)}, bf16[2,48,1280]{2,1,0:T(8,128)(2,1)S(1)}, u32[]{:S(2)}, u32[]{:S(2)}) collective-permute-start(bf16[2,48,1280]{2,1,0:T(8,128)(2,1)S(1)} %get-tuple-element.35), channel_id=1, source_target_pairs={{0,4},{1,5},{2,6},{3,7},{4,0},{5,1},{6,2},{7,3},{8,12},{9,13},{10,... | collective-permute-start | bytes 737288 | tf_op jit(solution)/shard_map/ppermute | solution.py:244
  27.6 7.8 %collective-permute-start.6 = (bf16[2,48,1024]{2,1,0:T(8,128)(2,1)S(1)}, bf16[2,48,1024]{2,1,0:T(8,128)(2,1)S(1)}, u32[]{:S(2)}, u32[]{:S(2)}) collective-permute-start(bf16[2,48,1024]{2,1,0:T(8,128)(2,1)S(1)} %get-tuple-element.36), channel_id=1, source_target_pairs={{0,2},{1,3},{2,0},{3,1},{4,6},{5,7},{6,4},{7,5},{8,10},{9,11},{10,... | collective-permute-start | bytes 589832 | tf_op jit(solution)/shard_map/ppermute | solution.py:244
  28.6 12.9 %collective-permute-start.8 = (bf16[2,48,1024]{2,1,0:T(8,128)(2,1)S(1)}, bf16[2,48,1024]{2,1,0:T(8,128)(2,1)S(1)}, u32[]{:S(2)}, u32[]{:S(2)}) collective-permute-start(bf16[2,48,1024]{2,1,0:T(8,128)(2,1)S(1)} %get-tuple-element.40), channel_id=1, source_target_pairs={{0,2},{1,3},{2,0},{3,1},{4,6},{5,7},{6,4},{7,5},{8,10},{9,11},{10,... | collective-permute-start | bytes 589832 | tf_op jit(solution)/shard_map/ppermute | solution.py:244
  29.6 18.8 %collective-permute-start.11 = (bf16[2,48,640]{2,1,0:T(8,128)(2,1)S(1)}, bf16[2,48,640]{2,1,0:T(8,128)(2,1)S(1)}, u32[]{:S(2)}, u32[]{:S(2)}) collective-permute-start(bf16[2,48,640]{2,1,0:T(8,128)(2,1)S(1)} %get-tuple-element.44), channel_id=1, source_target_pairs={{0,2},{1,3},{2,0},{3,1},{4,6},{5,7},{6,4},{7,5},{8,10},{9,11},{10,... | collective-permute-start | bytes 368648 | tf_op jit(solution)/shard_map/ppermute | solution.py:244
  38.0 13.0 %collective-permute-start.9 = (bf16[2,48,1024]{2,1,0:T(8,128)(2,1)S(1)}, bf16[2,48,1024]{2,1,0:T(8,128)(2,1)S(1)}, u32[]{:S(2)}, u32[]{:S(2)}) collective-permute-start(bf16[2,48,1024]{2,1,0:T(8,128)(2,1)S(1)} %get-tuple-element.42), channel_id=1, source_target_pairs={{0,4},{1,5},{2,6},{3,7},{4,0},{5,1},{6,2},{7,3},{8,12},{9,13},{10,... | collective-permute-start | bytes 589832 | tf_op jit(solution)/shard_map/ppermute | solution.py:244
  44.2 10.0 %collective-permute-start.10 = (bf16[2,48,1024]{2,1,0:T(8,128)(2,1)S(1)}, bf16[2,48,1024]{2,1,0:T(8,128)(2,1)S(1)}, u32[]{:S(2)}, u32[]{:S(2)}) collective-permute-start(bf16[2,48,1024]{2,1,0:T(8,128)(2,1)S(1)} %get-tuple-element.43), channel_id=1, source_target_pairs={{0,4},{1,5},{2,6},{3,7},{4,0},{5,1},{6,2},{7,3},{8,12},{9,13},{10,... | collective-permute-start | bytes 589832 | tf_op jit(solution)/shard_map/ppermute | solution.py:244
  45.8 13.5 %collective-permute-start.7 = (bf16[2,48,1152]{2,1,0:T(8,128)(2,1)S(1)}, bf16[2,48,1152]{2,1,0:T(8,128)(2,1)S(1)}, u32[]{:S(2)}, u32[]{:S(2)}) collective-permute-start(bf16[2,48,1152]{2,1,0:T(8,128)(2,1)S(1)} %get-tuple-element.39), channel_id=1, source_target_pairs={{0,8},{1,9},{2,10},{3,11},{4,12},{5,13},{6,14},{7,15},{8,0},{9,1},... | collective-permute-start | bytes 663560 | tf_op jit(solution)/shard_map/ppermute | solution.py:244
  50.5 11.3 %collective-permute-start.13 = (bf16[2,48,768]{2,1,0:T(8,128)(2,1)S(1)}, bf16[2,48,768]{2,1,0:T(8,128)(2,1)S(1)}, u32[]{:S(2)}, u32[]{:S(2)}) collective-permute-start(bf16[2,48,768]{2,1,0:T(8,128)(2,1)S(1)} %get-tuple-element.49), channel_id=1, source_target_pairs={{0,4},{1,5},{2,6},{3,7},{4,0},{5,1},{6,2},{7,3},{8,12},{9,13},{10,... | collective-permute-start | bytes 442376 | tf_op jit(solution)/shard_map/ppermute | solution.py:244
  53.6 19.2 %collective-permute-start.12 = (bf16[2,48,1024]{2,1,0:T(8,128)(2,1)S(1)}, bf16[2,48,1024]{2,1,0:T(8,128)(2,1)S(1)}, u32[]{:S(2)}, u32[]{:S(2)}) collective-permute-start(bf16[2,48,1024]{2,1,0:T(8,128)(2,1)S(1)} %get-tuple-element.48), channel_id=1, source_target_pairs={{0,8},{1,9},{2,10},{3,11},{4,12},{5,13},{6,14},{7,15},{8,0},{9,1},... | collective-permute-start | bytes 589832 | tf_op jit(solution)/shard_map/ppermute | solution.py:244
  56.8 20.2 %collective-permute-start.14 = (bf16[2,48,1024]{2,1,0:T(8,128)(2,1)S(1)}, bf16[2,48,1024]{2,1,0:T(8,128)(2,1)S(1)}, u32[]{:S(2)}, u32[]{:S(2)}) collective-permute-start(bf16[2,48,1024]{2,1,0:T(8,128)(2,1)S(1)} %get-tuple-element.51), channel_id=1, source_target_pairs={{0,8},{1,9},{2,10},{3,11},{4,12},{5,13},{6,14},{7,15},{8,0},{9,1},... | collective-permute-start | bytes 589832 | tf_op jit(solution)/shard_map/ppermute | solution.py:244
  64.4 15.3 %collective-permute-start.15 = (bf16[2,48,896]{2,1,0:T(8,128)(2,1)S(1)}, bf16[2,48,896]{2,1,0:T(8,128)(2,1)S(1)}, u32[]{:S(2)}, u32[]{:S(2)}) collective-permute-start(bf16[2,48,896]{2,1,0:T(8,128)(2,1)S(1)} %get-tuple-element.52), channel_id=1, source_target_pairs={{0,8},{1,9},{2,10},{3,11},{4,12},{5,13},{6,14},{7,15},{8,0},{9,1},... | collective-permute-start | bytes 516104 | tf_op jit(solution)/shard_map/ppermute | solution.py:244

commit v2 on v1

--- a/solution.py
+++ b/solution.py
@@ -102,53 +102,71 @@
     outs = refs[4 + 2 * count:]
     out_ref = outs[0]
     send_ref = None if last else outs[1]
-    wide_ref, stack_ref, sem = outs[1 if last else 2:]
+    wide_ref, even_ref, odd_ref = outs[1 if last else 2:]
     myself = lax.axis_index("pulse")
     half = half_ref[level, myself]
     rows = pl.ds(pl.multiple_of(half * (beams - window), 16), window)
     base = start - LANES
-    copies = []
     for number, (piece, source, target, width) in enumerate(plan):
         for child, ref in ((0, own_refs[number]), (1, far_refs[number])):
+            taken = rows if ref.shape[1] == beams else pl.ds(0, window)
             for part in range(2):
-                taken = rows if child == 0 else pl.ds(0, window)
-                copy = pltpu.make_async_copy(
-                    ref.at[part, taken, pl.ds(source, width)],
-                    wide_ref.at[child, part, :, pl.ds(target - base, width)],
-                    sem.at[child, number, part],
-                )
-                copy.start()
-                copies.append(copy)
+                wide_ref[child, part, :, target - base:target - base + width] = ref[
+                    part, taken, source:source + width
+                ]
+    edge = jnp.zeros((2, 2, window, LANES), jnp.bfloat16)
     if base < 0:
-        wide_ref[:, :, :, 0:LANES] = jnp.zeros((2, 2, window, LANES), jnp.bfloat16)
+        wide_ref[:, :, :, 0:LANES] = edge
     if stop + LANES > length:
-        wide_ref[:, :, :, stop - base:stop - base + LANES] = jnp.zeros(
-            (2, 2, window, LANES), jnp.bfloat16
-        )
+        wide_ref[:, :, :, stop - base:stop - base + LANES] = edge
     shifts = (shift_ref[level, myself], shift_ref[level, jnp.bitwise_xor(myself, 1 << level)])
-    for copy in copies:
-        copy.wait()
     span = stop - start
     tile = min(TILE, span)
-    reach = tile + LANES
-
-    def one_tile(step, carry):
-        column = pl.multiple_of(jnp.minimum(step * tile, span - tile), LANES)
-        for child in range(2):
-            for tap in range(rtaps):
-                shift = shifts[child] + (tap - 1 + LANES)
-                whole = pl.multiple_of(column + shift // LANES * LANES, LANES)
-                turn = lax.rem(reach - lax.rem(shift, LANES), reach)
-                piece = wide_ref[child, :, :, pl.ds(whole, reach)].reshape(2 * window, reach)
-                piece = pltpu.roll(piece, turn, 1)[:, :tile]
-                place = (child * rtaps + tap) * 2 * window
-                stack_ref[place:place + 2 * window, :] = piece
-        both = jnp.dot(mix_ref[0], stack_ref[...], preferred_element_type=jnp.float32)
+    tiles = pl.cdiv(span, tile)
+    lane = lax.broadcasted_iota(jnp.int32, (2 * window, LANES), 1).astype(jnp.int16)
+    moves = []
+    for child in range(2):
+        for tap in range(rtaps):
+            shift = shifts[child] + (tap - 1 + LANES)
+            part_tile = lax.rem(shift, LANES)
+            kept = jnp.full((2 * window, LANES), LANES - part_tile, jnp.int32).astype(jnp.int16)
+            turn = lax.rem(LANES - part_tile, LANES)
+            moves.append((child, tap, shift // LANES * LANES, turn, lane < kept))
+
+    def column_of(step):
+        return pl.multiple_of(jnp.minimum(step * tile, span - tile), LANES)
+
+    def build(stack_ref, step):
+        column = column_of(step)
+        for child, tap, whole, turn, kept in moves:
+            place = (child * rtaps + tap) * 2 * window
+            held = None
+            for block in range(tile // LANES + 1):
+                at = pl.multiple_of(column + whole + block * LANES, LANES)
+                piece = wide_ref[child, :, :, pl.ds(at, LANES)].reshape(2 * window, LANES)
+                piece = pltpu.roll(piece, turn, 1)
+                if block > 0:
+                    columns = pl.ds((block - 1) * LANES, LANES)
+                    stack_ref[place:place + 2 * window, columns] = jnp.where(kept, held, piece)
+                held = piece
+
+    def multiply(stack_ref, step):
+        column = column_of(step)
+        both = jnp.dot(mix_ref[level], stack_ref[...], preferred_element_type=jnp.float32)
         total = (both[:2 * beams] + both[2 * beams:]).astype(jnp.bfloat16)
         out_ref[:, :, pl.ds(column, tile)] = total.reshape(2, beams, tile)
+
+    def two_tiles(pair, carry):
+        build(odd_ref, 2 * pair + 1)
+        multiply(even_ref, 2 * pair)
+        build(even_ref, 2 * pair + 2)
+        multiply(odd_ref, 2 * pair + 1)
         return carry
 
-    lax.fori_loop(0, pl.cdiv(span, tile), one_tile, 0)
+    build(even_ref, 0)
+    lax.fori_loop(0, tiles // 2, two_tiles, 0)
+    if tiles % 2 == 1:
+        multiply(even_ref, tiles - 1)
     if not last:
         following = half_ref[level + 1, myself]
         other = pl.ds(pl.multiple_of((1 - following) * (beams - window), 16), window)
@@ -180,15 +198,13 @@
         functools.partial(
             merge_kernel, level, plan, start, stop, length, beams, window, rtaps, last
         ),
-        grid=(1,),
         out_shape=out_shape,
-        in_specs=[smem, smem, pl.BlockSpec((1, 4 * beams, depth), lambda i: (level, 0, 0))]
-        + [anywhere] * (2 * len(plan) + 1),
+        in_specs=[smem, smem, vmem] + [vmem] * (2 * len(plan)) + [anywhere],
         out_specs=[vmem] * len(out_shape),
         scratch_shapes=[
             pltpu.VMEM((2, 2, window, span + 2 * LANES), jnp.bfloat16),
             pltpu.VMEM((depth, min(TILE, span)), jnp.bfloat16),
-            pltpu.SemaphoreType.DMA((2, len(plan), 2)),
+            pltpu.VMEM((depth, min(TILE, span)), jnp.bfloat16),
         ],
         compiler_params=pltpu.CompilerParams(vmem_limit_bytes=24 * 2**20),
         cost_estimate=pl.CostEstimate(
@@ -207,35 +223,9 @@
     )
 
 
-def merge_order(levels, bounds):
-    sending = [8.0] + [18.0] * (levels - 2) + [36.0]
-    working, fixed = 3.0, 1.0
-    length = bounds[0][-1]
-    ready = {}
-    clock = 3.0
-    link = [clock] * levels
-    for chunk in range(CHUNKS):
-        link[0] += sending[0] * (bounds[0][chunk + 1] - bounds[0][chunk]) / length
-        ready[0, chunk] = link[0]
-    order = []
-    following = [0] * levels
-    while len(order) < levels * CHUNKS:
-        choices = [
-            (ready[level, following[level]], -level, level)
-            for level in range(levels)
-            if (level, following[level]) in ready
-        ]
-        now = [choice for choice in choices if choice[0] <= clock]
-        level = max(choice[2] for choice in now) if now else min(choices)[2]
-        chunk = following[level]
-        following[level] += 1
-        order.append((level, chunk))
-        width = (bounds[level + 1][chunk + 1] - bounds[level + 1][chunk]) / length
-        clock = max(clock, ready[level, chunk]) + fixed + working * width
-        if level < levels - 1:
-            link[level + 1] = max(link[level + 1], clock) + sending[level + 1] * width
-            ready[level + 1, chunk] = link[level + 1]
-    return order
+def merge_order(levels):
+    places = [(level, chunk) for level in range(levels) for chunk in range(CHUNKS)]
+    return sorted(places, key=lambda place: (place[0] + place[1], place[0]))
 
 
 def from_partner(value, bit):
@@ -256,18 +246,12 @@
         [0] + [min(end + (levels - level) * LANES, length) for end in ends]
         for level in range(levels + 1)
     ]
-    half = half_table[0, lax.axis_index("pulse")]
-    own = [beams_in[:, :, low:high] for low, high in zip(bounds[0][:-1], bounds[0][1:])]
-    gap = beams - window
-    send = [
-        jnp.where(half == 0, piece[:, gap:gap + window], piece[:, :window]) for piece in own
-    ]
-    far = [from_partner(piece, 0) for piece in send]
+    bounds[0] = [0, length]
     mix = mixing(ukern, rkern, angles, taps, half_table)
-    owns = [own] + [[None] * CHUNKS for _ in range(levels)]
-    fars = [far] + [[None] * CHUNKS for _ in range(levels - 1)]
+    owns = [[beams_in]] + [[None] * CHUNKS for _ in range(levels)]
+    fars = [[from_partner(beams_in, 0)]] + [[None] * CHUNKS for _ in range(levels - 1)]
     before = mix
-    for level, chunk in merge_order(levels, bounds):
+    for level, chunk in merge_order(levels):
         start, stop = bounds[level + 1][chunk], bounds[level + 1][chunk + 1]
         done = merge(
             level, levels, half_table, shifts, mix, owns[level], fars[level], bounds[level],

time: 83.6 us -> 73.8 us (0.88)
  Pallas kernels: 44.1 us -> 32.9 us
  other arithmetic: 6.58 us -> 2.53 us
  starting transfers between devices: 17.7 us -> 20.4 us
  local copies, waits for them, and re-layouts: 0.19 us -> 2.13 us
  waiting for transfers between devices: 14.5 us -> 15.4 us
    pallas_call x16, Pallas kernels: 42.1 us -> 30.9 us  [merge(): pl.pallas_call(functools.partial(merge_kernel, level, plan, start, stop,...]
    select_n x3 -> x0, other arithmetic: 4.1 us -> none  [on_device(): jnp.where(half == 0, piece[:, gap:gap + window], piece[:, :window])]
    ppermute x16 -> x13, starting transfers between devices: 17.7 us -> 20.4 us  [from_partner(): return lax.ppermute(value, 'pulse', pairs)]
    unnamed x15 -> x9, local copies, waits for them, and re-layouts: 0.11 us -> 2.13 us
    eq x1 -> x0, other arithmetic: 1.35 us -> none  [on_device(): half == 0]
    ppermute x16 -> x13, waiting for transfers between devices: 14.5 us -> 15.4 us  [from_partner(): return lax.ppermute(value, 'pulse', pairs)]
  transfers between devices with their start and end apart: 16 -> 13, of which waited for: 5 -> 4; matrix products, arithmetic and copies ran while one was open for 3% -> 3% of each run, Pallas kernels for 46% -> 36%
where the time goes in v2:
time: 73.8 us; the launch traced here: 73.5 us
  Pallas kernels  32.9 us (45%)
  starting transfers between devices  20.4 us (28%)
  waiting for transfers between devices  15.4 us (21%)
  other arithmetic  2.53 us (3%)
  local copies, waits for them, and re-layouts  2.13 us (3%)
    pallas_call x16, Pallas kernels, merge(): pl.pallas_call(functools.partial(merge_kernel, level, plan, start, stop,...  30.9 us
    ppermute x13, starting transfers between devices, from_partner(): return lax.ppermute(value, 'pulse', pairs)  20.4 us
    ppermute x13, waiting for transfers between devices, from_partner(): return lax.ppermute(value, 'pulse', pairs)  15.4 us
    unnamed x9, local copies, waits for them, and re-layouts  2.13 us
    pallas_call x1, Pallas kernels, mixing(): pl.pallas_call(functools.partial(prep_kernel, levels, beams, utaps), out_...  1.97 us
  transfers between devices with their start and end apart: 13, of which 4 were waited for; matrix products, arithmetic and copies ran while one was open for 3% of the time, Pallas kernels for 36%

profile of v2, /device:TPU:0, one launch (start us, length us, event | category | flops | bytes accessed | tf_op | source)
XLA Modules:
  0.0 73.5 jit_solution(13263259426692965635)
XLA Ops:
  0.0 0.5 collective-permute-start
  0.5 0.7 convert_element_type.3.ukern_ref
  1.1 0.8 %copy.8.rkern_ref = f32[16,4]{1,0:T(8,128)S(1)} copy(f32[16,4]{0,1:T(4,128)} %param.9) | data formatting | bytes 512 | tf_op args[2]
  1.9 0.8 %pad_add_fusion.taps_ref = s32[4,128]{1,0:T(4,128)S(1)} fusion(s32[4,64]{1,0:T(4,128)} %param.11), kind=kLoop, calls=%fused_computation.1 | loop fusion | flops 512 | bytes 3072 | tf_op jit(solution)/shard_map/concatenate | solution.py:93
  2.7 0.7 copy-done.1
  3.4 0.7 copy-done.3
  4.1 2.0 %mixing.1.refs_2_.refs_5_ = bf16[4,256,768]{2,1,0:T(8,128)(2,1)S(1)} custom-call(s32[4,16]{1,0:T(4,128)S(1)} %copy-done.1, f32[16,4]{1,0:T(8,128)S(1)} %copy.8.rkern_ref, f32[8,128]{1,0:T(8,128)S(1)} %bitcast.1, s32[4,128]{1,0:T(4,128)S(1)} %pad_add_fusion.taps_ref, f32[2,32]{1,0:T(2,128)S(1)} %convert_element_type.3.ukern_ref), custom_call_target="tpu_custom_call" | custom-call | tf_op jit(solution)/shard_map/mixing/pallas_call | solution.py:78
  6.1 0.0 collective-permute-done.refs_4_
  6.1 2.5 %merge_0.4 = (bf16[2,64,1408]{2,1,0:T(8,128)(2,1)S(1)}, bf16[2,48,1408]{2,1,0:T(8,128)(2,1)S(1)}) custom-call(s32[4,16]{1,0:T(4,128)S(1)} %copy-done.1, s32[4,16]{1,0:T(4,128)S(1)} %copy-done.2, bf16[4,256,768]{2,1,0:T(8,128)(2,1)S(1)} %mixing.1.refs_2_.refs_5_, bf16[2,64,4096]{2,1,0:T(8,128)(2,1)S(1)} %copy-done, ...), custom_call_target="tpu_custom_call" | custom-call | flops 553648128 | bytes 1441792 | tf_op jit(solution)/shard_map/merge_0/pallas_call | solution.py:197
  8.6 2.7 %collective-permute-start.1 = (bf16[2,48,1408]{2,1,0:T(8,128)(2,1)S(1)}, bf16[2,48,1408]{2,1,0:T(8,128)(2,1)S(1)}, u32[]{:S(2)}, u32[]{:S(2)}) collective-permute-start(bf16[2,48,1408]{2,1,0:T(8,128)(2,1)S(1)} %get-tuple-element.30), channel_id=1, source_target_pairs={{0,2},{1,3},{2,0},{3,1},{4,6},{5,7},{6,4},{7,5},{8,10},{9,11},{10,... | collective-permute-start | bytes 811016 | tf_op jit(solution)/shard_map/ppermute | solution.py:234
  11.2 1.9 %merge_0.5 = (bf16[2,64,1024]{2,1,0:T(8,128)(2,1)S(1)}, bf16[2,48,1024]{2,1,0:T(8,128)(2,1)S(1)}) custom-call(s32[4,16]{1,0:T(4,128)S(1)} %copy-done.1, s32[4,16]{1,0:T(4,128)S(1)} %copy-done.2, bf16[4,256,768]{2,1,0:T(8,128)(2,1)S(1)} %mixing.1.refs_2_.refs_5_, bf16[2,64,4096]{2,1,0:T(8,128)(2,1)S(1)} %copy-done, ...), custom_call_target="tpu_custom_call" | custom-call | flops 402653184 | bytes 1048576 | tf_op jit(solution)/shard_map/merge_0/pallas_call | solution.py:197
  13.2 5.1 %collective-permute-done.1.refs_4_.refs_5_ = bf16[2,48,1408]{2,1,0:T(8,128)(2,1)S(1)} collective-permute-done((bf16[2,48,1408]{2,1,0:T(8,128)(2,1)S(1)}, bf16[2,48,1408]{2,1,0:T(8,128)(2,1)S(1)}, u32[]{:S(2)}, u32[]{:S(2)}) %collective-permute-start.1) | collective-permute-done | bytes 270368 | tf_op jit(solution)/shard_map/ppermute | solution.py:234
  18.3 2.2 %merge_1.4 = (bf16[2,64,1280]{2,1,0:T(8,128)(2,1)S(1)}, bf16[2,48,1280]{2,1,0:T(8,128)(2,1)S(1)}) custom-call(s32[4,16]{1,0:T(4,128)S(1)} %copy-done.1, s32[4,16]{1,0:T(4,128)S(1)} %copy-done.2, bf16[4,256,768]{2,1,0:T(8,128)(2,1)S(1)} %mixing.1.refs_2_.refs_5_, bf16[2,64,1408]{2,1,0:T(8,128)(2,1)S(1)} %get-tuple-element.29.refs_5_.refs_3_, ...), custom_call_target="tpu_custom_call" | custom-call | flops 503316480 | bytes 1310720 | tf_op jit(solution)/shard_map/merge_1/pallas_call | solution.py:197
  20.5 1.9 %collective-permute-start.2 = (bf16[2,48,1280]{2,1,0:T(8,128)(2,1)S(1)}, bf16[2,48,1280]{2,1,0:T(8,128)(2,1)S(1)}, u32[]{:S(2)}, u32[]{:S(2)}) collective-permute-start(bf16[2,48,1280]{2,1,0:T(8,128)(2,1)S(1)} %get-tuple-element.33), channel_id=1, source_target_pairs={{0,4},{1,5},{2,6},{3,7},{4,0},{5,1},{6,2},{7,3},{8,12},{9,13},{10,... | collective-permute-start | bytes 737288 | tf_op jit(solution)/shard_map/ppermute | solution.py:234
  22.3 1.5 %collective-permute-start.3 = (bf16[2,48,1024]{2,1,0:T(8,128)(2,1)S(1)}, bf16[2,48,1024]{2,1,0:T(8,128)(2,1)S(1)}, u32[]{:S(2)}, u32[]{:S(2)}) collective-permute-start(bf16[2,48,1024]{2,1,0:T(8,128)(2,1)S(1)} %get-tuple-element.34), channel_id=1, source_target_pairs={{0,2},{1,3},{2,0},{3,1},{4,6},{5,7},{6,4},{7,5},{8,10},{9,11},{10,... | collective-permute-start | bytes 589832 | tf_op jit(solution)/shard_map/ppermute | solution.py:234
  23.9 1.9 %merge_0.6 = (bf16[2,64,1024]{2,1,0:T(8,128)(2,1)S(1)}, bf16[2,48,1024]{2,1,0:T(8,128)(2,1)S(1)}) custom-call(s32[4,16]{1,0:T(4,128)S(1)} %copy-done.1, s32[4,16]{1,0:T(4,128)S(1)} %copy-done.2, bf16[4,256,768]{2,1,0:T(8,128)(2,1)S(1)} %mixing.1.refs_2_.refs_5_, bf16[2,64,4096]{2,1,0:T(8,128)(2,1)S(1)} %copy-done, ...), custom_call_target="tpu_custom_call" | custom-call | flops 402653184 | bytes 1048576 | tf_op jit(solution)/shard_map/merge_0/pallas_call | solution.py:197
  25.8 0.6 collective-permute-start.6
  26.3 3.1 %collective-permute-done.3.refs_6_.refs_5_ = bf16[2,48,1024]{2,1,0:T(8,128)(2,1)S(1)} collective-permute-done((bf16[2,48,1024]{2,1,0:T(8,128)(2,1)S(1)}, bf16[2,48,1024]{2,1,0:T(8,128)(2,1)S(1)}, u32[]{:S(2)}, u32[]{:S(2)}) %collective-permute-start.3) | collective-permute-done | bytes 196640 | tf_op jit(solution)/shard_map/ppermute | solution.py:234
  29.4 1.9 %merge_1.5 = (bf16[2,64,1024]{2,1,0:T(8,128)(2,1)S(1)}, bf16[2,48,1024]{2,1,0:T(8,128)(2,1)S(1)}) custom-call(s32[4,16]{1,0:T(4,128)S(1)} %copy-done.1, s32[4,16]{1,0:T(4,128)S(1)} %copy-done.2, bf16[4,256,768]{2,1,0:T(8,128)(2,1)S(1)} %mixing.1.refs_2_.refs_5_, bf16[2,64,1408]{2,1,0:T(8,128)(2,1)S(1)} %get-tuple-element.29.refs_5_.refs_3_, ...), custom_call_target="tpu_custom_call" | custom-call | flops 402653184 | bytes 1048576 | tf_op jit(solution)/shard_map/merge_1/pallas_call | solution.py:197
  31.3 0.4 collective-permute-start.5
  31.8 0.0 collective-permute-done.2.refs_4_.refs_5_
  31.8 2.2 %merge_2.4 = (bf16[2,64,1152]{2,1,0:T(8,128)(2,1)S(1)}, bf16[2,48,1152]{2,1,0:T(8,128)(2,1)S(1)}) custom-call(s32[4,16]{1,0:T(4,128)S(1)} %copy-done.1, s32[4,16]{1,0:T(4,128)S(1)} %copy-done.2, bf16[4,256,768]{2,1,0:T(8,128)(2,1)S(1)} %mixing.1.refs_2_.refs_5_, bf16[2,64,1280]{2,1,0:T(8,128)(2,1)S(1)} %get-tuple-element.32.refs_5_.refs_3_, ...), custom_call_target="tpu_custom_call" | custom-call | flops 452984832 | bytes 1179648 | tf_op jit(solution)/shard_map/merge_2/pallas_call | solution.py:197
  33.9 2.8 %collective-permute-start.4 = (bf16[2,48,1152]{2,1,0:T(8,128)(2,1)S(1)}, bf16[2,48,1152]{2,1,0:T(8,128)(2,1)S(1)}, u32[]{:S(2)}, u32[]{:S(2)}) collective-permute-start(bf16[2,48,1152]{2,1,0:T(8,128)(2,1)S(1)} %get-tuple-element.38), channel_id=1, source_target_pairs={{0,8},{1,9},{2,10},{3,11},{4,12},{5,13},{6,14},{7,15},{8,0},{9,1},... | collective-permute-start | bytes 663560 | tf_op jit(solution)/shard_map/ppermute | solution.py:234
  36.7 1.6 %merge_0.7 = (bf16[2,64,640]{2,1,0:T(8,128)(2,1)S(1)}, bf16[2,48,640]{2,1,0:T(8,128)(2,1)S(1)}) custom-call(s32[4,16]{1,0:T(4,128)S(1)} %copy-done.1, s32[4,16]{1,0:T(4,128)S(1)} %copy-done.2, bf16[4,256,768]{2,1,0:T(8,128)(2,1)S(1)} %mixing.1.refs_2_.refs_5_, bf16[2,64,4096]{2,1,0:T(8,128)(2,1)S(1)} %copy-done, ...), custom_call_target="tpu_custom_call" | custom-call | flops 251658240 | bytes 655360 | tf_op jit(solution)/shard_map/merge_0/pallas_call | solution.py:197
  38.3 2.3 %collective-permute-start.9 = (bf16[2,48,640]{2,1,0:T(8,128)(2,1)S(1)}, bf16[2,48,640]{2,1,0:T(8,128)(2,1)S(1)}, u32[]{:S(2)}, u32[]{:S(2)}) collective-permute-start(bf16[2,48,640]{2,1,0:T(8,128)(2,1)S(1)} %get-tuple-element.46), channel_id=1, source_target_pairs={{0,2},{1,3},{2,0},{3,1},{4,6},{5,7},{6,4},{7,5},{8,10},{9,11},{10,... | collective-permute-start | bytes 368648 | tf_op jit(solution)/shard_map/ppermute | solution.py:234
  40.6 0.0 collective-permute-done.6.refs_6_.refs_5_
  40.6 1.9 %merge_1.6 = (bf16[2,64,1024]{2,1,0:T(8,128)(2,1)S(1)}, bf16[2,48,1024]{2,1,0:T(8,128)(2,1)S(1)}) custom-call(s32[4,16]{1,0:T(4,128)S(1)} %copy-done.1, s32[4,16]{1,0:T(4,128)S(1)} %copy-done.2, bf16[4,256,768]{2,1,0:T(8,128)(2,1)S(1)} %mixing.1.refs_2_.refs_5_, bf16[2,64,1024]{2,1,0:T(8,128)(2,1)S(1)} %get-tuple-element.31.refs_5_.refs_4_.refs_3_, ...), custom_call_target="tpu_custom_call" | custom-call | flops 402653184 | bytes 1048576 | tf_op jit(solution)/shard_map/merge_1/pallas_call | solution.py:197
  42.5 1.6 %collective-permute-start.8 = (bf16[2,48,1024]{2,1,0:T(8,128)(2,1)S(1)}, bf16[2,48,1024]{2,1,0:T(8,128)(2,1)S(1)}, u32[]{:S(2)}, u32[]{:S(2)}) collective-permute-start(bf16[2,48,1024]{2,1,0:T(8,128)(2,1)S(1)} %get-tuple-element.45), channel_id=1, source_target_pairs={{0,4},{1,5},{2,6},{3,7},{4,0},{5,1},{6,2},{7,3},{8,12},{9,13},{10,... | collective-permute-start | bytes 589832 | tf_op jit(solution)/shard_map/ppermute | solution.py:234
  44.1 0.0 collective-permute-done.5.refs_6_.refs_5_
  44.1 1.9 %merge_2.5 = (bf16[2,64,1024]{2,1,0:T(8,128)(2,1)S(1)}, bf16[2,48,1024]{2,1,0:T(8,128)(2,1)S(1)}) custom-call(s32[4,16]{1,0:T(4,128)S(1)} %copy-done.1, s32[4,16]{1,0:T(4,128)S(1)} %copy-done.2, bf16[4,256,768]{2,1,0:T(8,128)(2,1)S(1)} %mixing.1.refs_2_.refs_5_, bf16[2,64,1280]{2,1,0:T(8,128)(2,1)S(1)} %get-tuple-element.32.refs_5_.refs_3_, ...), custom_call_target="tpu_custom_call" | custom-call | flops 402653184 | bytes 1048576 | tf_op jit(solution)/shard_map/merge_2/pallas_call | solution.py:197
  46.0 0.4 collective-permute-start.7
  46.5 0.0 collective-permute-done.4.refs_4_.refs_5_
  46.5 1.9 %merge_3.4.refs_7_ = bf16[2,64,1024]{2,1,0:T(8,128)(2,1)S(1)} custom-call(s32[4,16]{1,0:T(4,128)S(1)} %copy-done.1, s32[4,16]{1,0:T(4,128)S(1)} %copy-done.2, bf16[4,256,768]{2,1,0:T(8,128)(2,1)S(1)} %mixing.1.refs_2_.refs_5_, bf16[2,64,1152]{2,1,0:T(8,128)(2,1)S(1)} %get-tuple-element.37.refs_5_.refs_3_, ...), custom_call_target="tpu_custom_call" | custom-call | flops 402653184 | bytes 1048576 | tf_op jit(solution)/shard_map/merge_3/pallas_call | solution.py:197
  48.4 0.0 collective-permute-done.9.refs_6_
  48.4 1.6 %merge_1.7 = (bf16[2,64,768]{2,1,0:T(8,128)(2,1)S(1)}, bf16[2,48,768]{2,1,0:T(8,128)(2,1)S(1)}) custom-call(s32[4,16]{1,0:T(4,128)S(1)} %copy-done.1, s32[4,16]{1,0:T(4,128)S(1)} %copy-done.2, bf16[4,256,768]{2,1,0:T(8,128)(2,1)S(1)} %mixing.1.refs_2_.refs_5_, bf16[2,64,1024]{2,1,0:T(8,128)(2,1)S(1)} %get-tuple-element.35.refs_7_.refs_4_.refs_3_, ...), custom_call_target="tpu_custom_call" | custom-call | flops 301989888 | bytes 786432 | tf_op jit(solution)/shard_map/merge_1/pallas_call | solution.py:197
  50.0 2.2 %collective-permute-start.11 = (bf16[2,48,768]{2,1,0:T(8,128)(2,1)S(1)}, bf16[2,48,768]{2,1,0:T(8,128)(2,1)S(1)}, u32[]{:S(2)}, u32[]{:S(2)}) collective-permute-start(bf16[2,48,768]{2,1,0:T(8,128)(2,1)S(1)} %get-tuple-element.50), channel_id=1, source_target_pairs={{0,4},{1,5},{2,6},{3,7},{4,0},{5,1},{6,2},{7,3},{8,12},{9,13},{10,... | collective-permute-start | bytes 442376 | tf_op jit(solution)/shard_map/ppermute | solution.py:234
  52.2 0.0 collective-permute-done.8.refs_6_.refs_5_
  52.2 1.9 %merge_2.6 = (bf16[2,64,1024]{2,1,0:T(8,128)(2,1)S(1)}, bf16[2,48,1024]{2,1,0:T(8,128)(2,1)S(1)}) custom-call(s32[4,16]{1,0:T(4,128)S(1)} %copy-done.1, s32[4,16]{1,0:T(4,128)S(1)} %copy-done.2, bf16[4,256,768]{2,1,0:T(8,128)(2,1)S(1)} %mixing.1.refs_2_.refs_5_, bf16[2,64,1024]{2,1,0:T(8,128)(2,1)S(1)} %get-tuple-element.36.refs_5_.refs_4_.refs_3_, ...), custom_call_target="tpu_custom_call" | custom-call | flops 402653184 | bytes 1048576 | tf_op jit(solution)/shard_map/merge_2/pallas_call | solution.py:197
  54.1 3.5 %collective-permute-start.10 = (bf16[2,48,1024]{2,1,0:T(8,128)(2,1)S(1)}, bf16[2,48,1024]{2,1,0:T(8,128)(2,1)S(1)}, u32[]{:S(2)}, u32[]{:S(2)}) collective-permute-start(bf16[2,48,1024]{2,1,0:T(8,128)(2,1)S(1)} %get-tuple-element.49), channel_id=1, source_target_pairs={{0,8},{1,9},{2,10},{3,11},{4,12},{5,13},{6,14},{7,15},{8,0},{9,1},... | collective-permute-start | bytes 589832 | tf_op jit(solution)/shard_map/ppermute | solution.py:234
  57.6 0.1 collective-permute-done.7.refs_6_.refs_5_
  57.7 1.9 %merge_3.5.refs_7_ = bf16[2,64,1024]{2,1,0:T(8,128)(2,1)S(1)} custom-call(s32[4,16]{1,0:T(4,128)S(1)} %copy-done.1, s32[4,16]{1,0:T(4,128)S(1)} %copy-done.2, bf16[4,256,768]{2,1,0:T(8,128)(2,1)S(1)} %mixing.1.refs_2_.refs_5_, bf16[2,64,1152]{2,1,0:T(8,128)(2,1)S(1)} %get-tuple-element.37.refs_5_.refs_3_, ...), custom_call_target="tpu_custom_call" | custom-call | flops 402653184 | bytes 1048576 | tf_op jit(solution)/shard_map/merge_3/pallas_call | solution.py:197
  59.6 0.0 collective-permute-done.11.refs_6_
  59.6 1.9 %merge_2.7 = (bf16[2,64,896]{2,1,0:T(8,128)(2,1)S(1)}, bf16[2,48,896]{2,1,0:T(8,128)(2,1)S(1)}) custom-call(s32[4,16]{1,0:T(4,128)S(1)} %copy-done.1, s32[4,16]{1,0:T(4,128)S(1)} %copy-done.2, bf16[4,256,768]{2,1,0:T(8,128)(2,1)S(1)} %mixing.1.refs_2_.refs_5_, bf16[2,64,1024]{2,1,0:T(8,128)(2,1)S(1)} %get-tuple-element.42.refs_7_.refs_4_.refs_3_, ...), custom_call_target="tpu_custom_call" | custom-call | flops 352321536 | bytes 917504 | tf_op jit(solution)/shard_map/merge_2/pallas_call | solution.py:197
  61.5 0.1 collective-permute-start.12
  61.6 7.1 %collective-permute-done.10.refs_6_.refs_5_ = bf16[2,48,1024]{2,1,0:T(8,128)(2,1)S(1)} collective-permute-done((bf16[2,48,1024]{2,1,0:T(8,128)(2,1)S(1)}, bf16[2,48,1024]{2,1,0:T(8,128)(2,1)S(1)}, u32[]{:S(2)}, u32[]{:S(2)}) %collective-permute-start.10) | collective-permute-done | bytes 196640 | tf_op jit(solution)/shard_map/ppermute | solution.py:234
  68.6 1.9 %merge_3.6.refs_7_ = bf16[2,64,1024]{2,1,0:T(8,128)(2,1)S(1)} custom-call(s32[4,16]{1,0:T(4,128)S(1)} %copy-done.1, s32[4,16]{1,0:T(4,128)S(1)} %copy-done.2, bf16[4,256,768]{2,1,0:T(8,128)(2,1)S(1)} %mixing.1.refs_2_.refs_5_, bf16[2,64,1024]{2,1,0:T(8,128)(2,1)S(1)} %get-tuple-element.43.refs_5_.refs_4_.refs_3_, ...), custom_call_target="tpu_custom_call" | custom-call | flops 402653184 | bytes 1048576 | tf_op jit(solution)/shard_map/merge_3/pallas_call | solution.py:197
  70.5 1.9 %merge_3.7 = bf16[2,64,1024]{2,1,0:T(8,128)(2,1)S(1)} custom-call(s32[4,16]{1,0:T(4,128)S(1)} %copy-done.1, s32[4,16]{1,0:T(4,128)S(1)} %copy-done.2, bf16[4,256,768]{2,1,0:T(8,128)(2,1)S(1)} %mixing.1.refs_2_.refs_5_, bf16[2,64,1024]{2,1,0:T(8,128)(2,1)S(1)} %get-tuple-element.48.refs_7_.refs_4_.refs_3_, ...), custom_call_target="tpu_custom_call" | custom-call | flops 402653184 | bytes 1048576 | tf_op jit(solution)/shard_map/merge_3/pallas_call | solution.py:197
  72.4 1.0 %pad_maximum_fusion = bf16[2,64,4096]{2,1,0:T(8,128)(2,1)} fusion(bf16[2,64,1024]{2,1,0:T(8,128)(2,1)S(1)} %merge_3.7, bf16[2,64,1024]{2,1,0:T(8,128)(2,1)S(1)} %merge_3.6.refs_7_, bf16[2,64,1024]{2,1,0:T(8,128)(2,1)S(1)} %merge_3.5.refs_7_, bf16[2,64,1024]{2,1,0:T(8,128)(2,1)S(1)} %merge_3.4.refs_7_), kind=kLoop, calls=%fused_computation | loop fusion | flops 4194304 | bytes 2097152 | tf_op jit(solution)/shard_map/concatenate | solution.py:263
  (7 shorter events, 0.0 us)
Async XLA Ops:
  0.0 6.1 %copy-start = (bf16[2,64,4096]{2,1,0:T(8,128)(2,1)S(1)}, bf16[2,64,4096]{2,1,0:T(8,128)(2,1)}, u32[]{:S(2)}) copy-start(bf16[2,64,4096]{2,1,0:T(8,128)(2,1)} %refs_3_.7) | copy-start | bytes 3145732
  0.0 6.1 %collective-permute-start = (bf16[2,64,4096]{2,1,0:T(8,128)(2,1)}, bf16[2,64,4096]{2,1,0:T(8,128)(2,1)S(1)}, u32[]{:S(2)}, u32[]{:S(2)}) collective-permute-start(bf16[2,64,4096]{2,1,0:T(8,128)(2,1)} %refs_3_.7), channel_id=1, source_target_pairs={{0,1},{1,0},{2,3},{3,2},{4,5},{5,4},{6,7},{7,6},{8,9},{9,8},{10,11... | collective-permute-start | bytes 3145736 | tf_op jit(solution)/shard_map/ppermute | solution.py:234
  2.7 0.7 copy-start.1
  3.4 0.7 copy-start.3
  4.1 2.0 %copy-start.2 = (s32[4,16]{1,0:T(4,128)S(1)}, s32[4,16]{1,0:T(4,128)}, u32[]{:S(2)}) copy-start(s32[4,16]{1,0:T(4,128)} %refs_1_.31) | copy-start | bytes 772
  8.6 9.7 %collective-permute-start.1 = (bf16[2,48,1408]{2,1,0:T(8,128)(2,1)S(1)}, bf16[2,48,1408]{2,1,0:T(8,128)(2,1)S(1)}, u32[]{:S(2)}, u32[]{:S(2)}) collective-permute-start(bf16[2,48,1408]{2,1,0:T(8,128)(2,1)S(1)} %get-tuple-element.30), channel_id=1, source_target_pairs={{0,2},{1,3},{2,0},{3,1},{4,6},{5,7},{6,4},{7,5},{8,10},{9,11},{10,... | collective-permute-start | bytes 811016 | tf_op jit(solution)/shard_map/ppermute | solution.py:234
  20.5 11.3 %collective-permute-start.2 = (bf16[2,48,1280]{2,1,0:T(8,128)(2,1)S(1)}, bf16[2,48,1280]{2,1,0:T(8,128)(2,1)S(1)}, u32[]{:S(2)}, u32[]{:S(2)}) collective-permute-start(bf16[2,48,1280]{2,1,0:T(8,128)(2,1)S(1)} %get-tuple-element.33), channel_id=1, source_target_pairs={{0,4},{1,5},{2,6},{3,7},{4,0},{5,1},{6,2},{7,3},{8,12},{9,13},{10,... | collective-permute-start | bytes 737288 | tf_op jit(solution)/shard_map/ppermute | solution.py:234
  22.3 7.1 %collective-permute-start.3 = (bf16[2,48,1024]{2,1,0:T(8,128)(2,1)S(1)}, bf16[2,48,1024]{2,1,0:T(8,128)(2,1)S(1)}, u32[]{:S(2)}, u32[]{:S(2)}) collective-permute-start(bf16[2,48,1024]{2,1,0:T(8,128)(2,1)S(1)} %get-tuple-element.34), channel_id=1, source_target_pairs={{0,2},{1,3},{2,0},{3,1},{4,6},{5,7},{6,4},{7,5},{8,10},{9,11},{10,... | collective-permute-start | bytes 589832 | tf_op jit(solution)/shard_map/ppermute | solution.py:234
  25.8 14.8 %collective-permute-start.6 = (bf16[2,48,1024]{2,1,0:T(8,128)(2,1)S(1)}, bf16[2,48,1024]{2,1,0:T(8,128)(2,1)S(1)}, u32[]{:S(2)}, u32[]{:S(2)}) collective-permute-start(bf16[2,48,1024]{2,1,0:T(8,128)(2,1)S(1)} %get-tuple-element.40), channel_id=1, source_target_pairs={{0,2},{1,3},{2,0},{3,1},{4,6},{5,7},{6,4},{7,5},{8,10},{9,11},{10,... | collective-permute-start | bytes 589832 | tf_op jit(solution)/shard_map/ppermute | solution.py:234
  31.3 12.8 %collective-permute-start.5 = (bf16[2,48,1024]{2,1,0:T(8,128)(2,1)S(1)}, bf16[2,48,1024]{2,1,0:T(8,128)(2,1)S(1)}, u32[]{:S(2)}, u32[]{:S(2)}) collective-permute-start(bf16[2,48,1024]{2,1,0:T(8,128)(2,1)S(1)} %get-tuple-element.39), channel_id=1, source_target_pairs={{0,4},{1,5},{2,6},{3,7},{4,0},{5,1},{6,2},{7,3},{8,12},{9,13},{10,... | collective-permute-start | bytes 589832 | tf_op jit(solution)/shard_map/ppermute | solution.py:234
  33.9 12.5 %collective-permute-start.4 = (bf16[2,48,1152]{2,1,0:T(8,128)(2,1)S(1)}, bf16[2,48,1152]{2,1,0:T(8,128)(2,1)S(1)}, u32[]{:S(2)}, u32[]{:S(2)}) collective-permute-start(bf16[2,48,1152]{2,1,0:T(8,128)(2,1)S(1)} %get-tuple-element.38), channel_id=1, source_target_pairs={{0,8},{1,9},{2,10},{3,11},{4,12},{5,13},{6,14},{7,15},{8,0},{9,1},... | collective-permute-start | bytes 663560 | tf_op jit(solution)/shard_map/ppermute | solution.py:234
  38.3 10.1 %collective-permute-start.9 = (bf16[2,48,640]{2,1,0:T(8,128)(2,1)S(1)}, bf16[2,48,640]{2,1,0:T(8,128)(2,1)S(1)}, u32[]{:S(2)}, u32[]{:S(2)}) collective-permute-start(bf16[2,48,640]{2,1,0:T(8,128)(2,1)S(1)} %get-tuple-element.46), channel_id=1, source_target_pairs={{0,2},{1,3},{2,0},{3,1},{4,6},{5,7},{6,4},{7,5},{8,10},{9,11},{10,... | collective-permute-start | bytes 368648 | tf_op jit(solution)/shard_map/ppermute | solution.py:234
  42.5 9.7 %collective-permute-start.8 = (bf16[2,48,1024]{2,1,0:T(8,128)(2,1)S(1)}, bf16[2,48,1024]{2,1,0:T(8,128)(2,1)S(1)}, u32[]{:S(2)}, u32[]{:S(2)}) collective-permute-start(bf16[2,48,1024]{2,1,0:T(8,128)(2,1)S(1)} %get-tuple-element.45), channel_id=1, source_target_pairs={{0,4},{1,5},{2,6},{3,7},{4,0},{5,1},{6,2},{7,3},{8,12},{9,13},{10,... | collective-permute-start | bytes 589832 | tf_op jit(solution)/shard_map/ppermute | solution.py:234
  46.0 11.6 %collective-permute-start.7 = (bf16[2,48,1024]{2,1,0:T(8,128)(2,1)S(1)}, bf16[2,48,1024]{2,1,0:T(8,128)(2,1)S(1)}, u32[]{:S(2)}, u32[]{:S(2)}) collective-permute-start(bf16[2,48,1024]{2,1,0:T(8,128)(2,1)S(1)} %get-tuple-element.44), channel_id=1, source_target_pairs={{0,8},{1,9},{2,10},{3,11},{4,12},{5,13},{6,14},{7,15},{8,0},{9,1},... | collective-permute-start | bytes 589832 | tf_op jit(solution)/shard_map/ppermute | solution.py:234
  50.0 9.6 %collective-permute-start.11 = (bf16[2,48,768]{2,1,0:T(8,128)(2,1)S(1)}, bf16[2,48,768]{2,1,0:T(8,128)(2,1)S(1)}, u32[]{:S(2)}, u32[]{:S(2)}) collective-permute-start(bf16[2,48,768]{2,1,0:T(8,128)(2,1)S(1)} %get-tuple-element.50), channel_id=1, source_target_pairs={{0,4},{1,5},{2,6},{3,7},{4,0},{5,1},{6,2},{7,3},{8,12},{9,13},{10,... | collective-permute-start | bytes 442376 | tf_op jit(solution)/shard_map/ppermute | solution.py:234
  54.1 14.5 %collective-permute-start.10 = (bf16[2,48,1024]{2,1,0:T(8,128)(2,1)S(1)}, bf16[2,48,1024]{2,1,0:T(8,128)(2,1)S(1)}, u32[]{:S(2)}, u32[]{:S(2)}) collective-permute-start(bf16[2,48,1024]{2,1,0:T(8,128)(2,1)S(1)} %get-tuple-element.49), channel_id=1, source_target_pairs={{0,8},{1,9},{2,10},{3,11},{4,12},{5,13},{6,14},{7,15},{8,0},{9,1},... | collective-permute-start | bytes 589832 | tf_op jit(solution)/shard_map/ppermute | solution.py:234
  61.5 9.0 %collective-permute-start.12 = (bf16[2,48,896]{2,1,0:T(8,128)(2,1)S(1)}, bf16[2,48,896]{2,1,0:T(8,128)(2,1)S(1)}, u32[]{:S(2)}, u32[]{:S(2)}) collective-permute-start(bf16[2,48,896]{2,1,0:T(8,128)(2,1)S(1)} %get-tuple-element.52), channel_id=1, source_target_pairs={{0,8},{1,9},{2,10},{3,11},{4,12},{5,13},{6,14},{7,15},{8,0},{9,1},... | collective-permute-start | bytes 516104 | tf_op jit(solution)/shard_map/ppermute | solution.py:234

commit v3 on v2

--- a/solution.py
+++ b/solution.py
@@ -9,14 +9,13 @@
 
 LANES = 128
 TILE = 256
-CHUNKS = 4
 SCALE = 0.70710678
 
 
-def prep_kernel(levels, beams, utaps, half_ref, rkern_ref, angles_ref, taps_ref, ukern_ref,
-                mix_ref, band_ref, flat_ref):
+def prep_kernel(levels, beams, utaps, phases, rtaps, whole_ref, real_ref, mix_ref, plan_ref, band_ref, flat_ref):
+    at_shifts, at_taps = levels, 2 * levels
+    at_ukern, at_rkern = 2 * levels, 2 * levels + 2
     window = beams // 2 + utaps // 2
-    phases, rtaps = rkern_ref.shape
     myself = lax.axis_index("pulse")
     lane = lax.broadcasted_iota(jnp.int32, (1, 2 * beams), 1)
     first = lane < beams
@@ -24,30 +23,50 @@
     depth = beams // 2 + utaps
     row = lax.broadcasted_iota(jnp.int32, (depth, 2 * beams), 0)
     offset = row - beam // 2 - 1
+    even = beam % 2 == 0
+    halves = whole_ref[0:levels, :].astype(jnp.float32)
+    shifts = whole_ref[at_shifts:at_shifts + levels, :].astype(jnp.float32)
+    place = lax.broadcasted_iota(jnp.int32, (levels, LANES), 1)
+    level_of = lax.broadcasted_iota(jnp.int32, (levels, LANES), 0)
+    partner = jnp.bitwise_xor(myself, lax.shift_left(jnp.ones_like(level_of), level_of))
+
+    def pick(table, index):
+        return jnp.sum(jnp.where(place == index, table, 0.0), axis=1, keepdims=True)
+
+    half_of = pick(halves, myself)
+    after_of = jnp.concatenate([half_of[1:], half_of[:1]], axis=0)
+    near_of = pick(shifts, myself) + LANES
+    far_of = pick(shifts, partner) + LANES
+    codes = ((half_of * 2 + after_of) * 256 + near_of) * 256 + far_of
+    for level in range(levels):
+        plan_ref[level] = jnp.broadcast_to(codes[level:level + 1, :], (8, LANES))
+    kernel = real_ref[at_ukern:at_ukern + 2, :]
     band = jnp.zeros((depth, 2 * beams), jnp.float32)
-    even = beam % 2 == 0
     for k in range(utaps):
-        value = jnp.where(even, ukern_ref[0, k], ukern_ref[1, k])
+        value = jnp.where(even, kernel[0:1, k:k + 1], kernel[1:2, k:k + 1])
         band = jnp.where(offset == k, value, band)
     band_ref[...] = band
-
-    def one_level(level, carry):
-        half = half_ref[level, myself]
+    table = real_ref[at_rkern:at_rkern + rtaps, :]
+    for level in range(levels):
+        low_half = half_of[level:level + 1, :] == 0.0
         bit = lax.rem(lax.shift_right_logical(myself, level), 2)
-        start = pl.multiple_of((1 - half) * (utaps // 2), 8)
-        near = band_ref[pl.ds(start, window), :]
-        chosen = taps_ref[pl.ds(level, 1), :]
+        near = jnp.where(
+            low_half, band_ref[utaps // 2:utaps // 2 + window, :], band_ref[0:window, :]
+        )
+        chosen = whole_ref[at_taps + level:at_taps + level + 1, :]
         weights = []
         for tap in range(rtaps):
             weight = jnp.zeros((1, 2 * beams), jnp.float32)
             for phase in range(phases):
-                weight = jnp.where(chosen == phase, rkern_ref[phase, tap], weight)
+                weight = jnp.where(
+                    chosen == phase, table[tap:tap + 1, phase:phase + 1], weight
+                )
             weights.append(weight)
         for child in range(2):
             side = bit if child == 0 else 1 - bit
-            angle = angles_ref[pl.ds(2 * level + side, 1), :]
+            angle = real_ref[pl.ds(2 * level + side, 1), :]
             turned = pltpu.roll(angle, beams, 1)
-            angle = jnp.where(first == (half == 0), angle, turned)
+            angle = jnp.where(first == low_half, angle, turned)
             cosine = SCALE * jnp.cos(angle)
             sine = SCALE * jnp.sin(angle)
             factors = (jnp.where(first, cosine, sine), jnp.where(first, -sine, cosine))
@@ -62,49 +81,74 @@
             columns = pl.ds(block * LANES, LANES)
             mix_ref[level, 0:2 * beams, columns] = high
             mix_ref[level, 2 * beams:4 * beams, columns] = low
-        return carry
-
-    lax.fori_loop(0, levels, one_level, 0)
-
-
-def mixing(ukern, rkern, angles, taps, half_table):
+
+
+def stacked(height, pieces):
+    total = jnp.zeros((height, LANES), pieces[0][0].dtype)
+    for piece, top, left in pieces:
+        below, right = height - top - piece.shape[0], LANES - left - piece.shape[1]
+        zero = jnp.zeros((), piece.dtype)
+        total = total + lax.pad(piece, zero, ((top, below, 0), (left, right, 0)))
+    return total
+
+
+def mixing(ukern, rkern, angles, taps, shifts, half_table):
     levels = half_table.shape[0]
     beams = taps.shape[1]
     utaps = ukern.shape[1]
+    phases, rtaps = rkern.shape
     window = beams // 2 + utaps // 2
-    depth = 2 * rkern.shape[1] * 2 * window
-    smem = pl.BlockSpec(memory_space=pltpu.SMEM)
+    depth = 2 * rtaps * 2 * window
     vmem = pl.BlockSpec(memory_space=pltpu.VMEM)
+
+    whole = stacked(
+        3 * levels,
+        [
+            (half_table, 0, 0),
+            (shifts, levels, 0),
+            (taps, 2 * levels, 0),
+            (taps, 2 * levels, beams),
+        ],
+    )
+    real = stacked(
+        2 * levels + 2 + rtaps,
+        [
+            (angles.reshape(2 * levels, 2 * beams), 0, 0),
+            (ukern.astype(jnp.float32), 2 * levels, 0),
+            (rkern.T, 2 * levels + 2, 0),
+        ],
+    )
     return pl.pallas_call(
-        functools.partial(prep_kernel, levels, beams, utaps),
-        out_shape=jax.ShapeDtypeStruct((levels, 4 * beams, depth), jnp.bfloat16),
-        in_specs=[smem, smem, vmem, vmem, smem],
-        out_specs=vmem,
+        functools.partial(prep_kernel, levels, beams, utaps, phases, rtaps),
+        out_shape=[
+            jax.ShapeDtypeStruct((levels, 4 * beams, depth), jnp.bfloat16),
+            jax.ShapeDtypeStruct((levels, 8, LANES), jnp.float32),
+        ],
+        in_specs=[vmem, vmem],
+        out_specs=[vmem, vmem],
         scratch_shapes=[
             pltpu.VMEM((beams // 2 + utaps, 2 * beams), jnp.float32),
             pltpu.VMEM((depth, 2 * beams), jnp.float32),
         ],
         compiler_params=pltpu.CompilerParams(vmem_limit_bytes=24 * 2**20),
+        cost_estimate=pl.CostEstimate(
+            flops=2 * 10**9, bytes_accessed=2 * levels * 4 * beams * depth, transcendentals=0
+        ),
         name="mixing",
-    )(
-        half_table,
-        rkern,
-        angles.reshape(2 * levels, 2 * beams),
-        jnp.concatenate([taps, taps], axis=1),
-        ukern.astype(jnp.float32),
-    )
+    )(whole, real)
 
 
 def merge_kernel(level, plan, start, stop, length, beams, window, rtaps, last, *refs):
-    half_ref, shift_ref, mix_ref = refs[:3]
+    code_ref, mix_ref = refs[:2]
     count = len(plan)
-    own_refs, far_refs = refs[3:3 + count], refs[3 + count:3 + 2 * count]
-    outs = refs[4 + 2 * count:]
+    own_refs, far_refs = refs[2:2 + count], refs[2 + count:2 + 2 * count]
+    outs = refs[3 + 2 * count:]
     out_ref = outs[0]
     send_ref = None if last else outs[1]
     wide_ref, even_ref, odd_ref = outs[1 if last else 2:]
-    myself = lax.axis_index("pulse")
-    half = half_ref[level, myself]
+    code = jnp.max(code_ref[level]).astype(jnp.int32)
+    half, following = code // 131072, code // 65536 % 2
+    shifts = (code // 256 % 256 - LANES, code % 256 - LANES)
     rows = pl.ds(pl.multiple_of(half * (beams - window), 16), window)
     base = start - LANES
     for number, (piece, source, target, width) in enumerate(plan):
@@ -119,7 +163,6 @@
         wide_ref[:, :, :, 0:LANES] = edge
     if stop + LANES > length:
         wide_ref[:, :, :, stop - base:stop - base + LANES] = edge
-    shifts = (shift_ref[level, myself], shift_ref[level, jnp.bitwise_xor(myself, 1 << level)])
     span = stop - start
     tile = min(TILE, span)
     tiles = pl.cdiv(span, tile)
@@ -168,7 +211,6 @@
     if tiles % 2 == 1:
         multiply(even_ref, tiles - 1)
     if not last:
-        following = half_ref[level + 1, myself]
         other = pl.ds(pl.multiple_of((1 - following) * (beams - window), 16), window)
         send_ref[...] = out_ref[:, other, :]
 
@@ -182,12 +224,11 @@
     return found
 
 
-def merge(level, levels, half_table, shifts, mix, own, far, bounds, start, stop, sizes, before):
+def merge(level, levels, codes, mix, own, far, bounds, start, stop, sizes, before):
     beams, window, rtaps, length = sizes
     last = level == levels - 1
     plan = pieces_of(bounds, max(start - LANES, 0), min(stop + LANES, length))
     span = stop - start
-    smem = pl.BlockSpec(memory_space=pltpu.SMEM)
     vmem = pl.BlockSpec(memory_space=pltpu.VMEM)
     anywhere = pl.BlockSpec(memory_space=pl.ANY)
     depth = mix.shape[2]
@@ -199,7 +240,7 @@
             merge_kernel, level, plan, start, stop, length, beams, window, rtaps, last
         ),
         out_shape=out_shape,
-        in_specs=[smem, smem, vmem] + [vmem] * (2 * len(plan)) + [anywhere],
+        in_specs=[vmem, vmem] + [vmem] * (2 * len(plan)) + [anywhere],
         out_specs=[vmem] * len(out_shape),
         scratch_shapes=[
             pltpu.VMEM((2, 2, window, span + 2 * LANES), jnp.bfloat16),
@@ -208,14 +249,13 @@
         ],
         compiler_params=pltpu.CompilerParams(vmem_limit_bytes=24 * 2**20),
         cost_estimate=pl.CostEstimate(
-            flops=2 * 4 * beams * depth * span,
-            bytes_accessed=8 * beams * span * 2,
+            flops=32 * beams * depth * span,
+            bytes_accessed=0,
             transcendentals=0,
         ),
         name=f"merge_{level}",
     )(
-        half_table,
-        shifts,
+        codes,
         mix,
         *[own[piece[0]] for piece in plan],
         *[far[piece[0]] for piece in plan],
@@ -223,9 +263,44 @@
     )
 
 
-def merge_order(levels):
-    places = [(level, chunk) for level in range(levels) for chunk in range(CHUNKS)]
-    return sorted(places, key=lambda place: (place[0] + place[1], place[0]))
+def chunk_bounds(level, levels, length):
+    marks = ((4, 12, 20, 28), (6, 14, 21, 29), (7, 16, 22), (8, 18))
+    tiles = length // LANES
+    chosen = marks[min(levels - level, len(marks) - 1)]
+    inner = [tiles * mark // 32 for mark in chosen]
+    return [0] + [mark * LANES for mark in inner] + [length]
+
+
+def merge_order(levels, bounds):
+    length = bounds[0][-1]
+    sending = [18.0] * (levels - 1) + [36.0]
+    fixed, working, starting, flying = 0.75, 9.0, 1.5, 2.0
+    clock = 5.0
+    arrival = {(0, 0): clock}
+    busy = [clock] * levels
+    following = [0] * levels
+    order = []
+    while len(order) < sum(len(bound) - 1 for bound in bounds[1:]):
+        choices = []
+        for level in range(levels):
+            chunk = following[level]
+            if chunk == len(bounds[level + 1]) - 1:
+                continue
+            needed = pieces_of(bounds[level], 0, min(bounds[level + 1][chunk + 1] + LANES, length))
+            times = [arrival.get((level, piece[0])) for piece in needed]
+            if None not in times:
+                choices.append((max(times + [clock]), -level, chunk))
+        begin, level, chunk = min(choices)
+        level = -level
+        following[level] += 1
+        order.append((level, chunk))
+        width = (bounds[level + 1][chunk + 1] - bounds[level + 1][chunk]) / length
+        clock = begin + fixed + working * width
+        if level < levels - 1:
+            clock += starting
+            busy[level + 1] = max(busy[level + 1], clock) + sending[level + 1] * width
+            arrival[level + 1, chunk] = busy[level + 1] + flying
+    return order
 
 
 def from_partner(value, bit):
@@ -240,21 +315,16 @@
     window = beams // 2 + utaps // 2
     levels = half_table.shape[0]
     sizes = (beams, window, rtaps, length)
-    step = length // CHUNKS
-    ends = [min((chunk + 1) * step, length) for chunk in range(CHUNKS)]
-    bounds = [
-        [0] + [min(end + (levels - level) * LANES, length) for end in ends]
-        for level in range(levels + 1)
-    ]
-    bounds[0] = [0, length]
-    mix = mixing(ukern, rkern, angles, taps, half_table)
-    owns = [[beams_in]] + [[None] * CHUNKS for _ in range(levels)]
-    fars = [[from_partner(beams_in, 0)]] + [[None] * CHUNKS for _ in range(levels - 1)]
+    bounds = [[0, length]]
+    bounds += [chunk_bounds(level, levels, length) for level in range(1, levels + 1)]
+    mix, codes = mixing(ukern, rkern, angles, taps, shifts, half_table)
+    owns = [[beams_in]] + [[None] * (len(bound) - 1) for bound in bounds[1:]]
+    fars = [[from_partner(beams_in, 0)]] + [[None] * (len(bound) - 1) for bound in bounds[1:]]
     before = mix
-    for level, chunk in merge_order(levels):
+    for level, chunk in merge_order(levels, bounds):
         start, stop = bounds[level + 1][chunk], bounds[level + 1][chunk + 1]
         done = merge(
-            level, levels, half_table, shifts, mix, owns[level], fars[level], bounds[level],
+            level, levels, codes, mix, owns[level], fars[level], bounds[level],
             start, stop, sizes, before,
         )
         before = owns[level + 1][chunk] = done[0]

time: 73.8 us -> 70.4 us (0.954)
  Pallas kernels: 32.9 us -> 24.5 us
  waiting for transfers between devices: 15.4 us -> 22.2 us
  local copies, waits for them, and re-layouts: 2.13 us -> 1.1 us
  other arithmetic: 2.53 us -> 1.54 us
    pallas_call x16 -> x17, Pallas kernels: 30.9 us -> 23.7 us  [merge(): pl.pallas_call(functools.partial(merge_kernel, level, plan, start, stop,...]
    ppermute x13, waiting for transfers between devices: 15.4 us -> 22.2 us  [from_partner(): return lax.ppermute(value, 'pulse', pairs)]
    concatenate x2 -> x0, other arithmetic: 1.87 us -> none  [the longest x1 1.04 us: on_device(): return jnp.concatenate(owns[levels], axis=2)]
    unnamed x9 -> x8, local copies, waits for them, and re-layouts: 2.13 us -> 0.44 us
    add x0 -> x2, other arithmetic: none -> 1.54 us  [stacked(): total = total + lax.pad(piece, zero, ((top, below, 0), (left, right, 0)))]
    pallas_call x1, Pallas kernels: 1.97 us -> 0.85 us  [mixing(): pl.pallas_call(functools.partial(prep_kernel, levels, beams, utaps, phase...]
  transfers between devices with their start and end apart: 13 -> 13, of which waited for: 4 -> 7; matrix products, arithmetic and copies ran while one was open for 3% -> 2% of each run, Pallas kernels for 36% -> 32%
where the time goes in v3:
time: 70.4 us; the launch traced here: 70.2 us
  Pallas kernels  24.5 us (35%)
  waiting for transfers between devices  22.2 us (32%)
  starting transfers between devices  20.6 us (29%)
  other arithmetic  1.54 us (2%)
  local copies, waits for them, and re-layouts  1.1 us (2%)
    pallas_call x17, Pallas kernels, merge(): pl.pallas_call(functools.partial(merge_kernel, level, plan, start, stop,...  23.7 us
    ppermute x13, waiting for transfers between devices, from_partner(): return lax.ppermute(value, 'pulse', pairs)  22.2 us
    ppermute x13, starting transfers between devices, from_partner(): return lax.ppermute(value, 'pulse', pairs)  20.6 us
    add x2, other arithmetic, stacked(): total = total + lax.pad(piece, zero, ((top, below, 0), (left, right, 0)))  1.54 us
  transfers between devices with their start and end apart: 13, of which 7 were waited for; matrix products, arithmetic and copies ran while one was open for 2% of the time, Pallas kernels for 32%

profile of v3, /device:TPU:0, one launch (start us, length us, event | category | flops | bytes accessed | tf_op | source)
XLA Modules:
  0.0 70.2 jit_solution(3643218972974509839)
XLA Ops:
  0.0 0.5 collective-permute-start
  0.5 0.7 %pad_add_fusion.real_ref = f32[14,128]{1,0:T(8,128)S(1)} fusion(f32[4,16]{1,0:T(4,128)} %bitcast.3, f32[8,128]{1,0:T(8,128)} %bitcast.2, bf16[2,32]{1,0:T(2,128)(2,1)} %param.8), kind=kLoop, calls=%fused_computation.5 | loop fusion | flops 5376 | bytes 11648 | tf_op jit(solution)/shard_map/add | solution.py:91
  1.2 0.8 %pad_add_fusion.1.whole_ref = s32[12,128]{1,0:T(8,128)S(1)} fusion(s32[4,64]{1,0:T(4,128)} %param.11, s32[4,16]{1,0:T(4,128)} %param.12, s32[4,16]{1,0:T(4,128)} %param.13), kind=kLoop, calls=%fused_computation.6 | loop fusion | flops 4608 | bytes 7680 | tf_op jit(solution)/shard_map/add | solution.py:91
  2.0 0.9 %mixing.1 = (bf16[4,256,768]{2,1,0:T(8,128)(2,1)S(1)}, f32[4,8,128]{2,1,0:T(8,128)S(1)}) custom-call(s32[12,128]{1,0:T(8,128)S(1)} %pad_add_fusion.1.whole_ref, f32[14,128]{1,0:T(8,128)S(1)} %pad_add_fusion.real_ref), custom_call_target="tpu_custom_call" | custom-call | flops 2000000000 | bytes 1572864 | tf_op jit(solution)/shard_map/mixing/pallas_call | solution.py:121
  2.9 0.1 collective-permute-done.refs_3_
  3.0 0.3 copy-done
  3.2 1.4 %merge_0.3 = (bf16[2,64,1024]{2,1,0:T(8,128)(2,1)S(1)}, bf16[2,48,1024]{2,1,0:T(8,128)(2,1)S(1)}) custom-call(f32[4,8,128]{2,1,0:T(8,128)S(1)} %get-tuple-element.31.refs_0_, bf16[4,256,768]{2,1,0:T(8,128)(2,1)S(1)} %get-tuple-element.32.refs_1_.refs_4_, bf16[2,64,4096]{2,1,0:T(8,128)(2,1)S(1)} %copy-done, ...), custom_call_target="tpu_custom_call" | custom-call | flops 1610612736 | tf_op jit(solution)/shard_map/merge_0/pallas_call | solution.py:238
  4.7 2.7 %collective-permute-start.1 = (bf16[2,48,1024]{2,1,0:T(8,128)(2,1)S(1)}, bf16[2,48,1024]{2,1,0:T(8,128)(2,1)S(1)}, u32[]{:S(2)}, u32[]{:S(2)}) collective-permute-start(bf16[2,48,1024]{2,1,0:T(8,128)(2,1)S(1)} %get-tuple-element.34), channel_id=1, source_target_pairs={{0,2},{1,3},{2,0},{3,1},{4,6},{5,7},{6,4},{7,5},{8,10},{9,11},{10,... | collective-permute-start | bytes 589832 | tf_op jit(solution)/shard_map/ppermute | solution.py:309
  7.4 1.7 %merge_0.4 = (bf16[2,64,1280]{2,1,0:T(8,128)(2,1)S(1)}, bf16[2,48,1280]{2,1,0:T(8,128)(2,1)S(1)}) custom-call(f32[4,8,128]{2,1,0:T(8,128)S(1)} %get-tuple-element.31.refs_0_, bf16[4,256,768]{2,1,0:T(8,128)(2,1)S(1)} %get-tuple-element.32.refs_1_.refs_4_, bf16[2,64,4096]{2,1,0:T(8,128)(2,1)S(1)} %copy-done, ...), custom_call_target="tpu_custom_call" | custom-call | flops 2013265920 | tf_op jit(solution)/shard_map/merge_0/pallas_call | solution.py:238
  9.1 0.1 collective-permute-start.3
  9.1 2.3 %merge_0.5 = (bf16[2,64,1792]{2,1,0:T(8,128)(2,1)S(1)}, bf16[2,48,1792]{2,1,0:T(8,128)(2,1)S(1)}) custom-call(f32[4,8,128]{2,1,0:T(8,128)S(1)} %get-tuple-element.31.refs_0_, bf16[4,256,768]{2,1,0:T(8,128)(2,1)S(1)} %get-tuple-element.32.refs_1_.refs_4_, bf16[2,64,4096]{2,1,0:T(8,128)(2,1)S(1)} %copy-done, ...), custom_call_target="tpu_custom_call" | custom-call | flops 2818572288 | tf_op jit(solution)/shard_map/merge_0/pallas_call | solution.py:238
  11.5 2.1 %collective-permute-start.4 = (bf16[2,48,1792]{2,1,0:T(8,128)(2,1)S(1)}, bf16[2,48,1792]{2,1,0:T(8,128)(2,1)S(1)}, u32[]{:S(2)}, u32[]{:S(2)}) collective-permute-start(bf16[2,48,1792]{2,1,0:T(8,128)(2,1)S(1)} %get-tuple-element.40), channel_id=1, source_target_pairs={{0,2},{1,3},{2,0},{3,1},{4,6},{5,7},{6,4},{7,5},{8,10},{9,11},{10,... | collective-permute-start | bytes 1032200 | tf_op jit(solution)/shard_map/ppermute | solution.py:309
  13.5 0.0 collective-permute-done.1.refs_3_.refs_4_
  13.5 1.5 %merge_1.4 = (bf16[2,64,896]{2,1,0:T(8,128)(2,1)S(1)}, bf16[2,48,896]{2,1,0:T(8,128)(2,1)S(1)}) custom-call(f32[4,8,128]{2,1,0:T(8,128)S(1)} %get-tuple-element.31.refs_0_, bf16[4,256,768]{2,1,0:T(8,128)(2,1)S(1)} %get-tuple-element.32.refs_1_.refs_4_, bf16[2,64,1024]{2,1,0:T(8,128)(2,1)S(1)} %get-tuple-element.33.refs_4_.refs_2_, ...), custom_call_target="tpu_custom_call" | custom-call | flops 1409286144 | tf_op jit(solution)/shard_map/merge_1/pallas_call | solution.py:238
  15.0 1.6 %collective-permute-start.2 = (bf16[2,48,896]{2,1,0:T(8,128)(2,1)S(1)}, bf16[2,48,896]{2,1,0:T(8,128)(2,1)S(1)}, u32[]{:S(2)}, u32[]{:S(2)}) collective-permute-start(bf16[2,48,896]{2,1,0:T(8,128)(2,1)S(1)} %get-tuple-element.38), channel_id=1, source_target_pairs={{0,4},{1,5},{2,6},{3,7},{4,0},{5,1},{6,2},{7,3},{8,12},{9,13},{10,... | collective-permute-start | bytes 516104 | tf_op jit(solution)/shard_map/ppermute | solution.py:309
  16.7 1.7 %collective-permute-done.3.refs_5_.refs_4_ = bf16[2,48,1280]{2,1,0:T(8,128)(2,1)S(1)} collective-permute-done((bf16[2,48,1280]{2,1,0:T(8,128)(2,1)S(1)}, bf16[2,48,1280]{2,1,0:T(8,128)(2,1)S(1)}, u32[]{:S(2)}, u32[]{:S(2)}) %collective-permute-start.3) | collective-permute-done | bytes 245792 | tf_op jit(solution)/shard_map/ppermute | solution.py:309
  18.4 1.7 %merge_1.5 = (bf16[2,64,1152]{2,1,0:T(8,128)(2,1)S(1)}, bf16[2,48,1152]{2,1,0:T(8,128)(2,1)S(1)}) custom-call(f32[4,8,128]{2,1,0:T(8,128)S(1)} %get-tuple-element.31.refs_0_, bf16[4,256,768]{2,1,0:T(8,128)(2,1)S(1)} %get-tuple-element.32.refs_1_.refs_4_, bf16[2,64,1024]{2,1,0:T(8,128)(2,1)S(1)} %get-tuple-element.33.refs_4_.refs_2_, ...), custom_call_target="tpu_custom_call" | custom-call | flops 1811939328 | tf_op jit(solution)/shard_map/merge_1/pallas_call | solution.py:238
  20.1 2.1 %collective-permute-start.6 = (bf16[2,48,1152]{2,1,0:T(8,128)(2,1)S(1)}, bf16[2,48,1152]{2,1,0:T(8,128)(2,1)S(1)}, u32[]{:S(2)}, u32[]{:S(2)}) collective-permute-start(bf16[2,48,1152]{2,1,0:T(8,128)(2,1)S(1)} %get-tuple-element.45), channel_id=1, source_target_pairs={{0,4},{1,5},{2,6},{3,7},{4,0},{5,1},{6,2},{7,3},{8,12},{9,13},{10,... | collective-permute-start | bytes 663560 | tf_op jit(solution)/shard_map/ppermute | solution.py:309
  22.2 3.3 %collective-permute-done.4.refs_5_.refs_3_ = bf16[2,48,1792]{2,1,0:T(8,128)(2,1)S(1)} collective-permute-done((bf16[2,48,1792]{2,1,0:T(8,128)(2,1)S(1)}, bf16[2,48,1792]{2,1,0:T(8,128)(2,1)S(1)}, u32[]{:S(2)}, u32[]{:S(2)}) %collective-permute-start.4) | collective-permute-done | bytes 344096 | tf_op jit(solution)/shard_map/ppermute | solution.py:309
  25.5 1.1 %merge_1.6 = (bf16[2,64,768]{2,1,0:T(8,128)(2,1)S(1)}, bf16[2,48,768]{2,1,0:T(8,128)(2,1)S(1)}) custom-call(f32[4,8,128]{2,1,0:T(8,128)S(1)} %get-tuple-element.31.refs_0_, bf16[4,256,768]{2,1,0:T(8,128)(2,1)S(1)} %get-tuple-element.32.refs_1_.refs_4_, bf16[2,64,1280]{2,1,0:T(8,128)(2,1)S(1)} %get-tuple-element.35.refs_4_.refs_3_.refs_2_, ...), custom_call_target="tpu_custom_call" | custom-call | flops 1207959552 | tf_op jit(solution)/shard_map/merge_1/pallas_call | solution.py:238
  26.6 1.9 %collective-permute-start.7 = (bf16[2,48,768]{2,1,0:T(8,128)(2,1)S(1)}, bf16[2,48,768]{2,1,0:T(8,128)(2,1)S(1)}, u32[]{:S(2)}, u32[]{:S(2)}) collective-permute-start(bf16[2,48,768]{2,1,0:T(8,128)(2,1)S(1)} %get-tuple-element.46), channel_id=1, source_target_pairs={{0,4},{1,5},{2,6},{3,7},{4,0},{5,1},{6,2},{7,3},{8,12},{9,13},{10,... | collective-permute-start | bytes 442376 | tf_op jit(solution)/shard_map/ppermute | solution.py:309
  28.5 0.0 collective-permute-done.2.refs_3_.refs_4_
  28.5 1.1 %merge_2.5 = (bf16[2,64,768]{2,1,0:T(8,128)(2,1)S(1)}, bf16[2,48,768]{2,1,0:T(8,128)(2,1)S(1)}) custom-call(f32[4,8,128]{2,1,0:T(8,128)S(1)} %get-tuple-element.31.refs_0_, bf16[4,256,768]{2,1,0:T(8,128)(2,1)S(1)} %get-tuple-element.32.refs_1_.refs_4_, bf16[2,64,896]{2,1,0:T(8,128)(2,1)S(1)} %get-tuple-element.37.refs_6_.refs_2_, ...), custom_call_target="tpu_custom_call" | custom-call | flops 1207959552 | tf_op jit(solution)/shard_map/merge_2/pallas_call | solution.py:238
  29.6 2.6 %collective-permute-start.5 = (bf16[2,48,768]{2,1,0:T(8,128)(2,1)S(1)}, bf16[2,48,768]{2,1,0:T(8,128)(2,1)S(1)}, u32[]{:S(2)}, u32[]{:S(2)}) collective-permute-start(bf16[2,48,768]{2,1,0:T(8,128)(2,1)S(1)} %get-tuple-element.44), channel_id=1, source_target_pairs={{0,8},{1,9},{2,10},{3,11},{4,12},{5,13},{6,14},{7,15},{8,0},{9,1},... | collective-permute-start | bytes 442376 | tf_op jit(solution)/shard_map/ppermute | solution.py:309
  32.2 1.4 %merge_2.6 = (bf16[2,64,1024]{2,1,0:T(8,128)(2,1)S(1)}, bf16[2,48,1024]{2,1,0:T(8,128)(2,1)S(1)}) custom-call(f32[4,8,128]{2,1,0:T(8,128)S(1)} %get-tuple-element.31.refs_0_, bf16[4,256,768]{2,1,0:T(8,128)(2,1)S(1)} %get-tuple-element.32.refs_1_.refs_4_, bf16[2,64,896]{2,1,0:T(8,128)(2,1)S(1)} %get-tuple-element.37.refs_6_.refs_2_, ...), custom_call_target="tpu_custom_call" | custom-call | flops 1610612736 | tf_op jit(solution)/shard_map/merge_2/pallas_call | solution.py:238
  33.7 0.4 collective-permute-start.8
  34.1 1.5 %merge_2.7 = (bf16[2,64,896]{2,1,0:T(8,128)(2,1)S(1)}, bf16[2,48,896]{2,1,0:T(8,128)(2,1)S(1)}) custom-call(f32[4,8,128]{2,1,0:T(8,128)S(1)} %get-tuple-element.31.refs_0_, bf16[4,256,768]{2,1,0:T(8,128)(2,1)S(1)} %get-tuple-element.32.refs_1_.refs_4_, bf16[2,64,1152]{2,1,0:T(8,128)(2,1)S(1)} %get-tuple-element.41.refs_6_.refs_3_.refs_2_, ...), custom_call_target="tpu_custom_call" | custom-call | flops 1409286144 | tf_op jit(solution)/shard_map/merge_2/pallas_call | solution.py:238
  35.5 2.6 %collective-permute-start.9 = (bf16[2,48,896]{2,1,0:T(8,128)(2,1)S(1)}, bf16[2,48,896]{2,1,0:T(8,128)(2,1)S(1)}, u32[]{:S(2)}, u32[]{:S(2)}) collective-permute-start(bf16[2,48,896]{2,1,0:T(8,128)(2,1)S(1)} %get-tuple-element.51), channel_id=1, source_target_pairs={{0,8},{1,9},{2,10},{3,11},{4,12},{5,13},{6,14},{7,15},{8,0},{9,1},... | collective-permute-start | bytes 516104 | tf_op jit(solution)/shard_map/ppermute | solution.py:309
  38.2 1.7 %merge_1.7 = (bf16[2,64,1280]{2,1,0:T(8,128)(2,1)S(1)}, bf16[2,48,1280]{2,1,0:T(8,128)(2,1)S(1)}) custom-call(f32[4,8,128]{2,1,0:T(8,128)S(1)} %get-tuple-element.31.refs_0_, bf16[4,256,768]{2,1,0:T(8,128)(2,1)S(1)} %get-tuple-element.32.refs_1_.refs_4_, bf16[2,64,1792]{2,1,0:T(8,128)(2,1)S(1)} %get-tuple-element.36.refs_4_.refs_3_.refs_2_, ...), custom_call_target="tpu_custom_call" | custom-call | flops 2013265920 | tf_op jit(solution)/shard_map/merge_1/pallas_call | solution.py:238
  39.9 0.9 %collective-permute-start.10 = (bf16[2,48,1280]{2,1,0:T(8,128)(2,1)S(1)}, bf16[2,48,1280]{2,1,0:T(8,128)(2,1)S(1)}, u32[]{:S(2)}, u32[]{:S(2)}) collective-permute-start(bf16[2,48,1280]{2,1,0:T(8,128)(2,1)S(1)} %get-tuple-element.52), channel_id=1, source_target_pairs={{0,4},{1,5},{2,6},{3,7},{4,0},{5,1},{6,2},{7,3},{8,12},{9,13},{10,... | collective-permute-start | bytes 737288 | tf_op jit(solution)/shard_map/ppermute | solution.py:309
  40.8 7.1 %collective-permute-done.5.refs_3_.refs_4_ = bf16[2,48,768]{2,1,0:T(8,128)(2,1)S(1)} collective-permute-done((bf16[2,48,768]{2,1,0:T(8,128)(2,1)S(1)}, bf16[2,48,768]{2,1,0:T(8,128)(2,1)S(1)}, u32[]{:S(2)}, u32[]{:S(2)}) %collective-permute-start.5) | collective-permute-done | bytes 147488 | tf_op jit(solution)/shard_map/ppermute | solution.py:309
  47.9 0.8 %merge_3.5.refs_6_ = bf16[2,64,512]{2,1,0:T(8,128)(2,1)S(1)} custom-call(f32[4,8,128]{2,1,0:T(8,128)S(1)} %get-tuple-element.31.refs_0_, bf16[4,256,768]{2,1,0:T(8,128)(2,1)S(1)} %get-tuple-element.32.refs_1_.refs_4_, bf16[2,64,768]{2,1,0:T(8,128)(2,1)S(1)} %get-tuple-element.43.refs_6_.refs_2_, ...), custom_call_target="tpu_custom_call" | custom-call | flops 805306368 | tf_op jit(solution)/shard_map/merge_3/pallas_call | solution.py:238
  48.8 3.3 %collective-permute-done.8.refs_5_.refs_4_ = bf16[2,48,1024]{2,1,0:T(8,128)(2,1)S(1)} collective-permute-done((bf16[2,48,1024]{2,1,0:T(8,128)(2,1)S(1)}, bf16[2,48,1024]{2,1,0:T(8,128)(2,1)S(1)}, u32[]{:S(2)}, u32[]{:S(2)}) %collective-permute-start.8) | collective-permute-done | bytes 196640 | tf_op jit(solution)/shard_map/ppermute | solution.py:309
  52.1 1.4 %merge_3.6.refs_6_ = bf16[2,64,1024]{2,1,0:T(8,128)(2,1)S(1)} custom-call(f32[4,8,128]{2,1,0:T(8,128)S(1)} %get-tuple-element.31.refs_0_, bf16[4,256,768]{2,1,0:T(8,128)(2,1)S(1)} %get-tuple-element.32.refs_1_.refs_4_, bf16[2,64,768]{2,1,0:T(8,128)(2,1)S(1)} %get-tuple-element.43.refs_6_.refs_2_, ...), custom_call_target="tpu_custom_call" | custom-call | flops 1610612736 | tf_op jit(solution)/shard_map/merge_3/pallas_call | solution.py:238
  53.6 1.9 %collective-permute-done.10.refs_5_.refs_3_ = bf16[2,48,1280]{2,1,0:T(8,128)(2,1)S(1)} collective-permute-done((bf16[2,48,1280]{2,1,0:T(8,128)(2,1)S(1)}, bf16[2,48,1280]{2,1,0:T(8,128)(2,1)S(1)}, u32[]{:S(2)}, u32[]{:S(2)}) %collective-permute-start.10) | collective-permute-done | bytes 245792 | tf_op jit(solution)/shard_map/ppermute | solution.py:309
  55.5 1.4 %merge_2.8 = (bf16[2,64,1024]{2,1,0:T(8,128)(2,1)S(1)}, bf16[2,48,1024]{2,1,0:T(8,128)(2,1)S(1)}) custom-call(f32[4,8,128]{2,1,0:T(8,128)S(1)} %get-tuple-element.31.refs_0_, bf16[4,256,768]{2,1,0:T(8,128)(2,1)S(1)} %get-tuple-element.32.refs_1_.refs_4_, bf16[2,64,768]{2,1,0:T(8,128)(2,1)S(1)} %get-tuple-element.42.refs_4_.refs_3_.refs_2_, ...), custom_call_target="tpu_custom_call" | custom-call | flops 1610612736 | tf_op jit(solution)/shard_map/merge_2/pallas_call | solution.py:238
  56.9 0.1 collective-permute-start.11
  57.0 0.0 collective-permute-done.9.refs_5_.refs_4_
  57.0 1.4 %merge_3.7.refs_4_ = bf16[2,64,1024]{2,1,0:T(8,128)(2,1)S(1)} custom-call(f32[4,8,128]{2,1,0:T(8,128)S(1)} %get-tuple-element.31.refs_0_, bf16[4,256,768]{2,1,0:T(8,128)(2,1)S(1)} %get-tuple-element.32.refs_1_.refs_4_, bf16[2,64,1024]{2,1,0:T(8,128)(2,1)S(1)} %get-tuple-element.47.refs_6_.refs_3_.refs_2_, ...), custom_call_target="tpu_custom_call" | custom-call | flops 1610612736 | tf_op jit(solution)/shard_map/merge_3/pallas_call | solution.py:238
  58.5 0.9 %merge_2.9 = (bf16[2,64,384]{2,1,0:T(8,128)(2,1)S(1)}, bf16[2,48,384]{2,1,0:T(8,128)(2,1)S(1)}) custom-call(f32[4,8,128]{2,1,0:T(8,128)S(1)} %get-tuple-element.31.refs_0_, bf16[4,256,768]{2,1,0:T(8,128)(2,1)S(1)} %get-tuple-element.32.refs_1_.refs_4_, bf16[2,64,1280]{2,1,0:T(8,128)(2,1)S(1)} %get-tuple-element.49.refs_4_.refs_3_.refs_2_, ...), custom_call_target="tpu_custom_call" | custom-call | flops 603979776 | tf_op jit(solution)/shard_map/merge_2/pallas_call | solution.py:238
  59.3 3.0 %collective-permute-start.12 = (bf16[2,48,384]{2,1,0:T(8,128)(2,1)S(1)}, bf16[2,48,384]{2,1,0:T(8,128)(2,1)S(1)}, u32[]{:S(2)}, u32[]{:S(2)}) collective-permute-start(bf16[2,48,384]{2,1,0:T(8,128)(2,1)S(1)} %get-tuple-element.56), channel_id=1, source_target_pairs={{0,8},{1,9},{2,10},{3,11},{4,12},{5,13},{6,14},{7,15},{8,0},{9,1},... | collective-permute-start | bytes 221192 | tf_op jit(solution)/shard_map/ppermute | solution.py:309
  62.3 4.8 %collective-permute-done.11.refs_5_.refs_4_ = bf16[2,48,1024]{2,1,0:T(8,128)(2,1)S(1)} collective-permute-done((bf16[2,48,1024]{2,1,0:T(8,128)(2,1)S(1)}, bf16[2,48,1024]{2,1,0:T(8,128)(2,1)S(1)}, u32[]{:S(2)}, u32[]{:S(2)}) %collective-permute-start.11) | collective-permute-done | bytes 196640 | tf_op jit(solution)/shard_map/ppermute | solution.py:309
  67.1 1.4 %merge_3.8.refs_6_ = bf16[2,64,1024]{2,1,0:T(8,128)(2,1)S(1)} custom-call(f32[4,8,128]{2,1,0:T(8,128)S(1)} %get-tuple-element.31.refs_0_, bf16[4,256,768]{2,1,0:T(8,128)(2,1)S(1)} %get-tuple-element.32.refs_1_.refs_4_, bf16[2,64,896]{2,1,0:T(8,128)(2,1)S(1)} %get-tuple-element.48.refs_4_.refs_3_.refs_2_, ...), custom_call_target="tpu_custom_call" | custom-call | flops 1610612736 | tf_op jit(solution)/shard_map/merge_3/pallas_call | solution.py:238
  68.5 0.0 copy-start.1
  68.5 0.0 collective-permute-done.12.refs_5_
  68.5 0.8 %merge_3.9 = bf16[2,64,512]{2,1,0:T(8,128)(2,1)S(1)} custom-call(f32[4,8,128]{2,1,0:T(8,128)S(1)} %get-tuple-element.31.refs_0_, bf16[4,256,768]{2,1,0:T(8,128)(2,1)S(1)} %get-tuple-element.32.refs_1_.refs_4_, bf16[2,64,1024]{2,1,0:T(8,128)(2,1)S(1)} %get-tuple-element.53.refs_6_.refs_3_.refs_2_, bf16[2,64,384]{2,1,0:T(8,128)(2,1)S(1)} %get-tuple-element.55.refs_6_.refs_3_, ...), custom_call_target="tpu_custom_call" | custom-call | flops 805306368 | tf_op jit(solution)/shard_map/merge_3/pallas_call | solution.py:238
  69.4 0.1 copy-done.1
  69.5 0.7 constant_dynamic-update-slice_fusion
  (7 shorter events, 0.1 us)
Async XLA Ops:
  0.0 3.0 %collective-permute-start = (bf16[2,64,4096]{2,1,0:T(8,128)(2,1)}, bf16[2,64,4096]{2,1,0:T(8,128)(2,1)S(1)}, u32[]{:S(2)}, u32[]{:S(2)}) collective-permute-start(bf16[2,64,4096]{2,1,0:T(8,128)(2,1)} %refs_2_.5), channel_id=1, source_target_pairs={{0,1},{1,0},{2,3},{3,2},{4,5},{5,4},{6,7},{7,6},{8,9},{9,8},{10,11... | collective-permute-start | bytes 3145736 | tf_op jit(solution)/shard_map/ppermute | solution.py:309
  2.0 1.2 %copy-start = (bf16[2,64,4096]{2,1,0:T(8,128)(2,1)S(1)}, bf16[2,64,4096]{2,1,0:T(8,128)(2,1)}, u32[]{:S(2)}) copy-start(bf16[2,64,4096]{2,1,0:T(8,128)(2,1)} %refs_2_.5) | copy-start | bytes 3145732
  4.7 8.9 %collective-permute-start.1 = (bf16[2,48,1024]{2,1,0:T(8,128)(2,1)S(1)}, bf16[2,48,1024]{2,1,0:T(8,128)(2,1)S(1)}, u32[]{:S(2)}, u32[]{:S(2)}) collective-permute-start(bf16[2,48,1024]{2,1,0:T(8,128)(2,1)S(1)} %get-tuple-element.34), channel_id=1, source_target_pairs={{0,2},{1,3},{2,0},{3,1},{4,6},{5,7},{6,4},{7,5},{8,10},{9,11},{10,... | collective-permute-start | bytes 589832 | tf_op jit(solution)/shard_map/ppermute | solution.py:309
  9.1 9.3 %collective-permute-start.3 = (bf16[2,48,1280]{2,1,0:T(8,128)(2,1)S(1)}, bf16[2,48,1280]{2,1,0:T(8,128)(2,1)S(1)}, u32[]{:S(2)}, u32[]{:S(2)}) collective-permute-start(bf16[2,48,1280]{2,1,0:T(8,128)(2,1)S(1)} %get-tuple-element.39), channel_id=1, source_target_pairs={{0,2},{1,3},{2,0},{3,1},{4,6},{5,7},{6,4},{7,5},{8,10},{9,11},{10,... | collective-permute-start | bytes 737288 | tf_op jit(solution)/shard_map/ppermute | solution.py:309
  11.5 14.0 %collective-permute-start.4 = (bf16[2,48,1792]{2,1,0:T(8,128)(2,1)S(1)}, bf16[2,48,1792]{2,1,0:T(8,128)(2,1)S(1)}, u32[]{:S(2)}, u32[]{:S(2)}) collective-permute-start(bf16[2,48,1792]{2,1,0:T(8,128)(2,1)S(1)} %get-tuple-element.40), channel_id=1, source_target_pairs={{0,2},{1,3},{2,0},{3,1},{4,6},{5,7},{6,4},{7,5},{8,10},{9,11},{10,... | collective-permute-start | bytes 1032200 | tf_op jit(solution)/shard_map/ppermute | solution.py:309
  15.0 13.5 %collective-permute-start.2 = (bf16[2,48,896]{2,1,0:T(8,128)(2,1)S(1)}, bf16[2,48,896]{2,1,0:T(8,128)(2,1)S(1)}, u32[]{:S(2)}, u32[]{:S(2)}) collective-permute-start(bf16[2,48,896]{2,1,0:T(8,128)(2,1)S(1)} %get-tuple-element.38), channel_id=1, source_target_pairs={{0,4},{1,5},{2,6},{3,7},{4,0},{5,1},{6,2},{7,3},{8,12},{9,13},{10,... | collective-permute-start | bytes 516104 | tf_op jit(solution)/shard_map/ppermute | solution.py:309
  20.1 12.1 %collective-permute-start.6 = (bf16[2,48,1152]{2,1,0:T(8,128)(2,1)S(1)}, bf16[2,48,1152]{2,1,0:T(8,128)(2,1)S(1)}, u32[]{:S(2)}, u32[]{:S(2)}) collective-permute-start(bf16[2,48,1152]{2,1,0:T(8,128)(2,1)S(1)} %get-tuple-element.45), channel_id=1, source_target_pairs={{0,4},{1,5},{2,6},{3,7},{4,0},{5,1},{6,2},{7,3},{8,12},{9,13},{10,... | collective-permute-start | bytes 663560 | tf_op jit(solution)/shard_map/ppermute | solution.py:309
  26.6 7.5 %collective-permute-start.7 = (bf16[2,48,768]{2,1,0:T(8,128)(2,1)S(1)}, bf16[2,48,768]{2,1,0:T(8,128)(2,1)S(1)}, u32[]{:S(2)}, u32[]{:S(2)}) collective-permute-start(bf16[2,48,768]{2,1,0:T(8,128)(2,1)S(1)} %get-tuple-element.46), channel_id=1, source_target_pairs={{0,4},{1,5},{2,6},{3,7},{4,0},{5,1},{6,2},{7,3},{8,12},{9,13},{10,... | collective-permute-start | bytes 442376 | tf_op jit(solution)/shard_map/ppermute | solution.py:309
  29.6 18.3 %collective-permute-start.5 = (bf16[2,48,768]{2,1,0:T(8,128)(2,1)S(1)}, bf16[2,48,768]{2,1,0:T(8,128)(2,1)S(1)}, u32[]{:S(2)}, u32[]{:S(2)}) collective-permute-start(bf16[2,48,768]{2,1,0:T(8,128)(2,1)S(1)} %get-tuple-element.44), channel_id=1, source_target_pairs={{0,8},{1,9},{2,10},{3,11},{4,12},{5,13},{6,14},{7,15},{8,0},{9,1},... | collective-permute-start | bytes 442376 | tf_op jit(solution)/shard_map/ppermute | solution.py:309
  33.7 18.4 %collective-permute-start.8 = (bf16[2,48,1024]{2,1,0:T(8,128)(2,1)S(1)}, bf16[2,48,1024]{2,1,0:T(8,128)(2,1)S(1)}, u32[]{:S(2)}, u32[]{:S(2)}) collective-permute-start(bf16[2,48,1024]{2,1,0:T(8,128)(2,1)S(1)} %get-tuple-element.50), channel_id=1, source_target_pairs={{0,8},{1,9},{2,10},{3,11},{4,12},{5,13},{6,14},{7,15},{8,0},{9,1},... | collective-permute-start | bytes 589832 | tf_op jit(solution)/shard_map/ppermute | solution.py:309
  35.5 21.5 %collective-permute-start.9 = (bf16[2,48,896]{2,1,0:T(8,128)(2,1)S(1)}, bf16[2,48,896]{2,1,0:T(8,128)(2,1)S(1)}, u32[]{:S(2)}, u32[]{:S(2)}) collective-permute-start(bf16[2,48,896]{2,1,0:T(8,128)(2,1)S(1)} %get-tuple-element.51), channel_id=1, source_target_pairs={{0,8},{1,9},{2,10},{3,11},{4,12},{5,13},{6,14},{7,15},{8,0},{9,1},... | collective-permute-start | bytes 516104 | tf_op jit(solution)/shard_map/ppermute | solution.py:309
  39.9 15.6 %collective-permute-start.10 = (bf16[2,48,1280]{2,1,0:T(8,128)(2,1)S(1)}, bf16[2,48,1280]{2,1,0:T(8,128)(2,1)S(1)}, u32[]{:S(2)}, u32[]{:S(2)}) collective-permute-start(bf16[2,48,1280]{2,1,0:T(8,128)(2,1)S(1)} %get-tuple-element.52), channel_id=1, source_target_pairs={{0,4},{1,5},{2,6},{3,7},{4,0},{5,1},{6,2},{7,3},{8,12},{9,13},{10,... | collective-permute-start | bytes 737288 | tf_op jit(solution)/shard_map/ppermute | solution.py:309
  56.9 10.1 %collective-permute-start.11 = (bf16[2,48,1024]{2,1,0:T(8,128)(2,1)S(1)}, bf16[2,48,1024]{2,1,0:T(8,128)(2,1)S(1)}, u32[]{:S(2)}, u32[]{:S(2)}) collective-permute-start(bf16[2,48,1024]{2,1,0:T(8,128)(2,1)S(1)} %get-tuple-element.54), channel_id=1, source_target_pairs={{0,8},{1,9},{2,10},{3,11},{4,12},{5,13},{6,14},{7,15},{8,0},{9,1},... | collective-permute-start | bytes 589832 | tf_op jit(solution)/shard_map/ppermute | solution.py:309
  59.3 9.2 %collective-permute-start.12 = (bf16[2,48,384]{2,1,0:T(8,128)(2,1)S(1)}, bf16[2,48,384]{2,1,0:T(8,128)(2,1)S(1)}, u32[]{:S(2)}, u32[]{:S(2)}) collective-permute-start(bf16[2,48,384]{2,1,0:T(8,128)(2,1)S(1)} %get-tuple-element.56), channel_id=1, source_target_pairs={{0,8},{1,9},{2,10},{3,11},{4,12},{5,13},{6,14},{7,15},{8,0},{9,1},... | collective-permute-start | bytes 221192 | tf_op jit(solution)/shard_map/ppermute | solution.py:309
  68.5 1.0 %copy-start.1 = (bf16[2,64,4096]{2,1,0:T(8,128)(2,1)}, bf16[2,64,4096]{2,1,0:T(8,128)(2,1)S(1)}, u32[]{:S(2)}) copy-start(bf16[2,64,4096]{2,1,0:T(8,128)(2,1)S(1)} %constant_dynamic-update-slice_fusion.1) | copy-start | bytes 3145732

commit v4 on v3

--- a/solution.py
+++ b/solution.py
@@ -151,12 +151,15 @@
     shifts = (code // 256 % 256 - LANES, code % 256 - LANES)
     rows = pl.ds(pl.multiple_of(half * (beams - window), 16), window)
     base = start - LANES
+    bit = lax.rem(lax.shift_right_logical(lax.axis_index("pulse"), level), 2)
+    other = 2 * (1 - bit)
     for number, (piece, source, target, width) in enumerate(plan):
         for child, ref in ((0, own_refs[number]), (1, far_refs[number])):
             taken = rows if ref.shape[1] == beams else pl.ds(0, window)
             for part in range(2):
+                which = part if ref.shape[0] == 2 else other + part
                 wide_ref[child, part, :, target - base:target - base + width] = ref[
-                    part, taken, source:source + width
+                    which, taken, source:source + width
                 ]
     edge = jnp.zeros((2, 2, window, LANES), jnp.bfloat16)
     if base < 0:
@@ -309,6 +312,12 @@
     return lax.ppermute(value, "pulse", pairs)
 
 
+def gathered(value, bit):
+    mask = 1 << bit
+    groups = [[s, s | mask] for s in range(lax.axis_size("pulse")) if s & mask == 0]
+    return lax.all_gather(value, "pulse", axis_index_groups=groups, tiled=True)
+
+
 def on_device(beams_in, ukern, rkern, angles, taps, shifts, half_table):
     beams, length = beams_in.shape[1:]
     utaps, rtaps = ukern.shape[1], rkern.shape[1]
@@ -329,7 +338,8 @@
         )
         before = owns[level + 1][chunk] = done[0]
         if level < levels - 1:
-            fars[level + 1][chunk] = from_partner(done[1], level + 1)
+            send = gathered if level + 2 == levels else from_partner
+            fars[level + 1][chunk] = send(done[1], level + 1)
     return jnp.concatenate(owns[levels], axis=2)
 
 

time: 70.4 us -> 95.3 us (1.35)
  blocking collectives: 0 us -> 50.7 us
  waiting for transfers between devices: 22.2 us -> 5.14 us
  starting transfers between devices: 20.6 us -> 11 us
    all_gather x0 -> x5, blocking collectives: none -> 50.7 us  [gathered(): return lax.all_gather(value, 'pulse', axis_index_groups=groups, tiled=True)]
    ppermute x13 -> x8, waiting for transfers between devices: 22.2 us -> 5.14 us  [from_partner(): return lax.ppermute(value, 'pulse', pairs)]
    ppermute x13 -> x8, starting transfers between devices: 20.6 us -> 11 us  [from_partner(): return lax.ppermute(value, 'pulse', pairs)]
  transfers between devices with their start and end apart: 13 -> 8, of which waited for: 7 -> 3; matrix products, arithmetic and copies ran while one was open for 2% -> 2% of each run, Pallas kernels for 32% -> 15%
where the time goes in v4:
time: 95.3 us; the launch traced here: 95.1 us
  blocking collectives  50.7 us (53%)
  Pallas kernels  24.6 us (26%)
  starting transfers between devices  11 us (12%)
  waiting for transfers between devices  5.14 us (5%)
  local copies, waits for them, and re-layouts  1.97 us (2%)
  other arithmetic  1.54 us (2%)
    all_gather x5, blocking collectives, gathered(): return lax.all_gather(value, 'pulse', axis_index_groups=groups, tiled=True)  50.7 us
    pallas_call x17, Pallas kernels, merge(): pl.pallas_call(functools.partial(merge_kernel, level, plan, start, stop,...  23.8 us
    ppermute x8, starting transfers between devices, from_partner(): return lax.ppermute(value, 'pulse', pairs)  11 us
    ppermute x8, waiting for transfers between devices, from_partner(): return lax.ppermute(value, 'pulse', pairs)  5.14 us
  transfers between devices with their start and end apart: 8, of which 3 were waited for; matrix products, arithmetic and copies ran while one was open for 2% of the time, Pallas kernels for 15%

profile of v4, /device:TPU:0, one launch (start us, length us, event | category | flops | bytes accessed | tf_op | source)
XLA Modules:
  0.0 95.1 jit_solution(17075100253342679902)
XLA Ops:
  0.0 0.5 collective-permute-start
  0.5 0.7 pad_add_fusion.real_ref
  1.2 0.8 pad_add_fusion.1.whole_ref
  2.0 0.0 copy-start
  2.0 0.9 mixing.1
  2.9 0.1 collective-permute-done.refs_3_
  3.0 0.3 copy-done
  3.2 1.5 %merge_0.3 = (bf16[2,64,1024]{2,1,0:T(8,128)(2,1)S(1)}, bf16[2,48,1024]{2,1,0:T(8,128)(2,1)S(1)}) custom-call(f32[4,8,128]{2,1,0:T(8,128)S(1)} %get-tuple-element.31.refs_0_, bf16[4,256,768]{2,1,0:T(8,128)(2,1)S(1)} %get-tuple-element.32.refs_1_.refs_4_, bf16[2,64,4096]{2,1,0:T(8,128)(2,1)S(1)} %copy-done, ...), custom_call_target="tpu_custom_call" | custom-call | flops 1610612736 | tf_op jit(solution)/shard_map/merge_0/pallas_call | solution.py:241
  4.7 2.7 %collective-permute-start.1 = (bf16[2,48,1024]{2,1,0:T(8,128)(2,1)S(1)}, bf16[2,48,1024]{2,1,0:T(8,128)(2,1)S(1)}, u32[]{:S(2)}, u32[]{:S(2)}) collective-permute-start(bf16[2,48,1024]{2,1,0:T(8,128)(2,1)S(1)} %get-tuple-element.34), channel_id=1, source_target_pairs={{0,2},{1,3},{2,0},{3,1},{4,6},{5,7},{6,4},{7,5},{8,10},{9,11},{10,... | collective-permute-start | bytes 589832 | tf_op jit(solution)/shard_map/ppermute | solution.py:312
  7.4 1.7 %merge_0.4 = (bf16[2,64,1280]{2,1,0:T(8,128)(2,1)S(1)}, bf16[2,48,1280]{2,1,0:T(8,128)(2,1)S(1)}) custom-call(f32[4,8,128]{2,1,0:T(8,128)S(1)} %get-tuple-element.31.refs_0_, bf16[4,256,768]{2,1,0:T(8,128)(2,1)S(1)} %get-tuple-element.32.refs_1_.refs_4_, bf16[2,64,4096]{2,1,0:T(8,128)(2,1)S(1)} %copy-done, ...), custom_call_target="tpu_custom_call" | custom-call | flops 2013265920 | tf_op jit(solution)/shard_map/merge_0/pallas_call | solution.py:241
  9.1 0.1 collective-permute-start.3
  9.1 2.3 %merge_0.5 = (bf16[2,64,1792]{2,1,0:T(8,128)(2,1)S(1)}, bf16[2,48,1792]{2,1,0:T(8,128)(2,1)S(1)}) custom-call(f32[4,8,128]{2,1,0:T(8,128)S(1)} %get-tuple-element.31.refs_0_, bf16[4,256,768]{2,1,0:T(8,128)(2,1)S(1)} %get-tuple-element.32.refs_1_.refs_4_, bf16[2,64,4096]{2,1,0:T(8,128)(2,1)S(1)} %copy-done, ...), custom_call_target="tpu_custom_call" | custom-call | flops 2818572288 | tf_op jit(solution)/shard_map/merge_0/pallas_call | solution.py:241
  11.5 2.1 %collective-permute-start.4 = (bf16[2,48,1792]{2,1,0:T(8,128)(2,1)S(1)}, bf16[2,48,1792]{2,1,0:T(8,128)(2,1)S(1)}, u32[]{:S(2)}, u32[]{:S(2)}) collective-permute-start(bf16[2,48,1792]{2,1,0:T(8,128)(2,1)S(1)} %get-tuple-element.40), channel_id=1, source_target_pairs={{0,2},{1,3},{2,0},{3,1},{4,6},{5,7},{6,4},{7,5},{8,10},{9,11},{10,... | collective-permute-start | bytes 1032200 | tf_op jit(solution)/shard_map/ppermute | solution.py:312
  13.5 0.0 collective-permute-done.1.refs_3_.refs_4_
  13.5 1.5 %merge_1.4 = (bf16[2,64,896]{2,1,0:T(8,128)(2,1)S(1)}, bf16[2,48,896]{2,1,0:T(8,128)(2,1)S(1)}) custom-call(f32[4,8,128]{2,1,0:T(8,128)S(1)} %get-tuple-element.31.refs_0_, bf16[4,256,768]{2,1,0:T(8,128)(2,1)S(1)} %get-tuple-element.32.refs_1_.refs_4_, bf16[2,64,1024]{2,1,0:T(8,128)(2,1)S(1)} %get-tuple-element.33.refs_4_.refs_2_, ...), custom_call_target="tpu_custom_call" | custom-call | flops 1409286144 | tf_op jit(solution)/shard_map/merge_1/pallas_call | solution.py:241
  15.0 1.7 %collective-permute-start.2 = (bf16[2,48,896]{2,1,0:T(8,128)(2,1)S(1)}, bf16[2,48,896]{2,1,0:T(8,128)(2,1)S(1)}, u32[]{:S(2)}, u32[]{:S(2)}) collective-permute-start(bf16[2,48,896]{2,1,0:T(8,128)(2,1)S(1)} %get-tuple-element.38), channel_id=1, source_target_pairs={{0,4},{1,5},{2,6},{3,7},{4,0},{5,1},{6,2},{7,3},{8,12},{9,13},{10,... | collective-permute-start | bytes 516104 | tf_op jit(solution)/shard_map/ppermute | solution.py:312
  16.7 1.7 %collective-permute-done.3.refs_5_.refs_4_ = bf16[2,48,1280]{2,1,0:T(8,128)(2,1)S(1)} collective-permute-done((bf16[2,48,1280]{2,1,0:T(8,128)(2,1)S(1)}, bf16[2,48,1280]{2,1,0:T(8,128)(2,1)S(1)}, u32[]{:S(2)}, u32[]{:S(2)}) %collective-permute-start.3) | collective-permute-done | bytes 245792 | tf_op jit(solution)/shard_map/ppermute | solution.py:312
  18.4 1.7 %merge_1.5 = (bf16[2,64,1152]{2,1,0:T(8,128)(2,1)S(1)}, bf16[2,48,1152]{2,1,0:T(8,128)(2,1)S(1)}) custom-call(f32[4,8,128]{2,1,0:T(8,128)S(1)} %get-tuple-element.31.refs_0_, bf16[4,256,768]{2,1,0:T(8,128)(2,1)S(1)} %get-tuple-element.32.refs_1_.refs_4_, bf16[2,64,1024]{2,1,0:T(8,128)(2,1)S(1)} %get-tuple-element.33.refs_4_.refs_2_, ...), custom_call_target="tpu_custom_call" | custom-call | flops 1811939328 | tf_op jit(solution)/shard_map/merge_1/pallas_call | solution.py:241
  20.1 2.1 %collective-permute-start.5 = (bf16[2,48,1152]{2,1,0:T(8,128)(2,1)S(1)}, bf16[2,48,1152]{2,1,0:T(8,128)(2,1)S(1)}, u32[]{:S(2)}, u32[]{:S(2)}) collective-permute-start(bf16[2,48,1152]{2,1,0:T(8,128)(2,1)S(1)} %get-tuple-element.45), channel_id=1, source_target_pairs={{0,4},{1,5},{2,6},{3,7},{4,0},{5,1},{6,2},{7,3},{8,12},{9,13},{10,... | collective-permute-start | bytes 663560 | tf_op jit(solution)/shard_map/ppermute | solution.py:312
  22.2 3.3 %collective-permute-done.4.refs_5_.refs_3_ = bf16[2,48,1792]{2,1,0:T(8,128)(2,1)S(1)} collective-permute-done((bf16[2,48,1792]{2,1,0:T(8,128)(2,1)S(1)}, bf16[2,48,1792]{2,1,0:T(8,128)(2,1)S(1)}, u32[]{:S(2)}, u32[]{:S(2)}) %collective-permute-start.4) | collective-permute-done | bytes 344096 | tf_op jit(solution)/shard_map/ppermute | solution.py:312
  25.5 1.1 %merge_1.6 = (bf16[2,64,768]{2,1,0:T(8,128)(2,1)S(1)}, bf16[2,48,768]{2,1,0:T(8,128)(2,1)S(1)}) custom-call(f32[4,8,128]{2,1,0:T(8,128)S(1)} %get-tuple-element.31.refs_0_, bf16[4,256,768]{2,1,0:T(8,128)(2,1)S(1)} %get-tuple-element.32.refs_1_.refs_4_, bf16[2,64,1280]{2,1,0:T(8,128)(2,1)S(1)} %get-tuple-element.35.refs_4_.refs_3_.refs_2_, ...), custom_call_target="tpu_custom_call" | custom-call | flops 1207959552 | tf_op jit(solution)/shard_map/merge_1/pallas_call | solution.py:241
  26.6 1.9 %collective-permute-start.6 = (bf16[2,48,768]{2,1,0:T(8,128)(2,1)S(1)}, bf16[2,48,768]{2,1,0:T(8,128)(2,1)S(1)}, u32[]{:S(2)}, u32[]{:S(2)}) collective-permute-start(bf16[2,48,768]{2,1,0:T(8,128)(2,1)S(1)} %get-tuple-element.46), channel_id=1, source_target_pairs={{0,4},{1,5},{2,6},{3,7},{4,0},{5,1},{6,2},{7,3},{8,12},{9,13},{10,... | collective-permute-start | bytes 442376 | tf_op jit(solution)/shard_map/ppermute | solution.py:312
  28.4 0.0 collective-permute-done.2.refs_3_.refs_4_
  28.4 1.1 %merge_2.5 = (bf16[2,64,768]{2,1,0:T(8,128)(2,1)S(1)}, bf16[2,48,768]{2,1,0:T(8,128)(2,1)S(1)}) custom-call(f32[4,8,128]{2,1,0:T(8,128)S(1)} %get-tuple-element.31.refs_0_, bf16[4,256,768]{2,1,0:T(8,128)(2,1)S(1)} %get-tuple-element.32.refs_1_.refs_4_, bf16[2,64,896]{2,1,0:T(8,128)(2,1)S(1)} %get-tuple-element.37.refs_6_.refs_2_, ...), custom_call_target="tpu_custom_call" | custom-call | flops 1207959552 | tf_op jit(solution)/shard_map/merge_2/pallas_call | solution.py:241
  29.5 9.8 %all_gather.15.refs_3_.refs_4_ = bf16[4,48,768]{2,1,0:T(8,128)(2,1)S(1)} all-gather(bf16[2,48,768]{2,1,0:T(8,128)(2,1)S(1)} %get-tuple-element.44), channel_id=1, replica_groups={{0,8},{1,9},{2,10},{3,11},{4,12},{5,13},{6,14},{7,15},{16,24},{17,25},{..., dimensions={0}, use_global_device_ids=true | all-gather | bytes 442368 | tf_op jit(solution)/shard_map/all_gather | solution.py:318
  39.3 0.0 collective-permute-done.5.refs_5_.refs_4_
  39.3 1.5 %merge_2.6 = (bf16[2,64,1024]{2,1,0:T(8,128)(2,1)S(1)}, bf16[2,48,1024]{2,1,0:T(8,128)(2,1)S(1)}) custom-call(f32[4,8,128]{2,1,0:T(8,128)S(1)} %get-tuple-element.31.refs_0_, bf16[4,256,768]{2,1,0:T(8,128)(2,1)S(1)} %get-tuple-element.32.refs_1_.refs_4_, bf16[2,64,896]{2,1,0:T(8,128)(2,1)S(1)} %get-tuple-element.37.refs_6_.refs_2_, ...), custom_call_target="tpu_custom_call" | custom-call | flops 1610612736 | tf_op jit(solution)/shard_map/merge_2/pallas_call | solution.py:241
  40.8 11.5 %all_gather.16.refs_5_.refs_4_ = bf16[4,48,1024]{2,1,0:T(8,128)(2,1)S(1)} all-gather(bf16[2,48,1024]{2,1,0:T(8,128)(2,1)S(1)} %get-tuple-element.50), channel_id=1, replica_groups={{0,8},{1,9},{2,10},{3,11},{4,12},{5,13},{6,14},{7,15},{16,24},{17,25},{..., dimensions={0}, use_global_device_ids=true | all-gather | bytes 589824 | tf_op jit(solution)/shard_map/all_gather | solution.py:318
  52.3 0.0 collective-permute-done.6.refs_5_.refs_4_
  52.3 1.5 %merge_2.7 = (bf16[2,64,896]{2,1,0:T(8,128)(2,1)S(1)}, bf16[2,48,896]{2,1,0:T(8,128)(2,1)S(1)}) custom-call(f32[4,8,128]{2,1,0:T(8,128)S(1)} %get-tuple-element.31.refs_0_, bf16[4,256,768]{2,1,0:T(8,128)(2,1)S(1)} %get-tuple-element.32.refs_1_.refs_4_, bf16[2,64,1152]{2,1,0:T(8,128)(2,1)S(1)} %get-tuple-element.41.refs_6_.refs_3_.refs_2_, ...), custom_call_target="tpu_custom_call" | custom-call | flops 1409286144 | tf_op jit(solution)/shard_map/merge_2/pallas_call | solution.py:241
  53.8 1.7 %merge_1.7 = (bf16[2,64,1280]{2,1,0:T(8,128)(2,1)S(1)}, bf16[2,48,1280]{2,1,0:T(8,128)(2,1)S(1)}) custom-call(f32[4,8,128]{2,1,0:T(8,128)S(1)} %get-tuple-element.31.refs_0_, bf16[4,256,768]{2,1,0:T(8,128)(2,1)S(1)} %get-tuple-element.32.refs_1_.refs_4_, bf16[2,64,1792]{2,1,0:T(8,128)(2,1)S(1)} %get-tuple-element.36.refs_4_.refs_3_.refs_2_, ...), custom_call_target="tpu_custom_call" | custom-call | flops 2013265920 | tf_op jit(solution)/shard_map/merge_1/pallas_call | solution.py:241
  55.5 0.1 collective-permute-start.7
  55.6 0.9 merge_3.5.refs_6_
  56.4 1.5 %merge_3.6.refs_6_ = bf16[2,64,1024]{2,1,0:T(8,128)(2,1)S(1)} custom-call(f32[4,8,128]{2,1,0:T(8,128)S(1)} %get-tuple-element.31.refs_0_, bf16[4,256,768]{2,1,0:T(8,128)(2,1)S(1)} %get-tuple-element.32.refs_1_.refs_4_, bf16[2,64,768]{2,1,0:T(8,128)(2,1)S(1)} %get-tuple-element.43.refs_6_.refs_2_, ...), custom_call_target="tpu_custom_call" | custom-call | flops 1610612736 | tf_op jit(solution)/shard_map/merge_3/pallas_call | solution.py:241
  57.9 11.6 %all_gather.17.refs_5_.refs_4_ = bf16[4,48,896]{2,1,0:T(8,128)(2,1)S(1)} all-gather(bf16[2,48,896]{2,1,0:T(8,128)(2,1)S(1)} %get-tuple-element.51), channel_id=1, replica_groups={{0,8},{1,9},{2,10},{3,11},{4,12},{5,13},{6,14},{7,15},{16,24},{17,25},{..., dimensions={0}, use_global_device_ids=true | all-gather | bytes 516096 | tf_op jit(solution)/shard_map/all_gather | solution.py:318
  69.5 0.0 collective-permute-done.7.refs_5_.refs_3_
  69.5 1.5 %merge_2.8 = (bf16[2,64,1024]{2,1,0:T(8,128)(2,1)S(1)}, bf16[2,48,1024]{2,1,0:T(8,128)(2,1)S(1)}) custom-call(f32[4,8,128]{2,1,0:T(8,128)S(1)} %get-tuple-element.31.refs_0_, bf16[4,256,768]{2,1,0:T(8,128)(2,1)S(1)} %get-tuple-element.32.refs_1_.refs_4_, bf16[2,64,768]{2,1,0:T(8,128)(2,1)S(1)} %get-tuple-element.42.refs_4_.refs_3_.refs_2_, ...), custom_call_target="tpu_custom_call" | custom-call | flops 1610612736 | tf_op jit(solution)/shard_map/merge_2/pallas_call | solution.py:241
  71.0 10.8 %all_gather.18.refs_5_.refs_4_ = bf16[4,48,1024]{2,1,0:T(8,128)(2,1)S(1)} all-gather(bf16[2,48,1024]{2,1,0:T(8,128)(2,1)S(1)} %get-tuple-element.54), channel_id=1, replica_groups={{0,8},{1,9},{2,10},{3,11},{4,12},{5,13},{6,14},{7,15},{16,24},{17,25},{..., dimensions={0}, use_global_device_ids=true | all-gather | bytes 589824 | tf_op jit(solution)/shard_map/all_gather | solution.py:318
  81.8 1.5 %merge_3.7.refs_4_ = bf16[2,64,1024]{2,1,0:T(8,128)(2,1)S(1)} custom-call(f32[4,8,128]{2,1,0:T(8,128)S(1)} %get-tuple-element.31.refs_0_, bf16[4,256,768]{2,1,0:T(8,128)(2,1)S(1)} %get-tuple-element.32.refs_1_.refs_4_, bf16[2,64,1024]{2,1,0:T(8,128)(2,1)S(1)} %get-tuple-element.47.refs_6_.refs_3_.refs_2_, ...), custom_call_target="tpu_custom_call" | custom-call | flops 1610612736 | tf_op jit(solution)/shard_map/merge_3/pallas_call | solution.py:241
  83.2 0.9 merge_2.9
  84.1 7.0 %all_gather.19.refs_5_ = bf16[4,48,384]{2,1,0:T(8,128)(2,1)S(1)} all-gather(bf16[2,48,384]{2,1,0:T(8,128)(2,1)S(1)} %get-tuple-element.56), channel_id=1, replica_groups={{0,8},{1,9},{2,10},{3,11},{4,12},{5,13},{6,14},{7,15},{16,24},{17,25},{..., dimensions={0}, use_global_device_ids=true | all-gather | bytes 221184 | tf_op jit(solution)/shard_map/all_gather | solution.py:318
  91.1 1.4 %merge_3.8.refs_6_ = bf16[2,64,1024]{2,1,0:T(8,128)(2,1)S(1)} custom-call(f32[4,8,128]{2,1,0:T(8,128)S(1)} %get-tuple-element.31.refs_0_, bf16[4,256,768]{2,1,0:T(8,128)(2,1)S(1)} %get-tuple-element.32.refs_1_.refs_4_, bf16[2,64,896]{2,1,0:T(8,128)(2,1)S(1)} %get-tuple-element.48.refs_4_.refs_3_.refs_2_, ...), custom_call_target="tpu_custom_call" | custom-call | flops 1610612736 | tf_op jit(solution)/shard_map/merge_3/pallas_call | solution.py:241
  92.6 0.9 merge_3.9
  93.5 0.0 copy-start.1
  93.5 1.0 %copy-done.1 = bf16[2,64,4096]{2,1,0:T(8,128)(2,1)} copy-done((bf16[2,64,4096]{2,1,0:T(8,128)(2,1)}, bf16[2,64,4096]{2,1,0:T(8,128)(2,1)S(1)}, u32[]{:S(2)}) %copy-start.1) | copy-done | bytes 1048600
  94.5 0.7 constant_dynamic-update-slice_fusion
  (4 shorter events, 0.1 us)
Async XLA Ops:
  0.0 3.0 %collective-permute-start = (bf16[2,64,4096]{2,1,0:T(8,128)(2,1)}, bf16[2,64,4096]{2,1,0:T(8,128)(2,1)S(1)}, u32[]{:S(2)}, u32[]{:S(2)}) collective-permute-start(bf16[2,64,4096]{2,1,0:T(8,128)(2,1)} %refs_2_.5), channel_id=1, source_target_pairs={{0,1},{1,0},{2,3},{3,2},{4,5},{5,4},{6,7},{7,6},{8,9},{9,8},{10,11... | collective-permute-start | bytes 3145736 | tf_op jit(solution)/shard_map/ppermute | solution.py:312
  2.0 1.2 %copy-start = (bf16[2,64,4096]{2,1,0:T(8,128)(2,1)S(1)}, bf16[2,64,4096]{2,1,0:T(8,128)(2,1)}, u32[]{:S(2)}) copy-start(bf16[2,64,4096]{2,1,0:T(8,128)(2,1)} %refs_2_.5) | copy-start | bytes 3145732
  4.7 8.9 %collective-permute-start.1 = (bf16[2,48,1024]{2,1,0:T(8,128)(2,1)S(1)}, bf16[2,48,1024]{2,1,0:T(8,128)(2,1)S(1)}, u32[]{:S(2)}, u32[]{:S(2)}) collective-permute-start(bf16[2,48,1024]{2,1,0:T(8,128)(2,1)S(1)} %get-tuple-element.34), channel_id=1, source_target_pairs={{0,2},{1,3},{2,0},{3,1},{4,6},{5,7},{6,4},{7,5},{8,10},{9,11},{10,... | collective-permute-start | bytes 589832 | tf_op jit(solution)/shard_map/ppermute | solution.py:312
  9.1 9.3 %collective-permute-start.3 = (bf16[2,48,1280]{2,1,0:T(8,128)(2,1)S(1)}, bf16[2,48,1280]{2,1,0:T(8,128)(2,1)S(1)}, u32[]{:S(2)}, u32[]{:S(2)}) collective-permute-start(bf16[2,48,1280]{2,1,0:T(8,128)(2,1)S(1)} %get-tuple-element.39), channel_id=1, source_target_pairs={{0,2},{1,3},{2,0},{3,1},{4,6},{5,7},{6,4},{7,5},{8,10},{9,11},{10,... | collective-permute-start | bytes 737288 | tf_op jit(solution)/shard_map/ppermute | solution.py:312
  11.5 14.0 %collective-permute-start.4 = (bf16[2,48,1792]{2,1,0:T(8,128)(2,1)S(1)}, bf16[2,48,1792]{2,1,0:T(8,128)(2,1)S(1)}, u32[]{:S(2)}, u32[]{:S(2)}) collective-permute-start(bf16[2,48,1792]{2,1,0:T(8,128)(2,1)S(1)} %get-tuple-element.40), channel_id=1, source_target_pairs={{0,2},{1,3},{2,0},{3,1},{4,6},{5,7},{6,4},{7,5},{8,10},{9,11},{10,... | collective-permute-start | bytes 1032200 | tf_op jit(solution)/shard_map/ppermute | solution.py:312
  15.0 13.4 %collective-permute-start.2 = (bf16[2,48,896]{2,1,0:T(8,128)(2,1)S(1)}, bf16[2,48,896]{2,1,0:T(8,128)(2,1)S(1)}, u32[]{:S(2)}, u32[]{:S(2)}) collective-permute-start(bf16[2,48,896]{2,1,0:T(8,128)(2,1)S(1)} %get-tuple-element.38), channel_id=1, source_target_pairs={{0,4},{1,5},{2,6},{3,7},{4,0},{5,1},{6,2},{7,3},{8,12},{9,13},{10,... | collective-permute-start | bytes 516104 | tf_op jit(solution)/shard_map/ppermute | solution.py:312
  20.1 19.2 %collective-permute-start.5 = (bf16[2,48,1152]{2,1,0:T(8,128)(2,1)S(1)}, bf16[2,48,1152]{2,1,0:T(8,128)(2,1)S(1)}, u32[]{:S(2)}, u32[]{:S(2)}) collective-permute-start(bf16[2,48,1152]{2,1,0:T(8,128)(2,1)S(1)} %get-tuple-element.45), channel_id=1, source_target_pairs={{0,4},{1,5},{2,6},{3,7},{4,0},{5,1},{6,2},{7,3},{8,12},{9,13},{10,... | collective-permute-start | bytes 663560 | tf_op jit(solution)/shard_map/ppermute | solution.py:312
  26.6 25.8 %collective-permute-start.6 = (bf16[2,48,768]{2,1,0:T(8,128)(2,1)S(1)}, bf16[2,48,768]{2,1,0:T(8,128)(2,1)S(1)}, u32[]{:S(2)}, u32[]{:S(2)}) collective-permute-start(bf16[2,48,768]{2,1,0:T(8,128)(2,1)S(1)} %get-tuple-element.46), channel_id=1, source_target_pairs={{0,4},{1,5},{2,6},{3,7},{4,0},{5,1},{6,2},{7,3},{8,12},{9,13},{10,... | collective-permute-start | bytes 442376 | tf_op jit(solution)/shard_map/ppermute | solution.py:312
  55.5 14.1 %collective-permute-start.7 = (bf16[2,48,1280]{2,1,0:T(8,128)(2,1)S(1)}, bf16[2,48,1280]{2,1,0:T(8,128)(2,1)S(1)}, u32[]{:S(2)}, u32[]{:S(2)}) collective-permute-start(bf16[2,48,1280]{2,1,0:T(8,128)(2,1)S(1)} %get-tuple-element.52), channel_id=1, source_target_pairs={{0,4},{1,5},{2,6},{3,7},{4,0},{5,1},{6,2},{7,3},{8,12},{9,13},{10,... | collective-permute-start | bytes 737288 | tf_op jit(solution)/shard_map/ppermute | solution.py:312
  93.5 1.0 %copy-start.1 = (bf16[2,64,4096]{2,1,0:T(8,128)(2,1)}, bf16[2,64,4096]{2,1,0:T(8,128)(2,1)S(1)}, u32[]{:S(2)}) copy-start(bf16[2,64,4096]{2,1,0:T(8,128)(2,1)S(1)} %constant_dynamic-update-slice_fusion.1) | copy-start | bytes 3145732

commit v5 on v3

--- a/solution.py
+++ b/solution.py
@@ -263,43 +263,42 @@
     )
 
 
+MARKS = (
+    (6, 12, 24),
+    (5, 11, 17, 23, 29),
+    (4, 10, 16, 22, 27),
+    (1, 3, 8, 22, 26),
+)
+ORDER = (
+    (0, 0), (0, 1), (0, 2), (1, 0), (1, 1), (2, 0), (1, 2), (2, 1), (0, 3), (1, 3), (2, 2),
+    (3, 0), (1, 4), (2, 3), (3, 1), (3, 2), (1, 5), (2, 4), (2, 5), (3, 3), (3, 4), (3, 5),
+)
+
+
 def chunk_bounds(level, levels, length):
-    marks = ((4, 12, 20, 28), (6, 14, 21, 29), (7, 16, 22), (8, 18))
+    marks = MARKS[len(MARKS) - 1 - min(levels - level, len(MARKS) - 1)]
     tiles = length // LANES
-    chosen = marks[min(levels - level, len(marks) - 1)]
-    inner = [tiles * mark // 32 for mark in chosen]
-    return [0] + [mark * LANES for mark in inner] + [length]
+    return [0] + [tiles * mark // 32 * LANES for mark in marks] + [length]
 
 
 def merge_order(levels, bounds):
+    if levels == len(MARKS):
+        return ORDER
     length = bounds[0][-1]
-    sending = [18.0] * (levels - 1) + [36.0]
-    fixed, working, starting, flying = 0.75, 9.0, 1.5, 2.0
-    clock = 5.0
-    arrival = {(0, 0): clock}
-    busy = [clock] * levels
-    following = [0] * levels
+    made = [0] * levels
     order = []
     while len(order) < sum(len(bound) - 1 for bound in bounds[1:]):
-        choices = []
+        ready = []
         for level in range(levels):
-            chunk = following[level]
-            if chunk == len(bounds[level + 1]) - 1:
-                continue
-            needed = pieces_of(bounds[level], 0, min(bounds[level + 1][chunk + 1] + LANES, length))
-            times = [arrival.get((level, piece[0])) for piece in needed]
-            if None not in times:
-                choices.append((max(times + [clock]), -level, chunk))
-        begin, level, chunk = min(choices)
-        level = -level
-        following[level] += 1
+            chunk = made[level]
+            if chunk < len(bounds[level + 1]) - 1:
+                stop = min(bounds[level + 1][chunk + 1] + LANES, length)
+                needed = len(pieces_of(bounds[level], 0, stop))
+                if level == 0 or needed <= made[level - 1]:
+                    ready.append((level + chunk, level, chunk))
+        _, level, chunk = min(ready)
+        made[level] += 1
         order.append((level, chunk))
-        width = (bounds[level + 1][chunk + 1] - bounds[level + 1][chunk]) / length
-        clock = begin + fixed + working * width
-        if level < levels - 1:
-            clock += starting
-            busy[level + 1] = max(busy[level + 1], clock) + sending[level + 1] * width
-            arrival[level + 1, chunk] = busy[level + 1] + flying
     return order
 
 

time: 70.4 us -> 66.4 us (0.943)
  waiting for transfers between devices: 22.2 us -> 12.6 us
  starting transfers between devices: 20.6 us -> 25.1 us
  Pallas kernels: 24.5 us -> 25.7 us
    ppermute x13 -> x17, waiting for transfers between devices: 22.2 us -> 12.6 us  [from_partner(): return lax.ppermute(value, 'pulse', pairs)]
    ppermute x13 -> x17, starting transfers between devices: 20.6 us -> 25.1 us  [from_partner(): return lax.ppermute(value, 'pulse', pairs)]
    pallas_call x17 -> x22, Pallas kernels: 23.7 us -> 24.8 us  [merge(): pl.pallas_call(functools.partial(merge_kernel, level, plan, start, stop,...]
  transfers between devices with their start and end apart: 13 -> 17, of which waited for: 7 -> 7; matrix products, arithmetic and copies ran while one was open for 2% -> 2% of each run, Pallas kernels for 32% -> 36%
where the time goes in v5:
time: 66.4 us; the launch traced here: 66.2 us
  Pallas kernels  25.7 us (39%)
  starting transfers between devices  25.1 us (38%)
  waiting for transfers between devices  12.6 us (19%)
  other arithmetic  1.54 us (2%)
  local copies, waits for them, and re-layouts  1.06 us (2%)
    ppermute x17, starting transfers between devices, from_partner(): return lax.ppermute(value, 'pulse', pairs)  25.1 us
    pallas_call x22, Pallas kernels, merge(): pl.pallas_call(functools.partial(merge_kernel, level, plan, start, stop,...  24.8 us
    ppermute x17, waiting for transfers between devices, from_partner(): return lax.ppermute(value, 'pulse', pairs)  12.6 us
    add x2, other arithmetic, stacked(): total = total + lax.pad(piece, zero, ((top, below, 0), (left, right, 0)))  1.54 us
  transfers between devices with their start and end apart: 17, of which 7 were waited for; matrix products, arithmetic and copies ran while one was open for 2% of the time, Pallas kernels for 36%

profile of v5, /device:TPU:0, one launch (start us, length us, event | category | flops | bytes accessed | tf_op | source)
XLA Modules:
  0.0 66.2 jit_solution(11697557206391686533)
XLA Ops:
  0.0 0.5 collective-permute-start
  0.5 0.7 %pad_add_fusion.real_ref = f32[14,128]{1,0:T(8,128)S(1)} fusion(f32[4,16]{1,0:T(4,128)} %bitcast.3, f32[8,128]{1,0:T(8,128)} %bitcast.2, bf16[2,32]{1,0:T(2,128)(2,1)} %param.8), kind=kLoop, calls=%fused_computation.6 | loop fusion | flops 5376 | bytes 11648 | tf_op jit(solution)/shard_map/add | solution.py:91
  1.2 0.8 %pad_add_fusion.1.whole_ref = s32[12,128]{1,0:T(8,128)S(1)} fusion(s32[4,64]{1,0:T(4,128)} %param.11, s32[4,16]{1,0:T(4,128)} %param.12, s32[4,16]{1,0:T(4,128)} %param.13), kind=kLoop, calls=%fused_computation.7 | loop fusion | flops 4608 | bytes 7680 | tf_op jit(solution)/shard_map/add | solution.py:91
  2.0 0.9 %mixing.1 = (bf16[4,256,768]{2,1,0:T(8,128)(2,1)S(1)}, f32[4,8,128]{2,1,0:T(8,128)S(1)}) custom-call(s32[12,128]{1,0:T(8,128)S(1)} %pad_add_fusion.1.whole_ref, f32[14,128]{1,0:T(8,128)S(1)} %pad_add_fusion.real_ref), custom_call_target="tpu_custom_call" | custom-call | flops 2000000000 | bytes 1572864 | tf_op jit(solution)/shard_map/mixing/pallas_call | solution.py:121
  3.0 0.3 copy-done
  3.2 1.1 %merge_0.4 = (bf16[2,64,768]{2,1,0:T(8,128)(2,1)S(1)}, bf16[2,48,768]{2,1,0:T(8,128)(2,1)S(1)}) custom-call(f32[4,8,128]{2,1,0:T(8,128)S(1)} %get-tuple-element.39.refs_0_, bf16[4,256,768]{2,1,0:T(8,128)(2,1)S(1)} %get-tuple-element.40.refs_1_.refs_4_, bf16[2,64,4096]{2,1,0:T(8,128)(2,1)S(1)} %copy-done, ...), custom_call_target="tpu_custom_call" | custom-call | flops 1207959552 | tf_op jit(solution)/shard_map/merge_0/pallas_call | solution.py:238
  4.3 2.7 %collective-permute-start.1 = (bf16[2,48,768]{2,1,0:T(8,128)(2,1)S(1)}, bf16[2,48,768]{2,1,0:T(8,128)(2,1)S(1)}, u32[]{:S(2)}, u32[]{:S(2)}) collective-permute-start(bf16[2,48,768]{2,1,0:T(8,128)(2,1)S(1)} %get-tuple-element.42), channel_id=1, source_target_pairs={{0,2},{1,3},{2,0},{3,1},{4,6},{5,7},{6,4},{7,5},{8,10},{9,11},{10,... | collective-permute-start | bytes 442376 | tf_op jit(solution)/shard_map/ppermute | solution.py:308
  7.0 1.1 %merge_0.5 = (bf16[2,64,768]{2,1,0:T(8,128)(2,1)S(1)}, bf16[2,48,768]{2,1,0:T(8,128)(2,1)S(1)}) custom-call(f32[4,8,128]{2,1,0:T(8,128)S(1)} %get-tuple-element.39.refs_0_, bf16[4,256,768]{2,1,0:T(8,128)(2,1)S(1)} %get-tuple-element.40.refs_1_.refs_4_, bf16[2,64,4096]{2,1,0:T(8,128)(2,1)S(1)} %copy-done, ...), custom_call_target="tpu_custom_call" | custom-call | flops 1207959552 | tf_op jit(solution)/shard_map/merge_0/pallas_call | solution.py:238
  8.2 2.0 %merge_0.6 = (bf16[2,64,1536]{2,1,0:T(8,128)(2,1)S(1)}, bf16[2,48,1536]{2,1,0:T(8,128)(2,1)S(1)}) custom-call(f32[4,8,128]{2,1,0:T(8,128)S(1)} %get-tuple-element.39.refs_0_, bf16[4,256,768]{2,1,0:T(8,128)(2,1)S(1)} %get-tuple-element.40.refs_1_.refs_4_, bf16[2,64,4096]{2,1,0:T(8,128)(2,1)S(1)} %copy-done, ...), custom_call_target="tpu_custom_call" | custom-call | flops 2415919104 | tf_op jit(solution)/shard_map/merge_0/pallas_call | solution.py:238
  10.2 2.1 %collective-permute-start.5 = (bf16[2,48,1536]{2,1,0:T(8,128)(2,1)S(1)}, bf16[2,48,1536]{2,1,0:T(8,128)(2,1)S(1)}, u32[]{:S(2)}, u32[]{:S(2)}) collective-permute-start(bf16[2,48,1536]{2,1,0:T(8,128)(2,1)S(1)} %get-tuple-element.51), channel_id=1, source_target_pairs={{0,2},{1,3},{2,0},{3,1},{4,6},{5,7},{6,4},{7,5},{8,10},{9,11},{10,... | collective-permute-start | bytes 884744 | tf_op jit(solution)/shard_map/ppermute | solution.py:308
  12.3 1.1 %merge_1.6 = (bf16[2,64,640]{2,1,0:T(8,128)(2,1)S(1)}, bf16[2,48,640]{2,1,0:T(8,128)(2,1)S(1)}) custom-call(f32[4,8,128]{2,1,0:T(8,128)S(1)} %get-tuple-element.39.refs_0_, bf16[4,256,768]{2,1,0:T(8,128)(2,1)S(1)} %get-tuple-element.40.refs_1_.refs_4_, bf16[2,64,768]{2,1,0:T(8,128)(2,1)S(1)} %get-tuple-element.41.refs_4_.refs_2_, ...), custom_call_target="tpu_custom_call" | custom-call | flops 1006632960 | tf_op jit(solution)/shard_map/merge_1/pallas_call | solution.py:238
  13.3 1.6 %collective-permute-start.2 = (bf16[2,48,640]{2,1,0:T(8,128)(2,1)S(1)}, bf16[2,48,640]{2,1,0:T(8,128)(2,1)S(1)}, u32[]{:S(2)}, u32[]{:S(2)}) collective-permute-start(bf16[2,48,640]{2,1,0:T(8,128)(2,1)S(1)} %get-tuple-element.46), channel_id=1, source_target_pairs={{0,4},{1,5},{2,6},{3,7},{4,0},{5,1},{6,2},{7,3},{8,12},{9,13},{10,... | collective-permute-start | bytes 368648 | tf_op jit(solution)/shard_map/ppermute | solution.py:308
  15.0 1.1 %merge_1.7 = (bf16[2,64,768]{2,1,0:T(8,128)(2,1)S(1)}, bf16[2,48,768]{2,1,0:T(8,128)(2,1)S(1)}) custom-call(f32[4,8,128]{2,1,0:T(8,128)S(1)} %get-tuple-element.39.refs_0_, bf16[4,256,768]{2,1,0:T(8,128)(2,1)S(1)} %get-tuple-element.40.refs_1_.refs_4_, bf16[2,64,768]{2,1,0:T(8,128)(2,1)S(1)} %get-tuple-element.41.refs_4_.refs_2_, ...), custom_call_target="tpu_custom_call" | custom-call | flops 1207959552 | tf_op jit(solution)/shard_map/merge_1/pallas_call | solution.py:238
  16.1 2.0 %collective-permute-start.6 = (bf16[2,48,768]{2,1,0:T(8,128)(2,1)S(1)}, bf16[2,48,768]{2,1,0:T(8,128)(2,1)S(1)}, u32[]{:S(2)}, u32[]{:S(2)}) collective-permute-start(bf16[2,48,768]{2,1,0:T(8,128)(2,1)S(1)} %get-tuple-element.53), channel_id=1, source_target_pairs={{0,4},{1,5},{2,6},{3,7},{4,0},{5,1},{6,2},{7,3},{8,12},{9,13},{10,... | collective-permute-start | bytes 442376 | tf_op jit(solution)/shard_map/ppermute | solution.py:308
  18.0 0.5 collective-permute-done.2.refs_3_.refs_4_
  18.5 0.9 %merge_2.6 = (bf16[2,64,512]{2,1,0:T(8,128)(2,1)S(1)}, bf16[2,48,512]{2,1,0:T(8,128)(2,1)S(1)}) custom-call(f32[4,8,128]{2,1,0:T(8,128)S(1)} %get-tuple-element.39.refs_0_, bf16[4,256,768]{2,1,0:T(8,128)(2,1)S(1)} %get-tuple-element.40.refs_1_.refs_4_, bf16[2,64,640]{2,1,0:T(8,128)(2,1)S(1)} %get-tuple-element.45.refs_6_.refs_2_, ...), custom_call_target="tpu_custom_call" | custom-call | flops 805306368 | tf_op jit(solution)/shard_map/merge_2/pallas_call | solution.py:238
  19.4 2.5 %collective-permute-start.4 = (bf16[2,48,512]{2,1,0:T(8,128)(2,1)S(1)}, bf16[2,48,512]{2,1,0:T(8,128)(2,1)S(1)}, u32[]{:S(2)}, u32[]{:S(2)}) collective-permute-start(bf16[2,48,512]{2,1,0:T(8,128)(2,1)S(1)} %get-tuple-element.50), channel_id=1, source_target_pairs={{0,8},{1,9},{2,10},{3,11},{4,12},{5,13},{6,14},{7,15},{8,0},{9,1},... | collective-permute-start | bytes 294920 | tf_op jit(solution)/shard_map/ppermute | solution.py:308
  21.8 1.1 %merge_1.8 = (bf16[2,64,768]{2,1,0:T(8,128)(2,1)S(1)}, bf16[2,48,768]{2,1,0:T(8,128)(2,1)S(1)}) custom-call(f32[4,8,128]{2,1,0:T(8,128)S(1)} %get-tuple-element.39.refs_0_, bf16[4,256,768]{2,1,0:T(8,128)(2,1)S(1)} %get-tuple-element.40.refs_1_.refs_4_, bf16[2,64,768]{2,1,0:T(8,128)(2,1)S(1)} %get-tuple-element.43.refs_4_.refs_3_.refs_2_, ...), custom_call_target="tpu_custom_call" | custom-call | flops 1207959552 | tf_op jit(solution)/shard_map/merge_1/pallas_call | solution.py:238
  22.9 1.1 %merge_2.7 = (bf16[2,64,768]{2,1,0:T(8,128)(2,1)S(1)}, bf16[2,48,768]{2,1,0:T(8,128)(2,1)S(1)}) custom-call(f32[4,8,128]{2,1,0:T(8,128)S(1)} %get-tuple-element.39.refs_0_, bf16[4,256,768]{2,1,0:T(8,128)(2,1)S(1)} %get-tuple-element.40.refs_1_.refs_4_, bf16[2,64,640]{2,1,0:T(8,128)(2,1)S(1)} %get-tuple-element.45.refs_6_.refs_2_, ...), custom_call_target="tpu_custom_call" | custom-call | flops 1207959552 | tf_op jit(solution)/shard_map/merge_2/pallas_call | solution.py:238
  24.0 2.4 %collective-permute-start.10 = (bf16[2,48,768]{2,1,0:T(8,128)(2,1)S(1)}, bf16[2,48,768]{2,1,0:T(8,128)(2,1)S(1)}, u32[]{:S(2)}, u32[]{:S(2)}) collective-permute-start(bf16[2,48,768]{2,1,0:T(8,128)(2,1)S(1)} %get-tuple-element.63), channel_id=1, source_target_pairs={{0,8},{1,9},{2,10},{3,11},{4,12},{5,13},{6,14},{7,15},{8,0},{9,1},... | collective-permute-start | bytes 442376 | tf_op jit(solution)/shard_map/ppermute | solution.py:308
  26.4 1.2 %collective-permute-start.7 = (bf16[2,48,768]{2,1,0:T(8,128)(2,1)S(1)}, bf16[2,48,768]{2,1,0:T(8,128)(2,1)S(1)}, u32[]{:S(2)}, u32[]{:S(2)}) collective-permute-start(bf16[2,48,768]{2,1,0:T(8,128)(2,1)S(1)} %get-tuple-element.54), channel_id=1, source_target_pairs={{0,4},{1,5},{2,6},{3,7},{4,0},{5,1},{6,2},{7,3},{8,12},{9,13},{10,... | collective-permute-start | bytes 442376 | tf_op jit(solution)/shard_map/ppermute | solution.py:308
  27.6 1.6 %merge_0.7 = (bf16[2,64,1024]{2,1,0:T(8,128)(2,1)S(1)}, bf16[2,48,1024]{2,1,0:T(8,128)(2,1)S(1)}) custom-call(f32[4,8,128]{2,1,0:T(8,128)S(1)} %get-tuple-element.39.refs_0_, bf16[4,256,768]{2,1,0:T(8,128)(2,1)S(1)} %get-tuple-element.40.refs_1_.refs_4_, bf16[2,64,4096]{2,1,0:T(8,128)(2,1)S(1)} %copy-done, ...), custom_call_target="tpu_custom_call" | custom-call | flops 1610612736 | tf_op jit(solution)/shard_map/merge_0/pallas_call | solution.py:238
  29.2 1.6 %collective-permute-start.9 = (bf16[2,48,1024]{2,1,0:T(8,128)(2,1)S(1)}, bf16[2,48,1024]{2,1,0:T(8,128)(2,1)S(1)}, u32[]{:S(2)}, u32[]{:S(2)}) collective-permute-start(bf16[2,48,1024]{2,1,0:T(8,128)(2,1)S(1)} %get-tuple-element.60), channel_id=1, source_target_pairs={{0,2},{1,3},{2,0},{3,1},{4,6},{5,7},{6,4},{7,5},{8,10},{9,11},{10,... | collective-permute-start | bytes 589832 | tf_op jit(solution)/shard_map/ppermute | solution.py:308
  30.8 1.1 %merge_1.9 = (bf16[2,64,768]{2,1,0:T(8,128)(2,1)S(1)}, bf16[2,48,768]{2,1,0:T(8,128)(2,1)S(1)}) custom-call(f32[4,8,128]{2,1,0:T(8,128)S(1)} %get-tuple-element.39.refs_0_, bf16[4,256,768]{2,1,0:T(8,128)(2,1)S(1)} %get-tuple-element.40.refs_1_.refs_4_, bf16[2,64,1536]{2,1,0:T(8,128)(2,1)S(1)} %get-tuple-element.44.refs_4_.refs_3_.refs_2_, ...), custom_call_target="tpu_custom_call" | custom-call | flops 1207959552 | tf_op jit(solution)/shard_map/merge_1/pallas_call | solution.py:238
  31.9 0.8 %collective-permute-start.8 = (bf16[2,48,768]{2,1,0:T(8,128)(2,1)S(1)}, bf16[2,48,768]{2,1,0:T(8,128)(2,1)S(1)}, u32[]{:S(2)}, u32[]{:S(2)}) collective-permute-start(bf16[2,48,768]{2,1,0:T(8,128)(2,1)S(1)} %get-tuple-element.59), channel_id=1, source_target_pairs={{0,4},{1,5},{2,6},{3,7},{4,0},{5,1},{6,2},{7,3},{8,12},{9,13},{10,... | collective-permute-start | bytes 442376 | tf_op jit(solution)/shard_map/ppermute | solution.py:308
  32.7 0.5 collective-permute-done.7.refs_5_.refs_4_
  33.1 1.1 %merge_2.8 = (bf16[2,64,768]{2,1,0:T(8,128)(2,1)S(1)}, bf16[2,48,768]{2,1,0:T(8,128)(2,1)S(1)}) custom-call(f32[4,8,128]{2,1,0:T(8,128)S(1)} %get-tuple-element.39.refs_0_, bf16[4,256,768]{2,1,0:T(8,128)(2,1)S(1)} %get-tuple-element.40.refs_1_.refs_4_, bf16[2,64,768]{2,1,0:T(8,128)(2,1)S(1)} %get-tuple-element.48.refs_4_.refs_3_.refs_2_, ...), custom_call_target="tpu_custom_call" | custom-call | flops 1207959552 | tf_op jit(solution)/shard_map/merge_2/pallas_call | solution.py:238
  34.2 2.1 %collective-permute-start.12 = (bf16[2,48,768]{2,1,0:T(8,128)(2,1)S(1)}, bf16[2,48,768]{2,1,0:T(8,128)(2,1)S(1)}, u32[]{:S(2)}, u32[]{:S(2)}) collective-permute-start(bf16[2,48,768]{2,1,0:T(8,128)(2,1)S(1)} %get-tuple-element.67), channel_id=1, source_target_pairs={{0,8},{1,9},{2,10},{3,11},{4,12},{5,13},{6,14},{7,15},{8,0},{9,1},... | collective-permute-start | bytes 442376 | tf_op jit(solution)/shard_map/ppermute | solution.py:308
  36.3 0.6 merge_3.6.refs_6_
  36.9 1.1 %merge_1.10 = (bf16[2,64,768]{2,1,0:T(8,128)(2,1)S(1)}, bf16[2,48,768]{2,1,0:T(8,128)(2,1)S(1)}) custom-call(f32[4,8,128]{2,1,0:T(8,128)S(1)} %get-tuple-element.39.refs_0_, bf16[4,256,768]{2,1,0:T(8,128)(2,1)S(1)} %get-tuple-element.40.refs_1_.refs_4_, bf16[2,64,1536]{2,1,0:T(8,128)(2,1)S(1)} %get-tuple-element.44.refs_4_.refs_3_.refs_2_, ...), custom_call_target="tpu_custom_call" | custom-call | flops 1207959552 | tf_op jit(solution)/shard_map/merge_1/pallas_call | solution.py:238
  38.0 2.1 %collective-permute-start.11 = (bf16[2,48,768]{2,1,0:T(8,128)(2,1)S(1)}, bf16[2,48,768]{2,1,0:T(8,128)(2,1)S(1)}, u32[]{:S(2)}, u32[]{:S(2)}) collective-permute-start(bf16[2,48,768]{2,1,0:T(8,128)(2,1)S(1)} %get-tuple-element.64), channel_id=1, source_target_pairs={{0,4},{1,5},{2,6},{3,7},{4,0},{5,1},{6,2},{7,3},{8,12},{9,13},{10,... | collective-permute-start | bytes 442376 | tf_op jit(solution)/shard_map/ppermute | solution.py:308
  40.1 0.9 %collective-permute-done.8.refs_5_.refs_4_ = bf16[2,48,768]{2,1,0:T(8,128)(2,1)S(1)} collective-permute-done((bf16[2,48,768]{2,1,0:T(8,128)(2,1)S(1)}, bf16[2,48,768]{2,1,0:T(8,128)(2,1)S(1)}, u32[]{:S(2)}, u32[]{:S(2)}) %collective-permute-start.8) | collective-permute-done | bytes 147488 | tf_op jit(solution)/shard_map/ppermute | solution.py:308
  41.1 1.1 %merge_2.9 = (bf16[2,64,768]{2,1,0:T(8,128)(2,1)S(1)}, bf16[2,48,768]{2,1,0:T(8,128)(2,1)S(1)}) custom-call(f32[4,8,128]{2,1,0:T(8,128)S(1)} %get-tuple-element.39.refs_0_, bf16[4,256,768]{2,1,0:T(8,128)(2,1)S(1)} %get-tuple-element.40.refs_1_.refs_4_, bf16[2,64,768]{2,1,0:T(8,128)(2,1)S(1)} %get-tuple-element.52.refs_6_.refs_3_.refs_2_, ...), custom_call_target="tpu_custom_call" | custom-call | flops 1207959552 | tf_op jit(solution)/shard_map/merge_2/pallas_call | solution.py:238
  42.2 0.6 merge_3.7.refs_6_
  42.8 1.1 %merge_3.8.refs_4_ = bf16[2,64,640]{2,1,0:T(8,128)(2,1)S(1)} custom-call(f32[4,8,128]{2,1,0:T(8,128)S(1)} %get-tuple-element.39.refs_0_, bf16[4,256,768]{2,1,0:T(8,128)(2,1)S(1)} %get-tuple-element.40.refs_1_.refs_4_, bf16[2,64,512]{2,1,0:T(8,128)(2,1)S(1)} %get-tuple-element.49.refs_6_.refs_2_, ...), custom_call_target="tpu_custom_call" | custom-call | flops 1006632960 | tf_op jit(solution)/shard_map/merge_3/pallas_call | solution.py:238
  43.9 0.9 %merge_1.11 = (bf16[2,64,384]{2,1,0:T(8,128)(2,1)S(1)}, bf16[2,48,384]{2,1,0:T(8,128)(2,1)S(1)}) custom-call(f32[4,8,128]{2,1,0:T(8,128)S(1)} %get-tuple-element.39.refs_0_, bf16[4,256,768]{2,1,0:T(8,128)(2,1)S(1)} %get-tuple-element.40.refs_1_.refs_4_, bf16[2,64,1024]{2,1,0:T(8,128)(2,1)S(1)} %get-tuple-element.56.refs_4_.refs_3_.refs_2_, ...), custom_call_target="tpu_custom_call" | custom-call | flops 603979776 | tf_op jit(solution)/shard_map/merge_1/pallas_call | solution.py:238
  44.8 0.9 %collective-permute-start.13 = (bf16[2,48,768]{2,1,0:T(8,128)(2,1)S(1)}, bf16[2,48,768]{2,1,0:T(8,128)(2,1)S(1)}, u32[]{:S(2)}, u32[]{:S(2)}) collective-permute-start(bf16[2,48,768]{2,1,0:T(8,128)(2,1)S(1)} %get-tuple-element.68), channel_id=1, source_target_pairs={{0,8},{1,9},{2,10},{3,11},{4,12},{5,13},{6,14},{7,15},{8,0},{9,1},... | collective-permute-start | bytes 442376 | tf_op jit(solution)/shard_map/ppermute | solution.py:308
  45.7 1.1 %merge_2.10 = (bf16[2,64,640]{2,1,0:T(8,128)(2,1)S(1)}, bf16[2,48,640]{2,1,0:T(8,128)(2,1)S(1)}) custom-call(f32[4,8,128]{2,1,0:T(8,128)S(1)} %get-tuple-element.39.refs_0_, bf16[4,256,768]{2,1,0:T(8,128)(2,1)S(1)} %get-tuple-element.40.refs_1_.refs_4_, bf16[2,64,768]{2,1,0:T(8,128)(2,1)S(1)} %get-tuple-element.57.refs_6_.refs_3_.refs_2_, ...), custom_call_target="tpu_custom_call" | custom-call | flops 1006632960 | tf_op jit(solution)/shard_map/merge_2/pallas_call | solution.py:238
  46.8 2.2 %collective-permute-start.14 = (bf16[2,48,640]{2,1,0:T(8,128)(2,1)S(1)}, bf16[2,48,640]{2,1,0:T(8,128)(2,1)S(1)}, u32[]{:S(2)}, u32[]{:S(2)}) collective-permute-start(bf16[2,48,640]{2,1,0:T(8,128)(2,1)S(1)} %get-tuple-element.69), channel_id=1, source_target_pairs={{0,8},{1,9},{2,10},{3,11},{4,12},{5,13},{6,14},{7,15},{8,0},{9,1},... | collective-permute-start | bytes 368648 | tf_op jit(solution)/shard_map/ppermute | solution.py:308
  49.0 0.4 collective-permute-done.15.refs_5_
  49.4 1.1 %merge_2.11 = (bf16[2,64,640]{2,1,0:T(8,128)(2,1)S(1)}, bf16[2,48,640]{2,1,0:T(8,128)(2,1)S(1)}) custom-call(f32[4,8,128]{2,1,0:T(8,128)S(1)} %get-tuple-element.39.refs_0_, bf16[4,256,768]{2,1,0:T(8,128)(2,1)S(1)} %get-tuple-element.40.refs_1_.refs_4_, bf16[2,64,768]{2,1,0:T(8,128)(2,1)S(1)} %get-tuple-element.61.refs_6_.refs_3_.refs_2_, ...), custom_call_target="tpu_custom_call" | custom-call | flops 1006632960 | tf_op jit(solution)/shard_map/merge_2/pallas_call | solution.py:238
  50.5 0.5 collective-permute-start.16
  51.0 7.8 %collective-permute-done.13.refs_8_.refs_4_ = bf16[2,48,768]{2,1,0:T(8,128)(2,1)S(1)} collective-permute-done((bf16[2,48,768]{2,1,0:T(8,128)(2,1)S(1)}, bf16[2,48,768]{2,1,0:T(8,128)(2,1)S(1)}, u32[]{:S(2)}, u32[]{:S(2)}) %collective-permute-start.13) | collective-permute-done | bytes 147488 | tf_op jit(solution)/shard_map/ppermute | solution.py:308
  58.8 2.3 %collective-permute-done.14.refs_9_.refs_5_.refs_4_ = bf16[2,48,640]{2,1,0:T(8,128)(2,1)S(1)} collective-permute-done((bf16[2,48,640]{2,1,0:T(8,128)(2,1)S(1)}, bf16[2,48,640]{2,1,0:T(8,128)(2,1)S(1)}, u32[]{:S(2)}, u32[]{:S(2)}) %collective-permute-start.14) | collective-permute-done | bytes 122912 | tf_op jit(solution)/shard_map/ppermute | solution.py:308
  61.1 2.3 %merge_3.9.refs_6_ = bf16[2,64,1792]{2,1,0:T(8,128)(2,1)S(1)} custom-call(f32[4,8,128]{2,1,0:T(8,128)S(1)} %get-tuple-element.39.refs_0_, bf16[4,256,768]{2,1,0:T(8,128)(2,1)S(1)} %get-tuple-element.40.refs_1_.refs_4_, bf16[2,64,768]{2,1,0:T(8,128)(2,1)S(1)} %get-tuple-element.55.refs_4_.refs_3_.refs_2_, ...), custom_call_target="tpu_custom_call" | custom-call | flops 2818572288 | tf_op jit(solution)/shard_map/merge_3/pallas_call | solution.py:238
  63.5 0.8 %merge_3.10.refs_6_ = bf16[2,64,512]{2,1,0:T(8,128)(2,1)S(1)} custom-call(f32[4,8,128]{2,1,0:T(8,128)S(1)} %get-tuple-element.39.refs_0_, bf16[4,256,768]{2,1,0:T(8,128)(2,1)S(1)} %get-tuple-element.40.refs_1_.refs_4_, bf16[2,64,768]{2,1,0:T(8,128)(2,1)S(1)} %get-tuple-element.62.refs_4_.refs_2_, ...), custom_call_target="tpu_custom_call" | custom-call | flops 805306368 | tf_op jit(solution)/shard_map/merge_3/pallas_call | solution.py:238
  64.4 1.1 %merge_3.11 = bf16[2,64,768]{2,1,0:T(8,128)(2,1)S(1)} custom-call(f32[4,8,128]{2,1,0:T(8,128)S(1)} %get-tuple-element.39.refs_0_, bf16[4,256,768]{2,1,0:T(8,128)(2,1)S(1)} %get-tuple-element.40.refs_1_.refs_4_, bf16[2,64,640]{2,1,0:T(8,128)(2,1)S(1)} %get-tuple-element.66.refs_6_.refs_5_.refs_3_.refs_2_, ...), custom_call_target="tpu_custom_call" | custom-call | flops 1207959552 | tf_op jit(solution)/shard_map/merge_3/pallas_call | solution.py:238
  65.5 0.7 %constant_dynamic-update-slice_fusion = bf16[2,64,4096]{2,1,0:T(8,128)(2,1)} fusion(bf16[2,64,4096]{2,1,0:T(8,128)(2,1)} %copy-done.1, bf16[2,64,768]{2,1,0:T(8,128)(2,1)S(1)} %merge_3.11), kind=kLoop, calls=%fused_computation | loop fusion | bytes 393216 | tf_op jit(solution)/shard_map/concatenate | solution.py:332
  (21 shorter events, 0.4 us)
Async XLA Ops:
  0.0 3.0 %collective-permute-start = (bf16[2,64,4096]{2,1,0:T(8,128)(2,1)}, bf16[2,64,4096]{2,1,0:T(8,128)(2,1)S(1)}, u32[]{:S(2)}, u32[]{:S(2)}) collective-permute-start(bf16[2,64,4096]{2,1,0:T(8,128)(2,1)} %refs_2_.7), channel_id=1, source_target_pairs={{0,1},{1,0},{2,3},{3,2},{4,5},{5,4},{6,7},{7,6},{8,9},{9,8},{10,11... | collective-permute-start | bytes 3145736 | tf_op jit(solution)/shard_map/ppermute | solution.py:308
  2.0 1.2 %copy-start = (bf16[2,64,4096]{2,1,0:T(8,128)(2,1)S(1)}, bf16[2,64,4096]{2,1,0:T(8,128)(2,1)}, u32[]{:S(2)}) copy-start(bf16[2,64,4096]{2,1,0:T(8,128)(2,1)} %refs_2_.7) | copy-start | bytes 3145732
  4.3 7.9 %collective-permute-start.1 = (bf16[2,48,768]{2,1,0:T(8,128)(2,1)S(1)}, bf16[2,48,768]{2,1,0:T(8,128)(2,1)S(1)}, u32[]{:S(2)}, u32[]{:S(2)}) collective-permute-start(bf16[2,48,768]{2,1,0:T(8,128)(2,1)S(1)} %get-tuple-element.42), channel_id=1, source_target_pairs={{0,2},{1,3},{2,0},{3,1},{4,6},{5,7},{6,4},{7,5},{8,10},{9,11},{10,... | collective-permute-start | bytes 442376 | tf_op jit(solution)/shard_map/ppermute | solution.py:308
  8.1 6.9 %collective-permute-start.3 = (bf16[2,48,768]{2,1,0:T(8,128)(2,1)S(1)}, bf16[2,48,768]{2,1,0:T(8,128)(2,1)S(1)}, u32[]{:S(2)}, u32[]{:S(2)}) collective-permute-start(bf16[2,48,768]{2,1,0:T(8,128)(2,1)S(1)} %get-tuple-element.47), channel_id=1, source_target_pairs={{0,2},{1,3},{2,0},{3,1},{4,6},{5,7},{6,4},{7,5},{8,10},{9,11},{10,... | collective-permute-start | bytes 442376 | tf_op jit(solution)/shard_map/ppermute | solution.py:308
  10.2 11.6 %collective-permute-start.5 = (bf16[2,48,1536]{2,1,0:T(8,128)(2,1)S(1)}, bf16[2,48,1536]{2,1,0:T(8,128)(2,1)S(1)}, u32[]{:S(2)}, u32[]{:S(2)}) collective-permute-start(bf16[2,48,1536]{2,1,0:T(8,128)(2,1)S(1)} %get-tuple-element.51), channel_id=1, source_target_pairs={{0,2},{1,3},{2,0},{3,1},{4,6},{5,7},{6,4},{7,5},{8,10},{9,11},{10,... | collective-permute-start | bytes 884744 | tf_op jit(solution)/shard_map/ppermute | solution.py:308
  13.3 5.2 %collective-permute-start.2 = (bf16[2,48,640]{2,1,0:T(8,128)(2,1)S(1)}, bf16[2,48,640]{2,1,0:T(8,128)(2,1)S(1)}, u32[]{:S(2)}, u32[]{:S(2)}) collective-permute-start(bf16[2,48,640]{2,1,0:T(8,128)(2,1)S(1)} %get-tuple-element.46), channel_id=1, source_target_pairs={{0,4},{1,5},{2,6},{3,7},{4,0},{5,1},{6,2},{7,3},{8,12},{9,13},{10,... | collective-permute-start | bytes 368648 | tf_op jit(solution)/shard_map/ppermute | solution.py:308
  16.1 6.9 %collective-permute-start.6 = (bf16[2,48,768]{2,1,0:T(8,128)(2,1)S(1)}, bf16[2,48,768]{2,1,0:T(8,128)(2,1)S(1)}, u32[]{:S(2)}, u32[]{:S(2)}) collective-permute-start(bf16[2,48,768]{2,1,0:T(8,128)(2,1)S(1)} %get-tuple-element.53), channel_id=1, source_target_pairs={{0,4},{1,5},{2,6},{3,7},{4,0},{5,1},{6,2},{7,3},{8,12},{9,13},{10,... | collective-permute-start | bytes 442376 | tf_op jit(solution)/shard_map/ppermute | solution.py:308
  19.4 17.0 %collective-permute-start.4 = (bf16[2,48,512]{2,1,0:T(8,128)(2,1)S(1)}, bf16[2,48,512]{2,1,0:T(8,128)(2,1)S(1)}, u32[]{:S(2)}, u32[]{:S(2)}) collective-permute-start(bf16[2,48,512]{2,1,0:T(8,128)(2,1)S(1)} %get-tuple-element.50), channel_id=1, source_target_pairs={{0,8},{1,9},{2,10},{3,11},{4,12},{5,13},{6,14},{7,15},{8,0},{9,1},... | collective-permute-start | bytes 294920 | tf_op jit(solution)/shard_map/ppermute | solution.py:308
  24.0 18.8 %collective-permute-start.10 = (bf16[2,48,768]{2,1,0:T(8,128)(2,1)S(1)}, bf16[2,48,768]{2,1,0:T(8,128)(2,1)S(1)}, u32[]{:S(2)}, u32[]{:S(2)}) collective-permute-start(bf16[2,48,768]{2,1,0:T(8,128)(2,1)S(1)} %get-tuple-element.63), channel_id=1, source_target_pairs={{0,8},{1,9},{2,10},{3,11},{4,12},{5,13},{6,14},{7,15},{8,0},{9,1},... | collective-permute-start | bytes 442376 | tf_op jit(solution)/shard_map/ppermute | solution.py:308
  26.4 6.7 %collective-permute-start.7 = (bf16[2,48,768]{2,1,0:T(8,128)(2,1)S(1)}, bf16[2,48,768]{2,1,0:T(8,128)(2,1)S(1)}, u32[]{:S(2)}, u32[]{:S(2)}) collective-permute-start(bf16[2,48,768]{2,1,0:T(8,128)(2,1)S(1)} %get-tuple-element.54), channel_id=1, source_target_pairs={{0,4},{1,5},{2,6},{3,7},{4,0},{5,1},{6,2},{7,3},{8,12},{9,13},{10,... | collective-permute-start | bytes 442376 | tf_op jit(solution)/shard_map/ppermute | solution.py:308
  29.2 7.7 %collective-permute-start.9 = (bf16[2,48,1024]{2,1,0:T(8,128)(2,1)S(1)}, bf16[2,48,1024]{2,1,0:T(8,128)(2,1)S(1)}, u32[]{:S(2)}, u32[]{:S(2)}) collective-permute-start(bf16[2,48,1024]{2,1,0:T(8,128)(2,1)S(1)} %get-tuple-element.60), channel_id=1, source_target_pairs={{0,2},{1,3},{2,0},{3,1},{4,6},{5,7},{6,4},{7,5},{8,10},{9,11},{10,... | collective-permute-start | bytes 589832 | tf_op jit(solution)/shard_map/ppermute | solution.py:308
  31.9 9.2 %collective-permute-start.8 = (bf16[2,48,768]{2,1,0:T(8,128)(2,1)S(1)}, bf16[2,48,768]{2,1,0:T(8,128)(2,1)S(1)}, u32[]{:S(2)}, u32[]{:S(2)}) collective-permute-start(bf16[2,48,768]{2,1,0:T(8,128)(2,1)S(1)} %get-tuple-element.59), channel_id=1, source_target_pairs={{0,4},{1,5},{2,6},{3,7},{4,0},{5,1},{6,2},{7,3},{8,12},{9,13},{10,... | collective-permute-start | bytes 442376 | tf_op jit(solution)/shard_map/ppermute | solution.py:308
  34.2 16.8 %collective-permute-start.12 = (bf16[2,48,768]{2,1,0:T(8,128)(2,1)S(1)}, bf16[2,48,768]{2,1,0:T(8,128)(2,1)S(1)}, u32[]{:S(2)}, u32[]{:S(2)}) collective-permute-start(bf16[2,48,768]{2,1,0:T(8,128)(2,1)S(1)} %get-tuple-element.67), channel_id=1, source_target_pairs={{0,8},{1,9},{2,10},{3,11},{4,12},{5,13},{6,14},{7,15},{8,0},{9,1},... | collective-permute-start | bytes 442376 | tf_op jit(solution)/shard_map/ppermute | solution.py:308
  38.0 7.7 %collective-permute-start.11 = (bf16[2,48,768]{2,1,0:T(8,128)(2,1)S(1)}, bf16[2,48,768]{2,1,0:T(8,128)(2,1)S(1)}, u32[]{:S(2)}, u32[]{:S(2)}) collective-permute-start(bf16[2,48,768]{2,1,0:T(8,128)(2,1)S(1)} %get-tuple-element.64), channel_id=1, source_target_pairs={{0,4},{1,5},{2,6},{3,7},{4,0},{5,1},{6,2},{7,3},{8,12},{9,13},{10,... | collective-permute-start | bytes 442376 | tf_op jit(solution)/shard_map/ppermute | solution.py:308
  44.7 4.7 %collective-permute-start.15 = (bf16[2,48,384]{2,1,0:T(8,128)(2,1)S(1)}, bf16[2,48,384]{2,1,0:T(8,128)(2,1)S(1)}, u32[]{:S(2)}, u32[]{:S(2)}) collective-permute-start(bf16[2,48,384]{2,1,0:T(8,128)(2,1)S(1)} %get-tuple-element.70), channel_id=1, source_target_pairs={{0,4},{1,5},{2,6},{3,7},{4,0},{5,1},{6,2},{7,3},{8,12},{9,13},{10,... | collective-permute-start | bytes 221192 | tf_op jit(solution)/shard_map/ppermute | solution.py:308
  44.8 14.0 %collective-permute-start.13 = (bf16[2,48,768]{2,1,0:T(8,128)(2,1)S(1)}, bf16[2,48,768]{2,1,0:T(8,128)(2,1)S(1)}, u32[]{:S(2)}, u32[]{:S(2)}) collective-permute-start(bf16[2,48,768]{2,1,0:T(8,128)(2,1)S(1)} %get-tuple-element.68), channel_id=1, source_target_pairs={{0,8},{1,9},{2,10},{3,11},{4,12},{5,13},{6,14},{7,15},{8,0},{9,1},... | collective-permute-start | bytes 442376 | tf_op jit(solution)/shard_map/ppermute | solution.py:308
  46.8 14.3 %collective-permute-start.14 = (bf16[2,48,640]{2,1,0:T(8,128)(2,1)S(1)}, bf16[2,48,640]{2,1,0:T(8,128)(2,1)S(1)}, u32[]{:S(2)}, u32[]{:S(2)}) collective-permute-start(bf16[2,48,640]{2,1,0:T(8,128)(2,1)S(1)} %get-tuple-element.69), channel_id=1, source_target_pairs={{0,8},{1,9},{2,10},{3,11},{4,12},{5,13},{6,14},{7,15},{8,0},{9,1},... | collective-permute-start | bytes 368648 | tf_op jit(solution)/shard_map/ppermute | solution.py:308
  50.5 13.9 %collective-permute-start.16 = (bf16[2,48,640]{2,1,0:T(8,128)(2,1)S(1)}, bf16[2,48,640]{2,1,0:T(8,128)(2,1)S(1)}, u32[]{:S(2)}, u32[]{:S(2)}) collective-permute-start(bf16[2,48,640]{2,1,0:T(8,128)(2,1)S(1)} %get-tuple-element.72), channel_id=1, source_target_pairs={{0,8},{1,9},{2,10},{3,11},{4,12},{5,13},{6,14},{7,15},{8,0},{9,1},... | collective-permute-start | bytes 368648 | tf_op jit(solution)/shard_map/ppermute | solution.py:308
  64.4 1.1 %copy-start.1 = (bf16[2,64,4096]{2,1,0:T(8,128)(2,1)}, bf16[2,64,4096]{2,1,0:T(8,128)(2,1)S(1)}, u32[]{:S(2)}) copy-start(bf16[2,64,4096]{2,1,0:T(8,128)(2,1)S(1)} %constant_dynamic-update-slice_fusion.1) | copy-start | bytes 3145732

commit v6 on v5

--- a/solution.py
+++ b/solution.py
@@ -9,10 +9,12 @@
 
 LANES = 128
 TILE = 256
+GROUP = 16
 SCALE = 0.70710678
 
 
-def prep_kernel(levels, beams, utaps, phases, rtaps, whole_ref, real_ref, mix_ref, plan_ref, band_ref, flat_ref):
+def prep_kernel(levels, beams, utaps, phases, rtaps, whole_ref, real_ref, mix_ref, weight_ref,
+                plan_ref, band_ref, flat_ref):
     at_shifts, at_taps = levels, 2 * levels
     at_ukern, at_rkern = 2 * levels, 2 * levels + 2
     window = beams // 2 + utaps // 2
@@ -54,14 +56,13 @@
             low_half, band_ref[utaps // 2:utaps // 2 + window, :], band_ref[0:window, :]
         )
         chosen = whole_ref[at_taps + level:at_taps + level + 1, :]
-        weights = []
         for tap in range(rtaps):
             weight = jnp.zeros((1, 2 * beams), jnp.float32)
             for phase in range(phases):
                 weight = jnp.where(
                     chosen == phase, table[tap:tap + 1, phase:phase + 1], weight
                 )
-            weights.append(weight)
+            weight_ref[level, tap] = jnp.broadcast_to(weight, (LANES, 2 * beams)).T
         for child in range(2):
             side = bit if child == 0 else 1 - bit
             angle = real_ref[pl.ds(2 * level + side, 1), :]
@@ -70,17 +71,16 @@
             cosine = SCALE * jnp.cos(angle)
             sine = SCALE * jnp.sin(angle)
             factors = (jnp.where(first, cosine, sine), jnp.where(first, -sine, cosine))
-            for tap in range(rtaps):
-                for part in range(2):
-                    place = ((child * rtaps + tap) * 2 + part) * window
-                    flat_ref[place:place + window, :] = near * (factors[part] * weights[tap])
-        for block in range(flat_ref.shape[0] // LANES):
-            mixed = flat_ref[block * LANES:(block + 1) * LANES, :].T
+            for part in range(2):
+                spot = (child * 2 + part) * window
+                flat_ref[spot:spot + window, :] = near * factors[part]
+        for top in range(0, 4 * window, LANES):
+            bottom = min(top + LANES, 4 * window)
+            mixed = flat_ref[top:bottom, :].T
             high = mixed.astype(jnp.bfloat16)
             low = (mixed - high.astype(jnp.float32)).astype(jnp.bfloat16)
-            columns = pl.ds(block * LANES, LANES)
-            mix_ref[level, 0:2 * beams, columns] = high
-            mix_ref[level, 2 * beams:4 * beams, columns] = low
+            mix_ref[level, 0:2 * beams, top:bottom] = high
+            mix_ref[level, 2 * beams:4 * beams, top:bottom] = low
 
 
 def stacked(height, pieces):
@@ -98,7 +98,7 @@
     utaps = ukern.shape[1]
     phases, rtaps = rkern.shape
     window = beams // 2 + utaps // 2
-    depth = 2 * rtaps * 2 * window
+    depth = 4 * window
     vmem = pl.BlockSpec(memory_space=pltpu.VMEM)
 
     whole = stacked(
@@ -122,30 +122,31 @@
         functools.partial(prep_kernel, levels, beams, utaps, phases, rtaps),
         out_shape=[
             jax.ShapeDtypeStruct((levels, 4 * beams, depth), jnp.bfloat16),
+            jax.ShapeDtypeStruct((levels, rtaps, 2 * beams, LANES), jnp.float32),
             jax.ShapeDtypeStruct((levels, 8, LANES), jnp.float32),
         ],
         in_specs=[vmem, vmem],
-        out_specs=[vmem, vmem],
+        out_specs=[vmem, vmem, vmem],
         scratch_shapes=[
             pltpu.VMEM((beams // 2 + utaps, 2 * beams), jnp.float32),
             pltpu.VMEM((depth, 2 * beams), jnp.float32),
         ],
         compiler_params=pltpu.CompilerParams(vmem_limit_bytes=24 * 2**20),
         cost_estimate=pl.CostEstimate(
-            flops=2 * 10**9, bytes_accessed=2 * levels * 4 * beams * depth, transcendentals=0
+            flops=2 * 10**9, bytes_accessed=32 * levels * beams * depth, transcendentals=0
         ),
         name="mixing",
     )(whole, real)
 
 
 def merge_kernel(level, plan, start, stop, length, beams, window, rtaps, last, *refs):
-    code_ref, mix_ref = refs[:2]
+    code_ref, mix_ref, weight_ref = refs[:3]
     count = len(plan)
-    own_refs, far_refs = refs[2:2 + count], refs[2 + count:2 + 2 * count]
-    outs = refs[3 + 2 * count:]
+    own_refs, far_refs = refs[3:3 + count], refs[3 + count:3 + 2 * count]
+    outs = refs[4 + 2 * count:]
     out_ref = outs[0]
     send_ref = None if last else outs[1]
-    wide_ref, even_ref, odd_ref = outs[1 if last else 2:]
+    wide_ref, even_ref, odd_ref, even_sum_ref, odd_sum_ref = outs[1 if last else 2:]
     code = jnp.max(code_ref[level]).astype(jnp.int32)
     half, following = code // 131072, code // 65536 % 2
     shifts = (code // 256 % 256 - LANES, code % 256 - LANES)
@@ -163,53 +164,72 @@
         wide_ref[:, :, :, 0:LANES] = edge
     if stop + LANES > length:
         wide_ref[:, :, :, stop - base:stop - base + LANES] = edge
+    wide_ref[:, :, :, stop - base + LANES:stop - base + 2 * LANES] = edge
     span = stop - start
     tile = min(TILE, span)
     tiles = pl.cdiv(span, tile)
     lane = lax.broadcasted_iota(jnp.int32, (2 * window, LANES), 1).astype(jnp.int16)
     moves = []
     for child in range(2):
-        for tap in range(rtaps):
-            shift = shifts[child] + (tap - 1 + LANES)
-            part_tile = lax.rem(shift, LANES)
-            kept = jnp.full((2 * window, LANES), LANES - part_tile, jnp.int32).astype(jnp.int16)
-            turn = lax.rem(LANES - part_tile, LANES)
-            moves.append((child, tap, shift // LANES * LANES, turn, lane < kept))
+        shift = shifts[child] + (LANES - 1)
+        part_tile = lax.rem(shift, LANES)
+        kept = jnp.full((2 * window, LANES), LANES - part_tile, jnp.int32).astype(jnp.int16)
+        turn = lax.rem(LANES - part_tile, LANES)
+        moves.append((child, shift // LANES * LANES, turn, lane < kept))
+    blocks = tile // LANES
+    place = lax.broadcasted_iota(jnp.int32, (GROUP, LANES), 1)
 
     def column_of(step):
         return pl.multiple_of(jnp.minimum(step * tile, span - tile), LANES)
 
     def build(stack_ref, step):
         column = column_of(step)
-        for child, tap, whole, turn, kept in moves:
-            place = (child * rtaps + tap) * 2 * window
+        for child, whole, turn, kept in moves:
+            top = child * 2 * window
             held = None
-            for block in range(tile // LANES + 1):
+            for block in range(blocks + 2):
                 at = pl.multiple_of(column + whole + block * LANES, LANES)
                 piece = wide_ref[child, :, :, pl.ds(at, LANES)].reshape(2 * window, LANES)
                 piece = pltpu.roll(piece, turn, 1)
                 if block > 0:
                     columns = pl.ds((block - 1) * LANES, LANES)
-                    stack_ref[place:place + 2 * window, columns] = jnp.where(kept, held, piece)
+                    stack_ref[top:top + 2 * window, columns] = jnp.where(kept, held, piece)
                 held = piece
 
-    def multiply(stack_ref, step):
+    def multiply(stack_ref, sum_ref, step):
         column = column_of(step)
         both = jnp.dot(mix_ref[level], stack_ref[...], preferred_element_type=jnp.float32)
-        total = (both[:2 * beams] + both[2 * beams:]).astype(jnp.bfloat16)
-        out_ref[:, :, pl.ds(column, tile)] = total.reshape(2, beams, tile)
+        sum_ref[...] = both[:2 * beams] + both[2 * beams:]
+        for top in range(0, 2 * beams, GROUP):
+            rows = pl.ds(top, GROUP)
+            turned = []
+            for block in range(blocks + 1):
+                value = sum_ref[rows, pl.ds(block * LANES, LANES)]
+                turned.append(
+                    [value] + [pltpu.roll(value, LANES - tap, 1) for tap in range(1, rtaps)]
+                )
+            for block in range(blocks):
+                total = weight_ref[level, 0, rows, :] * turned[block][0]
+                for tap in range(1, rtaps):
+                    moved = jnp.where(
+                        place < LANES - tap, turned[block][tap], turned[block + 1][tap]
+                    )
+                    total = total + weight_ref[level, tap, rows, :] * moved
+                columns = pl.ds(pl.multiple_of(column + block * LANES, LANES), LANES)
+                part, beam = top // beams, top % beams
+                out_ref[part, beam:beam + GROUP, columns] = total.astype(jnp.bfloat16)
 
     def two_tiles(pair, carry):
         build(odd_ref, 2 * pair + 1)
-        multiply(even_ref, 2 * pair)
+        multiply(even_ref, even_sum_ref, 2 * pair)
         build(even_ref, 2 * pair + 2)
-        multiply(odd_ref, 2 * pair + 1)
+        multiply(odd_ref, odd_sum_ref, 2 * pair + 1)
         return carry
 
     build(even_ref, 0)
     lax.fori_loop(0, tiles // 2, two_tiles, 0)
     if tiles % 2 == 1:
-        multiply(even_ref, tiles - 1)
+        multiply(even_ref, even_sum_ref, tiles - 1)
     if not last:
         other = pl.ds(pl.multiple_of((1 - following) * (beams - window), 16), window)
         send_ref[...] = out_ref[:, other, :]
@@ -224,7 +244,7 @@
     return found
 
 
-def merge(level, levels, codes, mix, own, far, bounds, start, stop, sizes, before):
+def merge(level, levels, codes, mix, weights, own, far, bounds, start, stop, sizes, before):
     beams, window, rtaps, length = sizes
     last = level == levels - 1
     plan = pieces_of(bounds, max(start - LANES, 0), min(stop + LANES, length))
@@ -232,6 +252,7 @@
     vmem = pl.BlockSpec(memory_space=pltpu.VMEM)
     anywhere = pl.BlockSpec(memory_space=pl.ANY)
     depth = mix.shape[2]
+    tile = min(TILE, span)
     out_shape = [jax.ShapeDtypeStruct((2, beams, span), jnp.bfloat16)]
     if not last:
         out_shape.append(jax.ShapeDtypeStruct((2, window, span), jnp.bfloat16))
@@ -240,16 +261,18 @@
             merge_kernel, level, plan, start, stop, length, beams, window, rtaps, last
         ),
         out_shape=out_shape,
-        in_specs=[vmem, vmem] + [vmem] * (2 * len(plan)) + [anywhere],
+        in_specs=[vmem] * (3 + 2 * len(plan)) + [anywhere],
         out_specs=[vmem] * len(out_shape),
         scratch_shapes=[
-            pltpu.VMEM((2, 2, window, span + 2 * LANES), jnp.bfloat16),
-            pltpu.VMEM((depth, min(TILE, span)), jnp.bfloat16),
-            pltpu.VMEM((depth, min(TILE, span)), jnp.bfloat16),
+            pltpu.VMEM((2, 2, window, span + 3 * LANES), jnp.bfloat16),
+            pltpu.VMEM((depth, tile + LANES), jnp.bfloat16),
+            pltpu.VMEM((depth, tile + LANES), jnp.bfloat16),
+            pltpu.VMEM((2 * beams, tile + LANES), jnp.float32),
+            pltpu.VMEM((2 * beams, tile + LANES), jnp.float32),
         ],
         compiler_params=pltpu.CompilerParams(vmem_limit_bytes=24 * 2**20),
         cost_estimate=pl.CostEstimate(
-            flops=32 * beams * depth * span,
+            flops=128 * beams * depth * span,
             bytes_accessed=0,
             transcendentals=0,
         ),
@@ -257,6 +280,7 @@
     )(
         codes,
         mix,
+        weights,
         *[own[piece[0]] for piece in plan],
         *[far[piece[0]] for piece in plan],
         before,
@@ -316,14 +340,14 @@
     sizes = (beams, window, rtaps, length)
     bounds = [[0, length]]
     bounds += [chunk_bounds(level, levels, length) for level in range(1, levels + 1)]
-    mix, codes = mixing(ukern, rkern, angles, taps, shifts, half_table)
+    mix, weights, codes = mixing(ukern, rkern, angles, taps, shifts, half_table)
     owns = [[beams_in]] + [[None] * (len(bound) - 1) for bound in bounds[1:]]
     fars = [[from_partner(beams_in, 0)]] + [[None] * (len(bound) - 1) for bound in bounds[1:]]
     before = mix
     for level, chunk in merge_order(levels, bounds):
         start, stop = bounds[level + 1][chunk], bounds[level + 1][chunk + 1]
         done = merge(
-            level, levels, codes, mix, owns[level], fars[level], bounds[level],
+            level, levels, codes, mix, weights, owns[level], fars[level], bounds[level],
             start, stop, sizes, before,
         )
         before = owns[level + 1][chunk] = done[0]

time: 66.4 us -> 66.5 us (level)
  waiting for transfers between devices: 12.6 us -> 11.3 us
  starting transfers between devices: 25.1 us -> 26.1 us
  other arithmetic: 1.54 us -> 0.81 us
    ppermute x17, waiting for transfers between devices: 12.6 us -> 11.3 us  [from_partner(): return lax.ppermute(value, 'pulse', pairs)]
    ppermute x17, starting transfers between devices: 25.1 us -> 26.1 us  [from_partner(): return lax.ppermute(value, 'pulse', pairs)]
    add x2, other arithmetic: 1.54 us -> 0.81 us  [stacked(): total = total + lax.pad(piece, zero, ((top, below, 0), (left, right, 0)))]
  transfers between devices with their start and end apart: 17 -> 17, of which waited for: 7 -> 6; matrix products, arithmetic and copies ran while one was open for 2% -> 1% of each run, Pallas kernels for 36% -> 36%
where the time goes in v6:
time: 66.5 us; the launch traced here: 66.3 us
  starting transfers between devices  26.1 us (39%)
  Pallas kernels  26.1 us (39%)
  waiting for transfers between devices  11.3 us (17%)
  local copies, waits for them, and re-layouts  1.67 us (3%)
  other arithmetic  0.81 us (1%)
    ppermute x17, starting transfers between devices, from_partner(): return lax.ppermute(value, 'pulse', pairs)  26.1 us
    pallas_call x22, Pallas kernels, merge(): pl.pallas_call(functools.partial(merge_kernel, level, plan, start, stop,...  25.4 us
    ppermute x17, waiting for transfers between devices, from_partner(): return lax.ppermute(value, 'pulse', pairs)  11.3 us
  transfers between devices with their start and end apart: 17, of which 6 were waited for; matrix products, arithmetic and copies ran while one was open for 1% of the time, Pallas kernels for 36%

profile of v6, /device:TPU:0, one launch (start us, length us, event | category | flops | bytes accessed | tf_op | source)
XLA Modules:
  0.0 66.3 jit_solution(11277910450303463792)
XLA Ops:
  0.0 0.5 collective-permute-start
  0.5 0.2 copy-done.4
  0.7 0.4 copy-done.6
  1.1 0.7 %pad_add_fusion.real_ref = f32[14,128]{1,0:T(8,128)S(1)} fusion(f32[4,16]{1,0:T(4,128)S(1)} %bitcast.3, f32[8,128]{1,0:T(8,128)} %bitcast.2, bf16[2,32]{1,0:T(2,128)(2,1)S(1)} %copy-done.6), kind=kLoop, calls=%fused_computation.6 | loop fusion | flops 5376 | bytes 11648 | tf_op jit(solution)/shard_map/add | solution.py:91
  1.9 0.7 %mixing.1 = (bf16[4,256,192]{2,1,0:T(8,128)(2,1)S(1)}, f32[4,4,128,128]{3,2,1,0:T(8,128)S(1)}, f32[4,8,128]{2,1,0:T(8,128)S(1)}) custom-call(s32[12,128]{1,0:T(8,128)S(1)} %pad_add_fusion.1.whole_ref, f32[14,128]{1,0:T(8,128)S(1)} %pad_add_fusion.real_ref), custom_call_target="tpu_custom_call" | custom-call | flops 2000000000 | bytes 1572864 | tf_op jit(solution)/shard_map/mixing/pallas_call | solution.py:121
  2.7 0.3 collective-permute-done.refs_4_
  3.2 1.1 %merge_0.4 = (bf16[2,64,768]{2,1,0:T(8,128)(2,1)S(1)}, bf16[2,48,768]{2,1,0:T(8,128)(2,1)S(1)}) custom-call(f32[4,8,128]{2,1,0:T(8,128)S(1)} %get-tuple-element.40.refs_0_, bf16[4,256,192]{2,1,0:T(8,128)(2,1)S(1)} %get-tuple-element.41.refs_1_.refs_5_, f32[4,4,128,128]{3,2,1,0:T(8,128)S(1)} %get-tuple-element.42.refs_2_, bf16[2,64,4096]{2,1,0:T(8,128)(2,1)S(1)} %copy-done, ...), custom_call_target="tpu_custom_call" | custom-call | flops 1207959552 | tf_op jit(solution)/shard_map/merge_0/pallas_call | solution.py:259
  4.2 2.7 %collective-permute-start.1 = (bf16[2,48,768]{2,1,0:T(8,128)(2,1)S(1)}, bf16[2,48,768]{2,1,0:T(8,128)(2,1)S(1)}, u32[]{:S(2)}, u32[]{:S(2)}) collective-permute-start(bf16[2,48,768]{2,1,0:T(8,128)(2,1)S(1)} %get-tuple-element.44), channel_id=1, source_target_pairs={{0,2},{1,3},{2,0},{3,1},{4,6},{5,7},{6,4},{7,5},{8,10},{9,11},{10,... | collective-permute-start | bytes 442376 | tf_op jit(solution)/shard_map/ppermute | solution.py:332
  7.0 1.1 %merge_0.5 = (bf16[2,64,768]{2,1,0:T(8,128)(2,1)S(1)}, bf16[2,48,768]{2,1,0:T(8,128)(2,1)S(1)}) custom-call(f32[4,8,128]{2,1,0:T(8,128)S(1)} %get-tuple-element.40.refs_0_, bf16[4,256,192]{2,1,0:T(8,128)(2,1)S(1)} %get-tuple-element.41.refs_1_.refs_5_, f32[4,4,128,128]{3,2,1,0:T(8,128)S(1)} %get-tuple-element.42.refs_2_, bf16[2,64,4096]{2,1,0:T(8,128)(2,1)S(1)} %copy-done, ...), custom_call_target="tpu_custom_call" | custom-call | flops 1207959552 | tf_op jit(solution)/shard_map/merge_0/pallas_call | solution.py:259
  8.1 2.3 %merge_0.6 = (bf16[2,64,1536]{2,1,0:T(8,128)(2,1)S(1)}, bf16[2,48,1536]{2,1,0:T(8,128)(2,1)S(1)}) custom-call(f32[4,8,128]{2,1,0:T(8,128)S(1)} %get-tuple-element.40.refs_0_, bf16[4,256,192]{2,1,0:T(8,128)(2,1)S(1)} %get-tuple-element.41.refs_1_.refs_5_, f32[4,4,128,128]{3,2,1,0:T(8,128)S(1)} %get-tuple-element.42.refs_2_, bf16[2,64,4096]{2,1,0:T(8,128)(2,1)S(1)} %copy-done, ...), custom_call_target="tpu_custom_call" | custom-call | flops 2415919104 | tf_op jit(solution)/shard_map/merge_0/pallas_call | solution.py:259
  10.4 2.1 %collective-permute-start.5 = (bf16[2,48,1536]{2,1,0:T(8,128)(2,1)S(1)}, bf16[2,48,1536]{2,1,0:T(8,128)(2,1)S(1)}, u32[]{:S(2)}, u32[]{:S(2)}) collective-permute-start(bf16[2,48,1536]{2,1,0:T(8,128)(2,1)S(1)} %get-tuple-element.53), channel_id=1, source_target_pairs={{0,2},{1,3},{2,0},{3,1},{4,6},{5,7},{6,4},{7,5},{8,10},{9,11},{10,... | collective-permute-start | bytes 884744 | tf_op jit(solution)/shard_map/ppermute | solution.py:332
  12.5 1.0 %merge_1.6 = (bf16[2,64,640]{2,1,0:T(8,128)(2,1)S(1)}, bf16[2,48,640]{2,1,0:T(8,128)(2,1)S(1)}) custom-call(f32[4,8,128]{2,1,0:T(8,128)S(1)} %get-tuple-element.40.refs_0_, bf16[4,256,192]{2,1,0:T(8,128)(2,1)S(1)} %get-tuple-element.41.refs_1_.refs_5_, f32[4,4,128,128]{3,2,1,0:T(8,128)S(1)} %get-tuple-element.42.refs_2_, ...), custom_call_target="tpu_custom_call" | custom-call | flops 1006632960 | tf_op jit(solution)/shard_map/merge_1/pallas_call | solution.py:259
  13.6 1.6 %collective-permute-start.2 = (bf16[2,48,640]{2,1,0:T(8,128)(2,1)S(1)}, bf16[2,48,640]{2,1,0:T(8,128)(2,1)S(1)}, u32[]{:S(2)}, u32[]{:S(2)}) collective-permute-start(bf16[2,48,640]{2,1,0:T(8,128)(2,1)S(1)} %get-tuple-element.48), channel_id=1, source_target_pairs={{0,4},{1,5},{2,6},{3,7},{4,0},{5,1},{6,2},{7,3},{8,12},{9,13},{10,... | collective-permute-start | bytes 368648 | tf_op jit(solution)/shard_map/ppermute | solution.py:332
  15.2 1.1 %merge_1.7 = (bf16[2,64,768]{2,1,0:T(8,128)(2,1)S(1)}, bf16[2,48,768]{2,1,0:T(8,128)(2,1)S(1)}) custom-call(f32[4,8,128]{2,1,0:T(8,128)S(1)} %get-tuple-element.40.refs_0_, bf16[4,256,192]{2,1,0:T(8,128)(2,1)S(1)} %get-tuple-element.41.refs_1_.refs_5_, f32[4,4,128,128]{3,2,1,0:T(8,128)S(1)} %get-tuple-element.42.refs_2_, ...), custom_call_target="tpu_custom_call" | custom-call | flops 1207959552 | tf_op jit(solution)/shard_map/merge_1/pallas_call | solution.py:259
  16.3 1.7 %collective-permute-start.6 = (bf16[2,48,768]{2,1,0:T(8,128)(2,1)S(1)}, bf16[2,48,768]{2,1,0:T(8,128)(2,1)S(1)}, u32[]{:S(2)}, u32[]{:S(2)}) collective-permute-start(bf16[2,48,768]{2,1,0:T(8,128)(2,1)S(1)} %get-tuple-element.55), channel_id=1, source_target_pairs={{0,4},{1,5},{2,6},{3,7},{4,0},{5,1},{6,2},{7,3},{8,12},{9,13},{10,... | collective-permute-start | bytes 442376 | tf_op jit(solution)/shard_map/ppermute | solution.py:332
  18.0 0.9 %collective-permute-done.2.refs_4_.refs_5_ = bf16[2,48,640]{2,1,0:T(8,128)(2,1)S(1)} collective-permute-done((bf16[2,48,640]{2,1,0:T(8,128)(2,1)S(1)}, bf16[2,48,640]{2,1,0:T(8,128)(2,1)S(1)}, u32[]{:S(2)}, u32[]{:S(2)}) %collective-permute-start.2) | collective-permute-done | bytes 122912 | tf_op jit(solution)/shard_map/ppermute | solution.py:332
  18.9 0.9 %merge_2.6 = (bf16[2,64,512]{2,1,0:T(8,128)(2,1)S(1)}, bf16[2,48,512]{2,1,0:T(8,128)(2,1)S(1)}) custom-call(f32[4,8,128]{2,1,0:T(8,128)S(1)} %get-tuple-element.40.refs_0_, bf16[4,256,192]{2,1,0:T(8,128)(2,1)S(1)} %get-tuple-element.41.refs_1_.refs_5_, f32[4,4,128,128]{3,2,1,0:T(8,128)S(1)} %get-tuple-element.42.refs_2_, ...), custom_call_target="tpu_custom_call" | custom-call | flops 805306368 | tf_op jit(solution)/shard_map/merge_2/pallas_call | solution.py:259
  19.8 2.6 %collective-permute-start.4 = (bf16[2,48,512]{2,1,0:T(8,128)(2,1)S(1)}, bf16[2,48,512]{2,1,0:T(8,128)(2,1)S(1)}, u32[]{:S(2)}, u32[]{:S(2)}) collective-permute-start(bf16[2,48,512]{2,1,0:T(8,128)(2,1)S(1)} %get-tuple-element.52), channel_id=1, source_target_pairs={{0,8},{1,9},{2,10},{3,11},{4,12},{5,13},{6,14},{7,15},{8,0},{9,1},... | collective-permute-start | bytes 294920 | tf_op jit(solution)/shard_map/ppermute | solution.py:332
  22.4 1.1 %merge_1.8 = (bf16[2,64,768]{2,1,0:T(8,128)(2,1)S(1)}, bf16[2,48,768]{2,1,0:T(8,128)(2,1)S(1)}) custom-call(f32[4,8,128]{2,1,0:T(8,128)S(1)} %get-tuple-element.40.refs_0_, bf16[4,256,192]{2,1,0:T(8,128)(2,1)S(1)} %get-tuple-element.41.refs_1_.refs_5_, f32[4,4,128,128]{3,2,1,0:T(8,128)S(1)} %get-tuple-element.42.refs_2_, ...), custom_call_target="tpu_custom_call" | custom-call | flops 1207959552 | tf_op jit(solution)/shard_map/merge_1/pallas_call | solution.py:259
  23.5 1.1 %merge_2.7 = (bf16[2,64,768]{2,1,0:T(8,128)(2,1)S(1)}, bf16[2,48,768]{2,1,0:T(8,128)(2,1)S(1)}) custom-call(f32[4,8,128]{2,1,0:T(8,128)S(1)} %get-tuple-element.40.refs_0_, bf16[4,256,192]{2,1,0:T(8,128)(2,1)S(1)} %get-tuple-element.41.refs_1_.refs_5_, f32[4,4,128,128]{3,2,1,0:T(8,128)S(1)} %get-tuple-element.42.refs_2_, ...), custom_call_target="tpu_custom_call" | custom-call | flops 1207959552 | tf_op jit(solution)/shard_map/merge_2/pallas_call | solution.py:259
  24.5 1.9 %collective-permute-start.10 = (bf16[2,48,768]{2,1,0:T(8,128)(2,1)S(1)}, bf16[2,48,768]{2,1,0:T(8,128)(2,1)S(1)}, u32[]{:S(2)}, u32[]{:S(2)}) collective-permute-start(bf16[2,48,768]{2,1,0:T(8,128)(2,1)S(1)} %get-tuple-element.65), channel_id=1, source_target_pairs={{0,8},{1,9},{2,10},{3,11},{4,12},{5,13},{6,14},{7,15},{8,0},{9,1},... | collective-permute-start | bytes 442376 | tf_op jit(solution)/shard_map/ppermute | solution.py:332
  26.4 1.0 %collective-permute-start.7 = (bf16[2,48,768]{2,1,0:T(8,128)(2,1)S(1)}, bf16[2,48,768]{2,1,0:T(8,128)(2,1)S(1)}, u32[]{:S(2)}, u32[]{:S(2)}) collective-permute-start(bf16[2,48,768]{2,1,0:T(8,128)(2,1)S(1)} %get-tuple-element.56), channel_id=1, source_target_pairs={{0,4},{1,5},{2,6},{3,7},{4,0},{5,1},{6,2},{7,3},{8,12},{9,13},{10,... | collective-permute-start | bytes 442376 | tf_op jit(solution)/shard_map/ppermute | solution.py:332
  27.4 1.8 %merge_0.7 = (bf16[2,64,1024]{2,1,0:T(8,128)(2,1)S(1)}, bf16[2,48,1024]{2,1,0:T(8,128)(2,1)S(1)}) custom-call(f32[4,8,128]{2,1,0:T(8,128)S(1)} %get-tuple-element.40.refs_0_, bf16[4,256,192]{2,1,0:T(8,128)(2,1)S(1)} %get-tuple-element.41.refs_1_.refs_5_, f32[4,4,128,128]{3,2,1,0:T(8,128)S(1)} %get-tuple-element.42.refs_2_, bf16[2,64,4096]{2,1,0:T(8,128)(2,1)S(1)} %copy-done, ...), custom_call_target="tpu_custom_call" | custom-call | flops 1610612736 | tf_op jit(solution)/shard_map/merge_0/pallas_call | solution.py:259
  29.2 1.8 %collective-permute-start.9 = (bf16[2,48,1024]{2,1,0:T(8,128)(2,1)S(1)}, bf16[2,48,1024]{2,1,0:T(8,128)(2,1)S(1)}, u32[]{:S(2)}, u32[]{:S(2)}) collective-permute-start(bf16[2,48,1024]{2,1,0:T(8,128)(2,1)S(1)} %get-tuple-element.62), channel_id=1, source_target_pairs={{0,2},{1,3},{2,0},{3,1},{4,6},{5,7},{6,4},{7,5},{8,10},{9,11},{10,... | collective-permute-start | bytes 589832 | tf_op jit(solution)/shard_map/ppermute | solution.py:332
  31.0 1.0 %merge_1.9 = (bf16[2,64,768]{2,1,0:T(8,128)(2,1)S(1)}, bf16[2,48,768]{2,1,0:T(8,128)(2,1)S(1)}) custom-call(f32[4,8,128]{2,1,0:T(8,128)S(1)} %get-tuple-element.40.refs_0_, bf16[4,256,192]{2,1,0:T(8,128)(2,1)S(1)} %get-tuple-element.41.refs_1_.refs_5_, f32[4,4,128,128]{3,2,1,0:T(8,128)S(1)} %get-tuple-element.42.refs_2_, ...), custom_call_target="tpu_custom_call" | custom-call | flops 1207959552 | tf_op jit(solution)/shard_map/merge_1/pallas_call | solution.py:259
  32.0 0.6 collective-permute-start.8
  32.6 0.6 collective-permute-done.7.refs_6_.refs_5_
  33.2 1.1 %merge_2.8 = (bf16[2,64,768]{2,1,0:T(8,128)(2,1)S(1)}, bf16[2,48,768]{2,1,0:T(8,128)(2,1)S(1)}) custom-call(f32[4,8,128]{2,1,0:T(8,128)S(1)} %get-tuple-element.40.refs_0_, bf16[4,256,192]{2,1,0:T(8,128)(2,1)S(1)} %get-tuple-element.41.refs_1_.refs_5_, f32[4,4,128,128]{3,2,1,0:T(8,128)S(1)} %get-tuple-element.42.refs_2_, ...), custom_call_target="tpu_custom_call" | custom-call | flops 1207959552 | tf_op jit(solution)/shard_map/merge_2/pallas_call | solution.py:259
  34.3 3.2 %collective-permute-start.12 = (bf16[2,48,768]{2,1,0:T(8,128)(2,1)S(1)}, bf16[2,48,768]{2,1,0:T(8,128)(2,1)S(1)}, u32[]{:S(2)}, u32[]{:S(2)}) collective-permute-start(bf16[2,48,768]{2,1,0:T(8,128)(2,1)S(1)} %get-tuple-element.69), channel_id=1, source_target_pairs={{0,8},{1,9},{2,10},{3,11},{4,12},{5,13},{6,14},{7,15},{8,0},{9,1},... | collective-permute-start | bytes 442376 | tf_op jit(solution)/shard_map/ppermute | solution.py:332
  37.5 0.6 merge_3.6.refs_7_
  38.1 1.1 %merge_1.10 = (bf16[2,64,768]{2,1,0:T(8,128)(2,1)S(1)}, bf16[2,48,768]{2,1,0:T(8,128)(2,1)S(1)}) custom-call(f32[4,8,128]{2,1,0:T(8,128)S(1)} %get-tuple-element.40.refs_0_, bf16[4,256,192]{2,1,0:T(8,128)(2,1)S(1)} %get-tuple-element.41.refs_1_.refs_5_, f32[4,4,128,128]{3,2,1,0:T(8,128)S(1)} %get-tuple-element.42.refs_2_, ...), custom_call_target="tpu_custom_call" | custom-call | flops 1207959552 | tf_op jit(solution)/shard_map/merge_1/pallas_call | solution.py:259
  39.2 2.9 %collective-permute-start.11 = (bf16[2,48,768]{2,1,0:T(8,128)(2,1)S(1)}, bf16[2,48,768]{2,1,0:T(8,128)(2,1)S(1)}, u32[]{:S(2)}, u32[]{:S(2)}) collective-permute-start(bf16[2,48,768]{2,1,0:T(8,128)(2,1)S(1)} %get-tuple-element.66), channel_id=1, source_target_pairs={{0,4},{1,5},{2,6},{3,7},{4,0},{5,1},{6,2},{7,3},{8,12},{9,13},{10,... | collective-permute-start | bytes 442376 | tf_op jit(solution)/shard_map/ppermute | solution.py:332
  42.0 1.1 %merge_2.9 = (bf16[2,64,768]{2,1,0:T(8,128)(2,1)S(1)}, bf16[2,48,768]{2,1,0:T(8,128)(2,1)S(1)}) custom-call(f32[4,8,128]{2,1,0:T(8,128)S(1)} %get-tuple-element.40.refs_0_, bf16[4,256,192]{2,1,0:T(8,128)(2,1)S(1)} %get-tuple-element.41.refs_1_.refs_5_, f32[4,4,128,128]{3,2,1,0:T(8,128)S(1)} %get-tuple-element.42.refs_2_, ...), custom_call_target="tpu_custom_call" | custom-call | flops 1207959552 | tf_op jit(solution)/shard_map/merge_2/pallas_call | solution.py:259
  43.1 0.7 %merge_3.7.refs_7_ = bf16[2,64,256]{2,1,0:T(8,128)(2,1)S(1)} custom-call(f32[4,8,128]{2,1,0:T(8,128)S(1)} %get-tuple-element.40.refs_0_, bf16[4,256,192]{2,1,0:T(8,128)(2,1)S(1)} %get-tuple-element.41.refs_1_.refs_5_, f32[4,4,128,128]{3,2,1,0:T(8,128)S(1)} %get-tuple-element.42.refs_2_, bf16[2,64,512]{2,1,0:T(8,128)(2,1)S(1)} %get-tuple-element.51.refs_7_.refs_3_, ...), custom_call_target="tpu_custom_call" | custom-call | flops 402653184 | tf_op jit(solution)/shard_map/merge_3/pallas_call | solution.py:259
  43.8 1.1 %merge_3.8.refs_5_ = bf16[2,64,640]{2,1,0:T(8,128)(2,1)S(1)} custom-call(f32[4,8,128]{2,1,0:T(8,128)S(1)} %get-tuple-element.40.refs_0_, bf16[4,256,192]{2,1,0:T(8,128)(2,1)S(1)} %get-tuple-element.41.refs_1_.refs_5_, f32[4,4,128,128]{3,2,1,0:T(8,128)S(1)} %get-tuple-element.42.refs_2_, bf16[2,64,512]{2,1,0:T(8,128)(2,1)S(1)} %get-tuple-element.51.refs_7_.refs_3_, ...), custom_call_target="tpu_custom_call" | custom-call | flops 1006632960 | tf_op jit(solution)/shard_map/merge_3/pallas_call | solution.py:259
  44.9 0.9 %merge_1.11 = (bf16[2,64,384]{2,1,0:T(8,128)(2,1)S(1)}, bf16[2,48,384]{2,1,0:T(8,128)(2,1)S(1)}) custom-call(f32[4,8,128]{2,1,0:T(8,128)S(1)} %get-tuple-element.40.refs_0_, bf16[4,256,192]{2,1,0:T(8,128)(2,1)S(1)} %get-tuple-element.41.refs_1_.refs_5_, f32[4,4,128,128]{3,2,1,0:T(8,128)S(1)} %get-tuple-element.42.refs_2_, ...), custom_call_target="tpu_custom_call" | custom-call | flops 603979776 | tf_op jit(solution)/shard_map/merge_1/pallas_call | solution.py:259
  45.8 0.7 collective-permute-start.13
  46.5 1.1 %merge_2.10 = (bf16[2,64,640]{2,1,0:T(8,128)(2,1)S(1)}, bf16[2,48,640]{2,1,0:T(8,128)(2,1)S(1)}) custom-call(f32[4,8,128]{2,1,0:T(8,128)S(1)} %get-tuple-element.40.refs_0_, bf16[4,256,192]{2,1,0:T(8,128)(2,1)S(1)} %get-tuple-element.41.refs_1_.refs_5_, f32[4,4,128,128]{3,2,1,0:T(8,128)S(1)} %get-tuple-element.42.refs_2_, ...), custom_call_target="tpu_custom_call" | custom-call | flops 1006632960 | tf_op jit(solution)/shard_map/merge_2/pallas_call | solution.py:259
  47.6 2.4 %collective-permute-start.14 = (bf16[2,48,640]{2,1,0:T(8,128)(2,1)S(1)}, bf16[2,48,640]{2,1,0:T(8,128)(2,1)S(1)}, u32[]{:S(2)}, u32[]{:S(2)}) collective-permute-start(bf16[2,48,640]{2,1,0:T(8,128)(2,1)S(1)} %get-tuple-element.71), channel_id=1, source_target_pairs={{0,8},{1,9},{2,10},{3,11},{4,12},{5,13},{6,14},{7,15},{8,0},{9,1},... | collective-permute-start | bytes 368648 | tf_op jit(solution)/shard_map/ppermute | solution.py:332
  50.0 0.7 %collective-permute-done.15.refs_6_ = bf16[2,48,384]{2,1,0:T(8,128)(2,1)S(1)} collective-permute-done((bf16[2,48,384]{2,1,0:T(8,128)(2,1)S(1)}, bf16[2,48,384]{2,1,0:T(8,128)(2,1)S(1)}, u32[]{:S(2)}, u32[]{:S(2)}) %collective-permute-start.15) | collective-permute-done | bytes 73760 | tf_op jit(solution)/shard_map/ppermute | solution.py:332
  50.6 1.1 %merge_2.11 = (bf16[2,64,640]{2,1,0:T(8,128)(2,1)S(1)}, bf16[2,48,640]{2,1,0:T(8,128)(2,1)S(1)}) custom-call(f32[4,8,128]{2,1,0:T(8,128)S(1)} %get-tuple-element.40.refs_0_, bf16[4,256,192]{2,1,0:T(8,128)(2,1)S(1)} %get-tuple-element.41.refs_1_.refs_5_, f32[4,4,128,128]{3,2,1,0:T(8,128)S(1)} %get-tuple-element.42.refs_2_, ...), custom_call_target="tpu_custom_call" | custom-call | flops 1006632960 | tf_op jit(solution)/shard_map/merge_2/pallas_call | solution.py:259
  51.7 0.3 collective-permute-start.16
  52.0 7.3 %collective-permute-done.13.refs_9_.refs_5_ = bf16[2,48,768]{2,1,0:T(8,128)(2,1)S(1)} collective-permute-done((bf16[2,48,768]{2,1,0:T(8,128)(2,1)S(1)}, bf16[2,48,768]{2,1,0:T(8,128)(2,1)S(1)}, u32[]{:S(2)}, u32[]{:S(2)}) %collective-permute-start.13) | collective-permute-done | bytes 147488 | tf_op jit(solution)/shard_map/ppermute | solution.py:332
  59.3 1.5 %collective-permute-done.14.refs_10_.refs_6_.refs_5_ = bf16[2,48,640]{2,1,0:T(8,128)(2,1)S(1)} collective-permute-done((bf16[2,48,640]{2,1,0:T(8,128)(2,1)S(1)}, bf16[2,48,640]{2,1,0:T(8,128)(2,1)S(1)}, u32[]{:S(2)}, u32[]{:S(2)}) %collective-permute-start.14) | collective-permute-done | bytes 122912 | tf_op jit(solution)/shard_map/ppermute | solution.py:332
  60.9 2.7 %merge_3.9.refs_7_ = bf16[2,64,1792]{2,1,0:T(8,128)(2,1)S(1)} custom-call(f32[4,8,128]{2,1,0:T(8,128)S(1)} %get-tuple-element.40.refs_0_, bf16[4,256,192]{2,1,0:T(8,128)(2,1)S(1)} %get-tuple-element.41.refs_1_.refs_5_, f32[4,4,128,128]{3,2,1,0:T(8,128)S(1)} %get-tuple-element.42.refs_2_, bf16[2,64,768]{2,1,0:T(8,128)(2,1)S(1)} %get-tuple-element.57.refs_5_.refs_4_.refs_3_, ...), custom_call_target="tpu_custom_call" | custom-call | flops 2818572288 | tf_op jit(solution)/shard_map/merge_3/pallas_call | solution.py:259
  63.6 0.9 %merge_3.10.refs_7_ = bf16[2,64,512]{2,1,0:T(8,128)(2,1)S(1)} custom-call(f32[4,8,128]{2,1,0:T(8,128)S(1)} %get-tuple-element.40.refs_0_, bf16[4,256,192]{2,1,0:T(8,128)(2,1)S(1)} %get-tuple-element.41.refs_1_.refs_5_, f32[4,4,128,128]{3,2,1,0:T(8,128)S(1)} %get-tuple-element.42.refs_2_, bf16[2,64,768]{2,1,0:T(8,128)(2,1)S(1)} %get-tuple-element.64.refs_5_.refs_3_, ...), custom_call_target="tpu_custom_call" | custom-call | flops 805306368 | tf_op jit(solution)/shard_map/merge_3/pallas_call | solution.py:259
  64.5 1.1 %merge_3.11 = bf16[2,64,768]{2,1,0:T(8,128)(2,1)S(1)} custom-call(f32[4,8,128]{2,1,0:T(8,128)S(1)} %get-tuple-element.40.refs_0_, bf16[4,256,192]{2,1,0:T(8,128)(2,1)S(1)} %get-tuple-element.41.refs_1_.refs_5_, f32[4,4,128,128]{3,2,1,0:T(8,128)S(1)} %get-tuple-element.42.refs_2_, bf16[2,64,640]{2,1,0:T(8,128)(2,1)S(1)} %get-tuple-element.68.refs_7_.refs_6_.refs_4_.refs_3_, ...), custom_call_target="tpu_custom_call" | custom-call | flops 1207959552 | tf_op jit(solution)/shard_map/merge_3/pallas_call | solution.py:259
  65.6 0.7 %constant_dynamic-update-slice_fusion = bf16[2,64,4096]{2,1,0:T(8,128)(2,1)} fusion(bf16[2,64,4096]{2,1,0:T(8,128)(2,1)} %copy-done.5, bf16[2,64,768]{2,1,0:T(8,128)(2,1)S(1)} %merge_3.11), kind=kLoop, calls=%fused_computation | loop fusion | bytes 393216 | tf_op jit(solution)/shard_map/concatenate | solution.py:356
  (31 shorter events, 0.6 us)
Async XLA Ops:
  0.0 0.7 %copy-start.4 = (f32[16,4]{0,1:T(4,128)S(1)}, f32[16,4]{0,1:T(4,128)}, u32[]{:S(2)}) copy-start(f32[16,4]{0,1:T(4,128)} %param.9) | copy-start | bytes 772
  0.0 3.0 %collective-permute-start = (bf16[2,64,4096]{2,1,0:T(8,128)(2,1)}, bf16[2,64,4096]{2,1,0:T(8,128)(2,1)S(1)}, u32[]{:S(2)}, u32[]{:S(2)}) collective-permute-start(bf16[2,64,4096]{2,1,0:T(8,128)(2,1)} %refs_3_.7), channel_id=1, source_target_pairs={{0,1},{1,0},{2,3},{3,2},{4,5},{5,4},{6,7},{7,6},{8,9},{9,8},{10,11... | collective-permute-start | bytes 3145736 | tf_op jit(solution)/shard_map/ppermute | solution.py:332
  0.5 0.7 copy-start.6
  1.1 0.7 %copy-start.1 = (s32[4,64]{1,0:T(4,128)S(1)}, s32[4,64]{1,0:T(4,128)}, u32[]{:S(2)}) copy-start(s32[4,64]{1,0:T(4,128)} %param.11) | copy-start | bytes 3076
  1.1 0.7 %copy-start.2 = (s32[4,16]{1,0:T(4,128)S(1)}, s32[4,16]{1,0:T(4,128)}, u32[]{:S(2)}) copy-start(s32[4,16]{1,0:T(4,128)} %param.12) | copy-start | bytes 772
  1.1 0.7 %copy-start.3 = (s32[4,16]{1,0:T(4,128)S(1)}, s32[4,16]{1,0:T(4,128)}, u32[]{:S(2)}) copy-start(s32[4,16]{1,0:T(4,128)} %param.13) | copy-start | bytes 772
  1.9 1.2 %copy-start = (bf16[2,64,4096]{2,1,0:T(8,128)(2,1)S(1)}, bf16[2,64,4096]{2,1,0:T(8,128)(2,1)}, u32[]{:S(2)}) copy-start(bf16[2,64,4096]{2,1,0:T(8,128)(2,1)} %refs_3_.7) | copy-start | bytes 3145732
  4.2 8.3 %collective-permute-start.1 = (bf16[2,48,768]{2,1,0:T(8,128)(2,1)S(1)}, bf16[2,48,768]{2,1,0:T(8,128)(2,1)S(1)}, u32[]{:S(2)}, u32[]{:S(2)}) collective-permute-start(bf16[2,48,768]{2,1,0:T(8,128)(2,1)S(1)} %get-tuple-element.44), channel_id=1, source_target_pairs={{0,2},{1,3},{2,0},{3,1},{4,6},{5,7},{6,4},{7,5},{8,10},{9,11},{10,... | collective-permute-start | bytes 442376 | tf_op jit(solution)/shard_map/ppermute | solution.py:332
  8.0 7.2 %collective-permute-start.3 = (bf16[2,48,768]{2,1,0:T(8,128)(2,1)S(1)}, bf16[2,48,768]{2,1,0:T(8,128)(2,1)S(1)}, u32[]{:S(2)}, u32[]{:S(2)}) collective-permute-start(bf16[2,48,768]{2,1,0:T(8,128)(2,1)S(1)} %get-tuple-element.49), channel_id=1, source_target_pairs={{0,2},{1,3},{2,0},{3,1},{4,6},{5,7},{6,4},{7,5},{8,10},{9,11},{10,... | collective-permute-start | bytes 442376 | tf_op jit(solution)/shard_map/ppermute | solution.py:332
  10.4 12.0 %collective-permute-start.5 = (bf16[2,48,1536]{2,1,0:T(8,128)(2,1)S(1)}, bf16[2,48,1536]{2,1,0:T(8,128)(2,1)S(1)}, u32[]{:S(2)}, u32[]{:S(2)}) collective-permute-start(bf16[2,48,1536]{2,1,0:T(8,128)(2,1)S(1)} %get-tuple-element.53), channel_id=1, source_target_pairs={{0,2},{1,3},{2,0},{3,1},{4,6},{5,7},{6,4},{7,5},{8,10},{9,11},{10,... | collective-permute-start | bytes 884744 | tf_op jit(solution)/shard_map/ppermute | solution.py:332
  13.6 5.3 %collective-permute-start.2 = (bf16[2,48,640]{2,1,0:T(8,128)(2,1)S(1)}, bf16[2,48,640]{2,1,0:T(8,128)(2,1)S(1)}, u32[]{:S(2)}, u32[]{:S(2)}) collective-permute-start(bf16[2,48,640]{2,1,0:T(8,128)(2,1)S(1)} %get-tuple-element.48), channel_id=1, source_target_pairs={{0,4},{1,5},{2,6},{3,7},{4,0},{5,1},{6,2},{7,3},{8,12},{9,13},{10,... | collective-permute-start | bytes 368648 | tf_op jit(solution)/shard_map/ppermute | solution.py:332
  16.3 7.2 %collective-permute-start.6 = (bf16[2,48,768]{2,1,0:T(8,128)(2,1)S(1)}, bf16[2,48,768]{2,1,0:T(8,128)(2,1)S(1)}, u32[]{:S(2)}, u32[]{:S(2)}) collective-permute-start(bf16[2,48,768]{2,1,0:T(8,128)(2,1)S(1)} %get-tuple-element.55), channel_id=1, source_target_pairs={{0,4},{1,5},{2,6},{3,7},{4,0},{5,1},{6,2},{7,3},{8,12},{9,13},{10,... | collective-permute-start | bytes 442376 | tf_op jit(solution)/shard_map/ppermute | solution.py:332
  19.8 17.7 %collective-permute-start.4 = (bf16[2,48,512]{2,1,0:T(8,128)(2,1)S(1)}, bf16[2,48,512]{2,1,0:T(8,128)(2,1)S(1)}, u32[]{:S(2)}, u32[]{:S(2)}) collective-permute-start(bf16[2,48,512]{2,1,0:T(8,128)(2,1)S(1)} %get-tuple-element.52), channel_id=1, source_target_pairs={{0,8},{1,9},{2,10},{3,11},{4,12},{5,13},{6,14},{7,15},{8,0},{9,1},... | collective-permute-start | bytes 294920 | tf_op jit(solution)/shard_map/ppermute | solution.py:332
  24.5 19.2 %collective-permute-start.10 = (bf16[2,48,768]{2,1,0:T(8,128)(2,1)S(1)}, bf16[2,48,768]{2,1,0:T(8,128)(2,1)S(1)}, u32[]{:S(2)}, u32[]{:S(2)}) collective-permute-start(bf16[2,48,768]{2,1,0:T(8,128)(2,1)S(1)} %get-tuple-element.65), channel_id=1, source_target_pairs={{0,8},{1,9},{2,10},{3,11},{4,12},{5,13},{6,14},{7,15},{8,0},{9,1},... | collective-permute-start | bytes 442376 | tf_op jit(solution)/shard_map/ppermute | solution.py:332
  26.4 6.8 %collective-permute-start.7 = (bf16[2,48,768]{2,1,0:T(8,128)(2,1)S(1)}, bf16[2,48,768]{2,1,0:T(8,128)(2,1)S(1)}, u32[]{:S(2)}, u32[]{:S(2)}) collective-permute-start(bf16[2,48,768]{2,1,0:T(8,128)(2,1)S(1)} %get-tuple-element.56), channel_id=1, source_target_pairs={{0,4},{1,5},{2,6},{3,7},{4,0},{5,1},{6,2},{7,3},{8,12},{9,13},{10,... | collective-permute-start | bytes 442376 | tf_op jit(solution)/shard_map/ppermute | solution.py:332
  29.2 8.9 %collective-permute-start.9 = (bf16[2,48,1024]{2,1,0:T(8,128)(2,1)S(1)}, bf16[2,48,1024]{2,1,0:T(8,128)(2,1)S(1)}, u32[]{:S(2)}, u32[]{:S(2)}) collective-permute-start(bf16[2,48,1024]{2,1,0:T(8,128)(2,1)S(1)} %get-tuple-element.62), channel_id=1, source_target_pairs={{0,2},{1,3},{2,0},{3,1},{4,6},{5,7},{6,4},{7,5},{8,10},{9,11},{10,... | collective-permute-start | bytes 589832 | tf_op jit(solution)/shard_map/ppermute | solution.py:332
  32.0 10.0 %collective-permute-start.8 = (bf16[2,48,768]{2,1,0:T(8,128)(2,1)S(1)}, bf16[2,48,768]{2,1,0:T(8,128)(2,1)S(1)}, u32[]{:S(2)}, u32[]{:S(2)}) collective-permute-start(bf16[2,48,768]{2,1,0:T(8,128)(2,1)S(1)} %get-tuple-element.61), channel_id=1, source_target_pairs={{0,4},{1,5},{2,6},{3,7},{4,0},{5,1},{6,2},{7,3},{8,12},{9,13},{10,... | collective-permute-start | bytes 442376 | tf_op jit(solution)/shard_map/ppermute | solution.py:332
  34.3 17.8 %collective-permute-start.12 = (bf16[2,48,768]{2,1,0:T(8,128)(2,1)S(1)}, bf16[2,48,768]{2,1,0:T(8,128)(2,1)S(1)}, u32[]{:S(2)}, u32[]{:S(2)}) collective-permute-start(bf16[2,48,768]{2,1,0:T(8,128)(2,1)S(1)} %get-tuple-element.69), channel_id=1, source_target_pairs={{0,8},{1,9},{2,10},{3,11},{4,12},{5,13},{6,14},{7,15},{8,0},{9,1},... | collective-permute-start | bytes 442376 | tf_op jit(solution)/shard_map/ppermute | solution.py:332
  39.2 7.3 %collective-permute-start.11 = (bf16[2,48,768]{2,1,0:T(8,128)(2,1)S(1)}, bf16[2,48,768]{2,1,0:T(8,128)(2,1)S(1)}, u32[]{:S(2)}, u32[]{:S(2)}) collective-permute-start(bf16[2,48,768]{2,1,0:T(8,128)(2,1)S(1)} %get-tuple-element.66), channel_id=1, source_target_pairs={{0,4},{1,5},{2,6},{3,7},{4,0},{5,1},{6,2},{7,3},{8,12},{9,13},{10,... | collective-permute-start | bytes 442376 | tf_op jit(solution)/shard_map/ppermute | solution.py:332
  45.7 4.9 %collective-permute-start.15 = (bf16[2,48,384]{2,1,0:T(8,128)(2,1)S(1)}, bf16[2,48,384]{2,1,0:T(8,128)(2,1)S(1)}, u32[]{:S(2)}, u32[]{:S(2)}) collective-permute-start(bf16[2,48,384]{2,1,0:T(8,128)(2,1)S(1)} %get-tuple-element.72), channel_id=1, source_target_pairs={{0,4},{1,5},{2,6},{3,7},{4,0},{5,1},{6,2},{7,3},{8,12},{9,13},{10,... | collective-permute-start | bytes 221192 | tf_op jit(solution)/shard_map/ppermute | solution.py:332
  45.8 13.5 %collective-permute-start.13 = (bf16[2,48,768]{2,1,0:T(8,128)(2,1)S(1)}, bf16[2,48,768]{2,1,0:T(8,128)(2,1)S(1)}, u32[]{:S(2)}, u32[]{:S(2)}) collective-permute-start(bf16[2,48,768]{2,1,0:T(8,128)(2,1)S(1)} %get-tuple-element.70), channel_id=1, source_target_pairs={{0,8},{1,9},{2,10},{3,11},{4,12},{5,13},{6,14},{7,15},{8,0},{9,1},... | collective-permute-start | bytes 442376 | tf_op jit(solution)/shard_map/ppermute | solution.py:332
  47.6 13.3 %collective-permute-start.14 = (bf16[2,48,640]{2,1,0:T(8,128)(2,1)S(1)}, bf16[2,48,640]{2,1,0:T(8,128)(2,1)S(1)}, u32[]{:S(2)}, u32[]{:S(2)}) collective-permute-start(bf16[2,48,640]{2,1,0:T(8,128)(2,1)S(1)} %get-tuple-element.71), channel_id=1, source_target_pairs={{0,8},{1,9},{2,10},{3,11},{4,12},{5,13},{6,14},{7,15},{8,0},{9,1},... | collective-permute-start | bytes 368648 | tf_op jit(solution)/shard_map/ppermute | solution.py:332
  51.7 12.8 %collective-permute-start.16 = (bf16[2,48,640]{2,1,0:T(8,128)(2,1)S(1)}, bf16[2,48,640]{2,1,0:T(8,128)(2,1)S(1)}, u32[]{:S(2)}, u32[]{:S(2)}) collective-permute-start(bf16[2,48,640]{2,1,0:T(8,128)(2,1)S(1)} %get-tuple-element.74), channel_id=1, source_target_pairs={{0,8},{1,9},{2,10},{3,11},{4,12},{5,13},{6,14},{7,15},{8,0},{9,1},... | collective-permute-start | bytes 368648 | tf_op jit(solution)/shard_map/ppermute | solution.py:332
  64.5 1.1 %copy-start.5 = (bf16[2,64,4096]{2,1,0:T(8,128)(2,1)}, bf16[2,64,4096]{2,1,0:T(8,128)(2,1)S(1)}, u32[]{:S(2)}) copy-start(bf16[2,64,4096]{2,1,0:T(8,128)(2,1)S(1)} %constant_dynamic-update-slice_fusion.1) | copy-start | bytes 3145732

commit v7 on v5

--- a/solution.py
+++ b/solution.py
@@ -145,7 +145,7 @@
     outs = refs[3 + 2 * count:]
     out_ref = outs[0]
     send_ref = None if last else outs[1]
-    wide_ref, even_ref, odd_ref = outs[1 if last else 2:]
+    wide_ref, even_ref, odd_ref, held_ref = outs[1 if last else 2:]
     code = jnp.max(code_ref[level]).astype(jnp.int32)
     half, following = code // 131072, code // 65536 % 2
     shifts = (code // 256 % 256 - LANES, code % 256 - LANES)
@@ -164,8 +164,7 @@
     if stop + LANES > length:
         wide_ref[:, :, :, stop - base:stop - base + LANES] = edge
     span = stop - start
-    tile = min(TILE, span)
-    tiles = pl.cdiv(span, tile)
+    tiles = pl.cdiv(span, TILE)
     lane = lax.broadcasted_iota(jnp.int32, (2 * window, LANES), 1).astype(jnp.int16)
     moves = []
     for child in range(2):
@@ -176,28 +175,26 @@
             turn = lax.rem(LANES - part_tile, LANES)
             moves.append((child, tap, shift // LANES * LANES, turn, lane < kept))
 
-    def column_of(step):
-        return pl.multiple_of(jnp.minimum(step * tile, span - tile), LANES)
+    def rolled(child, at, turn):
+        piece = wide_ref[child, :, :, pl.ds(pl.multiple_of(at, LANES), LANES)]
+        return pltpu.roll(piece.reshape(2 * window, LANES), turn, 1)
 
     def build(stack_ref, step):
-        column = column_of(step)
-        for child, tap, whole, turn, kept in moves:
+        for number, (child, tap, whole, turn, kept) in enumerate(moves):
             place = (child * rtaps + tap) * 2 * window
-            held = None
-            for block in range(tile // LANES + 1):
-                at = pl.multiple_of(column + whole + block * LANES, LANES)
-                piece = wide_ref[child, :, :, pl.ds(at, LANES)].reshape(2 * window, LANES)
-                piece = pltpu.roll(piece, turn, 1)
-                if block > 0:
-                    columns = pl.ds((block - 1) * LANES, LANES)
-                    stack_ref[place:place + 2 * window, columns] = jnp.where(kept, held, piece)
+            held = held_ref[number]
+            for block in range(TILE // LANES):
+                piece = rolled(child, step * TILE + whole + (block + 1) * LANES, turn)
+                columns = pl.ds(block * LANES, LANES)
+                stack_ref[place:place + 2 * window, columns] = jnp.where(kept, held, piece)
                 held = piece
+            held_ref[number] = held
 
     def multiply(stack_ref, step):
-        column = column_of(step)
+        column = pl.multiple_of(step * TILE, TILE)
         both = jnp.dot(mix_ref[level], stack_ref[...], preferred_element_type=jnp.float32)
         total = (both[:2 * beams] + both[2 * beams:]).astype(jnp.bfloat16)
-        out_ref[:, :, pl.ds(column, tile)] = total.reshape(2, beams, tile)
+        out_ref[:, :, pl.ds(column, TILE)] = total.reshape(2, beams, TILE)
 
     def two_tiles(pair, carry):
         build(odd_ref, 2 * pair + 1)
@@ -206,13 +203,15 @@
         multiply(odd_ref, 2 * pair + 1)
         return carry
 
+    for number, (child, tap, whole, turn, kept) in enumerate(moves):
+        held_ref[number] = rolled(child, whole, turn)
     build(even_ref, 0)
     lax.fori_loop(0, tiles // 2, two_tiles, 0)
     if tiles % 2 == 1:
         multiply(even_ref, tiles - 1)
     if not last:
         other = pl.ds(pl.multiple_of((1 - following) * (beams - window), 16), window)
-        send_ref[...] = out_ref[:, other, :]
+        send_ref[...] = out_ref[:, other, :span]
 
 
 def pieces_of(bounds, start, stop):
@@ -232,7 +231,8 @@
     vmem = pl.BlockSpec(memory_space=pltpu.VMEM)
     anywhere = pl.BlockSpec(memory_space=pl.ANY)
     depth = mix.shape[2]
-    out_shape = [jax.ShapeDtypeStruct((2, beams, span), jnp.bfloat16)]
+    padded = pl.cdiv(span, TILE) * TILE
+    out_shape = [jax.ShapeDtypeStruct((2, beams, padded), jnp.bfloat16)]
     if not last:
         out_shape.append(jax.ShapeDtypeStruct((2, window, span), jnp.bfloat16))
     return pl.pallas_call(
@@ -243,9 +243,10 @@
         in_specs=[vmem, vmem] + [vmem] * (2 * len(plan)) + [anywhere],
         out_specs=[vmem] * len(out_shape),
         scratch_shapes=[
-            pltpu.VMEM((2, 2, window, span + 2 * LANES), jnp.bfloat16),
-            pltpu.VMEM((depth, min(TILE, span)), jnp.bfloat16),
-            pltpu.VMEM((depth, min(TILE, span)), jnp.bfloat16),
+            pltpu.VMEM((2, 2, window, padded + TILE + 2 * LANES), jnp.bfloat16),
+            pltpu.VMEM((depth, TILE), jnp.bfloat16),
+            pltpu.VMEM((depth, TILE), jnp.bfloat16),
+            pltpu.VMEM((2 * rtaps, 2 * window, LANES), jnp.bfloat16),
         ],
         compiler_params=pltpu.CompilerParams(vmem_limit_bytes=24 * 2**20),
         cost_estimate=pl.CostEstimate(
@@ -329,7 +330,9 @@
         before = owns[level + 1][chunk] = done[0]
         if level < levels - 1:
             fars[level + 1][chunk] = from_partner(done[1], level + 1)
-    return jnp.concatenate(owns[levels], axis=2)
+    edges = bounds[levels]
+    made = [part[:, :, :high - low] for part, low, high in zip(owns[levels], edges, edges[1:])]
+    return jnp.concatenate(made, axis=2)
 
 
 def solution(mesh):

time: 66.4 us -> 64.9 us (0.977)
  Pallas kernels: 25.7 us -> 23.4 us
    pallas_call x22, Pallas kernels: 24.8 us -> 22.5 us  [merge(): pl.pallas_call(functools.partial(merge_kernel, level, plan, start, stop,...]
  transfers between devices with their start and end apart: 17 -> 17, of which waited for: 7 -> 6; matrix products, arithmetic and copies ran while one was open for 2% -> 3% of each run, Pallas kernels for 36% -> 33%
where the time goes in v7:
time: 64.9 us; the launch traced here: 64.7 us
  starting transfers between devices  25.7 us (40%)
  Pallas kernels  23.4 us (36%)
  waiting for transfers between devices  12.8 us (20%)
  other arithmetic  1.54 us (2%)
  local copies, waits for them, and re-layouts  1.08 us (2%)
    ppermute x17, starting transfers between devices, from_partner(): return lax.ppermute(value, 'pulse', pairs)  25.7 us
    pallas_call x22, Pallas kernels, merge(): pl.pallas_call(functools.partial(merge_kernel, level, plan, start, stop,...  22.5 us
    ppermute x17, waiting for transfers between devices, from_partner(): return lax.ppermute(value, 'pulse', pairs)  12.8 us
    add x2, other arithmetic, stacked(): total = total + lax.pad(piece, zero, ((top, below, 0), (left, right, 0)))  1.54 us
  transfers between devices with their start and end apart: 17, of which 6 were waited for; matrix products, arithmetic and copies ran while one was open for 3% of the time, Pallas kernels for 33%

profile of v7, /device:TPU:0, one launch (start us, length us, event | category | flops | bytes accessed | tf_op | source)
XLA Modules:
  0.0 64.7 jit_solution(2104745483372882765)
XLA Ops:
  0.0 0.5 collective-permute-start
  0.5 0.7 %pad_add_fusion.real_ref = f32[14,128]{1,0:T(8,128)S(1)} fusion(f32[4,16]{1,0:T(4,128)} %bitcast.3, f32[8,128]{1,0:T(8,128)} %bitcast.2, bf16[2,32]{1,0:T(2,128)(2,1)} %param.8), kind=kLoop, calls=%fused_computation.6 | loop fusion | flops 5376 | bytes 11648 | tf_op jit(solution)/shard_map/add | solution.py:91
  1.2 0.8 %pad_add_fusion.1.whole_ref = s32[12,128]{1,0:T(8,128)S(1)} fusion(s32[4,64]{1,0:T(4,128)} %param.11, s32[4,16]{1,0:T(4,128)} %param.12, s32[4,16]{1,0:T(4,128)} %param.13), kind=kLoop, calls=%fused_computation.7 | loop fusion | flops 4608 | bytes 7680 | tf_op jit(solution)/shard_map/add | solution.py:91
  2.0 0.9 %mixing.1 = (bf16[4,256,768]{2,1,0:T(8,128)(2,1)S(1)}, f32[4,8,128]{2,1,0:T(8,128)S(1)}) custom-call(s32[12,128]{1,0:T(8,128)S(1)} %pad_add_fusion.1.whole_ref, f32[14,128]{1,0:T(8,128)S(1)} %pad_add_fusion.real_ref), custom_call_target="tpu_custom_call" | custom-call | flops 2000000000 | bytes 1572864 | tf_op jit(solution)/shard_map/mixing/pallas_call | solution.py:121
  3.0 0.3 copy-done
  3.2 0.9 %merge_0.4 = (bf16[2,64,768]{2,1,0:T(8,128)(2,1)S(1)}, bf16[2,48,768]{2,1,0:T(8,128)(2,1)S(1)}) custom-call(f32[4,8,128]{2,1,0:T(8,128)S(1)} %get-tuple-element.39.refs_0_, bf16[4,256,768]{2,1,0:T(8,128)(2,1)S(1)} %get-tuple-element.40.refs_1_.refs_4_, bf16[2,64,4096]{2,1,0:T(8,128)(2,1)S(1)} %copy-done, ...), custom_call_target="tpu_custom_call" | custom-call | flops 1207959552 | tf_op jit(solution)/shard_map/merge_0/pallas_call | solution.py:238
  4.2 2.7 %collective-permute-start.1 = (bf16[2,48,768]{2,1,0:T(8,128)(2,1)S(1)}, bf16[2,48,768]{2,1,0:T(8,128)(2,1)S(1)}, u32[]{:S(2)}, u32[]{:S(2)}) collective-permute-start(bf16[2,48,768]{2,1,0:T(8,128)(2,1)S(1)} %get-tuple-element.42), channel_id=1, source_target_pairs={{0,2},{1,3},{2,0},{3,1},{4,6},{5,7},{6,4},{7,5},{8,10},{9,11},{10,... | collective-permute-start | bytes 442376 | tf_op jit(solution)/shard_map/ppermute | solution.py:309
  6.9 0.9 %merge_0.5 = (bf16[2,64,768]{2,1,0:T(8,128)(2,1)S(1)}, bf16[2,48,768]{2,1,0:T(8,128)(2,1)S(1)}) custom-call(f32[4,8,128]{2,1,0:T(8,128)S(1)} %get-tuple-element.39.refs_0_, bf16[4,256,768]{2,1,0:T(8,128)(2,1)S(1)} %get-tuple-element.40.refs_1_.refs_4_, bf16[2,64,4096]{2,1,0:T(8,128)(2,1)S(1)} %copy-done, ...), custom_call_target="tpu_custom_call" | custom-call | flops 1207959552 | tf_op jit(solution)/shard_map/merge_0/pallas_call | solution.py:238
  7.9 2.1 %merge_0.6 = (bf16[2,64,1536]{2,1,0:T(8,128)(2,1)S(1)}, bf16[2,48,1536]{2,1,0:T(8,128)(2,1)S(1)}) custom-call(f32[4,8,128]{2,1,0:T(8,128)S(1)} %get-tuple-element.39.refs_0_, bf16[4,256,768]{2,1,0:T(8,128)(2,1)S(1)} %get-tuple-element.40.refs_1_.refs_4_, bf16[2,64,4096]{2,1,0:T(8,128)(2,1)S(1)} %copy-done, ...), custom_call_target="tpu_custom_call" | custom-call | flops 2415919104 | tf_op jit(solution)/shard_map/merge_0/pallas_call | solution.py:238
  10.1 2.1 %collective-permute-start.5 = (bf16[2,48,1536]{2,1,0:T(8,128)(2,1)S(1)}, bf16[2,48,1536]{2,1,0:T(8,128)(2,1)S(1)}, u32[]{:S(2)}, u32[]{:S(2)}) collective-permute-start(bf16[2,48,1536]{2,1,0:T(8,128)(2,1)S(1)} %get-tuple-element.51), channel_id=1, source_target_pairs={{0,2},{1,3},{2,0},{3,1},{4,6},{5,7},{6,4},{7,5},{8,10},{9,11},{10,... | collective-permute-start | bytes 884744 | tf_op jit(solution)/shard_map/ppermute | solution.py:309
  12.1 0.9 %merge_1.6 = (bf16[2,64,768]{2,1,0:T(8,128)(2,1)S(1)}, bf16[2,48,640]{2,1,0:T(8,128)(2,1)S(1)}) custom-call(f32[4,8,128]{2,1,0:T(8,128)S(1)} %get-tuple-element.39.refs_0_, bf16[4,256,768]{2,1,0:T(8,128)(2,1)S(1)} %get-tuple-element.40.refs_1_.refs_4_, bf16[2,64,768]{2,1,0:T(8,128)(2,1)S(1)} %get-tuple-element.41.refs_4_.refs_2_, ...), custom_call_target="tpu_custom_call" | custom-call | flops 1006632960 | tf_op jit(solution)/shard_map/merge_1/pallas_call | solution.py:238
  13.1 1.7 %collective-permute-start.2 = (bf16[2,48,640]{2,1,0:T(8,128)(2,1)S(1)}, bf16[2,48,640]{2,1,0:T(8,128)(2,1)S(1)}, u32[]{:S(2)}, u32[]{:S(2)}) collective-permute-start(bf16[2,48,640]{2,1,0:T(8,128)(2,1)S(1)} %get-tuple-element.46), channel_id=1, source_target_pairs={{0,4},{1,5},{2,6},{3,7},{4,0},{5,1},{6,2},{7,3},{8,12},{9,13},{10,... | collective-permute-start | bytes 368648 | tf_op jit(solution)/shard_map/ppermute | solution.py:309
  14.7 0.9 %merge_1.7 = (bf16[2,64,768]{2,1,0:T(8,128)(2,1)S(1)}, bf16[2,48,768]{2,1,0:T(8,128)(2,1)S(1)}) custom-call(f32[4,8,128]{2,1,0:T(8,128)S(1)} %get-tuple-element.39.refs_0_, bf16[4,256,768]{2,1,0:T(8,128)(2,1)S(1)} %get-tuple-element.40.refs_1_.refs_4_, bf16[2,64,768]{2,1,0:T(8,128)(2,1)S(1)} %get-tuple-element.41.refs_4_.refs_2_, ...), custom_call_target="tpu_custom_call" | custom-call | flops 1207959552 | tf_op jit(solution)/shard_map/merge_1/pallas_call | solution.py:238
  15.7 2.1 %collective-permute-start.6 = (bf16[2,48,768]{2,1,0:T(8,128)(2,1)S(1)}, bf16[2,48,768]{2,1,0:T(8,128)(2,1)S(1)}, u32[]{:S(2)}, u32[]{:S(2)}) collective-permute-start(bf16[2,48,768]{2,1,0:T(8,128)(2,1)S(1)} %get-tuple-element.53), channel_id=1, source_target_pairs={{0,4},{1,5},{2,6},{3,7},{4,0},{5,1},{6,2},{7,3},{8,12},{9,13},{10,... | collective-permute-start | bytes 442376 | tf_op jit(solution)/shard_map/ppermute | solution.py:309
  17.7 0.4 collective-permute-done.2.refs_3_.refs_4_
  18.2 0.8 %merge_2.6 = (bf16[2,64,512]{2,1,0:T(8,128)(2,1)S(1)}, bf16[2,48,512]{2,1,0:T(8,128)(2,1)S(1)}) custom-call(f32[4,8,128]{2,1,0:T(8,128)S(1)} %get-tuple-element.39.refs_0_, bf16[4,256,768]{2,1,0:T(8,128)(2,1)S(1)} %get-tuple-element.40.refs_1_.refs_4_, bf16[2,64,768]{2,1,0:T(8,128)(2,1)S(1)} %get-tuple-element.45.refs_6_.refs_2_, ...), custom_call_target="tpu_custom_call" | custom-call | flops 805306368 | tf_op jit(solution)/shard_map/merge_2/pallas_call | solution.py:238
  19.0 2.6 %collective-permute-start.4 = (bf16[2,48,512]{2,1,0:T(8,128)(2,1)S(1)}, bf16[2,48,512]{2,1,0:T(8,128)(2,1)S(1)}, u32[]{:S(2)}, u32[]{:S(2)}) collective-permute-start(bf16[2,48,512]{2,1,0:T(8,128)(2,1)S(1)} %get-tuple-element.50), channel_id=1, source_target_pairs={{0,8},{1,9},{2,10},{3,11},{4,12},{5,13},{6,14},{7,15},{8,0},{9,1},... | collective-permute-start | bytes 294920 | tf_op jit(solution)/shard_map/ppermute | solution.py:309
  21.6 0.9 %merge_1.8 = (bf16[2,64,768]{2,1,0:T(8,128)(2,1)S(1)}, bf16[2,48,768]{2,1,0:T(8,128)(2,1)S(1)}) custom-call(f32[4,8,128]{2,1,0:T(8,128)S(1)} %get-tuple-element.39.refs_0_, bf16[4,256,768]{2,1,0:T(8,128)(2,1)S(1)} %get-tuple-element.40.refs_1_.refs_4_, bf16[2,64,768]{2,1,0:T(8,128)(2,1)S(1)} %get-tuple-element.43.refs_4_.refs_3_.refs_2_, ...), custom_call_target="tpu_custom_call" | custom-call | flops 1207959552 | tf_op jit(solution)/shard_map/merge_1/pallas_call | solution.py:238
  22.6 0.9 %merge_2.7 = (bf16[2,64,768]{2,1,0:T(8,128)(2,1)S(1)}, bf16[2,48,768]{2,1,0:T(8,128)(2,1)S(1)}) custom-call(f32[4,8,128]{2,1,0:T(8,128)S(1)} %get-tuple-element.39.refs_0_, bf16[4,256,768]{2,1,0:T(8,128)(2,1)S(1)} %get-tuple-element.40.refs_1_.refs_4_, bf16[2,64,768]{2,1,0:T(8,128)(2,1)S(1)} %get-tuple-element.45.refs_6_.refs_2_, ...), custom_call_target="tpu_custom_call" | custom-call | flops 1207959552 | tf_op jit(solution)/shard_map/merge_2/pallas_call | solution.py:238
  23.5 2.4 %collective-permute-start.10 = (bf16[2,48,768]{2,1,0:T(8,128)(2,1)S(1)}, bf16[2,48,768]{2,1,0:T(8,128)(2,1)S(1)}, u32[]{:S(2)}, u32[]{:S(2)}) collective-permute-start(bf16[2,48,768]{2,1,0:T(8,128)(2,1)S(1)} %get-tuple-element.63), channel_id=1, source_target_pairs={{0,8},{1,9},{2,10},{3,11},{4,12},{5,13},{6,14},{7,15},{8,0},{9,1},... | collective-permute-start | bytes 442376 | tf_op jit(solution)/shard_map/ppermute | solution.py:309
  26.0 1.2 %collective-permute-start.7 = (bf16[2,48,768]{2,1,0:T(8,128)(2,1)S(1)}, bf16[2,48,768]{2,1,0:T(8,128)(2,1)S(1)}, u32[]{:S(2)}, u32[]{:S(2)}) collective-permute-start(bf16[2,48,768]{2,1,0:T(8,128)(2,1)S(1)} %get-tuple-element.54), channel_id=1, source_target_pairs={{0,4},{1,5},{2,6},{3,7},{4,0},{5,1},{6,2},{7,3},{8,12},{9,13},{10,... | collective-permute-start | bytes 442376 | tf_op jit(solution)/shard_map/ppermute | solution.py:309
  27.1 1.4 %merge_0.7 = (bf16[2,64,1024]{2,1,0:T(8,128)(2,1)S(1)}, bf16[2,48,1024]{2,1,0:T(8,128)(2,1)S(1)}) custom-call(f32[4,8,128]{2,1,0:T(8,128)S(1)} %get-tuple-element.39.refs_0_, bf16[4,256,768]{2,1,0:T(8,128)(2,1)S(1)} %get-tuple-element.40.refs_1_.refs_4_, bf16[2,64,4096]{2,1,0:T(8,128)(2,1)S(1)} %copy-done, ...), custom_call_target="tpu_custom_call" | custom-call | flops 1610612736 | tf_op jit(solution)/shard_map/merge_0/pallas_call | solution.py:238
  28.5 1.6 %collective-permute-start.9 = (bf16[2,48,1024]{2,1,0:T(8,128)(2,1)S(1)}, bf16[2,48,1024]{2,1,0:T(8,128)(2,1)S(1)}, u32[]{:S(2)}, u32[]{:S(2)}) collective-permute-start(bf16[2,48,1024]{2,1,0:T(8,128)(2,1)S(1)} %get-tuple-element.60), channel_id=1, source_target_pairs={{0,2},{1,3},{2,0},{3,1},{4,6},{5,7},{6,4},{7,5},{8,10},{9,11},{10,... | collective-permute-start | bytes 589832 | tf_op jit(solution)/shard_map/ppermute | solution.py:309
  30.1 0.9 %merge_1.9 = (bf16[2,64,768]{2,1,0:T(8,128)(2,1)S(1)}, bf16[2,48,768]{2,1,0:T(8,128)(2,1)S(1)}) custom-call(f32[4,8,128]{2,1,0:T(8,128)S(1)} %get-tuple-element.39.refs_0_, bf16[4,256,768]{2,1,0:T(8,128)(2,1)S(1)} %get-tuple-element.40.refs_1_.refs_4_, bf16[2,64,1536]{2,1,0:T(8,128)(2,1)S(1)} %get-tuple-element.44.refs_4_.refs_3_.refs_2_, ...), custom_call_target="tpu_custom_call" | custom-call | flops 1207959552 | tf_op jit(solution)/shard_map/merge_1/pallas_call | solution.py:238
  31.1 0.8 %collective-permute-start.8 = (bf16[2,48,768]{2,1,0:T(8,128)(2,1)S(1)}, bf16[2,48,768]{2,1,0:T(8,128)(2,1)S(1)}, u32[]{:S(2)}, u32[]{:S(2)}) collective-permute-start(bf16[2,48,768]{2,1,0:T(8,128)(2,1)S(1)} %get-tuple-element.59), channel_id=1, source_target_pairs={{0,4},{1,5},{2,6},{3,7},{4,0},{5,1},{6,2},{7,3},{8,12},{9,13},{10,... | collective-permute-start | bytes 442376 | tf_op jit(solution)/shard_map/ppermute | solution.py:309
  31.8 0.9 %collective-permute-done.7.refs_5_.refs_4_ = bf16[2,48,768]{2,1,0:T(8,128)(2,1)S(1)} collective-permute-done((bf16[2,48,768]{2,1,0:T(8,128)(2,1)S(1)}, bf16[2,48,768]{2,1,0:T(8,128)(2,1)S(1)}, u32[]{:S(2)}, u32[]{:S(2)}) %collective-permute-start.7) | collective-permute-done | bytes 147488 | tf_op jit(solution)/shard_map/ppermute | solution.py:309
  32.7 0.9 %merge_2.8 = (bf16[2,64,768]{2,1,0:T(8,128)(2,1)S(1)}, bf16[2,48,768]{2,1,0:T(8,128)(2,1)S(1)}) custom-call(f32[4,8,128]{2,1,0:T(8,128)S(1)} %get-tuple-element.39.refs_0_, bf16[4,256,768]{2,1,0:T(8,128)(2,1)S(1)} %get-tuple-element.40.refs_1_.refs_4_, bf16[2,64,768]{2,1,0:T(8,128)(2,1)S(1)} %get-tuple-element.48.refs_4_.refs_3_.refs_2_, ...), custom_call_target="tpu_custom_call" | custom-call | flops 1207959552 | tf_op jit(solution)/shard_map/merge_2/pallas_call | solution.py:238
  33.7 2.5 %collective-permute-start.12 = (bf16[2,48,768]{2,1,0:T(8,128)(2,1)S(1)}, bf16[2,48,768]{2,1,0:T(8,128)(2,1)S(1)}, u32[]{:S(2)}, u32[]{:S(2)}) collective-permute-start(bf16[2,48,768]{2,1,0:T(8,128)(2,1)S(1)} %get-tuple-element.67), channel_id=1, source_target_pairs={{0,8},{1,9},{2,10},{3,11},{4,12},{5,13},{6,14},{7,15},{8,0},{9,1},... | collective-permute-start | bytes 442376 | tf_op jit(solution)/shard_map/ppermute | solution.py:309
  36.2 0.6 merge_3.6.refs_6_
  36.8 1.0 %merge_1.10 = (bf16[2,64,768]{2,1,0:T(8,128)(2,1)S(1)}, bf16[2,48,768]{2,1,0:T(8,128)(2,1)S(1)}) custom-call(f32[4,8,128]{2,1,0:T(8,128)S(1)} %get-tuple-element.39.refs_0_, bf16[4,256,768]{2,1,0:T(8,128)(2,1)S(1)} %get-tuple-element.40.refs_1_.refs_4_, bf16[2,64,1536]{2,1,0:T(8,128)(2,1)S(1)} %get-tuple-element.44.refs_4_.refs_3_.refs_2_, ...), custom_call_target="tpu_custom_call" | custom-call | flops 1207959552 | tf_op jit(solution)/shard_map/merge_1/pallas_call | solution.py:238
  37.8 1.9 %collective-permute-start.11 = (bf16[2,48,768]{2,1,0:T(8,128)(2,1)S(1)}, bf16[2,48,768]{2,1,0:T(8,128)(2,1)S(1)}, u32[]{:S(2)}, u32[]{:S(2)}) collective-permute-start(bf16[2,48,768]{2,1,0:T(8,128)(2,1)S(1)} %get-tuple-element.64), channel_id=1, source_target_pairs={{0,4},{1,5},{2,6},{3,7},{4,0},{5,1},{6,2},{7,3},{8,12},{9,13},{10,... | collective-permute-start | bytes 442376 | tf_op jit(solution)/shard_map/ppermute | solution.py:309
  39.7 0.9 %merge_2.9 = (bf16[2,64,768]{2,1,0:T(8,128)(2,1)S(1)}, bf16[2,48,768]{2,1,0:T(8,128)(2,1)S(1)}) custom-call(f32[4,8,128]{2,1,0:T(8,128)S(1)} %get-tuple-element.39.refs_0_, bf16[4,256,768]{2,1,0:T(8,128)(2,1)S(1)} %get-tuple-element.40.refs_1_.refs_4_, bf16[2,64,768]{2,1,0:T(8,128)(2,1)S(1)} %get-tuple-element.52.refs_6_.refs_3_.refs_2_, ...), custom_call_target="tpu_custom_call" | custom-call | flops 1207959552 | tf_op jit(solution)/shard_map/merge_2/pallas_call | solution.py:238
  40.6 0.6 merge_3.7.refs_6_
  41.3 0.9 %merge_3.8.refs_4_ = bf16[2,64,768]{2,1,0:T(8,128)(2,1)S(1)} custom-call(f32[4,8,128]{2,1,0:T(8,128)S(1)} %get-tuple-element.39.refs_0_, bf16[4,256,768]{2,1,0:T(8,128)(2,1)S(1)} %get-tuple-element.40.refs_1_.refs_4_, bf16[2,64,512]{2,1,0:T(8,128)(2,1)S(1)} %get-tuple-element.49.refs_6_.refs_2_, ...), custom_call_target="tpu_custom_call" | custom-call | flops 1006632960 | tf_op jit(solution)/shard_map/merge_3/pallas_call | solution.py:238
  42.2 0.8 %merge_1.11 = (bf16[2,64,512]{2,1,0:T(8,128)(2,1)S(1)}, bf16[2,48,384]{2,1,0:T(8,128)(2,1)S(1)}) custom-call(f32[4,8,128]{2,1,0:T(8,128)S(1)} %get-tuple-element.39.refs_0_, bf16[4,256,768]{2,1,0:T(8,128)(2,1)S(1)} %get-tuple-element.40.refs_1_.refs_4_, bf16[2,64,1024]{2,1,0:T(8,128)(2,1)S(1)} %get-tuple-element.56.refs_4_.refs_3_.refs_2_, ...), custom_call_target="tpu_custom_call" | custom-call | flops 603979776 | tf_op jit(solution)/shard_map/merge_1/pallas_call | solution.py:238
  43.0 0.2 collective-permute-start.15
  43.3 1.9 %collective-permute-start.13 = (bf16[2,48,768]{2,1,0:T(8,128)(2,1)S(1)}, bf16[2,48,768]{2,1,0:T(8,128)(2,1)S(1)}, u32[]{:S(2)}, u32[]{:S(2)}) collective-permute-start(bf16[2,48,768]{2,1,0:T(8,128)(2,1)S(1)} %get-tuple-element.68), channel_id=1, source_target_pairs={{0,8},{1,9},{2,10},{3,11},{4,12},{5,13},{6,14},{7,15},{8,0},{9,1},... | collective-permute-start | bytes 442376 | tf_op jit(solution)/shard_map/ppermute | solution.py:309
  45.2 0.9 %merge_2.10 = (bf16[2,64,768]{2,1,0:T(8,128)(2,1)S(1)}, bf16[2,48,640]{2,1,0:T(8,128)(2,1)S(1)}) custom-call(f32[4,8,128]{2,1,0:T(8,128)S(1)} %get-tuple-element.39.refs_0_, bf16[4,256,768]{2,1,0:T(8,128)(2,1)S(1)} %get-tuple-element.40.refs_1_.refs_4_, bf16[2,64,768]{2,1,0:T(8,128)(2,1)S(1)} %get-tuple-element.57.refs_6_.refs_3_.refs_2_, ...), custom_call_target="tpu_custom_call" | custom-call | flops 1006632960 | tf_op jit(solution)/shard_map/merge_2/pallas_call | solution.py:238
  46.1 1.1 %collective-permute-start.14 = (bf16[2,48,640]{2,1,0:T(8,128)(2,1)S(1)}, bf16[2,48,640]{2,1,0:T(8,128)(2,1)S(1)}, u32[]{:S(2)}, u32[]{:S(2)}) collective-permute-start(bf16[2,48,640]{2,1,0:T(8,128)(2,1)S(1)} %get-tuple-element.69), channel_id=1, source_target_pairs={{0,8},{1,9},{2,10},{3,11},{4,12},{5,13},{6,14},{7,15},{8,0},{9,1},... | collective-permute-start | bytes 368648 | tf_op jit(solution)/shard_map/ppermute | solution.py:309
  47.3 1.5 %collective-permute-done.15.refs_5_ = bf16[2,48,384]{2,1,0:T(8,128)(2,1)S(1)} collective-permute-done((bf16[2,48,384]{2,1,0:T(8,128)(2,1)S(1)}, bf16[2,48,384]{2,1,0:T(8,128)(2,1)S(1)}, u32[]{:S(2)}, u32[]{:S(2)}) %collective-permute-start.15) | collective-permute-done | bytes 73760 | tf_op jit(solution)/shard_map/ppermute | solution.py:309
  48.7 0.9 %merge_2.11 = (bf16[2,64,768]{2,1,0:T(8,128)(2,1)S(1)}, bf16[2,48,640]{2,1,0:T(8,128)(2,1)S(1)}) custom-call(f32[4,8,128]{2,1,0:T(8,128)S(1)} %get-tuple-element.39.refs_0_, bf16[4,256,768]{2,1,0:T(8,128)(2,1)S(1)} %get-tuple-element.40.refs_1_.refs_4_, bf16[2,64,768]{2,1,0:T(8,128)(2,1)S(1)} %get-tuple-element.61.refs_6_.refs_3_.refs_2_, ...), custom_call_target="tpu_custom_call" | custom-call | flops 1006632960 | tf_op jit(solution)/shard_map/merge_2/pallas_call | solution.py:238
  49.7 0.5 collective-permute-start.16
  50.2 7.4 %collective-permute-done.13.refs_8_.refs_4_ = bf16[2,48,768]{2,1,0:T(8,128)(2,1)S(1)} collective-permute-done((bf16[2,48,768]{2,1,0:T(8,128)(2,1)S(1)}, bf16[2,48,768]{2,1,0:T(8,128)(2,1)S(1)}, u32[]{:S(2)}, u32[]{:S(2)}) %collective-permute-start.13) | collective-permute-done | bytes 147488 | tf_op jit(solution)/shard_map/ppermute | solution.py:309
  57.6 2.4 %collective-permute-done.14.refs_9_.refs_5_.refs_4_ = bf16[2,48,640]{2,1,0:T(8,128)(2,1)S(1)} collective-permute-done((bf16[2,48,640]{2,1,0:T(8,128)(2,1)S(1)}, bf16[2,48,640]{2,1,0:T(8,128)(2,1)S(1)}, u32[]{:S(2)}, u32[]{:S(2)}) %collective-permute-start.14) | collective-permute-done | bytes 122912 | tf_op jit(solution)/shard_map/ppermute | solution.py:309
  60.0 2.1 %merge_3.9.refs_6_ = bf16[2,64,1792]{2,1,0:T(8,128)(2,1)S(1)} custom-call(f32[4,8,128]{2,1,0:T(8,128)S(1)} %get-tuple-element.39.refs_0_, bf16[4,256,768]{2,1,0:T(8,128)(2,1)S(1)} %get-tuple-element.40.refs_1_.refs_4_, bf16[2,64,768]{2,1,0:T(8,128)(2,1)S(1)} %get-tuple-element.55.refs_4_.refs_3_.refs_2_, ...), custom_call_target="tpu_custom_call" | custom-call | flops 2818572288 | tf_op jit(solution)/shard_map/merge_3/pallas_call | solution.py:238
  62.2 0.8 %merge_3.10.refs_6_ = bf16[2,64,512]{2,1,0:T(8,128)(2,1)S(1)} custom-call(f32[4,8,128]{2,1,0:T(8,128)S(1)} %get-tuple-element.39.refs_0_, bf16[4,256,768]{2,1,0:T(8,128)(2,1)S(1)} %get-tuple-element.40.refs_1_.refs_4_, bf16[2,64,768]{2,1,0:T(8,128)(2,1)S(1)} %get-tuple-element.62.refs_4_.refs_2_, ...), custom_call_target="tpu_custom_call" | custom-call | flops 805306368 | tf_op jit(solution)/shard_map/merge_3/pallas_call | solution.py:238
  63.1 0.9 %merge_3.11 = bf16[2,64,768]{2,1,0:T(8,128)(2,1)S(1)} custom-call(f32[4,8,128]{2,1,0:T(8,128)S(1)} %get-tuple-element.39.refs_0_, bf16[4,256,768]{2,1,0:T(8,128)(2,1)S(1)} %get-tuple-element.40.refs_1_.refs_4_, bf16[2,64,768]{2,1,0:T(8,128)(2,1)S(1)} %get-tuple-element.66.refs_6_.refs_5_.refs_3_.refs_2_, ...), custom_call_target="tpu_custom_call" | custom-call | flops 1207959552 | tf_op jit(solution)/shard_map/merge_3/pallas_call | solution.py:238
  64.0 0.7 %constant_dynamic-update-slice_fusion = bf16[2,64,4096]{2,1,0:T(8,128)(2,1)} fusion(bf16[2,64,4096]{2,1,0:T(8,128)(2,1)} %copy-done.1, bf16[2,64,768]{2,1,0:T(8,128)(2,1)S(1)} %merge_3.11), kind=kLoop, calls=%fused_computation.2 | loop fusion | bytes 393216 | tf_op jit(solution)/shard_map/concatenate | solution.py:335
  (21 shorter events, 0.3 us)
Async XLA Ops:
  0.0 3.0 %collective-permute-start = (bf16[2,64,4096]{2,1,0:T(8,128)(2,1)}, bf16[2,64,4096]{2,1,0:T(8,128)(2,1)S(1)}, u32[]{:S(2)}, u32[]{:S(2)}) collective-permute-start(bf16[2,64,4096]{2,1,0:T(8,128)(2,1)} %refs_2_.7), channel_id=1, source_target_pairs={{0,1},{1,0},{2,3},{3,2},{4,5},{5,4},{6,7},{7,6},{8,9},{9,8},{10,11... | collective-permute-start | bytes 3145736 | tf_op jit(solution)/shard_map/ppermute | solution.py:309
  2.0 1.2 %copy-start = (bf16[2,64,4096]{2,1,0:T(8,128)(2,1)S(1)}, bf16[2,64,4096]{2,1,0:T(8,128)(2,1)}, u32[]{:S(2)}) copy-start(bf16[2,64,4096]{2,1,0:T(8,128)(2,1)} %refs_2_.7) | copy-start | bytes 3145732
  4.2 8.0 %collective-permute-start.1 = (bf16[2,48,768]{2,1,0:T(8,128)(2,1)S(1)}, bf16[2,48,768]{2,1,0:T(8,128)(2,1)S(1)}, u32[]{:S(2)}, u32[]{:S(2)}) collective-permute-start(bf16[2,48,768]{2,1,0:T(8,128)(2,1)S(1)} %get-tuple-element.42), channel_id=1, source_target_pairs={{0,2},{1,3},{2,0},{3,1},{4,6},{5,7},{6,4},{7,5},{8,10},{9,11},{10,... | collective-permute-start | bytes 442376 | tf_op jit(solution)/shard_map/ppermute | solution.py:309
  7.8 6.9 %collective-permute-start.3 = (bf16[2,48,768]{2,1,0:T(8,128)(2,1)S(1)}, bf16[2,48,768]{2,1,0:T(8,128)(2,1)S(1)}, u32[]{:S(2)}, u32[]{:S(2)}) collective-permute-start(bf16[2,48,768]{2,1,0:T(8,128)(2,1)S(1)} %get-tuple-element.47), channel_id=1, source_target_pairs={{0,2},{1,3},{2,0},{3,1},{4,6},{5,7},{6,4},{7,5},{8,10},{9,11},{10,... | collective-permute-start | bytes 442376 | tf_op jit(solution)/shard_map/ppermute | solution.py:309
  10.1 11.6 %collective-permute-start.5 = (bf16[2,48,1536]{2,1,0:T(8,128)(2,1)S(1)}, bf16[2,48,1536]{2,1,0:T(8,128)(2,1)S(1)}, u32[]{:S(2)}, u32[]{:S(2)}) collective-permute-start(bf16[2,48,1536]{2,1,0:T(8,128)(2,1)S(1)} %get-tuple-element.51), channel_id=1, source_target_pairs={{0,2},{1,3},{2,0},{3,1},{4,6},{5,7},{6,4},{7,5},{8,10},{9,11},{10,... | collective-permute-start | bytes 884744 | tf_op jit(solution)/shard_map/ppermute | solution.py:309
  13.1 5.1 %collective-permute-start.2 = (bf16[2,48,640]{2,1,0:T(8,128)(2,1)S(1)}, bf16[2,48,640]{2,1,0:T(8,128)(2,1)S(1)}, u32[]{:S(2)}, u32[]{:S(2)}) collective-permute-start(bf16[2,48,640]{2,1,0:T(8,128)(2,1)S(1)} %get-tuple-element.46), channel_id=1, source_target_pairs={{0,4},{1,5},{2,6},{3,7},{4,0},{5,1},{6,2},{7,3},{8,12},{9,13},{10,... | collective-permute-start | bytes 368648 | tf_op jit(solution)/shard_map/ppermute | solution.py:309
  15.7 6.9 %collective-permute-start.6 = (bf16[2,48,768]{2,1,0:T(8,128)(2,1)S(1)}, bf16[2,48,768]{2,1,0:T(8,128)(2,1)S(1)}, u32[]{:S(2)}, u32[]{:S(2)}) collective-permute-start(bf16[2,48,768]{2,1,0:T(8,128)(2,1)S(1)} %get-tuple-element.53), channel_id=1, source_target_pairs={{0,4},{1,5},{2,6},{3,7},{4,0},{5,1},{6,2},{7,3},{8,12},{9,13},{10,... | collective-permute-start | bytes 442376 | tf_op jit(solution)/shard_map/ppermute | solution.py:309
  19.0 17.1 %collective-permute-start.4 = (bf16[2,48,512]{2,1,0:T(8,128)(2,1)S(1)}, bf16[2,48,512]{2,1,0:T(8,128)(2,1)S(1)}, u32[]{:S(2)}, u32[]{:S(2)}) collective-permute-start(bf16[2,48,512]{2,1,0:T(8,128)(2,1)S(1)} %get-tuple-element.50), channel_id=1, source_target_pairs={{0,8},{1,9},{2,10},{3,11},{4,12},{5,13},{6,14},{7,15},{8,0},{9,1},... | collective-permute-start | bytes 294920 | tf_op jit(solution)/shard_map/ppermute | solution.py:309
  23.5 17.7 %collective-permute-start.10 = (bf16[2,48,768]{2,1,0:T(8,128)(2,1)S(1)}, bf16[2,48,768]{2,1,0:T(8,128)(2,1)S(1)}, u32[]{:S(2)}, u32[]{:S(2)}) collective-permute-start(bf16[2,48,768]{2,1,0:T(8,128)(2,1)S(1)} %get-tuple-element.63), channel_id=1, source_target_pairs={{0,8},{1,9},{2,10},{3,11},{4,12},{5,13},{6,14},{7,15},{8,0},{9,1},... | collective-permute-start | bytes 442376 | tf_op jit(solution)/shard_map/ppermute | solution.py:309
  26.0 6.8 %collective-permute-start.7 = (bf16[2,48,768]{2,1,0:T(8,128)(2,1)S(1)}, bf16[2,48,768]{2,1,0:T(8,128)(2,1)S(1)}, u32[]{:S(2)}, u32[]{:S(2)}) collective-permute-start(bf16[2,48,768]{2,1,0:T(8,128)(2,1)S(1)} %get-tuple-element.54), channel_id=1, source_target_pairs={{0,4},{1,5},{2,6},{3,7},{4,0},{5,1},{6,2},{7,3},{8,12},{9,13},{10,... | collective-permute-start | bytes 442376 | tf_op jit(solution)/shard_map/ppermute | solution.py:309
  28.5 8.3 %collective-permute-start.9 = (bf16[2,48,1024]{2,1,0:T(8,128)(2,1)S(1)}, bf16[2,48,1024]{2,1,0:T(8,128)(2,1)S(1)}, u32[]{:S(2)}, u32[]{:S(2)}) collective-permute-start(bf16[2,48,1024]{2,1,0:T(8,128)(2,1)S(1)} %get-tuple-element.60), channel_id=1, source_target_pairs={{0,2},{1,3},{2,0},{3,1},{4,6},{5,7},{6,4},{7,5},{8,10},{9,11},{10,... | collective-permute-start | bytes 589832 | tf_op jit(solution)/shard_map/ppermute | solution.py:309
  31.1 8.6 %collective-permute-start.8 = (bf16[2,48,768]{2,1,0:T(8,128)(2,1)S(1)}, bf16[2,48,768]{2,1,0:T(8,128)(2,1)S(1)}, u32[]{:S(2)}, u32[]{:S(2)}) collective-permute-start(bf16[2,48,768]{2,1,0:T(8,128)(2,1)S(1)} %get-tuple-element.59), channel_id=1, source_target_pairs={{0,4},{1,5},{2,6},{3,7},{4,0},{5,1},{6,2},{7,3},{8,12},{9,13},{10,... | collective-permute-start | bytes 442376 | tf_op jit(solution)/shard_map/ppermute | solution.py:309
  33.7 16.5 %collective-permute-start.12 = (bf16[2,48,768]{2,1,0:T(8,128)(2,1)S(1)}, bf16[2,48,768]{2,1,0:T(8,128)(2,1)S(1)}, u32[]{:S(2)}, u32[]{:S(2)}) collective-permute-start(bf16[2,48,768]{2,1,0:T(8,128)(2,1)S(1)} %get-tuple-element.67), channel_id=1, source_target_pairs={{0,8},{1,9},{2,10},{3,11},{4,12},{5,13},{6,14},{7,15},{8,0},{9,1},... | collective-permute-start | bytes 442376 | tf_op jit(solution)/shard_map/ppermute | solution.py:309
  37.8 7.4 %collective-permute-start.11 = (bf16[2,48,768]{2,1,0:T(8,128)(2,1)S(1)}, bf16[2,48,768]{2,1,0:T(8,128)(2,1)S(1)}, u32[]{:S(2)}, u32[]{:S(2)}) collective-permute-start(bf16[2,48,768]{2,1,0:T(8,128)(2,1)S(1)} %get-tuple-element.64), channel_id=1, source_target_pairs={{0,4},{1,5},{2,6},{3,7},{4,0},{5,1},{6,2},{7,3},{8,12},{9,13},{10,... | collective-permute-start | bytes 442376 | tf_op jit(solution)/shard_map/ppermute | solution.py:309
  43.0 5.7 %collective-permute-start.15 = (bf16[2,48,384]{2,1,0:T(8,128)(2,1)S(1)}, bf16[2,48,384]{2,1,0:T(8,128)(2,1)S(1)}, u32[]{:S(2)}, u32[]{:S(2)}) collective-permute-start(bf16[2,48,384]{2,1,0:T(8,128)(2,1)S(1)} %get-tuple-element.70), channel_id=1, source_target_pairs={{0,4},{1,5},{2,6},{3,7},{4,0},{5,1},{6,2},{7,3},{8,12},{9,13},{10,... | collective-permute-start | bytes 221192 | tf_op jit(solution)/shard_map/ppermute | solution.py:309
  43.3 14.3 %collective-permute-start.13 = (bf16[2,48,768]{2,1,0:T(8,128)(2,1)S(1)}, bf16[2,48,768]{2,1,0:T(8,128)(2,1)S(1)}, u32[]{:S(2)}, u32[]{:S(2)}) collective-permute-start(bf16[2,48,768]{2,1,0:T(8,128)(2,1)S(1)} %get-tuple-element.68), channel_id=1, source_target_pairs={{0,8},{1,9},{2,10},{3,11},{4,12},{5,13},{6,14},{7,15},{8,0},{9,1},... | collective-permute-start | bytes 442376 | tf_op jit(solution)/shard_map/ppermute | solution.py:309
  46.1 13.9 %collective-permute-start.14 = (bf16[2,48,640]{2,1,0:T(8,128)(2,1)S(1)}, bf16[2,48,640]{2,1,0:T(8,128)(2,1)S(1)}, u32[]{:S(2)}, u32[]{:S(2)}) collective-permute-start(bf16[2,48,640]{2,1,0:T(8,128)(2,1)S(1)} %get-tuple-element.69), channel_id=1, source_target_pairs={{0,8},{1,9},{2,10},{3,11},{4,12},{5,13},{6,14},{7,15},{8,0},{9,1},... | collective-permute-start | bytes 368648 | tf_op jit(solution)/shard_map/ppermute | solution.py:309
  49.7 13.4 %collective-permute-start.16 = (bf16[2,48,640]{2,1,0:T(8,128)(2,1)S(1)}, bf16[2,48,640]{2,1,0:T(8,128)(2,1)S(1)}, u32[]{:S(2)}, u32[]{:S(2)}) collective-permute-start(bf16[2,48,640]{2,1,0:T(8,128)(2,1)S(1)} %get-tuple-element.72), channel_id=1, source_target_pairs={{0,8},{1,9},{2,10},{3,11},{4,12},{5,13},{6,14},{7,15},{8,0},{9,1},... | collective-permute-start | bytes 368648 | tf_op jit(solution)/shard_map/ppermute | solution.py:309
  63.0 1.0 %copy-start.1 = (bf16[2,64,4096]{2,1,0:T(8,128)(2,1)}, bf16[2,64,4096]{2,1,0:T(8,128)(2,1)S(1)}, u32[]{:S(2)}) copy-start(bf16[2,64,4096]{2,1,0:T(8,128)(2,1)S(1)} %constant_dynamic-update-slice_fusion.1) | copy-start | bytes 3145732

commit v8 on v7

--- a/solution.py
+++ b/solution.py
@@ -206,9 +206,13 @@
     for number, (child, tap, whole, turn, kept) in enumerate(moves):
         held_ref[number] = rolled(child, whole, turn)
     build(even_ref, 0)
-    lax.fori_loop(0, tiles // 2, two_tiles, 0)
+    lax.fori_loop(0, (tiles - 1) // 2, two_tiles, 0)
     if tiles % 2 == 1:
         multiply(even_ref, tiles - 1)
+    else:
+        build(odd_ref, tiles - 1)
+        multiply(even_ref, tiles - 2)
+        multiply(odd_ref, tiles - 1)
     if not last:
         other = pl.ds(pl.multiple_of((1 - following) * (beams - window), 16), window)
         send_ref[...] = out_ref[:, other, :span]
@@ -250,7 +254,7 @@
         ],
         compiler_params=pltpu.CompilerParams(vmem_limit_bytes=24 * 2**20),
         cost_estimate=pl.CostEstimate(
-            flops=32 * beams * depth * span,
+            flops=(8 if last else 32) * beams * depth * span,
             bytes_accessed=0,
             transcendentals=0,
         ),
@@ -265,14 +269,14 @@
 
 
 MARKS = (
-    (6, 12, 24),
-    (5, 11, 17, 23, 29),
-    (4, 10, 16, 22, 27),
-    (1, 3, 8, 22, 26),
+    (6, 13, 26),
+    (5, 12, 20, 25),
+    (4, 11, 17, 24, 29),
+    (7, 15, 21, 28),
 )
 ORDER = (
-    (0, 0), (0, 1), (0, 2), (1, 0), (1, 1), (2, 0), (1, 2), (2, 1), (0, 3), (1, 3), (2, 2),
-    (3, 0), (1, 4), (2, 3), (3, 1), (3, 2), (1, 5), (2, 4), (2, 5), (3, 3), (3, 4), (3, 5),
+    (0, 0), (0, 1), (0, 2), (1, 0), (1, 1), (2, 0), (1, 2), (2, 1), (1, 3), (0, 3), (2, 2),
+    (3, 0), (1, 4), (2, 3), (3, 1), (2, 4), (3, 2), (2, 5), (3, 3), (3, 4),
 )
 
 

time: 64.9 us -> 63.1 us (0.972)
  Pallas kernels: 23.4 us -> 22.2 us
  waiting for transfers between devices: 12.8 us -> 11.9 us
    pallas_call x22 -> x20, Pallas kernels: 22.5 us -> 21.3 us  [merge(): pl.pallas_call(functools.partial(merge_kernel, level, plan, start, stop,...]
    ppermute x17 -> x16, waiting for transfers between devices: 12.8 us -> 11.9 us  [from_partner(): return lax.ppermute(value, 'pulse', pairs)]
    ppermute x17 -> x16, starting transfers between devices: 25.7 us -> 26.1 us  [from_partner(): return lax.ppermute(value, 'pulse', pairs)]
  transfers between devices with their start and end apart: 17 -> 16, of which waited for: 6 -> 7; matrix products, arithmetic and copies ran while one was open for 3% -> 3% of each run, Pallas kernels for 33% -> 32%
where the time goes in v8:
time: 63.1 us; the launch traced here: 63 us
  starting transfers between devices  26.1 us (41%)
  Pallas kernels  22.2 us (35%)
  waiting for transfers between devices  11.9 us (19%)
  other arithmetic  1.54 us (2%)
  local copies, waits for them, and re-layouts  1.03 us (2%)
    ppermute x16, starting transfers between devices, from_partner(): return lax.ppermute(value, 'pulse', pairs)  26.1 us
    pallas_call x20, Pallas kernels, merge(): pl.pallas_call(functools.partial(merge_kernel, level, plan, start, stop,...  21.3 us
    ppermute x16, waiting for transfers between devices, from_partner(): return lax.ppermute(value, 'pulse', pairs)  11.9 us
    add x2, other arithmetic, stacked(): total = total + lax.pad(piece, zero, ((top, below, 0), (left, right, 0)))  1.54 us
  transfers between devices with their start and end apart: 16, of which 7 were waited for; matrix products, arithmetic and copies ran while one was open for 3% of the time, Pallas kernels for 32%

profile of v8, /device:TPU:0, one launch (start us, length us, event | category | flops | bytes accessed | tf_op | source)
XLA Modules:
  0.0 63.0 jit_solution(590186124017457950)
XLA Ops:
  0.0 0.5 collective-permute-start
  0.5 0.7 %pad_add_fusion.real_ref = f32[14,128]{1,0:T(8,128)S(1)} fusion(f32[4,16]{1,0:T(4,128)} %bitcast.3, f32[8,128]{1,0:T(8,128)} %bitcast.2, bf16[2,32]{1,0:T(2,128)(2,1)} %param.8), kind=kLoop, calls=%fused_computation.5 | loop fusion | flops 5376 | bytes 11648 | tf_op jit(solution)/shard_map/add | solution.py:91
  1.2 0.8 %pad_add_fusion.1.whole_ref = s32[12,128]{1,0:T(8,128)S(1)} fusion(s32[4,64]{1,0:T(4,128)} %param.11, s32[4,16]{1,0:T(4,128)} %param.12, s32[4,16]{1,0:T(4,128)} %param.13), kind=kLoop, calls=%fused_computation.6 | loop fusion | flops 4608 | bytes 7680 | tf_op jit(solution)/shard_map/add | solution.py:91
  2.0 0.9 %mixing.1 = (bf16[4,256,768]{2,1,0:T(8,128)(2,1)S(1)}, f32[4,8,128]{2,1,0:T(8,128)S(1)}) custom-call(s32[12,128]{1,0:T(8,128)S(1)} %pad_add_fusion.1.whole_ref, f32[14,128]{1,0:T(8,128)S(1)} %pad_add_fusion.real_ref), custom_call_target="tpu_custom_call" | custom-call | flops 2000000000 | bytes 1572864 | tf_op jit(solution)/shard_map/mixing/pallas_call | solution.py:121
  2.9 0.1 collective-permute-done.refs_3_
  3.0 0.3 copy-done
  3.2 0.9 %merge_0.4 = (bf16[2,64,768]{2,1,0:T(8,128)(2,1)S(1)}, bf16[2,48,768]{2,1,0:T(8,128)(2,1)S(1)}) custom-call(f32[4,8,128]{2,1,0:T(8,128)S(1)} %get-tuple-element.37.refs_0_, bf16[4,256,768]{2,1,0:T(8,128)(2,1)S(1)} %get-tuple-element.38.refs_1_.refs_4_, bf16[2,64,4096]{2,1,0:T(8,128)(2,1)S(1)} %copy-done, ...), custom_call_target="tpu_custom_call" | custom-call | flops 1207959552 | tf_op jit(solution)/shard_map/merge_0/pallas_call | solution.py:242
  4.2 2.7 %collective-permute-start.1 = (bf16[2,48,768]{2,1,0:T(8,128)(2,1)S(1)}, bf16[2,48,768]{2,1,0:T(8,128)(2,1)S(1)}, u32[]{:S(2)}, u32[]{:S(2)}) collective-permute-start(bf16[2,48,768]{2,1,0:T(8,128)(2,1)S(1)} %get-tuple-element.40), channel_id=1, source_target_pairs={{0,2},{1,3},{2,0},{3,1},{4,6},{5,7},{6,4},{7,5},{8,10},{9,11},{10,... | collective-permute-start | bytes 442376 | tf_op jit(solution)/shard_map/ppermute | solution.py:313
  6.9 1.1 %merge_0.5 = (bf16[2,64,1024]{2,1,0:T(8,128)(2,1)S(1)}, bf16[2,48,896]{2,1,0:T(8,128)(2,1)S(1)}) custom-call(f32[4,8,128]{2,1,0:T(8,128)S(1)} %get-tuple-element.37.refs_0_, bf16[4,256,768]{2,1,0:T(8,128)(2,1)S(1)} %get-tuple-element.38.refs_1_.refs_4_, bf16[2,64,4096]{2,1,0:T(8,128)(2,1)S(1)} %copy-done, ...), custom_call_target="tpu_custom_call" | custom-call | flops 1409286144 | tf_op jit(solution)/shard_map/merge_0/pallas_call | solution.py:242
  8.0 0.1 collective-permute-start.3
  8.1 2.3 %merge_0.6 = (bf16[2,64,1792]{2,1,0:T(8,128)(2,1)S(1)}, bf16[2,48,1664]{2,1,0:T(8,128)(2,1)S(1)}) custom-call(f32[4,8,128]{2,1,0:T(8,128)S(1)} %get-tuple-element.37.refs_0_, bf16[4,256,768]{2,1,0:T(8,128)(2,1)S(1)} %get-tuple-element.38.refs_1_.refs_4_, bf16[2,64,4096]{2,1,0:T(8,128)(2,1)S(1)} %copy-done, ...), custom_call_target="tpu_custom_call" | custom-call | flops 2617245696 | tf_op jit(solution)/shard_map/merge_0/pallas_call | solution.py:242
  10.4 2.1 %collective-permute-start.5 = (bf16[2,48,1664]{2,1,0:T(8,128)(2,1)S(1)}, bf16[2,48,1664]{2,1,0:T(8,128)(2,1)S(1)}, u32[]{:S(2)}, u32[]{:S(2)}) collective-permute-start(bf16[2,48,1664]{2,1,0:T(8,128)(2,1)S(1)} %get-tuple-element.49), channel_id=1, source_target_pairs={{0,2},{1,3},{2,0},{3,1},{4,6},{5,7},{6,4},{7,5},{8,10},{9,11},{10,... | collective-permute-start | bytes 958472 | tf_op jit(solution)/shard_map/ppermute | solution.py:313
  12.5 0.9 %merge_1.5 = (bf16[2,64,768]{2,1,0:T(8,128)(2,1)S(1)}, bf16[2,48,640]{2,1,0:T(8,128)(2,1)S(1)}) custom-call(f32[4,8,128]{2,1,0:T(8,128)S(1)} %get-tuple-element.37.refs_0_, bf16[4,256,768]{2,1,0:T(8,128)(2,1)S(1)} %get-tuple-element.38.refs_1_.refs_4_, bf16[2,64,768]{2,1,0:T(8,128)(2,1)S(1)} %get-tuple-element.39.refs_4_.refs_2_, ...), custom_call_target="tpu_custom_call" | custom-call | flops 1006632960 | tf_op jit(solution)/shard_map/merge_1/pallas_call | solution.py:242
  13.4 1.6 %collective-permute-start.2 = (bf16[2,48,640]{2,1,0:T(8,128)(2,1)S(1)}, bf16[2,48,640]{2,1,0:T(8,128)(2,1)S(1)}, u32[]{:S(2)}, u32[]{:S(2)}) collective-permute-start(bf16[2,48,640]{2,1,0:T(8,128)(2,1)S(1)} %get-tuple-element.44), channel_id=1, source_target_pairs={{0,4},{1,5},{2,6},{3,7},{4,0},{5,1},{6,2},{7,3},{8,12},{9,13},{10,... | collective-permute-start | bytes 368648 | tf_op jit(solution)/shard_map/ppermute | solution.py:313
  15.1 0.3 collective-permute-done.3.refs_5_.refs_4_
  15.4 1.1 %merge_1.6 = (bf16[2,64,1024]{2,1,0:T(8,128)(2,1)S(1)}, bf16[2,48,896]{2,1,0:T(8,128)(2,1)S(1)}) custom-call(f32[4,8,128]{2,1,0:T(8,128)S(1)} %get-tuple-element.37.refs_0_, bf16[4,256,768]{2,1,0:T(8,128)(2,1)S(1)} %get-tuple-element.38.refs_1_.refs_4_, bf16[2,64,768]{2,1,0:T(8,128)(2,1)S(1)} %get-tuple-element.39.refs_4_.refs_2_, ...), custom_call_target="tpu_custom_call" | custom-call | flops 1409286144 | tf_op jit(solution)/shard_map/merge_1/pallas_call | solution.py:242
  16.5 1.9 %collective-permute-start.4 = (bf16[2,48,896]{2,1,0:T(8,128)(2,1)S(1)}, bf16[2,48,896]{2,1,0:T(8,128)(2,1)S(1)}, u32[]{:S(2)}, u32[]{:S(2)}) collective-permute-start(bf16[2,48,896]{2,1,0:T(8,128)(2,1)S(1)} %get-tuple-element.48), channel_id=1, source_target_pairs={{0,4},{1,5},{2,6},{3,7},{4,0},{5,1},{6,2},{7,3},{8,12},{9,13},{10,... | collective-permute-start | bytes 516104 | tf_op jit(solution)/shard_map/ppermute | solution.py:313
  18.5 0.8 %merge_2.6 = (bf16[2,64,512]{2,1,0:T(8,128)(2,1)S(1)}, bf16[2,48,512]{2,1,0:T(8,128)(2,1)S(1)}) custom-call(f32[4,8,128]{2,1,0:T(8,128)S(1)} %get-tuple-element.37.refs_0_, bf16[4,256,768]{2,1,0:T(8,128)(2,1)S(1)} %get-tuple-element.38.refs_1_.refs_4_, bf16[2,64,768]{2,1,0:T(8,128)(2,1)S(1)} %get-tuple-element.43.refs_6_.refs_2_, ...), custom_call_target="tpu_custom_call" | custom-call | flops 805306368 | tf_op jit(solution)/shard_map/merge_2/pallas_call | solution.py:242
  19.3 2.7 %collective-permute-start.6 = (bf16[2,48,512]{2,1,0:T(8,128)(2,1)S(1)}, bf16[2,48,512]{2,1,0:T(8,128)(2,1)S(1)}, u32[]{:S(2)}, u32[]{:S(2)}) collective-permute-start(bf16[2,48,512]{2,1,0:T(8,128)(2,1)S(1)} %get-tuple-element.52), channel_id=1, source_target_pairs={{0,8},{1,9},{2,10},{3,11},{4,12},{5,13},{6,14},{7,15},{8,0},{9,1},... | collective-permute-start | bytes 294920 | tf_op jit(solution)/shard_map/ppermute | solution.py:313
  22.0 1.1 %merge_1.7 = (bf16[2,64,1024]{2,1,0:T(8,128)(2,1)S(1)}, bf16[2,48,1024]{2,1,0:T(8,128)(2,1)S(1)}) custom-call(f32[4,8,128]{2,1,0:T(8,128)S(1)} %get-tuple-element.37.refs_0_, bf16[4,256,768]{2,1,0:T(8,128)(2,1)S(1)} %get-tuple-element.38.refs_1_.refs_4_, bf16[2,64,1024]{2,1,0:T(8,128)(2,1)S(1)} %get-tuple-element.41.refs_4_.refs_3_.refs_2_, ...), custom_call_target="tpu_custom_call" | custom-call | flops 1610612736 | tf_op jit(solution)/shard_map/merge_1/pallas_call | solution.py:242
  23.1 1.8 %collective-permute-start.8 = (bf16[2,48,1024]{2,1,0:T(8,128)(2,1)S(1)}, bf16[2,48,1024]{2,1,0:T(8,128)(2,1)S(1)}, u32[]{:S(2)}, u32[]{:S(2)}) collective-permute-start(bf16[2,48,1024]{2,1,0:T(8,128)(2,1)S(1)} %get-tuple-element.54), channel_id=1, source_target_pairs={{0,4},{1,5},{2,6},{3,7},{4,0},{5,1},{6,2},{7,3},{8,12},{9,13},{10,... | collective-permute-start | bytes 589832 | tf_op jit(solution)/shard_map/ppermute | solution.py:313
  24.9 1.1 %merge_2.7 = (bf16[2,64,1024]{2,1,0:T(8,128)(2,1)S(1)}, bf16[2,48,896]{2,1,0:T(8,128)(2,1)S(1)}) custom-call(f32[4,8,128]{2,1,0:T(8,128)S(1)} %get-tuple-element.37.refs_0_, bf16[4,256,768]{2,1,0:T(8,128)(2,1)S(1)} %get-tuple-element.38.refs_1_.refs_4_, bf16[2,64,768]{2,1,0:T(8,128)(2,1)S(1)} %get-tuple-element.43.refs_6_.refs_2_, ...), custom_call_target="tpu_custom_call" | custom-call | flops 1409286144 | tf_op jit(solution)/shard_map/merge_2/pallas_call | solution.py:242
  26.0 2.7 %collective-permute-start.7 = (bf16[2,48,896]{2,1,0:T(8,128)(2,1)S(1)}, bf16[2,48,896]{2,1,0:T(8,128)(2,1)S(1)}, u32[]{:S(2)}, u32[]{:S(2)}) collective-permute-start(bf16[2,48,896]{2,1,0:T(8,128)(2,1)S(1)} %get-tuple-element.53), channel_id=1, source_target_pairs={{0,8},{1,9},{2,10},{3,11},{4,12},{5,13},{6,14},{7,15},{8,0},{9,1},... | collective-permute-start | bytes 516104 | tf_op jit(solution)/shard_map/ppermute | solution.py:313
  28.7 0.9 %merge_1.8 = (bf16[2,64,768]{2,1,0:T(8,128)(2,1)S(1)}, bf16[2,48,640]{2,1,0:T(8,128)(2,1)S(1)}) custom-call(f32[4,8,128]{2,1,0:T(8,128)S(1)} %get-tuple-element.37.refs_0_, bf16[4,256,768]{2,1,0:T(8,128)(2,1)S(1)} %get-tuple-element.38.refs_1_.refs_4_, bf16[2,64,1792]{2,1,0:T(8,128)(2,1)S(1)} %get-tuple-element.42.refs_4_.refs_3_.refs_2_, ...), custom_call_target="tpu_custom_call" | custom-call | flops 1006632960 | tf_op jit(solution)/shard_map/merge_1/pallas_call | solution.py:242
  29.6 0.5 collective-permute-start.10
  30.1 1.0 %merge_0.7 = (bf16[2,64,768]{2,1,0:T(8,128)(2,1)S(1)}, bf16[2,48,768]{2,1,0:T(8,128)(2,1)S(1)}) custom-call(f32[4,8,128]{2,1,0:T(8,128)S(1)} %get-tuple-element.37.refs_0_, bf16[4,256,768]{2,1,0:T(8,128)(2,1)S(1)} %get-tuple-element.38.refs_1_.refs_4_, bf16[2,64,4096]{2,1,0:T(8,128)(2,1)S(1)} %copy-done, ...), custom_call_target="tpu_custom_call" | custom-call | flops 1207959552 | tf_op jit(solution)/shard_map/merge_0/pallas_call | solution.py:242
  31.1 1.8 %collective-permute-start.11 = (bf16[2,48,768]{2,1,0:T(8,128)(2,1)S(1)}, bf16[2,48,768]{2,1,0:T(8,128)(2,1)S(1)}, u32[]{:S(2)}, u32[]{:S(2)}) collective-permute-start(bf16[2,48,768]{2,1,0:T(8,128)(2,1)S(1)} %get-tuple-element.60), channel_id=1, source_target_pairs={{0,2},{1,3},{2,0},{3,1},{4,6},{5,7},{6,4},{7,5},{8,10},{9,11},{10,... | collective-permute-start | bytes 442376 | tf_op jit(solution)/shard_map/ppermute | solution.py:313
  32.9 1.0 %merge_2.8 = (bf16[2,64,768]{2,1,0:T(8,128)(2,1)S(1)}, bf16[2,48,768]{2,1,0:T(8,128)(2,1)S(1)}) custom-call(f32[4,8,128]{2,1,0:T(8,128)S(1)} %get-tuple-element.37.refs_0_, bf16[4,256,768]{2,1,0:T(8,128)(2,1)S(1)} %get-tuple-element.38.refs_1_.refs_4_, bf16[2,64,1024]{2,1,0:T(8,128)(2,1)S(1)} %get-tuple-element.46.refs_4_.refs_3_.refs_2_, ...), custom_call_target="tpu_custom_call" | custom-call | flops 1207959552 | tf_op jit(solution)/shard_map/merge_2/pallas_call | solution.py:242
  33.8 1.7 %collective-permute-start.9 = (bf16[2,48,768]{2,1,0:T(8,128)(2,1)S(1)}, bf16[2,48,768]{2,1,0:T(8,128)(2,1)S(1)}, u32[]{:S(2)}, u32[]{:S(2)}) collective-permute-start(bf16[2,48,768]{2,1,0:T(8,128)(2,1)S(1)} %get-tuple-element.58), channel_id=1, source_target_pairs={{0,8},{1,9},{2,10},{3,11},{4,12},{5,13},{6,14},{7,15},{8,0},{9,1},... | collective-permute-start | bytes 442376 | tf_op jit(solution)/shard_map/ppermute | solution.py:313
  35.6 0.3 collective-permute-done.7.refs_5_.refs_4_
  35.9 1.1 %merge_3.5.refs_6_ = bf16[2,64,1024]{2,1,0:T(8,128)(2,1)S(1)} custom-call(f32[4,8,128]{2,1,0:T(8,128)S(1)} %get-tuple-element.37.refs_0_, bf16[4,256,768]{2,1,0:T(8,128)(2,1)S(1)} %get-tuple-element.38.refs_1_.refs_4_, bf16[2,64,512]{2,1,0:T(8,128)(2,1)S(1)} %get-tuple-element.47.refs_6_.refs_2_, ...), custom_call_target="tpu_custom_call" | custom-call | flops 352321536 | tf_op jit(solution)/shard_map/merge_3/pallas_call | solution.py:242
  37.0 1.1 %merge_1.9 = (bf16[2,64,1024]{2,1,0:T(8,128)(2,1)S(1)}, bf16[2,48,896]{2,1,0:T(8,128)(2,1)S(1)}) custom-call(f32[4,8,128]{2,1,0:T(8,128)S(1)} %get-tuple-element.37.refs_0_, bf16[4,256,768]{2,1,0:T(8,128)(2,1)S(1)} %get-tuple-element.38.refs_1_.refs_4_, bf16[2,64,1792]{2,1,0:T(8,128)(2,1)S(1)} %get-tuple-element.42.refs_4_.refs_3_.refs_2_, ...), custom_call_target="tpu_custom_call" | custom-call | flops 1409286144 | tf_op jit(solution)/shard_map/merge_1/pallas_call | solution.py:242
  38.1 2.8 %collective-permute-start.13 = (bf16[2,48,896]{2,1,0:T(8,128)(2,1)S(1)}, bf16[2,48,896]{2,1,0:T(8,128)(2,1)S(1)}, u32[]{:S(2)}, u32[]{:S(2)}) collective-permute-start(bf16[2,48,896]{2,1,0:T(8,128)(2,1)S(1)} %get-tuple-element.64), channel_id=1, source_target_pairs={{0,4},{1,5},{2,6},{3,7},{4,0},{5,1},{6,2},{7,3},{8,12},{9,13},{10,... | collective-permute-start | bytes 516104 | tf_op jit(solution)/shard_map/ppermute | solution.py:313
  40.9 1.1 %merge_2.9 = (bf16[2,64,1024]{2,1,0:T(8,128)(2,1)S(1)}, bf16[2,48,896]{2,1,0:T(8,128)(2,1)S(1)}) custom-call(f32[4,8,128]{2,1,0:T(8,128)S(1)} %get-tuple-element.37.refs_0_, bf16[4,256,768]{2,1,0:T(8,128)(2,1)S(1)} %get-tuple-element.38.refs_1_.refs_4_, bf16[2,64,1024]{2,1,0:T(8,128)(2,1)S(1)} %get-tuple-element.50.refs_6_.refs_3_.refs_2_, ...), custom_call_target="tpu_custom_call" | custom-call | flops 1409286144 | tf_op jit(solution)/shard_map/merge_2/pallas_call | solution.py:242
  42.0 1.2 %collective-permute-start.12 = (bf16[2,48,896]{2,1,0:T(8,128)(2,1)S(1)}, bf16[2,48,896]{2,1,0:T(8,128)(2,1)S(1)}, u32[]{:S(2)}, u32[]{:S(2)}) collective-permute-start(bf16[2,48,896]{2,1,0:T(8,128)(2,1)S(1)} %get-tuple-element.63), channel_id=1, source_target_pairs={{0,8},{1,9},{2,10},{3,11},{4,12},{5,13},{6,14},{7,15},{8,0},{9,1},... | collective-permute-start | bytes 516104 | tf_op jit(solution)/shard_map/ppermute | solution.py:313
  43.2 1.1 %merge_3.6.refs_6_ = bf16[2,64,1024]{2,1,0:T(8,128)(2,1)S(1)} custom-call(f32[4,8,128]{2,1,0:T(8,128)S(1)} %get-tuple-element.37.refs_0_, bf16[4,256,768]{2,1,0:T(8,128)(2,1)S(1)} %get-tuple-element.38.refs_1_.refs_4_, bf16[2,64,1024]{2,1,0:T(8,128)(2,1)S(1)} %get-tuple-element.51.refs_4_.refs_3_.refs_2_, ...), custom_call_target="tpu_custom_call" | custom-call | flops 402653184 | tf_op jit(solution)/shard_map/merge_3/pallas_call | solution.py:242
  44.3 2.0 %collective-permute-done.13.refs_5_.refs_3_ = bf16[2,48,896]{2,1,0:T(8,128)(2,1)S(1)} collective-permute-done((bf16[2,48,896]{2,1,0:T(8,128)(2,1)S(1)}, bf16[2,48,896]{2,1,0:T(8,128)(2,1)S(1)}, u32[]{:S(2)}, u32[]{:S(2)}) %collective-permute-start.13) | collective-permute-done | bytes 172064 | tf_op jit(solution)/shard_map/ppermute | solution.py:313
  46.3 1.0 %merge_2.10 = (bf16[2,64,768]{2,1,0:T(8,128)(2,1)S(1)}, bf16[2,48,640]{2,1,0:T(8,128)(2,1)S(1)}) custom-call(f32[4,8,128]{2,1,0:T(8,128)S(1)} %get-tuple-element.37.refs_0_, bf16[4,256,768]{2,1,0:T(8,128)(2,1)S(1)} %get-tuple-element.38.refs_1_.refs_4_, bf16[2,64,768]{2,1,0:T(8,128)(2,1)S(1)} %get-tuple-element.55.refs_4_.refs_3_.refs_2_, ...), custom_call_target="tpu_custom_call" | custom-call | flops 1006632960 | tf_op jit(solution)/shard_map/merge_2/pallas_call | solution.py:242
  47.3 2.0 %collective-permute-start.14 = (bf16[2,48,640]{2,1,0:T(8,128)(2,1)S(1)}, bf16[2,48,640]{2,1,0:T(8,128)(2,1)S(1)}, u32[]{:S(2)}, u32[]{:S(2)}) collective-permute-start(bf16[2,48,640]{2,1,0:T(8,128)(2,1)S(1)} %get-tuple-element.66), channel_id=1, source_target_pairs={{0,8},{1,9},{2,10},{3,11},{4,12},{5,13},{6,14},{7,15},{8,0},{9,1},... | collective-permute-start | bytes 368648 | tf_op jit(solution)/shard_map/ppermute | solution.py:313
  49.3 5.1 %collective-permute-done.12.refs_5_.refs_4_ = bf16[2,48,896]{2,1,0:T(8,128)(2,1)S(1)} collective-permute-done((bf16[2,48,896]{2,1,0:T(8,128)(2,1)S(1)}, bf16[2,48,896]{2,1,0:T(8,128)(2,1)S(1)}, u32[]{:S(2)}, u32[]{:S(2)}) %collective-permute-start.12) | collective-permute-done | bytes 172064 | tf_op jit(solution)/shard_map/ppermute | solution.py:313
  54.4 0.9 %merge_3.7.refs_4_ = bf16[2,64,768]{2,1,0:T(8,128)(2,1)S(1)} custom-call(f32[4,8,128]{2,1,0:T(8,128)S(1)} %get-tuple-element.37.refs_0_, bf16[4,256,768]{2,1,0:T(8,128)(2,1)S(1)} %get-tuple-element.38.refs_1_.refs_4_, bf16[2,64,768]{2,1,0:T(8,128)(2,1)S(1)} %get-tuple-element.57.refs_6_.refs_3_.refs_2_, ...), custom_call_target="tpu_custom_call" | custom-call | flops 301989888 | tf_op jit(solution)/shard_map/merge_3/pallas_call | solution.py:242
  55.3 0.8 %merge_2.11 = (bf16[2,64,512]{2,1,0:T(8,128)(2,1)S(1)}, bf16[2,48,384]{2,1,0:T(8,128)(2,1)S(1)}) custom-call(f32[4,8,128]{2,1,0:T(8,128)S(1)} %get-tuple-element.37.refs_0_, bf16[4,256,768]{2,1,0:T(8,128)(2,1)S(1)} %get-tuple-element.38.refs_1_.refs_4_, bf16[2,64,1024]{2,1,0:T(8,128)(2,1)S(1)} %get-tuple-element.61.refs_6_.refs_3_.refs_2_, ...), custom_call_target="tpu_custom_call" | custom-call | flops 603979776 | tf_op jit(solution)/shard_map/merge_2/pallas_call | solution.py:242
  56.2 0.1 collective-permute-start.15
  56.3 0.9 %collective-permute-done.14.refs_5_.refs_4_ = bf16[2,48,640]{2,1,0:T(8,128)(2,1)S(1)} collective-permute-done((bf16[2,48,640]{2,1,0:T(8,128)(2,1)S(1)}, bf16[2,48,640]{2,1,0:T(8,128)(2,1)S(1)}, u32[]{:S(2)}, u32[]{:S(2)}) %collective-permute-start.14) | collective-permute-done | bytes 122912 | tf_op jit(solution)/shard_map/ppermute | solution.py:313
  57.2 1.1 %merge_3.8.refs_6_ = bf16[2,64,1024]{2,1,0:T(8,128)(2,1)S(1)} custom-call(f32[4,8,128]{2,1,0:T(8,128)S(1)} %get-tuple-element.37.refs_0_, bf16[4,256,768]{2,1,0:T(8,128)(2,1)S(1)} %get-tuple-element.38.refs_1_.refs_4_, bf16[2,64,1024]{2,1,0:T(8,128)(2,1)S(1)} %get-tuple-element.62.refs_6_.refs_3_.refs_2_, ...), custom_call_target="tpu_custom_call" | custom-call | flops 352321536 | tf_op jit(solution)/shard_map/merge_3/pallas_call | solution.py:242
  58.3 3.2 %collective-permute-done.15.refs_5_ = bf16[2,48,384]{2,1,0:T(8,128)(2,1)S(1)} collective-permute-done((bf16[2,48,384]{2,1,0:T(8,128)(2,1)S(1)}, bf16[2,48,384]{2,1,0:T(8,128)(2,1)S(1)}, u32[]{:S(2)}, u32[]{:S(2)}) %collective-permute-start.15) | collective-permute-done | bytes 73760 | tf_op jit(solution)/shard_map/ppermute | solution.py:313
  61.5 0.8 %merge_3.9 = bf16[2,64,512]{2,1,0:T(8,128)(2,1)S(1)} custom-call(f32[4,8,128]{2,1,0:T(8,128)S(1)} %get-tuple-element.37.refs_0_, bf16[4,256,768]{2,1,0:T(8,128)(2,1)S(1)} %get-tuple-element.38.refs_1_.refs_4_, bf16[2,64,768]{2,1,0:T(8,128)(2,1)S(1)} %get-tuple-element.65.refs_6_.refs_3_.refs_2_, bf16[2,64,512]{2,1,0:T(8,128)(2,1)S(1)} %get-tuple-element.67.refs_6_.refs_3_, ...), custom_call_target="tpu_custom_call" | custom-call | flops 201326592 | tf_op jit(solution)/shard_map/merge_3/pallas_call | solution.py:242
  62.3 0.7 %constant_dynamic-update-slice_fusion = bf16[2,64,4096]{2,1,0:T(8,128)(2,1)} fusion(bf16[2,64,4096]{2,1,0:T(8,128)(2,1)} %copy-done.1, bf16[2,64,512]{2,1,0:T(8,128)(2,1)S(1)} %merge_3.9), kind=kLoop, calls=%fused_computation.2 | loop fusion | bytes 262144 | tf_op jit(solution)/shard_map/concatenate | solution.py:339
  (16 shorter events, 0.1 us)
Async XLA Ops:
  0.0 3.0 %collective-permute-start = (bf16[2,64,4096]{2,1,0:T(8,128)(2,1)}, bf16[2,64,4096]{2,1,0:T(8,128)(2,1)S(1)}, u32[]{:S(2)}, u32[]{:S(2)}) collective-permute-start(bf16[2,64,4096]{2,1,0:T(8,128)(2,1)} %refs_2_.7), channel_id=1, source_target_pairs={{0,1},{1,0},{2,3},{3,2},{4,5},{5,4},{6,7},{7,6},{8,9},{9,8},{10,11... | collective-permute-start | bytes 3145736 | tf_op jit(solution)/shard_map/ppermute | solution.py:313
  2.0 1.2 %copy-start = (bf16[2,64,4096]{2,1,0:T(8,128)(2,1)S(1)}, bf16[2,64,4096]{2,1,0:T(8,128)(2,1)}, u32[]{:S(2)}) copy-start(bf16[2,64,4096]{2,1,0:T(8,128)(2,1)} %refs_2_.7) | copy-start | bytes 3145732
  4.2 8.3 %collective-permute-start.1 = (bf16[2,48,768]{2,1,0:T(8,128)(2,1)S(1)}, bf16[2,48,768]{2,1,0:T(8,128)(2,1)S(1)}, u32[]{:S(2)}, u32[]{:S(2)}) collective-permute-start(bf16[2,48,768]{2,1,0:T(8,128)(2,1)S(1)} %get-tuple-element.40), channel_id=1, source_target_pairs={{0,2},{1,3},{2,0},{3,1},{4,6},{5,7},{6,4},{7,5},{8,10},{9,11},{10,... | collective-permute-start | bytes 442376 | tf_op jit(solution)/shard_map/ppermute | solution.py:313
  8.0 7.4 %collective-permute-start.3 = (bf16[2,48,896]{2,1,0:T(8,128)(2,1)S(1)}, bf16[2,48,896]{2,1,0:T(8,128)(2,1)S(1)}, u32[]{:S(2)}, u32[]{:S(2)}) collective-permute-start(bf16[2,48,896]{2,1,0:T(8,128)(2,1)S(1)} %get-tuple-element.45), channel_id=1, source_target_pairs={{0,2},{1,3},{2,0},{3,1},{4,6},{5,7},{6,4},{7,5},{8,10},{9,11},{10,... | collective-permute-start | bytes 516104 | tf_op jit(solution)/shard_map/ppermute | solution.py:313
  10.4 11.5 %collective-permute-start.5 = (bf16[2,48,1664]{2,1,0:T(8,128)(2,1)S(1)}, bf16[2,48,1664]{2,1,0:T(8,128)(2,1)S(1)}, u32[]{:S(2)}, u32[]{:S(2)}) collective-permute-start(bf16[2,48,1664]{2,1,0:T(8,128)(2,1)S(1)} %get-tuple-element.49), channel_id=1, source_target_pairs={{0,2},{1,3},{2,0},{3,1},{4,6},{5,7},{6,4},{7,5},{8,10},{9,11},{10,... | collective-permute-start | bytes 958472 | tf_op jit(solution)/shard_map/ppermute | solution.py:313
  13.4 5.0 %collective-permute-start.2 = (bf16[2,48,640]{2,1,0:T(8,128)(2,1)S(1)}, bf16[2,48,640]{2,1,0:T(8,128)(2,1)S(1)}, u32[]{:S(2)}, u32[]{:S(2)}) collective-permute-start(bf16[2,48,640]{2,1,0:T(8,128)(2,1)S(1)} %get-tuple-element.44), channel_id=1, source_target_pairs={{0,4},{1,5},{2,6},{3,7},{4,0},{5,1},{6,2},{7,3},{8,12},{9,13},{10,... | collective-permute-start | bytes 368648 | tf_op jit(solution)/shard_map/ppermute | solution.py:313
  16.5 8.3 %collective-permute-start.4 = (bf16[2,48,896]{2,1,0:T(8,128)(2,1)S(1)}, bf16[2,48,896]{2,1,0:T(8,128)(2,1)S(1)}, u32[]{:S(2)}, u32[]{:S(2)}) collective-permute-start(bf16[2,48,896]{2,1,0:T(8,128)(2,1)S(1)} %get-tuple-element.48), channel_id=1, source_target_pairs={{0,4},{1,5},{2,6},{3,7},{4,0},{5,1},{6,2},{7,3},{8,12},{9,13},{10,... | collective-permute-start | bytes 516104 | tf_op jit(solution)/shard_map/ppermute | solution.py:313
  19.3 16.3 %collective-permute-start.6 = (bf16[2,48,512]{2,1,0:T(8,128)(2,1)S(1)}, bf16[2,48,512]{2,1,0:T(8,128)(2,1)S(1)}, u32[]{:S(2)}, u32[]{:S(2)}) collective-permute-start(bf16[2,48,512]{2,1,0:T(8,128)(2,1)S(1)} %get-tuple-element.52), channel_id=1, source_target_pairs={{0,8},{1,9},{2,10},{3,11},{4,12},{5,13},{6,14},{7,15},{8,0},{9,1},... | collective-permute-start | bytes 294920 | tf_op jit(solution)/shard_map/ppermute | solution.py:313
  23.1 9.8 %collective-permute-start.8 = (bf16[2,48,1024]{2,1,0:T(8,128)(2,1)S(1)}, bf16[2,48,1024]{2,1,0:T(8,128)(2,1)S(1)}, u32[]{:S(2)}, u32[]{:S(2)}) collective-permute-start(bf16[2,48,1024]{2,1,0:T(8,128)(2,1)S(1)} %get-tuple-element.54), channel_id=1, source_target_pairs={{0,4},{1,5},{2,6},{3,7},{4,0},{5,1},{6,2},{7,3},{8,12},{9,13},{10,... | collective-permute-start | bytes 589832 | tf_op jit(solution)/shard_map/ppermute | solution.py:313
  26.0 9.9 %collective-permute-start.7 = (bf16[2,48,896]{2,1,0:T(8,128)(2,1)S(1)}, bf16[2,48,896]{2,1,0:T(8,128)(2,1)S(1)}, u32[]{:S(2)}, u32[]{:S(2)}) collective-permute-start(bf16[2,48,896]{2,1,0:T(8,128)(2,1)S(1)} %get-tuple-element.53), channel_id=1, source_target_pairs={{0,8},{1,9},{2,10},{3,11},{4,12},{5,13},{6,14},{7,15},{8,0},{9,1},... | collective-permute-start | bytes 516104 | tf_op jit(solution)/shard_map/ppermute | solution.py:313
  29.6 11.3 %collective-permute-start.10 = (bf16[2,48,640]{2,1,0:T(8,128)(2,1)S(1)}, bf16[2,48,640]{2,1,0:T(8,128)(2,1)S(1)}, u32[]{:S(2)}, u32[]{:S(2)}) collective-permute-start(bf16[2,48,640]{2,1,0:T(8,128)(2,1)S(1)} %get-tuple-element.59), channel_id=1, source_target_pairs={{0,4},{1,5},{2,6},{3,7},{4,0},{5,1},{6,2},{7,3},{8,12},{9,13},{10,... | collective-permute-start | bytes 368648 | tf_op jit(solution)/shard_map/ppermute | solution.py:313
  31.1 5.9 %collective-permute-start.11 = (bf16[2,48,768]{2,1,0:T(8,128)(2,1)S(1)}, bf16[2,48,768]{2,1,0:T(8,128)(2,1)S(1)}, u32[]{:S(2)}, u32[]{:S(2)}) collective-permute-start(bf16[2,48,768]{2,1,0:T(8,128)(2,1)S(1)} %get-tuple-element.60), channel_id=1, source_target_pairs={{0,2},{1,3},{2,0},{3,1},{4,6},{5,7},{6,4},{7,5},{8,10},{9,11},{10,... | collective-permute-start | bytes 442376 | tf_op jit(solution)/shard_map/ppermute | solution.py:313
  33.8 9.4 %collective-permute-start.9 = (bf16[2,48,768]{2,1,0:T(8,128)(2,1)S(1)}, bf16[2,48,768]{2,1,0:T(8,128)(2,1)S(1)}, u32[]{:S(2)}, u32[]{:S(2)}) collective-permute-start(bf16[2,48,768]{2,1,0:T(8,128)(2,1)S(1)} %get-tuple-element.58), channel_id=1, source_target_pairs={{0,8},{1,9},{2,10},{3,11},{4,12},{5,13},{6,14},{7,15},{8,0},{9,1},... | collective-permute-start | bytes 442376 | tf_op jit(solution)/shard_map/ppermute | solution.py:313
  38.1 8.2 %collective-permute-start.13 = (bf16[2,48,896]{2,1,0:T(8,128)(2,1)S(1)}, bf16[2,48,896]{2,1,0:T(8,128)(2,1)S(1)}, u32[]{:S(2)}, u32[]{:S(2)}) collective-permute-start(bf16[2,48,896]{2,1,0:T(8,128)(2,1)S(1)} %get-tuple-element.64), channel_id=1, source_target_pairs={{0,4},{1,5},{2,6},{3,7},{4,0},{5,1},{6,2},{7,3},{8,12},{9,13},{10,... | collective-permute-start | bytes 516104 | tf_op jit(solution)/shard_map/ppermute | solution.py:313
  42.0 12.4 %collective-permute-start.12 = (bf16[2,48,896]{2,1,0:T(8,128)(2,1)S(1)}, bf16[2,48,896]{2,1,0:T(8,128)(2,1)S(1)}, u32[]{:S(2)}, u32[]{:S(2)}) collective-permute-start(bf16[2,48,896]{2,1,0:T(8,128)(2,1)S(1)} %get-tuple-element.63), channel_id=1, source_target_pairs={{0,8},{1,9},{2,10},{3,11},{4,12},{5,13},{6,14},{7,15},{8,0},{9,1},... | collective-permute-start | bytes 516104 | tf_op jit(solution)/shard_map/ppermute | solution.py:313
  47.3 9.9 %collective-permute-start.14 = (bf16[2,48,640]{2,1,0:T(8,128)(2,1)S(1)}, bf16[2,48,640]{2,1,0:T(8,128)(2,1)S(1)}, u32[]{:S(2)}, u32[]{:S(2)}) collective-permute-start(bf16[2,48,640]{2,1,0:T(8,128)(2,1)S(1)} %get-tuple-element.66), channel_id=1, source_target_pairs={{0,8},{1,9},{2,10},{3,11},{4,12},{5,13},{6,14},{7,15},{8,0},{9,1},... | collective-permute-start | bytes 368648 | tf_op jit(solution)/shard_map/ppermute | solution.py:313
  56.2 5.3 %collective-permute-start.15 = (bf16[2,48,384]{2,1,0:T(8,128)(2,1)S(1)}, bf16[2,48,384]{2,1,0:T(8,128)(2,1)S(1)}, u32[]{:S(2)}, u32[]{:S(2)}) collective-permute-start(bf16[2,48,384]{2,1,0:T(8,128)(2,1)S(1)} %get-tuple-element.68), channel_id=1, source_target_pairs={{0,8},{1,9},{2,10},{3,11},{4,12},{5,13},{6,14},{7,15},{8,0},{9,1},... | collective-permute-start | bytes 221192 | tf_op jit(solution)/shard_map/ppermute | solution.py:313
  58.3 4.0 %copy-start.1 = (bf16[2,64,4096]{2,1,0:T(8,128)(2,1)}, bf16[2,64,4096]{2,1,0:T(8,128)(2,1)S(1)}, u32[]{:S(2)}) copy-start(bf16[2,64,4096]{2,1,0:T(8,128)(2,1)S(1)} %slice_dynamic-update-slice_fusion) | copy-start | bytes 3145732

commit v9 on v8

--- a/solution.py
+++ b/solution.py
@@ -269,14 +269,14 @@
 
 
 MARKS = (
-    (6, 13, 26),
-    (5, 12, 20, 25),
-    (4, 11, 17, 24, 29),
-    (7, 15, 21, 28),
+    (8, 16),
+    (7, 15, 21, 27),
+    (6, 14, 20, 26),
+    (5, 13, 25),
 )
 ORDER = (
-    (0, 0), (0, 1), (0, 2), (1, 0), (1, 1), (2, 0), (1, 2), (2, 1), (1, 3), (0, 3), (2, 2),
-    (3, 0), (1, 4), (2, 3), (3, 1), (2, 4), (3, 2), (2, 5), (3, 3), (3, 4),
+    (0, 0), (0, 1), (0, 2), (1, 0), (1, 1), (2, 0), (1, 2), (2, 1), (1, 3), (3, 0), (1, 4),
+    (2, 2), (3, 1), (2, 3), (2, 4), (3, 2), (3, 3),
 )
 
 

time: 63.1 us -> 62 us (0.983)
  waiting for transfers between devices: 11.9 us -> 16.7 us
  starting transfers between devices: 26.1 us -> 21.5 us
  Pallas kernels: 22.2 us -> 20.5 us
  other arithmetic: 1.54 us -> 2.62 us
  local copies, waits for them, and re-layouts: 1.03 us -> 0.3 us
    ppermute x16 -> x14, waiting for transfers between devices: 11.9 us -> 16.7 us  [from_partner(): return lax.ppermute(value, 'pulse', pairs)]
    ppermute x16 -> x14, starting transfers between devices: 26.1 us -> 21.5 us  [from_partner(): return lax.ppermute(value, 'pulse', pairs)]
    pallas_call x20 -> x17, Pallas kernels: 21.3 us -> 19.7 us  [merge(): pl.pallas_call(functools.partial(merge_kernel, level, plan, start, stop,...]
    concatenate x0 -> x1, other arithmetic: none -> 1.08 us  [on_device(): return jnp.concatenate(made, axis=2)]
    concatenate x1 -> x0, local copies, waits for them, and re-layouts: 0.67 us -> none  [on_device(): return jnp.concatenate(made, axis=2)]
  transfers between devices with their start and end apart: 16 -> 14, of which waited for: 7 -> 8; matrix products, arithmetic and copies ran while one was open for 3% -> 2% of each run, Pallas kernels for 32% -> 30%
where the time goes in v9:
time: 62 us; the launch traced here: 61.8 us
  starting transfers between devices  21.5 us (35%)
  Pallas kernels  20.5 us (33%)
  waiting for transfers between devices  16.7 us (27%)
  other arithmetic  2.62 us (4%)
    ppermute x14, starting transfers between devices, from_partner(): return lax.ppermute(value, 'pulse', pairs)  21.5 us
    pallas_call x17, Pallas kernels, merge(): pl.pallas_call(functools.partial(merge_kernel, level, plan, start, stop,...  19.7 us
    ppermute x14, waiting for transfers between devices, from_partner(): return lax.ppermute(value, 'pulse', pairs)  16.7 us
    add x2, other arithmetic, stacked(): total = total + lax.pad(piece, zero, ((top, below, 0), (left, right, 0)))  1.54 us
  transfers between devices with their start and end apart: 14, of which 8 were waited for; matrix products, arithmetic and copies ran while one was open for 2% of the time, Pallas kernels for 30%

profile of v9, /device:TPU:0, one launch (start us, length us, event | category | flops | bytes accessed | tf_op | source)
XLA Modules:
  0.0 61.8 jit_solution(2575182977531237248)
XLA Ops:
  0.0 0.5 collective-permute-start
  0.5 0.7 %pad_add_fusion.real_ref = f32[14,128]{1,0:T(8,128)S(1)} fusion(f32[4,16]{1,0:T(4,128)} %bitcast.3, f32[8,128]{1,0:T(8,128)} %bitcast.2, bf16[2,32]{1,0:T(2,128)(2,1)} %param.8), kind=kLoop, calls=%fused_computation.1 | loop fusion | flops 5376 | bytes 11648 | tf_op jit(solution)/shard_map/add | solution.py:91
  1.2 0.8 %pad_add_fusion.1.whole_ref = s32[12,128]{1,0:T(8,128)S(1)} fusion(s32[4,64]{1,0:T(4,128)} %param.11, s32[4,16]{1,0:T(4,128)} %param.12, s32[4,16]{1,0:T(4,128)} %param.13), kind=kLoop, calls=%fused_computation.2 | loop fusion | flops 4608 | bytes 7680 | tf_op jit(solution)/shard_map/add | solution.py:91
  2.0 0.9 %mixing.1 = (bf16[4,256,768]{2,1,0:T(8,128)(2,1)S(1)}, f32[4,8,128]{2,1,0:T(8,128)S(1)}) custom-call(s32[12,128]{1,0:T(8,128)S(1)} %pad_add_fusion.1.whole_ref, f32[14,128]{1,0:T(8,128)S(1)} %pad_add_fusion.real_ref), custom_call_target="tpu_custom_call" | custom-call | flops 2000000000 | bytes 1572864 | tf_op jit(solution)/shard_map/mixing/pallas_call | solution.py:121
  2.9 0.1 collective-permute-done.refs_3_
  3.0 0.3 copy-done.1
  3.2 1.1 %merge_0.3 = (bf16[2,64,1024]{2,1,0:T(8,128)(2,1)S(1)}, bf16[2,48,1024]{2,1,0:T(8,128)(2,1)S(1)}) custom-call(f32[4,8,128]{2,1,0:T(8,128)S(1)} %get-tuple-element.33.refs_0_, bf16[4,256,768]{2,1,0:T(8,128)(2,1)S(1)} %get-tuple-element.34.refs_1_.refs_4_, bf16[2,64,4096]{2,1,0:T(8,128)(2,1)S(1)} %copy-done.1, ...), custom_call_target="tpu_custom_call" | custom-call | flops 1610612736 | tf_op jit(solution)/shard_map/merge_0/pallas_call | solution.py:242
  4.4 2.7 %collective-permute-start.1 = (bf16[2,48,1024]{2,1,0:T(8,128)(2,1)S(1)}, bf16[2,48,1024]{2,1,0:T(8,128)(2,1)S(1)}, u32[]{:S(2)}, u32[]{:S(2)}) collective-permute-start(bf16[2,48,1024]{2,1,0:T(8,128)(2,1)S(1)} %get-tuple-element.36), channel_id=1, source_target_pairs={{0,2},{1,3},{2,0},{3,1},{4,6},{5,7},{6,4},{7,5},{8,10},{9,11},{10,... | collective-permute-start | bytes 589832 | tf_op jit(solution)/shard_map/ppermute | solution.py:313
  7.1 1.1 %merge_0.4 = (bf16[2,64,1024]{2,1,0:T(8,128)(2,1)S(1)}, bf16[2,48,1024]{2,1,0:T(8,128)(2,1)S(1)}) custom-call(f32[4,8,128]{2,1,0:T(8,128)S(1)} %get-tuple-element.33.refs_0_, bf16[4,256,768]{2,1,0:T(8,128)(2,1)S(1)} %get-tuple-element.34.refs_1_.refs_4_, bf16[2,64,4096]{2,1,0:T(8,128)(2,1)S(1)} %copy-done.1, ...), custom_call_target="tpu_custom_call" | custom-call | flops 1610612736 | tf_op jit(solution)/shard_map/merge_0/pallas_call | solution.py:242
  8.2 0.1 collective-permute-start.3
  8.3 2.5 %merge_0.5 = (bf16[2,64,2048]{2,1,0:T(8,128)(2,1)S(1)}, bf16[2,48,2048]{2,1,0:T(8,128)(2,1)S(1)}) custom-call(f32[4,8,128]{2,1,0:T(8,128)S(1)} %get-tuple-element.33.refs_0_, bf16[4,256,768]{2,1,0:T(8,128)(2,1)S(1)} %get-tuple-element.34.refs_1_.refs_4_, bf16[2,64,4096]{2,1,0:T(8,128)(2,1)S(1)} %copy-done.1, ...), custom_call_target="tpu_custom_call" | custom-call | flops 3221225472 | tf_op jit(solution)/shard_map/merge_0/pallas_call | solution.py:242
  10.8 2.1 %collective-permute-start.5 = (bf16[2,48,2048]{2,1,0:T(8,128)(2,1)S(1)}, bf16[2,48,2048]{2,1,0:T(8,128)(2,1)S(1)}, u32[]{:S(2)}, u32[]{:S(2)}) collective-permute-start(bf16[2,48,2048]{2,1,0:T(8,128)(2,1)S(1)} %get-tuple-element.45), channel_id=1, source_target_pairs={{0,2},{1,3},{2,0},{3,1},{4,6},{5,7},{6,4},{7,5},{8,10},{9,11},{10,... | collective-permute-start | bytes 1179656 | tf_op jit(solution)/shard_map/ppermute | solution.py:313
  12.9 1.1 %merge_1.5 = (bf16[2,64,1024]{2,1,0:T(8,128)(2,1)S(1)}, bf16[2,48,896]{2,1,0:T(8,128)(2,1)S(1)}) custom-call(f32[4,8,128]{2,1,0:T(8,128)S(1)} %get-tuple-element.33.refs_0_, bf16[4,256,768]{2,1,0:T(8,128)(2,1)S(1)} %get-tuple-element.34.refs_1_.refs_4_, bf16[2,64,1024]{2,1,0:T(8,128)(2,1)S(1)} %get-tuple-element.35.refs_4_.refs_2_, ...), custom_call_target="tpu_custom_call" | custom-call | flops 1409286144 | tf_op jit(solution)/shard_map/merge_1/pallas_call | solution.py:242
  14.0 2.0 %collective-permute-start.2 = (bf16[2,48,896]{2,1,0:T(8,128)(2,1)S(1)}, bf16[2,48,896]{2,1,0:T(8,128)(2,1)S(1)}, u32[]{:S(2)}, u32[]{:S(2)}) collective-permute-start(bf16[2,48,896]{2,1,0:T(8,128)(2,1)S(1)} %get-tuple-element.40), channel_id=1, source_target_pairs={{0,4},{1,5},{2,6},{3,7},{4,0},{5,1},{6,2},{7,3},{8,12},{9,13},{10,... | collective-permute-start | bytes 516104 | tf_op jit(solution)/shard_map/ppermute | solution.py:313
  16.0 1.0 %collective-permute-done.3.refs_5_.refs_4_ = bf16[2,48,1024]{2,1,0:T(8,128)(2,1)S(1)} collective-permute-done((bf16[2,48,1024]{2,1,0:T(8,128)(2,1)S(1)}, bf16[2,48,1024]{2,1,0:T(8,128)(2,1)S(1)}, u32[]{:S(2)}, u32[]{:S(2)}) %collective-permute-start.3) | collective-permute-done | bytes 196640 | tf_op jit(solution)/shard_map/ppermute | solution.py:313
  17.0 1.1 %merge_1.6 = (bf16[2,64,1024]{2,1,0:T(8,128)(2,1)S(1)}, bf16[2,48,1024]{2,1,0:T(8,128)(2,1)S(1)}) custom-call(f32[4,8,128]{2,1,0:T(8,128)S(1)} %get-tuple-element.33.refs_0_, bf16[4,256,768]{2,1,0:T(8,128)(2,1)S(1)} %get-tuple-element.34.refs_1_.refs_4_, bf16[2,64,1024]{2,1,0:T(8,128)(2,1)S(1)} %get-tuple-element.35.refs_4_.refs_2_, ...), custom_call_target="tpu_custom_call" | custom-call | flops 1610612736 | tf_op jit(solution)/shard_map/merge_1/pallas_call | solution.py:242
  18.2 2.1 %collective-permute-start.6 = (bf16[2,48,1024]{2,1,0:T(8,128)(2,1)S(1)}, bf16[2,48,1024]{2,1,0:T(8,128)(2,1)S(1)}, u32[]{:S(2)}, u32[]{:S(2)}) collective-permute-start(bf16[2,48,1024]{2,1,0:T(8,128)(2,1)S(1)} %get-tuple-element.46), channel_id=1, source_target_pairs={{0,4},{1,5},{2,6},{3,7},{4,0},{5,1},{6,2},{7,3},{8,12},{9,13},{10,... | collective-permute-start | bytes 589832 | tf_op jit(solution)/shard_map/ppermute | solution.py:313
  20.2 1.0 %merge_2.5 = (bf16[2,64,768]{2,1,0:T(8,128)(2,1)S(1)}, bf16[2,48,768]{2,1,0:T(8,128)(2,1)S(1)}) custom-call(f32[4,8,128]{2,1,0:T(8,128)S(1)} %get-tuple-element.33.refs_0_, bf16[4,256,768]{2,1,0:T(8,128)(2,1)S(1)} %get-tuple-element.34.refs_1_.refs_4_, bf16[2,64,1024]{2,1,0:T(8,128)(2,1)S(1)} %get-tuple-element.39.refs_6_.refs_2_, ...), custom_call_target="tpu_custom_call" | custom-call | flops 1207959552 | tf_op jit(solution)/shard_map/merge_2/pallas_call | solution.py:242
  21.2 2.7 %collective-permute-start.4 = (bf16[2,48,768]{2,1,0:T(8,128)(2,1)S(1)}, bf16[2,48,768]{2,1,0:T(8,128)(2,1)S(1)}, u32[]{:S(2)}, u32[]{:S(2)}) collective-permute-start(bf16[2,48,768]{2,1,0:T(8,128)(2,1)S(1)} %get-tuple-element.44), channel_id=1, source_target_pairs={{0,8},{1,9},{2,10},{3,11},{4,12},{5,13},{6,14},{7,15},{8,0},{9,1},... | collective-permute-start | bytes 442376 | tf_op jit(solution)/shard_map/ppermute | solution.py:313
  23.8 1.3 %collective-permute-done.5.refs_5_.refs_3_ = bf16[2,48,2048]{2,1,0:T(8,128)(2,1)S(1)} collective-permute-done((bf16[2,48,2048]{2,1,0:T(8,128)(2,1)S(1)}, bf16[2,48,2048]{2,1,0:T(8,128)(2,1)S(1)}, u32[]{:S(2)}, u32[]{:S(2)}) %collective-permute-start.5) | collective-permute-done | bytes 393248 | tf_op jit(solution)/shard_map/ppermute | solution.py:313
  25.2 0.9 %merge_1.7 = (bf16[2,64,768]{2,1,0:T(8,128)(2,1)S(1)}, bf16[2,48,768]{2,1,0:T(8,128)(2,1)S(1)}) custom-call(f32[4,8,128]{2,1,0:T(8,128)S(1)} %get-tuple-element.33.refs_0_, bf16[4,256,768]{2,1,0:T(8,128)(2,1)S(1)} %get-tuple-element.34.refs_1_.refs_4_, bf16[2,64,1024]{2,1,0:T(8,128)(2,1)S(1)} %get-tuple-element.37.refs_4_.refs_3_.refs_2_, ...), custom_call_target="tpu_custom_call" | custom-call | flops 1207959552 | tf_op jit(solution)/shard_map/merge_1/pallas_call | solution.py:242
  26.1 1.9 %collective-permute-start.8 = (bf16[2,48,768]{2,1,0:T(8,128)(2,1)S(1)}, bf16[2,48,768]{2,1,0:T(8,128)(2,1)S(1)}, u32[]{:S(2)}, u32[]{:S(2)}) collective-permute-start(bf16[2,48,768]{2,1,0:T(8,128)(2,1)S(1)} %get-tuple-element.51), channel_id=1, source_target_pairs={{0,4},{1,5},{2,6},{3,7},{4,0},{5,1},{6,2},{7,3},{8,12},{9,13},{10,... | collective-permute-start | bytes 442376 | tf_op jit(solution)/shard_map/ppermute | solution.py:313
  28.0 0.0 collective-permute-done.6.refs_5_.refs_4_
  28.0 1.1 %merge_2.6 = (bf16[2,64,1024]{2,1,0:T(8,128)(2,1)S(1)}, bf16[2,48,1024]{2,1,0:T(8,128)(2,1)S(1)}) custom-call(f32[4,8,128]{2,1,0:T(8,128)S(1)} %get-tuple-element.33.refs_0_, bf16[4,256,768]{2,1,0:T(8,128)(2,1)S(1)} %get-tuple-element.34.refs_1_.refs_4_, bf16[2,64,1024]{2,1,0:T(8,128)(2,1)S(1)} %get-tuple-element.39.refs_6_.refs_2_, ...), custom_call_target="tpu_custom_call" | custom-call | flops 1610612736 | tf_op jit(solution)/shard_map/merge_2/pallas_call | solution.py:242
  29.1 2.7 %collective-permute-start.7 = (bf16[2,48,1024]{2,1,0:T(8,128)(2,1)S(1)}, bf16[2,48,1024]{2,1,0:T(8,128)(2,1)S(1)}, u32[]{:S(2)}, u32[]{:S(2)}) collective-permute-start(bf16[2,48,1024]{2,1,0:T(8,128)(2,1)S(1)} %get-tuple-element.50), channel_id=1, source_target_pairs={{0,8},{1,9},{2,10},{3,11},{4,12},{5,13},{6,14},{7,15},{8,0},{9,1},... | collective-permute-start | bytes 589832 | tf_op jit(solution)/shard_map/ppermute | solution.py:313
  31.8 0.9 %merge_1.8 = (bf16[2,64,768]{2,1,0:T(8,128)(2,1)S(1)}, bf16[2,48,768]{2,1,0:T(8,128)(2,1)S(1)}) custom-call(f32[4,8,128]{2,1,0:T(8,128)S(1)} %get-tuple-element.33.refs_0_, bf16[4,256,768]{2,1,0:T(8,128)(2,1)S(1)} %get-tuple-element.34.refs_1_.refs_4_, bf16[2,64,2048]{2,1,0:T(8,128)(2,1)S(1)} %get-tuple-element.38.refs_4_.refs_3_.refs_2_, ...), custom_call_target="tpu_custom_call" | custom-call | flops 1207959552 | tf_op jit(solution)/shard_map/merge_1/pallas_call | solution.py:242
  32.7 0.5 collective-permute-start.9
  33.3 0.0 collective-permute-done.4.refs_3_.refs_4_
  33.3 0.9 %merge_3.4.refs_4_ = bf16[2,64,768]{2,1,0:T(8,128)(2,1)S(1)} custom-call(f32[4,8,128]{2,1,0:T(8,128)S(1)} %get-tuple-element.33.refs_0_, bf16[4,256,768]{2,1,0:T(8,128)(2,1)S(1)} %get-tuple-element.34.refs_1_.refs_4_, bf16[2,64,768]{2,1,0:T(8,128)(2,1)S(1)} %get-tuple-element.43.refs_6_.refs_2_, ...), custom_call_target="tpu_custom_call" | custom-call | flops 251658240 | tf_op jit(solution)/shard_map/merge_3/pallas_call | solution.py:242
  34.2 0.0 copy-start
  34.2 0.9 %merge_1.9 = (bf16[2,64,768]{2,1,0:T(8,128)(2,1)S(1)}, bf16[2,48,640]{2,1,0:T(8,128)(2,1)S(1)}) custom-call(f32[4,8,128]{2,1,0:T(8,128)S(1)} %get-tuple-element.33.refs_0_, bf16[4,256,768]{2,1,0:T(8,128)(2,1)S(1)} %get-tuple-element.34.refs_1_.refs_4_, bf16[2,64,2048]{2,1,0:T(8,128)(2,1)S(1)} %get-tuple-element.38.refs_4_.refs_3_.refs_2_, ...), custom_call_target="tpu_custom_call" | custom-call | flops 1006632960 | tf_op jit(solution)/shard_map/merge_1/pallas_call | solution.py:242
  35.1 1.7 %collective-permute-start.12 = (bf16[2,48,640]{2,1,0:T(8,128)(2,1)S(1)}, bf16[2,48,640]{2,1,0:T(8,128)(2,1)S(1)}, u32[]{:S(2)}, u32[]{:S(2)}) collective-permute-start(bf16[2,48,640]{2,1,0:T(8,128)(2,1)S(1)} %get-tuple-element.58), channel_id=1, source_target_pairs={{0,4},{1,5},{2,6},{3,7},{4,0},{5,1},{6,2},{7,3},{8,12},{9,13},{10,... | collective-permute-start | bytes 368648 | tf_op jit(solution)/shard_map/ppermute | solution.py:313
  36.8 0.9 %merge_2.7 = (bf16[2,64,768]{2,1,0:T(8,128)(2,1)S(1)}, bf16[2,48,768]{2,1,0:T(8,128)(2,1)S(1)}) custom-call(f32[4,8,128]{2,1,0:T(8,128)S(1)} %get-tuple-element.33.refs_0_, bf16[4,256,768]{2,1,0:T(8,128)(2,1)S(1)} %get-tuple-element.34.refs_1_.refs_4_, bf16[2,64,1024]{2,1,0:T(8,128)(2,1)S(1)} %get-tuple-element.42.refs_4_.refs_3_.refs_2_, ...), custom_call_target="tpu_custom_call" | custom-call | flops 1207959552 | tf_op jit(solution)/shard_map/merge_2/pallas_call | solution.py:242
  37.7 0.4 collective-permute-start.10
  38.1 3.0 %collective-permute-done.7.refs_5_ = bf16[2,48,1024]{2,1,0:T(8,128)(2,1)S(1)} collective-permute-done((bf16[2,48,1024]{2,1,0:T(8,128)(2,1)S(1)}, bf16[2,48,1024]{2,1,0:T(8,128)(2,1)S(1)}, u32[]{:S(2)}, u32[]{:S(2)}) %collective-permute-start.7) | collective-permute-done | bytes 196640 | tf_op jit(solution)/shard_map/ppermute | solution.py:313
  41.2 1.1 %merge_3.5.refs_6_ = bf16[2,64,1024]{2,1,0:T(8,128)(2,1)S(1)} custom-call(f32[4,8,128]{2,1,0:T(8,128)S(1)} %get-tuple-element.33.refs_0_, bf16[4,256,768]{2,1,0:T(8,128)(2,1)S(1)} %get-tuple-element.34.refs_1_.refs_4_, bf16[2,64,768]{2,1,0:T(8,128)(2,1)S(1)} %get-tuple-element.43.refs_6_.refs_2_, ...), custom_call_target="tpu_custom_call" | custom-call | flops 402653184 | tf_op jit(solution)/shard_map/merge_3/pallas_call | solution.py:242
  42.2 2.4 %collective-permute-done.9.refs_5_.refs_4_ = bf16[2,48,768]{2,1,0:T(8,128)(2,1)S(1)} collective-permute-done((bf16[2,48,768]{2,1,0:T(8,128)(2,1)S(1)}, bf16[2,48,768]{2,1,0:T(8,128)(2,1)S(1)}, u32[]{:S(2)}, u32[]{:S(2)}) %collective-permute-start.9) | collective-permute-done | bytes 147488 | tf_op jit(solution)/shard_map/ppermute | solution.py:313
  44.6 0.9 %merge_2.8 = (bf16[2,64,768]{2,1,0:T(8,128)(2,1)S(1)}, bf16[2,48,768]{2,1,0:T(8,128)(2,1)S(1)}) custom-call(f32[4,8,128]{2,1,0:T(8,128)S(1)} %get-tuple-element.33.refs_0_, bf16[4,256,768]{2,1,0:T(8,128)(2,1)S(1)} %get-tuple-element.34.refs_1_.refs_4_, bf16[2,64,768]{2,1,0:T(8,128)(2,1)S(1)} %get-tuple-element.47.refs_6_.refs_3_.refs_2_, ...), custom_call_target="tpu_custom_call" | custom-call | flops 1207959552 | tf_op jit(solution)/shard_map/merge_2/pallas_call | solution.py:242
  45.6 0.1 collective-permute-start.11
  45.7 0.7 %collective-permute-done.12.refs_5_ = bf16[2,48,640]{2,1,0:T(8,128)(2,1)S(1)} collective-permute-done((bf16[2,48,640]{2,1,0:T(8,128)(2,1)S(1)}, bf16[2,48,640]{2,1,0:T(8,128)(2,1)S(1)}, u32[]{:S(2)}, u32[]{:S(2)}) %collective-permute-start.12) | collective-permute-done | bytes 122912 | tf_op jit(solution)/shard_map/ppermute | solution.py:313
  46.4 0.9 %merge_2.9 = (bf16[2,64,768]{2,1,0:T(8,128)(2,1)S(1)}, bf16[2,48,768]{2,1,0:T(8,128)(2,1)S(1)}) custom-call(f32[4,8,128]{2,1,0:T(8,128)S(1)} %get-tuple-element.33.refs_0_, bf16[4,256,768]{2,1,0:T(8,128)(2,1)S(1)} %get-tuple-element.34.refs_1_.refs_4_, bf16[2,64,768]{2,1,0:T(8,128)(2,1)S(1)} %get-tuple-element.49.refs_4_.refs_3_.refs_2_, ...), custom_call_target="tpu_custom_call" | custom-call | flops 1207959552 | tf_op jit(solution)/shard_map/merge_2/pallas_call | solution.py:242
  47.3 2.3 %collective-permute-start.13 = (bf16[2,48,768]{2,1,0:T(8,128)(2,1)S(1)}, bf16[2,48,768]{2,1,0:T(8,128)(2,1)S(1)}, u32[]{:S(2)}, u32[]{:S(2)}) collective-permute-start(bf16[2,48,768]{2,1,0:T(8,128)(2,1)S(1)} %get-tuple-element.60), channel_id=1, source_target_pairs={{0,8},{1,9},{2,10},{3,11},{4,12},{5,13},{6,14},{7,15},{8,0},{9,1},... | collective-permute-start | bytes 442376 | tf_op jit(solution)/shard_map/ppermute | solution.py:313
  49.6 7.3 %collective-permute-done.11.refs_7_.refs_4_ = bf16[2,48,768]{2,1,0:T(8,128)(2,1)S(1)} collective-permute-done((bf16[2,48,768]{2,1,0:T(8,128)(2,1)S(1)}, bf16[2,48,768]{2,1,0:T(8,128)(2,1)S(1)}, u32[]{:S(2)}, u32[]{:S(2)}) %collective-permute-start.11) | collective-permute-done | bytes 147488 | tf_op jit(solution)/shard_map/ppermute | solution.py:313
  56.9 1.9 %merge_3.6.refs_6_ = bf16[2,64,1536]{2,1,0:T(8,128)(2,1)S(1)} custom-call(f32[4,8,128]{2,1,0:T(8,128)S(1)} %get-tuple-element.33.refs_0_, bf16[4,256,768]{2,1,0:T(8,128)(2,1)S(1)} %get-tuple-element.34.refs_1_.refs_4_, bf16[2,64,1024]{2,1,0:T(8,128)(2,1)S(1)} %get-tuple-element.48.refs_4_.refs_3_.refs_2_, ...), custom_call_target="tpu_custom_call" | custom-call | flops 603979776 | tf_op jit(solution)/shard_map/merge_3/pallas_call | solution.py:242
  58.8 0.0 slice-start
  58.8 0.8 %collective-permute-done.13.refs_5_ = bf16[2,48,768]{2,1,0:T(8,128)(2,1)S(1)} collective-permute-done((bf16[2,48,768]{2,1,0:T(8,128)(2,1)S(1)}, bf16[2,48,768]{2,1,0:T(8,128)(2,1)S(1)}, u32[]{:S(2)}, u32[]{:S(2)}) %collective-permute-start.13) | collective-permute-done | bytes 147488 | tf_op jit(solution)/shard_map/ppermute | solution.py:313
  59.7 1.0 %merge_3.7 = bf16[2,64,1024]{2,1,0:T(8,128)(2,1)S(1)} custom-call(f32[4,8,128]{2,1,0:T(8,128)S(1)} %get-tuple-element.33.refs_0_, bf16[4,256,768]{2,1,0:T(8,128)(2,1)S(1)} %get-tuple-element.34.refs_1_.refs_4_, bf16[2,64,768]{2,1,0:T(8,128)(2,1)S(1)} %get-tuple-element.55.refs_6_.refs_4_.refs_2_, bf16[2,64,768]{2,1,0:T(8,128)(2,1)S(1)} %get-tuple-element.59.refs_8_.refs_3_, ...), custom_call_target="tpu_custom_call" | custom-call | flops 352321536 | tf_op jit(solution)/shard_map/merge_3/pallas_call | solution.py:242
  60.7 1.1 %pad_maximum_fusion = bf16[2,64,4096]{2,1,0:T(8,128)(2,1)} fusion(bf16[2,64,896]{2,1,0:T(8,128)(2,1)S(1)} %slice.9, bf16[2,64,1536]{2,1,0:T(8,128)(2,1)S(1)} %merge_3.6.refs_6_, bf16[2,64,1024]{2,1,0:T(8,128)(2,1)S(1)} %merge_3.5.refs_6_, bf16[2,64,640]{2,1,0:T(8,128)(2,1)S(1)} %slice-done), kind=kLoop, calls=%fused_computation | loop fusion | flops 4194304 | bytes 2097152 | tf_op jit(solution)/shard_map/concatenate | solution.py:339
  (8 shorter events, 0.0 us)
Async XLA Ops:
  0.0 3.0 %collective-permute-start = (bf16[2,64,4096]{2,1,0:T(8,128)(2,1)}, bf16[2,64,4096]{2,1,0:T(8,128)(2,1)S(1)}, u32[]{:S(2)}, u32[]{:S(2)}) collective-permute-start(bf16[2,64,4096]{2,1,0:T(8,128)(2,1)} %refs_2_.5), channel_id=1, source_target_pairs={{0,1},{1,0},{2,3},{3,2},{4,5},{5,4},{6,7},{7,6},{8,9},{9,8},{10,11... | collective-permute-start | bytes 3145736 | tf_op jit(solution)/shard_map/ppermute | solution.py:313
  2.0 1.2 %copy-start.1 = (bf16[2,64,4096]{2,1,0:T(8,128)(2,1)S(1)}, bf16[2,64,4096]{2,1,0:T(8,128)(2,1)}, u32[]{:S(2)}) copy-start(bf16[2,64,4096]{2,1,0:T(8,128)(2,1)} %refs_2_.5) | copy-start | bytes 3145732
  4.4 8.5 %collective-permute-start.1 = (bf16[2,48,1024]{2,1,0:T(8,128)(2,1)S(1)}, bf16[2,48,1024]{2,1,0:T(8,128)(2,1)S(1)}, u32[]{:S(2)}, u32[]{:S(2)}) collective-permute-start(bf16[2,48,1024]{2,1,0:T(8,128)(2,1)S(1)} %get-tuple-element.36), channel_id=1, source_target_pairs={{0,2},{1,3},{2,0},{3,1},{4,6},{5,7},{6,4},{7,5},{8,10},{9,11},{10,... | collective-permute-start | bytes 589832 | tf_op jit(solution)/shard_map/ppermute | solution.py:313
  8.2 8.8 %collective-permute-start.3 = (bf16[2,48,1024]{2,1,0:T(8,128)(2,1)S(1)}, bf16[2,48,1024]{2,1,0:T(8,128)(2,1)S(1)}, u32[]{:S(2)}, u32[]{:S(2)}) collective-permute-start(bf16[2,48,1024]{2,1,0:T(8,128)(2,1)S(1)} %get-tuple-element.41), channel_id=1, source_target_pairs={{0,2},{1,3},{2,0},{3,1},{4,6},{5,7},{6,4},{7,5},{8,10},{9,11},{10,... | collective-permute-start | bytes 589832 | tf_op jit(solution)/shard_map/ppermute | solution.py:313
  10.8 14.4 %collective-permute-start.5 = (bf16[2,48,2048]{2,1,0:T(8,128)(2,1)S(1)}, bf16[2,48,2048]{2,1,0:T(8,128)(2,1)S(1)}, u32[]{:S(2)}, u32[]{:S(2)}) collective-permute-start(bf16[2,48,2048]{2,1,0:T(8,128)(2,1)S(1)} %get-tuple-element.45), channel_id=1, source_target_pairs={{0,2},{1,3},{2,0},{3,1},{4,6},{5,7},{6,4},{7,5},{8,10},{9,11},{10,... | collective-permute-start | bytes 1179656 | tf_op jit(solution)/shard_map/ppermute | solution.py:313
  14.0 6.2 %collective-permute-start.2 = (bf16[2,48,896]{2,1,0:T(8,128)(2,1)S(1)}, bf16[2,48,896]{2,1,0:T(8,128)(2,1)S(1)}, u32[]{:S(2)}, u32[]{:S(2)}) collective-permute-start(bf16[2,48,896]{2,1,0:T(8,128)(2,1)S(1)} %get-tuple-element.40), channel_id=1, source_target_pairs={{0,4},{1,5},{2,6},{3,7},{4,0},{5,1},{6,2},{7,3},{8,12},{9,13},{10,... | collective-permute-start | bytes 516104 | tf_op jit(solution)/shard_map/ppermute | solution.py:313
  18.2 9.8 %collective-permute-start.6 = (bf16[2,48,1024]{2,1,0:T(8,128)(2,1)S(1)}, bf16[2,48,1024]{2,1,0:T(8,128)(2,1)S(1)}, u32[]{:S(2)}, u32[]{:S(2)}) collective-permute-start(bf16[2,48,1024]{2,1,0:T(8,128)(2,1)S(1)} %get-tuple-element.46), channel_id=1, source_target_pairs={{0,4},{1,5},{2,6},{3,7},{4,0},{5,1},{6,2},{7,3},{8,12},{9,13},{10,... | collective-permute-start | bytes 589832 | tf_op jit(solution)/shard_map/ppermute | solution.py:313
  21.2 12.1 %collective-permute-start.4 = (bf16[2,48,768]{2,1,0:T(8,128)(2,1)S(1)}, bf16[2,48,768]{2,1,0:T(8,128)(2,1)S(1)}, u32[]{:S(2)}, u32[]{:S(2)}) collective-permute-start(bf16[2,48,768]{2,1,0:T(8,128)(2,1)S(1)} %get-tuple-element.44), channel_id=1, source_target_pairs={{0,8},{1,9},{2,10},{3,11},{4,12},{5,13},{6,14},{7,15},{8,0},{9,1},... | collective-permute-start | bytes 442376 | tf_op jit(solution)/shard_map/ppermute | solution.py:313
  26.1 10.7 %collective-permute-start.8 = (bf16[2,48,768]{2,1,0:T(8,128)(2,1)S(1)}, bf16[2,48,768]{2,1,0:T(8,128)(2,1)S(1)}, u32[]{:S(2)}, u32[]{:S(2)}) collective-permute-start(bf16[2,48,768]{2,1,0:T(8,128)(2,1)S(1)} %get-tuple-element.51), channel_id=1, source_target_pairs={{0,4},{1,5},{2,6},{3,7},{4,0},{5,1},{6,2},{7,3},{8,12},{9,13},{10,... | collective-permute-start | bytes 442376 | tf_op jit(solution)/shard_map/ppermute | solution.py:313
  29.1 12.0 %collective-permute-start.7 = (bf16[2,48,1024]{2,1,0:T(8,128)(2,1)S(1)}, bf16[2,48,1024]{2,1,0:T(8,128)(2,1)S(1)}, u32[]{:S(2)}, u32[]{:S(2)}) collective-permute-start(bf16[2,48,1024]{2,1,0:T(8,128)(2,1)S(1)} %get-tuple-element.50), channel_id=1, source_target_pairs={{0,8},{1,9},{2,10},{3,11},{4,12},{5,13},{6,14},{7,15},{8,0},{9,1},... | collective-permute-start | bytes 589832 | tf_op jit(solution)/shard_map/ppermute | solution.py:313
  32.7 11.9 %collective-permute-start.9 = (bf16[2,48,768]{2,1,0:T(8,128)(2,1)S(1)}, bf16[2,48,768]{2,1,0:T(8,128)(2,1)S(1)}, u32[]{:S(2)}, u32[]{:S(2)}) collective-permute-start(bf16[2,48,768]{2,1,0:T(8,128)(2,1)S(1)} %get-tuple-element.54), channel_id=1, source_target_pairs={{0,4},{1,5},{2,6},{3,7},{4,0},{5,1},{6,2},{7,3},{8,12},{9,13},{10,... | collective-permute-start | bytes 442376 | tf_op jit(solution)/shard_map/ppermute | solution.py:313
  34.2 15.4 %copy-start = (bf16[2,64,768]{2,1,0:T(8,128)(2,1)}, bf16[2,64,768]{2,1,0:T(8,128)(2,1)S(1)}, u32[]{:S(2)}) copy-start(bf16[2,64,768]{2,1,0:T(8,128)(2,1)S(1)} %merge_3.4.refs_4_) | copy-start | bytes 589828
  35.1 11.2 %collective-permute-start.12 = (bf16[2,48,640]{2,1,0:T(8,128)(2,1)S(1)}, bf16[2,48,640]{2,1,0:T(8,128)(2,1)S(1)}, u32[]{:S(2)}, u32[]{:S(2)}) collective-permute-start(bf16[2,48,640]{2,1,0:T(8,128)(2,1)S(1)} %get-tuple-element.58), channel_id=1, source_target_pairs={{0,4},{1,5},{2,6},{3,7},{4,0},{5,1},{6,2},{7,3},{8,12},{9,13},{10,... | collective-permute-start | bytes 368648 | tf_op jit(solution)/shard_map/ppermute | solution.py:313
  37.7 11.8 %collective-permute-start.10 = (bf16[2,48,768]{2,1,0:T(8,128)(2,1)S(1)}, bf16[2,48,768]{2,1,0:T(8,128)(2,1)S(1)}, u32[]{:S(2)}, u32[]{:S(2)}) collective-permute-start(bf16[2,48,768]{2,1,0:T(8,128)(2,1)S(1)} %get-tuple-element.56), channel_id=1, source_target_pairs={{0,8},{1,9},{2,10},{3,11},{4,12},{5,13},{6,14},{7,15},{8,0},{9,1},... | collective-permute-start | bytes 442376 | tf_op jit(solution)/shard_map/ppermute | solution.py:313
  45.6 11.3 %collective-permute-start.11 = (bf16[2,48,768]{2,1,0:T(8,128)(2,1)S(1)}, bf16[2,48,768]{2,1,0:T(8,128)(2,1)S(1)}, u32[]{:S(2)}, u32[]{:S(2)}) collective-permute-start(bf16[2,48,768]{2,1,0:T(8,128)(2,1)S(1)} %get-tuple-element.57), channel_id=1, source_target_pairs={{0,8},{1,9},{2,10},{3,11},{4,12},{5,13},{6,14},{7,15},{8,0},{9,1},... | collective-permute-start | bytes 442376 | tf_op jit(solution)/shard_map/ppermute | solution.py:313
  47.3 12.3 %collective-permute-start.13 = (bf16[2,48,768]{2,1,0:T(8,128)(2,1)S(1)}, bf16[2,48,768]{2,1,0:T(8,128)(2,1)S(1)}, u32[]{:S(2)}, u32[]{:S(2)}) collective-permute-start(bf16[2,48,768]{2,1,0:T(8,128)(2,1)S(1)} %get-tuple-element.60), channel_id=1, source_target_pairs={{0,8},{1,9},{2,10},{3,11},{4,12},{5,13},{6,14},{7,15},{8,0},{9,1},... | collective-permute-start | bytes 442376 | tf_op jit(solution)/shard_map/ppermute | solution.py:313
  58.8 1.9 %slice-start = ((bf16[2,64,768]{2,1,0:T(8,128)(2,1)}), bf16[2,64,640]{2,1,0:T(8,128)(2,1)S(1)}, s32[]{:S(2)}) async-start(bf16[2,64,768]{2,1,0:T(8,128)(2,1)} %copy-done), calls=%async_computation | async-start | bytes 327680 | tf_op jit(solution)/shard_map/slice | solution.py:338

commit v10 on v9

--- a/solution.py
+++ b/solution.py
@@ -272,11 +272,11 @@
     (8, 16),
     (7, 15, 21, 27),
     (6, 14, 20, 26),
-    (5, 13, 25),
+    (5, 13, 19, 25),
 )
 ORDER = (
     (0, 0), (0, 1), (0, 2), (1, 0), (1, 1), (2, 0), (1, 2), (2, 1), (1, 3), (3, 0), (1, 4),
-    (2, 2), (3, 1), (2, 3), (2, 4), (3, 2), (3, 3),
+    (2, 2), (3, 1), (2, 3), (2, 4), (3, 2), (3, 3), (3, 4),
 )
 
 

time: 62 us -> 61.6 us (level)
  other arithmetic: 2.62 us -> 1.54 us
  local copies, waits for them, and re-layouts: 0.3 us -> 1.05 us
    concatenate x1 -> x0, other arithmetic: 1.08 us -> none  [on_device(): return jnp.concatenate(made, axis=2)]
    concatenate x0 -> x1, local copies, waits for them, and re-layouts: none -> 0.71 us  [on_device(): return jnp.concatenate(made, axis=2)]
    pallas_call x17 -> x18, Pallas kernels: 19.7 us -> 19.6 us  [merge(): pl.pallas_call(functools.partial(merge_kernel, level, plan, start, stop,...]
  transfers between devices with their start and end apart: 14 -> 14, of which waited for: 8 -> 8; matrix products, arithmetic and copies ran while one was open for 2% -> 3% of each run, Pallas kernels for 30% -> 30%
where the time goes in v10:
time: 61.6 us; the launch traced here: 61.4 us
  starting transfers between devices  21.5 us (35%)
  Pallas kernels  20.5 us (33%)
  waiting for transfers between devices  16.7 us (27%)
  other arithmetic  1.54 us (2%)
  local copies, waits for them, and re-layouts  1.05 us (2%)
    ppermute x14, starting transfers between devices, from_partner(): return lax.ppermute(value, 'pulse', pairs)  21.5 us
    pallas_call x18, Pallas kernels, merge(): pl.pallas_call(functools.partial(merge_kernel, level, plan, start, stop,...  19.6 us
    ppermute x14, waiting for transfers between devices, from_partner(): return lax.ppermute(value, 'pulse', pairs)  16.7 us
    add x2, other arithmetic, stacked(): total = total + lax.pad(piece, zero, ((top, below, 0), (left, right, 0)))  1.54 us
  transfers between devices with their start and end apart: 14, of which 8 were waited for; matrix products, arithmetic and copies ran while one was open for 3% of the time, Pallas kernels for 30%

profile of v10, /device:TPU:0, one launch (start us, length us, event | category | flops | bytes accessed | tf_op | source)
XLA Modules:
  0.0 61.4 jit_solution(17300298601953555859)
XLA Ops:
  0.0 0.5 collective-permute-start
  0.5 0.7 %pad_add_fusion.real_ref = f32[14,128]{1,0:T(8,128)S(1)} fusion(f32[4,16]{1,0:T(4,128)} %bitcast.3, f32[8,128]{1,0:T(8,128)} %bitcast.2, bf16[2,32]{1,0:T(2,128)(2,1)} %param.8), kind=kLoop, calls=%fused_computation.5 | loop fusion | flops 5376 | bytes 11648 | tf_op jit(solution)/shard_map/add | solution.py:91
  1.2 0.8 %pad_add_fusion.1.whole_ref = s32[12,128]{1,0:T(8,128)S(1)} fusion(s32[4,64]{1,0:T(4,128)} %param.11, s32[4,16]{1,0:T(4,128)} %param.12, s32[4,16]{1,0:T(4,128)} %param.13), kind=kLoop, calls=%fused_computation.6 | loop fusion | flops 4608 | bytes 7680 | tf_op jit(solution)/shard_map/add | solution.py:91
  2.0 0.9 %mixing.1 = (bf16[4,256,768]{2,1,0:T(8,128)(2,1)S(1)}, f32[4,8,128]{2,1,0:T(8,128)S(1)}) custom-call(s32[12,128]{1,0:T(8,128)S(1)} %pad_add_fusion.1.whole_ref, f32[14,128]{1,0:T(8,128)S(1)} %pad_add_fusion.real_ref), custom_call_target="tpu_custom_call" | custom-call | flops 2000000000 | bytes 1572864 | tf_op jit(solution)/shard_map/mixing/pallas_call | solution.py:121
  2.9 0.1 collective-permute-done.refs_3_
  3.0 0.3 copy-done
  3.2 1.1 %merge_0.3 = (bf16[2,64,1024]{2,1,0:T(8,128)(2,1)S(1)}, bf16[2,48,1024]{2,1,0:T(8,128)(2,1)S(1)}) custom-call(f32[4,8,128]{2,1,0:T(8,128)S(1)} %get-tuple-element.33.refs_0_, bf16[4,256,768]{2,1,0:T(8,128)(2,1)S(1)} %get-tuple-element.34.refs_1_.refs_4_, bf16[2,64,4096]{2,1,0:T(8,128)(2,1)S(1)} %copy-done, ...), custom_call_target="tpu_custom_call" | custom-call | flops 1610612736 | tf_op jit(solution)/shard_map/merge_0/pallas_call | solution.py:242
  4.4 2.7 %collective-permute-start.1 = (bf16[2,48,1024]{2,1,0:T(8,128)(2,1)S(1)}, bf16[2,48,1024]{2,1,0:T(8,128)(2,1)S(1)}, u32[]{:S(2)}, u32[]{:S(2)}) collective-permute-start(bf16[2,48,1024]{2,1,0:T(8,128)(2,1)S(1)} %get-tuple-element.36), channel_id=1, source_target_pairs={{0,2},{1,3},{2,0},{3,1},{4,6},{5,7},{6,4},{7,5},{8,10},{9,11},{10,... | collective-permute-start | bytes 589832 | tf_op jit(solution)/shard_map/ppermute | solution.py:313
  7.1 1.1 %merge_0.4 = (bf16[2,64,1024]{2,1,0:T(8,128)(2,1)S(1)}, bf16[2,48,1024]{2,1,0:T(8,128)(2,1)S(1)}) custom-call(f32[4,8,128]{2,1,0:T(8,128)S(1)} %get-tuple-element.33.refs_0_, bf16[4,256,768]{2,1,0:T(8,128)(2,1)S(1)} %get-tuple-element.34.refs_1_.refs_4_, bf16[2,64,4096]{2,1,0:T(8,128)(2,1)S(1)} %copy-done, ...), custom_call_target="tpu_custom_call" | custom-call | flops 1610612736 | tf_op jit(solution)/shard_map/merge_0/pallas_call | solution.py:242
  8.2 0.1 collective-permute-start.3
  8.3 2.5 %merge_0.5 = (bf16[2,64,2048]{2,1,0:T(8,128)(2,1)S(1)}, bf16[2,48,2048]{2,1,0:T(8,128)(2,1)S(1)}) custom-call(f32[4,8,128]{2,1,0:T(8,128)S(1)} %get-tuple-element.33.refs_0_, bf16[4,256,768]{2,1,0:T(8,128)(2,1)S(1)} %get-tuple-element.34.refs_1_.refs_4_, bf16[2,64,4096]{2,1,0:T(8,128)(2,1)S(1)} %copy-done, ...), custom_call_target="tpu_custom_call" | custom-call | flops 3221225472 | tf_op jit(solution)/shard_map/merge_0/pallas_call | solution.py:242
  10.8 2.1 %collective-permute-start.5 = (bf16[2,48,2048]{2,1,0:T(8,128)(2,1)S(1)}, bf16[2,48,2048]{2,1,0:T(8,128)(2,1)S(1)}, u32[]{:S(2)}, u32[]{:S(2)}) collective-permute-start(bf16[2,48,2048]{2,1,0:T(8,128)(2,1)S(1)} %get-tuple-element.45), channel_id=1, source_target_pairs={{0,2},{1,3},{2,0},{3,1},{4,6},{5,7},{6,4},{7,5},{8,10},{9,11},{10,... | collective-permute-start | bytes 1179656 | tf_op jit(solution)/shard_map/ppermute | solution.py:313
  12.9 0.0 collective-permute-done.1.refs_3_.refs_4_
  12.9 1.1 %merge_1.5 = (bf16[2,64,1024]{2,1,0:T(8,128)(2,1)S(1)}, bf16[2,48,896]{2,1,0:T(8,128)(2,1)S(1)}) custom-call(f32[4,8,128]{2,1,0:T(8,128)S(1)} %get-tuple-element.33.refs_0_, bf16[4,256,768]{2,1,0:T(8,128)(2,1)S(1)} %get-tuple-element.34.refs_1_.refs_4_, bf16[2,64,1024]{2,1,0:T(8,128)(2,1)S(1)} %get-tuple-element.35.refs_4_.refs_2_, ...), custom_call_target="tpu_custom_call" | custom-call | flops 1409286144 | tf_op jit(solution)/shard_map/merge_1/pallas_call | solution.py:242
  14.0 2.0 %collective-permute-start.2 = (bf16[2,48,896]{2,1,0:T(8,128)(2,1)S(1)}, bf16[2,48,896]{2,1,0:T(8,128)(2,1)S(1)}, u32[]{:S(2)}, u32[]{:S(2)}) collective-permute-start(bf16[2,48,896]{2,1,0:T(8,128)(2,1)S(1)} %get-tuple-element.40), channel_id=1, source_target_pairs={{0,4},{1,5},{2,6},{3,7},{4,0},{5,1},{6,2},{7,3},{8,12},{9,13},{10,... | collective-permute-start | bytes 516104 | tf_op jit(solution)/shard_map/ppermute | solution.py:313
  16.0 1.0 %collective-permute-done.3.refs_5_.refs_4_ = bf16[2,48,1024]{2,1,0:T(8,128)(2,1)S(1)} collective-permute-done((bf16[2,48,1024]{2,1,0:T(8,128)(2,1)S(1)}, bf16[2,48,1024]{2,1,0:T(8,128)(2,1)S(1)}, u32[]{:S(2)}, u32[]{:S(2)}) %collective-permute-start.3) | collective-permute-done | bytes 196640 | tf_op jit(solution)/shard_map/ppermute | solution.py:313
  17.0 1.1 %merge_1.6 = (bf16[2,64,1024]{2,1,0:T(8,128)(2,1)S(1)}, bf16[2,48,1024]{2,1,0:T(8,128)(2,1)S(1)}) custom-call(f32[4,8,128]{2,1,0:T(8,128)S(1)} %get-tuple-element.33.refs_0_, bf16[4,256,768]{2,1,0:T(8,128)(2,1)S(1)} %get-tuple-element.34.refs_1_.refs_4_, bf16[2,64,1024]{2,1,0:T(8,128)(2,1)S(1)} %get-tuple-element.35.refs_4_.refs_2_, ...), custom_call_target="tpu_custom_call" | custom-call | flops 1610612736 | tf_op jit(solution)/shard_map/merge_1/pallas_call | solution.py:242
  18.2 2.1 %collective-permute-start.6 = (bf16[2,48,1024]{2,1,0:T(8,128)(2,1)S(1)}, bf16[2,48,1024]{2,1,0:T(8,128)(2,1)S(1)}, u32[]{:S(2)}, u32[]{:S(2)}) collective-permute-start(bf16[2,48,1024]{2,1,0:T(8,128)(2,1)S(1)} %get-tuple-element.46), channel_id=1, source_target_pairs={{0,4},{1,5},{2,6},{3,7},{4,0},{5,1},{6,2},{7,3},{8,12},{9,13},{10,... | collective-permute-start | bytes 589832 | tf_op jit(solution)/shard_map/ppermute | solution.py:313
  20.2 0.0 collective-permute-done.2.refs_3_.refs_4_
  20.2 0.9 %merge_2.5 = (bf16[2,64,768]{2,1,0:T(8,128)(2,1)S(1)}, bf16[2,48,768]{2,1,0:T(8,128)(2,1)S(1)}) custom-call(f32[4,8,128]{2,1,0:T(8,128)S(1)} %get-tuple-element.33.refs_0_, bf16[4,256,768]{2,1,0:T(8,128)(2,1)S(1)} %get-tuple-element.34.refs_1_.refs_4_, bf16[2,64,1024]{2,1,0:T(8,128)(2,1)S(1)} %get-tuple-element.39.refs_6_.refs_2_, ...), custom_call_target="tpu_custom_call" | custom-call | flops 1207959552 | tf_op jit(solution)/shard_map/merge_2/pallas_call | solution.py:242
  21.2 2.7 %collective-permute-start.4 = (bf16[2,48,768]{2,1,0:T(8,128)(2,1)S(1)}, bf16[2,48,768]{2,1,0:T(8,128)(2,1)S(1)}, u32[]{:S(2)}, u32[]{:S(2)}) collective-permute-start(bf16[2,48,768]{2,1,0:T(8,128)(2,1)S(1)} %get-tuple-element.44), channel_id=1, source_target_pairs={{0,8},{1,9},{2,10},{3,11},{4,12},{5,13},{6,14},{7,15},{8,0},{9,1},... | collective-permute-start | bytes 442376 | tf_op jit(solution)/shard_map/ppermute | solution.py:313
  23.8 1.3 %collective-permute-done.5.refs_5_.refs_3_ = bf16[2,48,2048]{2,1,0:T(8,128)(2,1)S(1)} collective-permute-done((bf16[2,48,2048]{2,1,0:T(8,128)(2,1)S(1)}, bf16[2,48,2048]{2,1,0:T(8,128)(2,1)S(1)}, u32[]{:S(2)}, u32[]{:S(2)}) %collective-permute-start.5) | collective-permute-done | bytes 393248 | tf_op jit(solution)/shard_map/ppermute | solution.py:313
  25.2 0.9 %merge_1.7 = (bf16[2,64,768]{2,1,0:T(8,128)(2,1)S(1)}, bf16[2,48,768]{2,1,0:T(8,128)(2,1)S(1)}) custom-call(f32[4,8,128]{2,1,0:T(8,128)S(1)} %get-tuple-element.33.refs_0_, bf16[4,256,768]{2,1,0:T(8,128)(2,1)S(1)} %get-tuple-element.34.refs_1_.refs_4_, bf16[2,64,1024]{2,1,0:T(8,128)(2,1)S(1)} %get-tuple-element.37.refs_4_.refs_3_.refs_2_, ...), custom_call_target="tpu_custom_call" | custom-call | flops 1207959552 | tf_op jit(solution)/shard_map/merge_1/pallas_call | solution.py:242
  26.1 1.9 %collective-permute-start.8 = (bf16[2,48,768]{2,1,0:T(8,128)(2,1)S(1)}, bf16[2,48,768]{2,1,0:T(8,128)(2,1)S(1)}, u32[]{:S(2)}, u32[]{:S(2)}) collective-permute-start(bf16[2,48,768]{2,1,0:T(8,128)(2,1)S(1)} %get-tuple-element.51), channel_id=1, source_target_pairs={{0,4},{1,5},{2,6},{3,7},{4,0},{5,1},{6,2},{7,3},{8,12},{9,13},{10,... | collective-permute-start | bytes 442376 | tf_op jit(solution)/shard_map/ppermute | solution.py:313
  28.0 1.1 %merge_2.6 = (bf16[2,64,1024]{2,1,0:T(8,128)(2,1)S(1)}, bf16[2,48,1024]{2,1,0:T(8,128)(2,1)S(1)}) custom-call(f32[4,8,128]{2,1,0:T(8,128)S(1)} %get-tuple-element.33.refs_0_, bf16[4,256,768]{2,1,0:T(8,128)(2,1)S(1)} %get-tuple-element.34.refs_1_.refs_4_, bf16[2,64,1024]{2,1,0:T(8,128)(2,1)S(1)} %get-tuple-element.39.refs_6_.refs_2_, ...), custom_call_target="tpu_custom_call" | custom-call | flops 1610612736 | tf_op jit(solution)/shard_map/merge_2/pallas_call | solution.py:242
  29.1 2.6 %collective-permute-start.7 = (bf16[2,48,1024]{2,1,0:T(8,128)(2,1)S(1)}, bf16[2,48,1024]{2,1,0:T(8,128)(2,1)S(1)}, u32[]{:S(2)}, u32[]{:S(2)}) collective-permute-start(bf16[2,48,1024]{2,1,0:T(8,128)(2,1)S(1)} %get-tuple-element.50), channel_id=1, source_target_pairs={{0,8},{1,9},{2,10},{3,11},{4,12},{5,13},{6,14},{7,15},{8,0},{9,1},... | collective-permute-start | bytes 589832 | tf_op jit(solution)/shard_map/ppermute | solution.py:313
  31.8 0.9 %merge_1.8 = (bf16[2,64,768]{2,1,0:T(8,128)(2,1)S(1)}, bf16[2,48,768]{2,1,0:T(8,128)(2,1)S(1)}) custom-call(f32[4,8,128]{2,1,0:T(8,128)S(1)} %get-tuple-element.33.refs_0_, bf16[4,256,768]{2,1,0:T(8,128)(2,1)S(1)} %get-tuple-element.34.refs_1_.refs_4_, bf16[2,64,2048]{2,1,0:T(8,128)(2,1)S(1)} %get-tuple-element.38.refs_4_.refs_3_.refs_2_, ...), custom_call_target="tpu_custom_call" | custom-call | flops 1207959552 | tf_op jit(solution)/shard_map/merge_1/pallas_call | solution.py:242
  32.7 0.5 collective-permute-start.10
  33.3 0.9 %merge_3.5.refs_4_ = bf16[2,64,768]{2,1,0:T(8,128)(2,1)S(1)} custom-call(f32[4,8,128]{2,1,0:T(8,128)S(1)} %get-tuple-element.33.refs_0_, bf16[4,256,768]{2,1,0:T(8,128)(2,1)S(1)} %get-tuple-element.34.refs_1_.refs_4_, bf16[2,64,768]{2,1,0:T(8,128)(2,1)S(1)} %get-tuple-element.43.refs_6_.refs_2_, ...), custom_call_target="tpu_custom_call" | custom-call | flops 251658240 | tf_op jit(solution)/shard_map/merge_3/pallas_call | solution.py:242
  34.2 0.9 %merge_1.9 = (bf16[2,64,768]{2,1,0:T(8,128)(2,1)S(1)}, bf16[2,48,640]{2,1,0:T(8,128)(2,1)S(1)}) custom-call(f32[4,8,128]{2,1,0:T(8,128)S(1)} %get-tuple-element.33.refs_0_, bf16[4,256,768]{2,1,0:T(8,128)(2,1)S(1)} %get-tuple-element.34.refs_1_.refs_4_, bf16[2,64,2048]{2,1,0:T(8,128)(2,1)S(1)} %get-tuple-element.38.refs_4_.refs_3_.refs_2_, ...), custom_call_target="tpu_custom_call" | custom-call | flops 1006632960 | tf_op jit(solution)/shard_map/merge_1/pallas_call | solution.py:242
  35.2 1.6 %collective-permute-start.11 = (bf16[2,48,640]{2,1,0:T(8,128)(2,1)S(1)}, bf16[2,48,640]{2,1,0:T(8,128)(2,1)S(1)}, u32[]{:S(2)}, u32[]{:S(2)}) collective-permute-start(bf16[2,48,640]{2,1,0:T(8,128)(2,1)S(1)} %get-tuple-element.56), channel_id=1, source_target_pairs={{0,4},{1,5},{2,6},{3,7},{4,0},{5,1},{6,2},{7,3},{8,12},{9,13},{10,... | collective-permute-start | bytes 368648 | tf_op jit(solution)/shard_map/ppermute | solution.py:313
  36.8 0.9 %merge_2.7 = (bf16[2,64,768]{2,1,0:T(8,128)(2,1)S(1)}, bf16[2,48,768]{2,1,0:T(8,128)(2,1)S(1)}) custom-call(f32[4,8,128]{2,1,0:T(8,128)S(1)} %get-tuple-element.33.refs_0_, bf16[4,256,768]{2,1,0:T(8,128)(2,1)S(1)} %get-tuple-element.34.refs_1_.refs_4_, bf16[2,64,1024]{2,1,0:T(8,128)(2,1)S(1)} %get-tuple-element.42.refs_4_.refs_3_.refs_2_, ...), custom_call_target="tpu_custom_call" | custom-call | flops 1207959552 | tf_op jit(solution)/shard_map/merge_2/pallas_call | solution.py:242
  37.7 0.4 collective-permute-start.9
  38.2 3.0 %collective-permute-done.7.refs_5_.refs_4_ = bf16[2,48,1024]{2,1,0:T(8,128)(2,1)S(1)} collective-permute-done((bf16[2,48,1024]{2,1,0:T(8,128)(2,1)S(1)}, bf16[2,48,1024]{2,1,0:T(8,128)(2,1)S(1)}, u32[]{:S(2)}, u32[]{:S(2)}) %collective-permute-start.7) | collective-permute-done | bytes 196640 | tf_op jit(solution)/shard_map/ppermute | solution.py:313
  41.2 1.1 %merge_3.6.refs_6_ = bf16[2,64,1024]{2,1,0:T(8,128)(2,1)S(1)} custom-call(f32[4,8,128]{2,1,0:T(8,128)S(1)} %get-tuple-element.33.refs_0_, bf16[4,256,768]{2,1,0:T(8,128)(2,1)S(1)} %get-tuple-element.34.refs_1_.refs_4_, bf16[2,64,768]{2,1,0:T(8,128)(2,1)S(1)} %get-tuple-element.43.refs_6_.refs_2_, ...), custom_call_target="tpu_custom_call" | custom-call | flops 402653184 | tf_op jit(solution)/shard_map/merge_3/pallas_call | solution.py:242
  42.2 2.4 %collective-permute-done.10.refs_5_.refs_4_ = bf16[2,48,768]{2,1,0:T(8,128)(2,1)S(1)} collective-permute-done((bf16[2,48,768]{2,1,0:T(8,128)(2,1)S(1)}, bf16[2,48,768]{2,1,0:T(8,128)(2,1)S(1)}, u32[]{:S(2)}, u32[]{:S(2)}) %collective-permute-start.10) | collective-permute-done | bytes 147488 | tf_op jit(solution)/shard_map/ppermute | solution.py:313
  44.6 0.9 %merge_2.8 = (bf16[2,64,768]{2,1,0:T(8,128)(2,1)S(1)}, bf16[2,48,768]{2,1,0:T(8,128)(2,1)S(1)}) custom-call(f32[4,8,128]{2,1,0:T(8,128)S(1)} %get-tuple-element.33.refs_0_, bf16[4,256,768]{2,1,0:T(8,128)(2,1)S(1)} %get-tuple-element.34.refs_1_.refs_4_, bf16[2,64,768]{2,1,0:T(8,128)(2,1)S(1)} %get-tuple-element.47.refs_6_.refs_3_.refs_2_, ...), custom_call_target="tpu_custom_call" | custom-call | flops 1207959552 | tf_op jit(solution)/shard_map/merge_2/pallas_call | solution.py:242
  45.6 0.1 collective-permute-start.12
  45.7 0.7 %collective-permute-done.11.refs_5_ = bf16[2,48,640]{2,1,0:T(8,128)(2,1)S(1)} collective-permute-done((bf16[2,48,640]{2,1,0:T(8,128)(2,1)S(1)}, bf16[2,48,640]{2,1,0:T(8,128)(2,1)S(1)}, u32[]{:S(2)}, u32[]{:S(2)}) %collective-permute-start.11) | collective-permute-done | bytes 122912 | tf_op jit(solution)/shard_map/ppermute | solution.py:313
  46.4 0.9 %merge_2.9 = (bf16[2,64,768]{2,1,0:T(8,128)(2,1)S(1)}, bf16[2,48,768]{2,1,0:T(8,128)(2,1)S(1)}) custom-call(f32[4,8,128]{2,1,0:T(8,128)S(1)} %get-tuple-element.33.refs_0_, bf16[4,256,768]{2,1,0:T(8,128)(2,1)S(1)} %get-tuple-element.34.refs_1_.refs_4_, bf16[2,64,768]{2,1,0:T(8,128)(2,1)S(1)} %get-tuple-element.49.refs_4_.refs_3_.refs_2_, ...), custom_call_target="tpu_custom_call" | custom-call | flops 1207959552 | tf_op jit(solution)/shard_map/merge_2/pallas_call | solution.py:242
  47.3 2.3 %collective-permute-start.13 = (bf16[2,48,768]{2,1,0:T(8,128)(2,1)S(1)}, bf16[2,48,768]{2,1,0:T(8,128)(2,1)S(1)}, u32[]{:S(2)}, u32[]{:S(2)}) collective-permute-start(bf16[2,48,768]{2,1,0:T(8,128)(2,1)S(1)} %get-tuple-element.60), channel_id=1, source_target_pairs={{0,8},{1,9},{2,10},{3,11},{4,12},{5,13},{6,14},{7,15},{8,0},{9,1},... | collective-permute-start | bytes 442376 | tf_op jit(solution)/shard_map/ppermute | solution.py:313
  49.6 0.9 %merge_3.7.refs_6_ = bf16[2,64,768]{2,1,0:T(8,128)(2,1)S(1)} custom-call(f32[4,8,128]{2,1,0:T(8,128)S(1)} %get-tuple-element.33.refs_0_, bf16[4,256,768]{2,1,0:T(8,128)(2,1)S(1)} %get-tuple-element.34.refs_1_.refs_4_, bf16[2,64,1024]{2,1,0:T(8,128)(2,1)S(1)} %get-tuple-element.48.refs_4_.refs_3_.refs_2_, ...), custom_call_target="tpu_custom_call" | custom-call | flops 301989888 | tf_op jit(solution)/shard_map/merge_3/pallas_call | solution.py:242
  50.5 6.2 %collective-permute-done.12.refs_5_.refs_4_ = bf16[2,48,768]{2,1,0:T(8,128)(2,1)S(1)} collective-permute-done((bf16[2,48,768]{2,1,0:T(8,128)(2,1)S(1)}, bf16[2,48,768]{2,1,0:T(8,128)(2,1)S(1)}, u32[]{:S(2)}, u32[]{:S(2)}) %collective-permute-start.12) | collective-permute-done | bytes 147488 | tf_op jit(solution)/shard_map/ppermute | solution.py:313
  56.8 0.9 %merge_3.8.refs_6_ = bf16[2,64,768]{2,1,0:T(8,128)(2,1)S(1)} custom-call(f32[4,8,128]{2,1,0:T(8,128)S(1)} %get-tuple-element.33.refs_0_, bf16[4,256,768]{2,1,0:T(8,128)(2,1)S(1)} %get-tuple-element.34.refs_1_.refs_4_, bf16[2,64,768]{2,1,0:T(8,128)(2,1)S(1)} %get-tuple-element.53.refs_6_.refs_3_.refs_2_, ...), custom_call_target="tpu_custom_call" | custom-call | flops 301989888 | tf_op jit(solution)/shard_map/merge_3/pallas_call | solution.py:242
  57.7 0.0 copy-start.1
  57.7 1.9 %collective-permute-done.13.refs_5_ = bf16[2,48,768]{2,1,0:T(8,128)(2,1)S(1)} collective-permute-done((bf16[2,48,768]{2,1,0:T(8,128)(2,1)S(1)}, bf16[2,48,768]{2,1,0:T(8,128)(2,1)S(1)}, u32[]{:S(2)}, u32[]{:S(2)}) %collective-permute-start.13) | collective-permute-done | bytes 147488 | tf_op jit(solution)/shard_map/ppermute | solution.py:313
  59.7 1.0 %merge_3.9 = bf16[2,64,1024]{2,1,0:T(8,128)(2,1)S(1)} custom-call(f32[4,8,128]{2,1,0:T(8,128)S(1)} %get-tuple-element.33.refs_0_, bf16[4,256,768]{2,1,0:T(8,128)(2,1)S(1)} %get-tuple-element.34.refs_1_.refs_4_, bf16[2,64,768]{2,1,0:T(8,128)(2,1)S(1)} %get-tuple-element.57.refs_6_.refs_3_.refs_2_, bf16[2,64,768]{2,1,0:T(8,128)(2,1)S(1)} %get-tuple-element.58.refs_6_.refs_3_, ...), custom_call_target="tpu_custom_call" | custom-call | flops 352321536 | tf_op jit(solution)/shard_map/merge_3/pallas_call | solution.py:242
  60.7 0.7 %slice_dynamic-update-slice_fusion = bf16[2,64,4096]{2,1,0:T(8,128)(2,1)} fusion(bf16[2,64,4096]{2,1,0:T(8,128)(2,1)} %copy-done.1, bf16[2,64,1024]{2,1,0:T(8,128)(2,1)S(1)} %merge_3.9), kind=kLoop, calls=%fused_computation | loop fusion | bytes 458752 | tf_op jit(solution)/shard_map/concatenate | solution.py:339
  (10 shorter events, 0.1 us)
Async XLA Ops:
  0.0 3.0 %collective-permute-start = (bf16[2,64,4096]{2,1,0:T(8,128)(2,1)}, bf16[2,64,4096]{2,1,0:T(8,128)(2,1)S(1)}, u32[]{:S(2)}, u32[]{:S(2)}) collective-permute-start(bf16[2,64,4096]{2,1,0:T(8,128)(2,1)} %refs_2_.5), channel_id=1, source_target_pairs={{0,1},{1,0},{2,3},{3,2},{4,5},{5,4},{6,7},{7,6},{8,9},{9,8},{10,11... | collective-permute-start | bytes 3145736 | tf_op jit(solution)/shard_map/ppermute | solution.py:313
  2.0 1.2 %copy-start = (bf16[2,64,4096]{2,1,0:T(8,128)(2,1)S(1)}, bf16[2,64,4096]{2,1,0:T(8,128)(2,1)}, u32[]{:S(2)}) copy-start(bf16[2,64,4096]{2,1,0:T(8,128)(2,1)} %refs_2_.5) | copy-start | bytes 3145732
  4.4 8.5 %collective-permute-start.1 = (bf16[2,48,1024]{2,1,0:T(8,128)(2,1)S(1)}, bf16[2,48,1024]{2,1,0:T(8,128)(2,1)S(1)}, u32[]{:S(2)}, u32[]{:S(2)}) collective-permute-start(bf16[2,48,1024]{2,1,0:T(8,128)(2,1)S(1)} %get-tuple-element.36), channel_id=1, source_target_pairs={{0,2},{1,3},{2,0},{3,1},{4,6},{5,7},{6,4},{7,5},{8,10},{9,11},{10,... | collective-permute-start | bytes 589832 | tf_op jit(solution)/shard_map/ppermute | solution.py:313
  8.2 8.8 %collective-permute-start.3 = (bf16[2,48,1024]{2,1,0:T(8,128)(2,1)S(1)}, bf16[2,48,1024]{2,1,0:T(8,128)(2,1)S(1)}, u32[]{:S(2)}, u32[]{:S(2)}) collective-permute-start(bf16[2,48,1024]{2,1,0:T(8,128)(2,1)S(1)} %get-tuple-element.41), channel_id=1, source_target_pairs={{0,2},{1,3},{2,0},{3,1},{4,6},{5,7},{6,4},{7,5},{8,10},{9,11},{10,... | collective-permute-start | bytes 589832 | tf_op jit(solution)/shard_map/ppermute | solution.py:313
  10.8 14.4 %collective-permute-start.5 = (bf16[2,48,2048]{2,1,0:T(8,128)(2,1)S(1)}, bf16[2,48,2048]{2,1,0:T(8,128)(2,1)S(1)}, u32[]{:S(2)}, u32[]{:S(2)}) collective-permute-start(bf16[2,48,2048]{2,1,0:T(8,128)(2,1)S(1)} %get-tuple-element.45), channel_id=1, source_target_pairs={{0,2},{1,3},{2,0},{3,1},{4,6},{5,7},{6,4},{7,5},{8,10},{9,11},{10,... | collective-permute-start | bytes 1179656 | tf_op jit(solution)/shard_map/ppermute | solution.py:313
  14.0 6.2 %collective-permute-start.2 = (bf16[2,48,896]{2,1,0:T(8,128)(2,1)S(1)}, bf16[2,48,896]{2,1,0:T(8,128)(2,1)S(1)}, u32[]{:S(2)}, u32[]{:S(2)}) collective-permute-start(bf16[2,48,896]{2,1,0:T(8,128)(2,1)S(1)} %get-tuple-element.40), channel_id=1, source_target_pairs={{0,4},{1,5},{2,6},{3,7},{4,0},{5,1},{6,2},{7,3},{8,12},{9,13},{10,... | collective-permute-start | bytes 516104 | tf_op jit(solution)/shard_map/ppermute | solution.py:313
  18.2 9.8 %collective-permute-start.6 = (bf16[2,48,1024]{2,1,0:T(8,128)(2,1)S(1)}, bf16[2,48,1024]{2,1,0:T(8,128)(2,1)S(1)}, u32[]{:S(2)}, u32[]{:S(2)}) collective-permute-start(bf16[2,48,1024]{2,1,0:T(8,128)(2,1)S(1)} %get-tuple-element.46), channel_id=1, source_target_pairs={{0,4},{1,5},{2,6},{3,7},{4,0},{5,1},{6,2},{7,3},{8,12},{9,13},{10,... | collective-permute-start | bytes 589832 | tf_op jit(solution)/shard_map/ppermute | solution.py:313
  21.2 12.1 %collective-permute-start.4 = (bf16[2,48,768]{2,1,0:T(8,128)(2,1)S(1)}, bf16[2,48,768]{2,1,0:T(8,128)(2,1)S(1)}, u32[]{:S(2)}, u32[]{:S(2)}) collective-permute-start(bf16[2,48,768]{2,1,0:T(8,128)(2,1)S(1)} %get-tuple-element.44), channel_id=1, source_target_pairs={{0,8},{1,9},{2,10},{3,11},{4,12},{5,13},{6,14},{7,15},{8,0},{9,1},... | collective-permute-start | bytes 442376 | tf_op jit(solution)/shard_map/ppermute | solution.py:313
  26.1 10.7 %collective-permute-start.8 = (bf16[2,48,768]{2,1,0:T(8,128)(2,1)S(1)}, bf16[2,48,768]{2,1,0:T(8,128)(2,1)S(1)}, u32[]{:S(2)}, u32[]{:S(2)}) collective-permute-start(bf16[2,48,768]{2,1,0:T(8,128)(2,1)S(1)} %get-tuple-element.51), channel_id=1, source_target_pairs={{0,4},{1,5},{2,6},{3,7},{4,0},{5,1},{6,2},{7,3},{8,12},{9,13},{10,... | collective-permute-start | bytes 442376 | tf_op jit(solution)/shard_map/ppermute | solution.py:313
  29.1 12.0 %collective-permute-start.7 = (bf16[2,48,1024]{2,1,0:T(8,128)(2,1)S(1)}, bf16[2,48,1024]{2,1,0:T(8,128)(2,1)S(1)}, u32[]{:S(2)}, u32[]{:S(2)}) collective-permute-start(bf16[2,48,1024]{2,1,0:T(8,128)(2,1)S(1)} %get-tuple-element.50), channel_id=1, source_target_pairs={{0,8},{1,9},{2,10},{3,11},{4,12},{5,13},{6,14},{7,15},{8,0},{9,1},... | collective-permute-start | bytes 589832 | tf_op jit(solution)/shard_map/ppermute | solution.py:313
  32.7 11.9 %collective-permute-start.10 = (bf16[2,48,768]{2,1,0:T(8,128)(2,1)S(1)}, bf16[2,48,768]{2,1,0:T(8,128)(2,1)S(1)}, u32[]{:S(2)}, u32[]{:S(2)}) collective-permute-start(bf16[2,48,768]{2,1,0:T(8,128)(2,1)S(1)} %get-tuple-element.55), channel_id=1, source_target_pairs={{0,4},{1,5},{2,6},{3,7},{4,0},{5,1},{6,2},{7,3},{8,12},{9,13},{10,... | collective-permute-start | bytes 442376 | tf_op jit(solution)/shard_map/ppermute | solution.py:313
  35.2 11.2 %collective-permute-start.11 = (bf16[2,48,640]{2,1,0:T(8,128)(2,1)S(1)}, bf16[2,48,640]{2,1,0:T(8,128)(2,1)S(1)}, u32[]{:S(2)}, u32[]{:S(2)}) collective-permute-start(bf16[2,48,640]{2,1,0:T(8,128)(2,1)S(1)} %get-tuple-element.56), channel_id=1, source_target_pairs={{0,4},{1,5},{2,6},{3,7},{4,0},{5,1},{6,2},{7,3},{8,12},{9,13},{10,... | collective-permute-start | bytes 368648 | tf_op jit(solution)/shard_map/ppermute | solution.py:313
  37.7 11.9 %collective-permute-start.9 = (bf16[2,48,768]{2,1,0:T(8,128)(2,1)S(1)}, bf16[2,48,768]{2,1,0:T(8,128)(2,1)S(1)}, u32[]{:S(2)}, u32[]{:S(2)}) collective-permute-start(bf16[2,48,768]{2,1,0:T(8,128)(2,1)S(1)} %get-tuple-element.54), channel_id=1, source_target_pairs={{0,8},{1,9},{2,10},{3,11},{4,12},{5,13},{6,14},{7,15},{8,0},{9,1},... | collective-permute-start | bytes 442376 | tf_op jit(solution)/shard_map/ppermute | solution.py:313
  45.6 11.2 %collective-permute-start.12 = (bf16[2,48,768]{2,1,0:T(8,128)(2,1)S(1)}, bf16[2,48,768]{2,1,0:T(8,128)(2,1)S(1)}, u32[]{:S(2)}, u32[]{:S(2)}) collective-permute-start(bf16[2,48,768]{2,1,0:T(8,128)(2,1)S(1)} %get-tuple-element.59), channel_id=1, source_target_pairs={{0,8},{1,9},{2,10},{3,11},{4,12},{5,13},{6,14},{7,15},{8,0},{9,1},... | collective-permute-start | bytes 442376 | tf_op jit(solution)/shard_map/ppermute | solution.py:313
  47.3 12.3 %collective-permute-start.13 = (bf16[2,48,768]{2,1,0:T(8,128)(2,1)S(1)}, bf16[2,48,768]{2,1,0:T(8,128)(2,1)S(1)}, u32[]{:S(2)}, u32[]{:S(2)}) collective-permute-start(bf16[2,48,768]{2,1,0:T(8,128)(2,1)S(1)} %get-tuple-element.60), channel_id=1, source_target_pairs={{0,8},{1,9},{2,10},{3,11},{4,12},{5,13},{6,14},{7,15},{8,0},{9,1},... | collective-permute-start | bytes 442376 | tf_op jit(solution)/shard_map/ppermute | solution.py:313
  57.7 3.0 %copy-start.1 = (bf16[2,64,4096]{2,1,0:T(8,128)(2,1)}, bf16[2,64,4096]{2,1,0:T(8,128)(2,1)S(1)}, u32[]{:S(2)}) copy-start(bf16[2,64,4096]{2,1,0:T(8,128)(2,1)S(1)} %constant_dynamic-update-slice_fusion) | copy-start | bytes 3145732

commit v11 on v10

--- a/solution.py
+++ b/solution.py
@@ -307,10 +307,16 @@
     return order
 
 
-def from_partner(value, bit):
+def from_partner(value, bit, turned=False):
     mask = 1 << bit
-    pairs = [(source, source ^ mask) for source in range(lax.axis_size("pulse"))]
-    return lax.ppermute(value, "pulse", pairs)
+    pulses, scenes = lax.axis_size("pulse"), lax.axis_size("scene")
+    order = range(scenes - 1, -1, -1) if turned else range(scenes)
+    pairs = [
+        (scene * pulses + source, scene * pulses + (source ^ mask))
+        for scene in order
+        for source in range(pulses)
+    ]
+    return lax.ppermute(value, ("scene", "pulse"), pairs)
 
 
 def on_device(beams_in, ukern, rkern, angles, taps, shifts, half_table):
@@ -333,7 +339,8 @@
         )
         before = owns[level + 1][chunk] = done[0]
         if level < levels - 1:
-            fars[level + 1][chunk] = from_partner(done[1], level + 1)
+            turned = level == levels - 2 and chunk % 2 == 1
+            fars[level + 1][chunk] = from_partner(done[1], level + 1, turned)
     edges = bounds[levels]
     made = [part[:, :, :high - low] for part, low, high in zip(owns[levels], edges, edges[1:])]
     return jnp.concatenate(made, axis=2)

time: 61.6 us -> 61.6 us (level)
  no operation moved by 1% of the time
where the time goes in v11:
time: 61.6 us; the launch traced here: 61.4 us
  starting transfers between devices  21.5 us (35%)
  Pallas kernels  20.5 us (33%)
  waiting for transfers between devices  16.7 us (27%)
  other arithmetic  1.54 us (2%)
  local copies, waits for them, and re-layouts  1.05 us (2%)
    ppermute x14, starting transfers between devices, from_partner(): return lax.ppermute(value, ('scene', 'pulse'), pairs)  21.5 us
    pallas_call x18, Pallas kernels, merge(): pl.pallas_call(functools.partial(merge_kernel, level, plan, start, stop,...  19.6 us
    ppermute x14, waiting for transfers between devices, from_partner(): return lax.ppermute(value, ('scene', 'pulse'), pairs)  16.7 us
    add x2, other arithmetic, stacked(): total = total + lax.pad(piece, zero, ((top, below, 0), (left, right, 0)))  1.54 us
  transfers between devices with their start and end apart: 14, of which 8 were waited for; matrix products, arithmetic and copies ran while one was open for 3% of the time, Pallas kernels for 30%

profile of v11, /device:TPU:0, one launch (start us, length us, event | category | flops | bytes accessed | tf_op | source)
XLA Modules:
  0.0 61.4 jit_solution(17300298601953555859)
XLA Ops:
  0.0 0.5 collective-permute-start
  0.5 0.7 %pad_add_fusion.real_ref = f32[14,128]{1,0:T(8,128)S(1)} fusion(f32[4,16]{1,0:T(4,128)} %bitcast.3, f32[8,128]{1,0:T(8,128)} %bitcast.2, bf16[2,32]{1,0:T(2,128)(2,1)} %param.8), kind=kLoop, calls=%fused_computation.5 | loop fusion | flops 5376 | bytes 11648 | tf_op jit(solution)/shard_map/add | solution.py:91
  1.2 0.8 %pad_add_fusion.1.whole_ref = s32[12,128]{1,0:T(8,128)S(1)} fusion(s32[4,64]{1,0:T(4,128)} %param.11, s32[4,16]{1,0:T(4,128)} %param.12, s32[4,16]{1,0:T(4,128)} %param.13), kind=kLoop, calls=%fused_computation.6 | loop fusion | flops 4608 | bytes 7680 | tf_op jit(solution)/shard_map/add | solution.py:91
  2.0 0.9 %mixing.1 = (bf16[4,256,768]{2,1,0:T(8,128)(2,1)S(1)}, f32[4,8,128]{2,1,0:T(8,128)S(1)}) custom-call(s32[12,128]{1,0:T(8,128)S(1)} %pad_add_fusion.1.whole_ref, f32[14,128]{1,0:T(8,128)S(1)} %pad_add_fusion.real_ref), custom_call_target="tpu_custom_call" | custom-call | flops 2000000000 | bytes 1572864 | tf_op jit(solution)/shard_map/mixing/pallas_call | solution.py:121
  2.9 0.1 collective-permute-done.refs_3_
  3.0 0.3 copy-done
  3.2 1.1 %merge_0.3 = (bf16[2,64,1024]{2,1,0:T(8,128)(2,1)S(1)}, bf16[2,48,1024]{2,1,0:T(8,128)(2,1)S(1)}) custom-call(f32[4,8,128]{2,1,0:T(8,128)S(1)} %get-tuple-element.33.refs_0_, bf16[4,256,768]{2,1,0:T(8,128)(2,1)S(1)} %get-tuple-element.34.refs_1_.refs_4_, bf16[2,64,4096]{2,1,0:T(8,128)(2,1)S(1)} %copy-done, ...), custom_call_target="tpu_custom_call" | custom-call | flops 1610612736 | tf_op jit(solution)/shard_map/merge_0/pallas_call | solution.py:242
  4.4 2.7 %collective-permute-start.1 = (bf16[2,48,1024]{2,1,0:T(8,128)(2,1)S(1)}, bf16[2,48,1024]{2,1,0:T(8,128)(2,1)S(1)}, u32[]{:S(2)}, u32[]{:S(2)}) collective-permute-start(bf16[2,48,1024]{2,1,0:T(8,128)(2,1)S(1)} %get-tuple-element.36), channel_id=1, source_target_pairs={{0,2},{1,3},{2,0},{3,1},{4,6},{5,7},{6,4},{7,5},{8,10},{9,11},{10,... | collective-permute-start | bytes 589832 | tf_op jit(solution)/shard_map/ppermute | solution.py:319
  7.0 1.1 %merge_0.4 = (bf16[2,64,1024]{2,1,0:T(8,128)(2,1)S(1)}, bf16[2,48,1024]{2,1,0:T(8,128)(2,1)S(1)}) custom-call(f32[4,8,128]{2,1,0:T(8,128)S(1)} %get-tuple-element.33.refs_0_, bf16[4,256,768]{2,1,0:T(8,128)(2,1)S(1)} %get-tuple-element.34.refs_1_.refs_4_, bf16[2,64,4096]{2,1,0:T(8,128)(2,1)S(1)} %copy-done, ...), custom_call_target="tpu_custom_call" | custom-call | flops 1610612736 | tf_op jit(solution)/shard_map/merge_0/pallas_call | solution.py:242
  8.2 0.1 collective-permute-start.3
  8.3 2.5 %merge_0.5 = (bf16[2,64,2048]{2,1,0:T(8,128)(2,1)S(1)}, bf16[2,48,2048]{2,1,0:T(8,128)(2,1)S(1)}) custom-call(f32[4,8,128]{2,1,0:T(8,128)S(1)} %get-tuple-element.33.refs_0_, bf16[4,256,768]{2,1,0:T(8,128)(2,1)S(1)} %get-tuple-element.34.refs_1_.refs_4_, bf16[2,64,4096]{2,1,0:T(8,128)(2,1)S(1)} %copy-done, ...), custom_call_target="tpu_custom_call" | custom-call | flops 3221225472 | tf_op jit(solution)/shard_map/merge_0/pallas_call | solution.py:242
  10.8 2.1 %collective-permute-start.5 = (bf16[2,48,2048]{2,1,0:T(8,128)(2,1)S(1)}, bf16[2,48,2048]{2,1,0:T(8,128)(2,1)S(1)}, u32[]{:S(2)}, u32[]{:S(2)}) collective-permute-start(bf16[2,48,2048]{2,1,0:T(8,128)(2,1)S(1)} %get-tuple-element.45), channel_id=1, source_target_pairs={{0,2},{1,3},{2,0},{3,1},{4,6},{5,7},{6,4},{7,5},{8,10},{9,11},{10,... | collective-permute-start | bytes 1179656 | tf_op jit(solution)/shard_map/ppermute | solution.py:319
  12.8 0.0 collective-permute-done.1.refs_3_.refs_4_
  12.9 1.1 %merge_1.5 = (bf16[2,64,1024]{2,1,0:T(8,128)(2,1)S(1)}, bf16[2,48,896]{2,1,0:T(8,128)(2,1)S(1)}) custom-call(f32[4,8,128]{2,1,0:T(8,128)S(1)} %get-tuple-element.33.refs_0_, bf16[4,256,768]{2,1,0:T(8,128)(2,1)S(1)} %get-tuple-element.34.refs_1_.refs_4_, bf16[2,64,1024]{2,1,0:T(8,128)(2,1)S(1)} %get-tuple-element.35.refs_4_.refs_2_, ...), custom_call_target="tpu_custom_call" | custom-call | flops 1409286144 | tf_op jit(solution)/shard_map/merge_1/pallas_call | solution.py:242
  14.0 2.0 %collective-permute-start.2 = (bf16[2,48,896]{2,1,0:T(8,128)(2,1)S(1)}, bf16[2,48,896]{2,1,0:T(8,128)(2,1)S(1)}, u32[]{:S(2)}, u32[]{:S(2)}) collective-permute-start(bf16[2,48,896]{2,1,0:T(8,128)(2,1)S(1)} %get-tuple-element.40), channel_id=1, source_target_pairs={{0,4},{1,5},{2,6},{3,7},{4,0},{5,1},{6,2},{7,3},{8,12},{9,13},{10,... | collective-permute-start | bytes 516104 | tf_op jit(solution)/shard_map/ppermute | solution.py:319
  16.0 1.0 %collective-permute-done.3.refs_5_.refs_4_ = bf16[2,48,1024]{2,1,0:T(8,128)(2,1)S(1)} collective-permute-done((bf16[2,48,1024]{2,1,0:T(8,128)(2,1)S(1)}, bf16[2,48,1024]{2,1,0:T(8,128)(2,1)S(1)}, u32[]{:S(2)}, u32[]{:S(2)}) %collective-permute-start.3) | collective-permute-done | bytes 196640 | tf_op jit(solution)/shard_map/ppermute | solution.py:319
  17.0 1.1 %merge_1.6 = (bf16[2,64,1024]{2,1,0:T(8,128)(2,1)S(1)}, bf16[2,48,1024]{2,1,0:T(8,128)(2,1)S(1)}) custom-call(f32[4,8,128]{2,1,0:T(8,128)S(1)} %get-tuple-element.33.refs_0_, bf16[4,256,768]{2,1,0:T(8,128)(2,1)S(1)} %get-tuple-element.34.refs_1_.refs_4_, bf16[2,64,1024]{2,1,0:T(8,128)(2,1)S(1)} %get-tuple-element.35.refs_4_.refs_2_, ...), custom_call_target="tpu_custom_call" | custom-call | flops 1610612736 | tf_op jit(solution)/shard_map/merge_1/pallas_call | solution.py:242
  18.1 2.1 %collective-permute-start.6 = (bf16[2,48,1024]{2,1,0:T(8,128)(2,1)S(1)}, bf16[2,48,1024]{2,1,0:T(8,128)(2,1)S(1)}, u32[]{:S(2)}, u32[]{:S(2)}) collective-permute-start(bf16[2,48,1024]{2,1,0:T(8,128)(2,1)S(1)} %get-tuple-element.46), channel_id=1, source_target_pairs={{0,4},{1,5},{2,6},{3,7},{4,0},{5,1},{6,2},{7,3},{8,12},{9,13},{10,... | collective-permute-start | bytes 589832 | tf_op jit(solution)/shard_map/ppermute | solution.py:319
  20.2 0.0 collective-permute-done.2.refs_3_.refs_4_
  20.2 0.9 %merge_2.5 = (bf16[2,64,768]{2,1,0:T(8,128)(2,1)S(1)}, bf16[2,48,768]{2,1,0:T(8,128)(2,1)S(1)}) custom-call(f32[4,8,128]{2,1,0:T(8,128)S(1)} %get-tuple-element.33.refs_0_, bf16[4,256,768]{2,1,0:T(8,128)(2,1)S(1)} %get-tuple-element.34.refs_1_.refs_4_, bf16[2,64,1024]{2,1,0:T(8,128)(2,1)S(1)} %get-tuple-element.39.refs_6_.refs_2_, ...), custom_call_target="tpu_custom_call" | custom-call | flops 1207959552 | tf_op jit(solution)/shard_map/merge_2/pallas_call | solution.py:242
  21.2 2.6 %collective-permute-start.4 = (bf16[2,48,768]{2,1,0:T(8,128)(2,1)S(1)}, bf16[2,48,768]{2,1,0:T(8,128)(2,1)S(1)}, u32[]{:S(2)}, u32[]{:S(2)}) collective-permute-start(bf16[2,48,768]{2,1,0:T(8,128)(2,1)S(1)} %get-tuple-element.44), channel_id=1, source_target_pairs={{0,8},{1,9},{2,10},{3,11},{4,12},{5,13},{6,14},{7,15},{8,0},{9,1},... | collective-permute-start | bytes 442376 | tf_op jit(solution)/shard_map/ppermute | solution.py:319
  23.8 1.3 %collective-permute-done.5.refs_5_.refs_3_ = bf16[2,48,2048]{2,1,0:T(8,128)(2,1)S(1)} collective-permute-done((bf16[2,48,2048]{2,1,0:T(8,128)(2,1)S(1)}, bf16[2,48,2048]{2,1,0:T(8,128)(2,1)S(1)}, u32[]{:S(2)}, u32[]{:S(2)}) %collective-permute-start.5) | collective-permute-done | bytes 393248 | tf_op jit(solution)/shard_map/ppermute | solution.py:319
  25.2 0.9 %merge_1.7 = (bf16[2,64,768]{2,1,0:T(8,128)(2,1)S(1)}, bf16[2,48,768]{2,1,0:T(8,128)(2,1)S(1)}) custom-call(f32[4,8,128]{2,1,0:T(8,128)S(1)} %get-tuple-element.33.refs_0_, bf16[4,256,768]{2,1,0:T(8,128)(2,1)S(1)} %get-tuple-element.34.refs_1_.refs_4_, bf16[2,64,1024]{2,1,0:T(8,128)(2,1)S(1)} %get-tuple-element.37.refs_4_.refs_3_.refs_2_, ...), custom_call_target="tpu_custom_call" | custom-call | flops 1207959552 | tf_op jit(solution)/shard_map/merge_1/pallas_call | solution.py:242
  26.1 1.9 %collective-permute-start.8 = (bf16[2,48,768]{2,1,0:T(8,128)(2,1)S(1)}, bf16[2,48,768]{2,1,0:T(8,128)(2,1)S(1)}, u32[]{:S(2)}, u32[]{:S(2)}) collective-permute-start(bf16[2,48,768]{2,1,0:T(8,128)(2,1)S(1)} %get-tuple-element.51), channel_id=1, source_target_pairs={{0,4},{1,5},{2,6},{3,7},{4,0},{5,1},{6,2},{7,3},{8,12},{9,13},{10,... | collective-permute-start | bytes 442376 | tf_op jit(solution)/shard_map/ppermute | solution.py:319
  28.0 1.1 %merge_2.6 = (bf16[2,64,1024]{2,1,0:T(8,128)(2,1)S(1)}, bf16[2,48,1024]{2,1,0:T(8,128)(2,1)S(1)}) custom-call(f32[4,8,128]{2,1,0:T(8,128)S(1)} %get-tuple-element.33.refs_0_, bf16[4,256,768]{2,1,0:T(8,128)(2,1)S(1)} %get-tuple-element.34.refs_1_.refs_4_, bf16[2,64,1024]{2,1,0:T(8,128)(2,1)S(1)} %get-tuple-element.39.refs_6_.refs_2_, ...), custom_call_target="tpu_custom_call" | custom-call | flops 1610612736 | tf_op jit(solution)/shard_map/merge_2/pallas_call | solution.py:242
  29.1 2.6 %collective-permute-start.7 = (bf16[2,48,1024]{2,1,0:T(8,128)(2,1)S(1)}, bf16[2,48,1024]{2,1,0:T(8,128)(2,1)S(1)}, u32[]{:S(2)}, u32[]{:S(2)}) collective-permute-start(bf16[2,48,1024]{2,1,0:T(8,128)(2,1)S(1)} %get-tuple-element.50), channel_id=1, source_target_pairs={{16,24},{17,25},{18,26},{19,27},{20,28},{21,29},{22,30},{23,31},{2... | collective-permute-start | bytes 589832 | tf_op jit(solution)/shard_map/ppermute | solution.py:319
  31.8 1.0 %merge_1.8 = (bf16[2,64,768]{2,1,0:T(8,128)(2,1)S(1)}, bf16[2,48,768]{2,1,0:T(8,128)(2,1)S(1)}) custom-call(f32[4,8,128]{2,1,0:T(8,128)S(1)} %get-tuple-element.33.refs_0_, bf16[4,256,768]{2,1,0:T(8,128)(2,1)S(1)} %get-tuple-element.34.refs_1_.refs_4_, bf16[2,64,2048]{2,1,0:T(8,128)(2,1)S(1)} %get-tuple-element.38.refs_4_.refs_3_.refs_2_, ...), custom_call_target="tpu_custom_call" | custom-call | flops 1207959552 | tf_op jit(solution)/shard_map/merge_1/pallas_call | solution.py:242
  32.7 0.5 collective-permute-start.10
  33.3 0.9 %merge_3.5.refs_4_ = bf16[2,64,768]{2,1,0:T(8,128)(2,1)S(1)} custom-call(f32[4,8,128]{2,1,0:T(8,128)S(1)} %get-tuple-element.33.refs_0_, bf16[4,256,768]{2,1,0:T(8,128)(2,1)S(1)} %get-tuple-element.34.refs_1_.refs_4_, bf16[2,64,768]{2,1,0:T(8,128)(2,1)S(1)} %get-tuple-element.43.refs_6_.refs_2_, ...), custom_call_target="tpu_custom_call" | custom-call | flops 251658240 | tf_op jit(solution)/shard_map/merge_3/pallas_call | solution.py:242
  34.2 0.9 %merge_1.9 = (bf16[2,64,768]{2,1,0:T(8,128)(2,1)S(1)}, bf16[2,48,640]{2,1,0:T(8,128)(2,1)S(1)}) custom-call(f32[4,8,128]{2,1,0:T(8,128)S(1)} %get-tuple-element.33.refs_0_, bf16[4,256,768]{2,1,0:T(8,128)(2,1)S(1)} %get-tuple-element.34.refs_1_.refs_4_, bf16[2,64,2048]{2,1,0:T(8,128)(2,1)S(1)} %get-tuple-element.38.refs_4_.refs_3_.refs_2_, ...), custom_call_target="tpu_custom_call" | custom-call | flops 1006632960 | tf_op jit(solution)/shard_map/merge_1/pallas_call | solution.py:242
  35.2 1.6 %collective-permute-start.11 = (bf16[2,48,640]{2,1,0:T(8,128)(2,1)S(1)}, bf16[2,48,640]{2,1,0:T(8,128)(2,1)S(1)}, u32[]{:S(2)}, u32[]{:S(2)}) collective-permute-start(bf16[2,48,640]{2,1,0:T(8,128)(2,1)S(1)} %get-tuple-element.56), channel_id=1, source_target_pairs={{0,4},{1,5},{2,6},{3,7},{4,0},{5,1},{6,2},{7,3},{8,12},{9,13},{10,... | collective-permute-start | bytes 368648 | tf_op jit(solution)/shard_map/ppermute | solution.py:319
  36.8 0.9 %merge_2.7 = (bf16[2,64,768]{2,1,0:T(8,128)(2,1)S(1)}, bf16[2,48,768]{2,1,0:T(8,128)(2,1)S(1)}) custom-call(f32[4,8,128]{2,1,0:T(8,128)S(1)} %get-tuple-element.33.refs_0_, bf16[4,256,768]{2,1,0:T(8,128)(2,1)S(1)} %get-tuple-element.34.refs_1_.refs_4_, bf16[2,64,1024]{2,1,0:T(8,128)(2,1)S(1)} %get-tuple-element.42.refs_4_.refs_3_.refs_2_, ...), custom_call_target="tpu_custom_call" | custom-call | flops 1207959552 | tf_op jit(solution)/shard_map/merge_2/pallas_call | solution.py:242
  37.7 0.4 collective-permute-start.9
  38.2 3.0 %collective-permute-done.7.refs_5_.refs_4_ = bf16[2,48,1024]{2,1,0:T(8,128)(2,1)S(1)} collective-permute-done((bf16[2,48,1024]{2,1,0:T(8,128)(2,1)S(1)}, bf16[2,48,1024]{2,1,0:T(8,128)(2,1)S(1)}, u32[]{:S(2)}, u32[]{:S(2)}) %collective-permute-start.7) | collective-permute-done | bytes 196640 | tf_op jit(solution)/shard_map/ppermute | solution.py:319
  41.2 1.1 %merge_3.6.refs_6_ = bf16[2,64,1024]{2,1,0:T(8,128)(2,1)S(1)} custom-call(f32[4,8,128]{2,1,0:T(8,128)S(1)} %get-tuple-element.33.refs_0_, bf16[4,256,768]{2,1,0:T(8,128)(2,1)S(1)} %get-tuple-element.34.refs_1_.refs_4_, bf16[2,64,768]{2,1,0:T(8,128)(2,1)S(1)} %get-tuple-element.43.refs_6_.refs_2_, ...), custom_call_target="tpu_custom_call" | custom-call | flops 402653184 | tf_op jit(solution)/shard_map/merge_3/pallas_call | solution.py:242
  42.2 2.4 %collective-permute-done.10.refs_5_.refs_4_ = bf16[2,48,768]{2,1,0:T(8,128)(2,1)S(1)} collective-permute-done((bf16[2,48,768]{2,1,0:T(8,128)(2,1)S(1)}, bf16[2,48,768]{2,1,0:T(8,128)(2,1)S(1)}, u32[]{:S(2)}, u32[]{:S(2)}) %collective-permute-start.10) | collective-permute-done | bytes 147488 | tf_op jit(solution)/shard_map/ppermute | solution.py:319
  44.6 0.9 %merge_2.8 = (bf16[2,64,768]{2,1,0:T(8,128)(2,1)S(1)}, bf16[2,48,768]{2,1,0:T(8,128)(2,1)S(1)}) custom-call(f32[4,8,128]{2,1,0:T(8,128)S(1)} %get-tuple-element.33.refs_0_, bf16[4,256,768]{2,1,0:T(8,128)(2,1)S(1)} %get-tuple-element.34.refs_1_.refs_4_, bf16[2,64,768]{2,1,0:T(8,128)(2,1)S(1)} %get-tuple-element.47.refs_6_.refs_3_.refs_2_, ...), custom_call_target="tpu_custom_call" | custom-call | flops 1207959552 | tf_op jit(solution)/shard_map/merge_2/pallas_call | solution.py:242
  45.6 0.1 collective-permute-start.12
  45.7 0.7 %collective-permute-done.11.refs_5_ = bf16[2,48,640]{2,1,0:T(8,128)(2,1)S(1)} collective-permute-done((bf16[2,48,640]{2,1,0:T(8,128)(2,1)S(1)}, bf16[2,48,640]{2,1,0:T(8,128)(2,1)S(1)}, u32[]{:S(2)}, u32[]{:S(2)}) %collective-permute-start.11) | collective-permute-done | bytes 122912 | tf_op jit(solution)/shard_map/ppermute | solution.py:319
  46.4 0.9 %merge_2.9 = (bf16[2,64,768]{2,1,0:T(8,128)(2,1)S(1)}, bf16[2,48,768]{2,1,0:T(8,128)(2,1)S(1)}) custom-call(f32[4,8,128]{2,1,0:T(8,128)S(1)} %get-tuple-element.33.refs_0_, bf16[4,256,768]{2,1,0:T(8,128)(2,1)S(1)} %get-tuple-element.34.refs_1_.refs_4_, bf16[2,64,768]{2,1,0:T(8,128)(2,1)S(1)} %get-tuple-element.49.refs_4_.refs_3_.refs_2_, ...), custom_call_target="tpu_custom_call" | custom-call | flops 1207959552 | tf_op jit(solution)/shard_map/merge_2/pallas_call | solution.py:242
  47.3 2.3 %collective-permute-start.13 = (bf16[2,48,768]{2,1,0:T(8,128)(2,1)S(1)}, bf16[2,48,768]{2,1,0:T(8,128)(2,1)S(1)}, u32[]{:S(2)}, u32[]{:S(2)}) collective-permute-start(bf16[2,48,768]{2,1,0:T(8,128)(2,1)S(1)} %get-tuple-element.60), channel_id=1, source_target_pairs={{0,8},{1,9},{2,10},{3,11},{4,12},{5,13},{6,14},{7,15},{8,0},{9,1},... | collective-permute-start | bytes 442376 | tf_op jit(solution)/shard_map/ppermute | solution.py:319
  49.6 0.9 %merge_3.7.refs_6_ = bf16[2,64,768]{2,1,0:T(8,128)(2,1)S(1)} custom-call(f32[4,8,128]{2,1,0:T(8,128)S(1)} %get-tuple-element.33.refs_0_, bf16[4,256,768]{2,1,0:T(8,128)(2,1)S(1)} %get-tuple-element.34.refs_1_.refs_4_, bf16[2,64,1024]{2,1,0:T(8,128)(2,1)S(1)} %get-tuple-element.48.refs_4_.refs_3_.refs_2_, ...), custom_call_target="tpu_custom_call" | custom-call | flops 301989888 | tf_op jit(solution)/shard_map/merge_3/pallas_call | solution.py:242
  50.5 6.3 %collective-permute-done.12.refs_5_.refs_4_ = bf16[2,48,768]{2,1,0:T(8,128)(2,1)S(1)} collective-permute-done((bf16[2,48,768]{2,1,0:T(8,128)(2,1)S(1)}, bf16[2,48,768]{2,1,0:T(8,128)(2,1)S(1)}, u32[]{:S(2)}, u32[]{:S(2)}) %collective-permute-start.12) | collective-permute-done | bytes 147488 | tf_op jit(solution)/shard_map/ppermute | solution.py:319
  56.8 0.9 %merge_3.8.refs_6_ = bf16[2,64,768]{2,1,0:T(8,128)(2,1)S(1)} custom-call(f32[4,8,128]{2,1,0:T(8,128)S(1)} %get-tuple-element.33.refs_0_, bf16[4,256,768]{2,1,0:T(8,128)(2,1)S(1)} %get-tuple-element.34.refs_1_.refs_4_, bf16[2,64,768]{2,1,0:T(8,128)(2,1)S(1)} %get-tuple-element.53.refs_6_.refs_3_.refs_2_, ...), custom_call_target="tpu_custom_call" | custom-call | flops 301989888 | tf_op jit(solution)/shard_map/merge_3/pallas_call | solution.py:242
  57.8 0.0 copy-start.1
  57.8 1.9 %collective-permute-done.13.refs_5_ = bf16[2,48,768]{2,1,0:T(8,128)(2,1)S(1)} collective-permute-done((bf16[2,48,768]{2,1,0:T(8,128)(2,1)S(1)}, bf16[2,48,768]{2,1,0:T(8,128)(2,1)S(1)}, u32[]{:S(2)}, u32[]{:S(2)}) %collective-permute-start.13) | collective-permute-done | bytes 147488 | tf_op jit(solution)/shard_map/ppermute | solution.py:319
  59.7 1.0 %merge_3.9 = bf16[2,64,1024]{2,1,0:T(8,128)(2,1)S(1)} custom-call(f32[4,8,128]{2,1,0:T(8,128)S(1)} %get-tuple-element.33.refs_0_, bf16[4,256,768]{2,1,0:T(8,128)(2,1)S(1)} %get-tuple-element.34.refs_1_.refs_4_, bf16[2,64,768]{2,1,0:T(8,128)(2,1)S(1)} %get-tuple-element.57.refs_6_.refs_3_.refs_2_, bf16[2,64,768]{2,1,0:T(8,128)(2,1)S(1)} %get-tuple-element.58.refs_6_.refs_3_, ...), custom_call_target="tpu_custom_call" | custom-call | flops 352321536 | tf_op jit(solution)/shard_map/merge_3/pallas_call | solution.py:242
  60.7 0.7 %slice_dynamic-update-slice_fusion = bf16[2,64,4096]{2,1,0:T(8,128)(2,1)} fusion(bf16[2,64,4096]{2,1,0:T(8,128)(2,1)} %copy-done.1, bf16[2,64,1024]{2,1,0:T(8,128)(2,1)S(1)} %merge_3.9), kind=kLoop, calls=%fused_computation | loop fusion | bytes 458752 | tf_op jit(solution)/shard_map/concatenate | solution.py:346
  (10 shorter events, 0.1 us)
Async XLA Ops:
  0.0 3.0 %collective-permute-start = (bf16[2,64,4096]{2,1,0:T(8,128)(2,1)}, bf16[2,64,4096]{2,1,0:T(8,128)(2,1)S(1)}, u32[]{:S(2)}, u32[]{:S(2)}) collective-permute-start(bf16[2,64,4096]{2,1,0:T(8,128)(2,1)} %refs_2_.5), channel_id=1, source_target_pairs={{0,1},{1,0},{2,3},{3,2},{4,5},{5,4},{6,7},{7,6},{8,9},{9,8},{10,11... | collective-permute-start | bytes 3145736 | tf_op jit(solution)/shard_map/ppermute | solution.py:319
  2.0 1.2 %copy-start = (bf16[2,64,4096]{2,1,0:T(8,128)(2,1)S(1)}, bf16[2,64,4096]{2,1,0:T(8,128)(2,1)}, u32[]{:S(2)}) copy-start(bf16[2,64,4096]{2,1,0:T(8,128)(2,1)} %refs_2_.5) | copy-start | bytes 3145732
  4.4 8.5 %collective-permute-start.1 = (bf16[2,48,1024]{2,1,0:T(8,128)(2,1)S(1)}, bf16[2,48,1024]{2,1,0:T(8,128)(2,1)S(1)}, u32[]{:S(2)}, u32[]{:S(2)}) collective-permute-start(bf16[2,48,1024]{2,1,0:T(8,128)(2,1)S(1)} %get-tuple-element.36), channel_id=1, source_target_pairs={{0,2},{1,3},{2,0},{3,1},{4,6},{5,7},{6,4},{7,5},{8,10},{9,11},{10,... | collective-permute-start | bytes 589832 | tf_op jit(solution)/shard_map/ppermute | solution.py:319
  8.2 8.8 %collective-permute-start.3 = (bf16[2,48,1024]{2,1,0:T(8,128)(2,1)S(1)}, bf16[2,48,1024]{2,1,0:T(8,128)(2,1)S(1)}, u32[]{:S(2)}, u32[]{:S(2)}) collective-permute-start(bf16[2,48,1024]{2,1,0:T(8,128)(2,1)S(1)} %get-tuple-element.41), channel_id=1, source_target_pairs={{0,2},{1,3},{2,0},{3,1},{4,6},{5,7},{6,4},{7,5},{8,10},{9,11},{10,... | collective-permute-start | bytes 589832 | tf_op jit(solution)/shard_map/ppermute | solution.py:319
  10.8 14.4 %collective-permute-start.5 = (bf16[2,48,2048]{2,1,0:T(8,128)(2,1)S(1)}, bf16[2,48,2048]{2,1,0:T(8,128)(2,1)S(1)}, u32[]{:S(2)}, u32[]{:S(2)}) collective-permute-start(bf16[2,48,2048]{2,1,0:T(8,128)(2,1)S(1)} %get-tuple-element.45), channel_id=1, source_target_pairs={{0,2},{1,3},{2,0},{3,1},{4,6},{5,7},{6,4},{7,5},{8,10},{9,11},{10,... | collective-permute-start | bytes 1179656 | tf_op jit(solution)/shard_map/ppermute | solution.py:319
  14.0 6.2 %collective-permute-start.2 = (bf16[2,48,896]{2,1,0:T(8,128)(2,1)S(1)}, bf16[2,48,896]{2,1,0:T(8,128)(2,1)S(1)}, u32[]{:S(2)}, u32[]{:S(2)}) collective-permute-start(bf16[2,48,896]{2,1,0:T(8,128)(2,1)S(1)} %get-tuple-element.40), channel_id=1, source_target_pairs={{0,4},{1,5},{2,6},{3,7},{4,0},{5,1},{6,2},{7,3},{8,12},{9,13},{10,... | collective-permute-start | bytes 516104 | tf_op jit(solution)/shard_map/ppermute | solution.py:319
  18.1 9.9 %collective-permute-start.6 = (bf16[2,48,1024]{2,1,0:T(8,128)(2,1)S(1)}, bf16[2,48,1024]{2,1,0:T(8,128)(2,1)S(1)}, u32[]{:S(2)}, u32[]{:S(2)}) collective-permute-start(bf16[2,48,1024]{2,1,0:T(8,128)(2,1)S(1)} %get-tuple-element.46), channel_id=1, source_target_pairs={{0,4},{1,5},{2,6},{3,7},{4,0},{5,1},{6,2},{7,3},{8,12},{9,13},{10,... | collective-permute-start | bytes 589832 | tf_op jit(solution)/shard_map/ppermute | solution.py:319
  21.2 12.1 %collective-permute-start.4 = (bf16[2,48,768]{2,1,0:T(8,128)(2,1)S(1)}, bf16[2,48,768]{2,1,0:T(8,128)(2,1)S(1)}, u32[]{:S(2)}, u32[]{:S(2)}) collective-permute-start(bf16[2,48,768]{2,1,0:T(8,128)(2,1)S(1)} %get-tuple-element.44), channel_id=1, source_target_pairs={{0,8},{1,9},{2,10},{3,11},{4,12},{5,13},{6,14},{7,15},{8,0},{9,1},... | collective-permute-start | bytes 442376 | tf_op jit(solution)/shard_map/ppermute | solution.py:319
  26.1 10.7 %collective-permute-start.8 = (bf16[2,48,768]{2,1,0:T(8,128)(2,1)S(1)}, bf16[2,48,768]{2,1,0:T(8,128)(2,1)S(1)}, u32[]{:S(2)}, u32[]{:S(2)}) collective-permute-start(bf16[2,48,768]{2,1,0:T(8,128)(2,1)S(1)} %get-tuple-element.51), channel_id=1, source_target_pairs={{0,4},{1,5},{2,6},{3,7},{4,0},{5,1},{6,2},{7,3},{8,12},{9,13},{10,... | collective-permute-start | bytes 442376 | tf_op jit(solution)/shard_map/ppermute | solution.py:319
  29.1 12.0 %collective-permute-start.7 = (bf16[2,48,1024]{2,1,0:T(8,128)(2,1)S(1)}, bf16[2,48,1024]{2,1,0:T(8,128)(2,1)S(1)}, u32[]{:S(2)}, u32[]{:S(2)}) collective-permute-start(bf16[2,48,1024]{2,1,0:T(8,128)(2,1)S(1)} %get-tuple-element.50), channel_id=1, source_target_pairs={{16,24},{17,25},{18,26},{19,27},{20,28},{21,29},{22,30},{23,31},{2... | collective-permute-start | bytes 589832 | tf_op jit(solution)/shard_map/ppermute | solution.py:319
  32.7 11.9 %collective-permute-start.10 = (bf16[2,48,768]{2,1,0:T(8,128)(2,1)S(1)}, bf16[2,48,768]{2,1,0:T(8,128)(2,1)S(1)}, u32[]{:S(2)}, u32[]{:S(2)}) collective-permute-start(bf16[2,48,768]{2,1,0:T(8,128)(2,1)S(1)} %get-tuple-element.55), channel_id=1, source_target_pairs={{0,4},{1,5},{2,6},{3,7},{4,0},{5,1},{6,2},{7,3},{8,12},{9,13},{10,... | collective-permute-start | bytes 442376 | tf_op jit(solution)/shard_map/ppermute | solution.py:319
  35.2 11.2 %collective-permute-start.11 = (bf16[2,48,640]{2,1,0:T(8,128)(2,1)S(1)}, bf16[2,48,640]{2,1,0:T(8,128)(2,1)S(1)}, u32[]{:S(2)}, u32[]{:S(2)}) collective-permute-start(bf16[2,48,640]{2,1,0:T(8,128)(2,1)S(1)} %get-tuple-element.56), channel_id=1, source_target_pairs={{0,4},{1,5},{2,6},{3,7},{4,0},{5,1},{6,2},{7,3},{8,12},{9,13},{10,... | collective-permute-start | bytes 368648 | tf_op jit(solution)/shard_map/ppermute | solution.py:319
  37.7 11.9 %collective-permute-start.9 = (bf16[2,48,768]{2,1,0:T(8,128)(2,1)S(1)}, bf16[2,48,768]{2,1,0:T(8,128)(2,1)S(1)}, u32[]{:S(2)}, u32[]{:S(2)}) collective-permute-start(bf16[2,48,768]{2,1,0:T(8,128)(2,1)S(1)} %get-tuple-element.54), channel_id=1, source_target_pairs={{0,8},{1,9},{2,10},{3,11},{4,12},{5,13},{6,14},{7,15},{8,0},{9,1},... | collective-permute-start | bytes 442376 | tf_op jit(solution)/shard_map/ppermute | solution.py:319
  45.6 11.3 %collective-permute-start.12 = (bf16[2,48,768]{2,1,0:T(8,128)(2,1)S(1)}, bf16[2,48,768]{2,1,0:T(8,128)(2,1)S(1)}, u32[]{:S(2)}, u32[]{:S(2)}) collective-permute-start(bf16[2,48,768]{2,1,0:T(8,128)(2,1)S(1)} %get-tuple-element.59), channel_id=1, source_target_pairs={{16,24},{17,25},{18,26},{19,27},{20,28},{21,29},{22,30},{23,31},{2... | collective-permute-start | bytes 442376 | tf_op jit(solution)/shard_map/ppermute | solution.py:319
  47.3 12.3 %collective-permute-start.13 = (bf16[2,48,768]{2,1,0:T(8,128)(2,1)S(1)}, bf16[2,48,768]{2,1,0:T(8,128)(2,1)S(1)}, u32[]{:S(2)}, u32[]{:S(2)}) collective-permute-start(bf16[2,48,768]{2,1,0:T(8,128)(2,1)S(1)} %get-tuple-element.60), channel_id=1, source_target_pairs={{0,8},{1,9},{2,10},{3,11},{4,12},{5,13},{6,14},{7,15},{8,0},{9,1},... | collective-permute-start | bytes 442376 | tf_op jit(solution)/shard_map/ppermute | solution.py:319
  57.8 2.9 %copy-start.1 = (bf16[2,64,4096]{2,1,0:T(8,128)(2,1)}, bf16[2,64,4096]{2,1,0:T(8,128)(2,1)S(1)}, u32[]{:S(2)}) copy-start(bf16[2,64,4096]{2,1,0:T(8,128)(2,1)S(1)} %constant_dynamic-update-slice_fusion) | copy-start | bytes 3145732

commit v12 on v10

--- a/solution.py
+++ b/solution.py
@@ -146,7 +146,7 @@
     out_ref = outs[0]
     send_ref = None if last else outs[1]
     wide_ref, even_ref, odd_ref, held_ref = outs[1 if last else 2:]
-    code = jnp.max(code_ref[level]).astype(jnp.int32)
+    code = code_ref[level][0, 0].astype(jnp.int32)
     half, following = code // 131072, code // 65536 % 2
     shifts = (code // 256 % 256 - LANES, code % 256 - LANES)
     rows = pl.ds(pl.multiple_of(half * (beams - window), 16), window)
@@ -165,6 +165,8 @@
         wide_ref[:, :, :, stop - base:stop - base + LANES] = edge
     span = stop - start
     tiles = pl.cdiv(span, TILE)
+    other = pl.ds(pl.multiple_of((1 - following) * (beams - window), 16), window)
+    inline = not last and span % TILE == 0
     lane = lax.broadcasted_iota(jnp.int32, (2 * window, LANES), 1).astype(jnp.int16)
     moves = []
     for child in range(2):
@@ -195,6 +197,8 @@
         both = jnp.dot(mix_ref[level], stack_ref[...], preferred_element_type=jnp.float32)
         total = (both[:2 * beams] + both[2 * beams:]).astype(jnp.bfloat16)
         out_ref[:, :, pl.ds(column, TILE)] = total.reshape(2, beams, TILE)
+        if inline:
+            send_ref[:, :, pl.ds(column, TILE)] = out_ref[:, other, pl.ds(column, TILE)]
 
     def two_tiles(pair, carry):
         build(odd_ref, 2 * pair + 1)
@@ -213,8 +217,7 @@
         build(odd_ref, tiles - 1)
         multiply(even_ref, tiles - 2)
         multiply(odd_ref, tiles - 1)
-    if not last:
-        other = pl.ds(pl.multiple_of((1 - following) * (beams - window), 16), window)
+    if not last and not inline:
         send_ref[...] = out_ref[:, other, :span]
 
 

time: 61.6 us -> 61.2 us (level)
  Pallas kernels: 20.5 us -> 19.1 us
  waiting for transfers between devices: 16.7 us -> 17.5 us
    pallas_call x18, Pallas kernels: 19.6 us -> 18.2 us  [merge(): pl.pallas_call(functools.partial(merge_kernel, level, plan, start, stop,...]
    ppermute x14, waiting for transfers between devices: 16.7 us -> 17.5 us  [from_partner(): return lax.ppermute(value, 'pulse', pairs)]
  transfers between devices with their start and end apart: 14 -> 14, of which waited for: 8 -> 8; matrix products, arithmetic and copies ran while one was open for 3% -> 3% of each run, Pallas kernels for 30% -> 28%
where the time goes in v12:
time: 61.2 us; the launch traced here: 61 us
  starting transfers between devices  21.6 us (35%)
  Pallas kernels  19.1 us (31%)
  waiting for transfers between devices  17.5 us (29%)
  other arithmetic  1.54 us (3%)
  local copies, waits for them, and re-layouts  1.05 us (2%)
    ppermute x14, starting transfers between devices, from_partner(): return lax.ppermute(value, 'pulse', pairs)  21.6 us
    pallas_call x18, Pallas kernels, merge(): pl.pallas_call(functools.partial(merge_kernel, level, plan, start, stop,...  18.2 us
    ppermute x14, waiting for transfers between devices, from_partner(): return lax.ppermute(value, 'pulse', pairs)  17.5 us
    add x2, other arithmetic, stacked(): total = total + lax.pad(piece, zero, ((top, below, 0), (left, right, 0)))  1.54 us
  transfers between devices with their start and end apart: 14, of which 8 were waited for; matrix products, arithmetic and copies ran while one was open for 3% of the time, Pallas kernels for 28%

profile of v12, /device:TPU:0, one launch (start us, length us, event | category | flops | bytes accessed | tf_op | source)
XLA Modules:
  0.0 61.0 jit_solution(7144213261832374444)
XLA Ops:
  0.0 0.5 collective-permute-start
  0.5 0.7 %pad_add_fusion.real_ref = f32[14,128]{1,0:T(8,128)S(1)} fusion(f32[4,16]{1,0:T(4,128)} %bitcast.3, f32[8,128]{1,0:T(8,128)} %bitcast.2, bf16[2,32]{1,0:T(2,128)(2,1)} %param.8), kind=kLoop, calls=%fused_computation.5 | loop fusion | flops 5376 | bytes 11648 | tf_op jit(solution)/shard_map/add | solution.py:91
  1.2 0.8 %pad_add_fusion.1.whole_ref = s32[12,128]{1,0:T(8,128)S(1)} fusion(s32[4,64]{1,0:T(4,128)} %param.11, s32[4,16]{1,0:T(4,128)} %param.12, s32[4,16]{1,0:T(4,128)} %param.13), kind=kLoop, calls=%fused_computation.6 | loop fusion | flops 4608 | bytes 7680 | tf_op jit(solution)/shard_map/add | solution.py:91
  2.0 0.9 %mixing.1 = (bf16[4,256,768]{2,1,0:T(8,128)(2,1)S(1)}, f32[4,8,128]{2,1,0:T(8,128)S(1)}) custom-call(s32[12,128]{1,0:T(8,128)S(1)} %pad_add_fusion.1.whole_ref, f32[14,128]{1,0:T(8,128)S(1)} %pad_add_fusion.real_ref), custom_call_target="tpu_custom_call" | custom-call | flops 2000000000 | bytes 1572864 | tf_op jit(solution)/shard_map/mixing/pallas_call | solution.py:121
  2.9 0.1 collective-permute-done.refs_3_
  3.0 0.3 copy-done
  3.2 1.1 %merge_0.3 = (bf16[2,64,1024]{2,1,0:T(8,128)(2,1)S(1)}, bf16[2,48,1024]{2,1,0:T(8,128)(2,1)S(1)}) custom-call(f32[4,8,128]{2,1,0:T(8,128)S(1)} %get-tuple-element.33.refs_0_, bf16[4,256,768]{2,1,0:T(8,128)(2,1)S(1)} %get-tuple-element.34.refs_1_.refs_4_, bf16[2,64,4096]{2,1,0:T(8,128)(2,1)S(1)} %copy-done, ...), custom_call_target="tpu_custom_call" | custom-call | flops 1610612736 | tf_op jit(solution)/shard_map/merge_0/pallas_call | solution.py:245
  4.3 2.7 %collective-permute-start.1 = (bf16[2,48,1024]{2,1,0:T(8,128)(2,1)S(1)}, bf16[2,48,1024]{2,1,0:T(8,128)(2,1)S(1)}, u32[]{:S(2)}, u32[]{:S(2)}) collective-permute-start(bf16[2,48,1024]{2,1,0:T(8,128)(2,1)S(1)} %get-tuple-element.36), channel_id=1, source_target_pairs={{0,2},{1,3},{2,0},{3,1},{4,6},{5,7},{6,4},{7,5},{8,10},{9,11},{10,... | collective-permute-start | bytes 589832 | tf_op jit(solution)/shard_map/ppermute | solution.py:316
  7.0 1.1 %merge_0.4 = (bf16[2,64,1024]{2,1,0:T(8,128)(2,1)S(1)}, bf16[2,48,1024]{2,1,0:T(8,128)(2,1)S(1)}) custom-call(f32[4,8,128]{2,1,0:T(8,128)S(1)} %get-tuple-element.33.refs_0_, bf16[4,256,768]{2,1,0:T(8,128)(2,1)S(1)} %get-tuple-element.34.refs_1_.refs_4_, bf16[2,64,4096]{2,1,0:T(8,128)(2,1)S(1)} %copy-done, ...), custom_call_target="tpu_custom_call" | custom-call | flops 1610612736 | tf_op jit(solution)/shard_map/merge_0/pallas_call | solution.py:245
  8.1 0.1 collective-permute-start.3
  8.1 2.5 %merge_0.5 = (bf16[2,64,2048]{2,1,0:T(8,128)(2,1)S(1)}, bf16[2,48,2048]{2,1,0:T(8,128)(2,1)S(1)}) custom-call(f32[4,8,128]{2,1,0:T(8,128)S(1)} %get-tuple-element.33.refs_0_, bf16[4,256,768]{2,1,0:T(8,128)(2,1)S(1)} %get-tuple-element.34.refs_1_.refs_4_, bf16[2,64,4096]{2,1,0:T(8,128)(2,1)S(1)} %copy-done, ...), custom_call_target="tpu_custom_call" | custom-call | flops 3221225472 | tf_op jit(solution)/shard_map/merge_0/pallas_call | solution.py:245
  10.6 2.1 %collective-permute-start.5 = (bf16[2,48,2048]{2,1,0:T(8,128)(2,1)S(1)}, bf16[2,48,2048]{2,1,0:T(8,128)(2,1)S(1)}, u32[]{:S(2)}, u32[]{:S(2)}) collective-permute-start(bf16[2,48,2048]{2,1,0:T(8,128)(2,1)S(1)} %get-tuple-element.45), channel_id=1, source_target_pairs={{0,2},{1,3},{2,0},{3,1},{4,6},{5,7},{6,4},{7,5},{8,10},{9,11},{10,... | collective-permute-start | bytes 1179656 | tf_op jit(solution)/shard_map/ppermute | solution.py:316
  12.7 0.0 collective-permute-done.1.refs_3_.refs_4_
  12.7 1.0 %merge_1.5 = (bf16[2,64,1024]{2,1,0:T(8,128)(2,1)S(1)}, bf16[2,48,896]{2,1,0:T(8,128)(2,1)S(1)}) custom-call(f32[4,8,128]{2,1,0:T(8,128)S(1)} %get-tuple-element.33.refs_0_, bf16[4,256,768]{2,1,0:T(8,128)(2,1)S(1)} %get-tuple-element.34.refs_1_.refs_4_, bf16[2,64,1024]{2,1,0:T(8,128)(2,1)S(1)} %get-tuple-element.35.refs_4_.refs_2_, ...), custom_call_target="tpu_custom_call" | custom-call | flops 1409286144 | tf_op jit(solution)/shard_map/merge_1/pallas_call | solution.py:245
  13.8 2.1 %collective-permute-start.2 = (bf16[2,48,896]{2,1,0:T(8,128)(2,1)S(1)}, bf16[2,48,896]{2,1,0:T(8,128)(2,1)S(1)}, u32[]{:S(2)}, u32[]{:S(2)}) collective-permute-start(bf16[2,48,896]{2,1,0:T(8,128)(2,1)S(1)} %get-tuple-element.40), channel_id=1, source_target_pairs={{0,4},{1,5},{2,6},{3,7},{4,0},{5,1},{6,2},{7,3},{8,12},{9,13},{10,... | collective-permute-start | bytes 516104 | tf_op jit(solution)/shard_map/ppermute | solution.py:316
  15.9 1.1 %collective-permute-done.3.refs_5_.refs_4_ = bf16[2,48,1024]{2,1,0:T(8,128)(2,1)S(1)} collective-permute-done((bf16[2,48,1024]{2,1,0:T(8,128)(2,1)S(1)}, bf16[2,48,1024]{2,1,0:T(8,128)(2,1)S(1)}, u32[]{:S(2)}, u32[]{:S(2)}) %collective-permute-start.3) | collective-permute-done | bytes 196640 | tf_op jit(solution)/shard_map/ppermute | solution.py:316
  17.0 1.1 %merge_1.6 = (bf16[2,64,1024]{2,1,0:T(8,128)(2,1)S(1)}, bf16[2,48,1024]{2,1,0:T(8,128)(2,1)S(1)}) custom-call(f32[4,8,128]{2,1,0:T(8,128)S(1)} %get-tuple-element.33.refs_0_, bf16[4,256,768]{2,1,0:T(8,128)(2,1)S(1)} %get-tuple-element.34.refs_1_.refs_4_, bf16[2,64,1024]{2,1,0:T(8,128)(2,1)S(1)} %get-tuple-element.35.refs_4_.refs_2_, ...), custom_call_target="tpu_custom_call" | custom-call | flops 1610612736 | tf_op jit(solution)/shard_map/merge_1/pallas_call | solution.py:245
  18.0 2.1 %collective-permute-start.6 = (bf16[2,48,1024]{2,1,0:T(8,128)(2,1)S(1)}, bf16[2,48,1024]{2,1,0:T(8,128)(2,1)S(1)}, u32[]{:S(2)}, u32[]{:S(2)}) collective-permute-start(bf16[2,48,1024]{2,1,0:T(8,128)(2,1)S(1)} %get-tuple-element.46), channel_id=1, source_target_pairs={{0,4},{1,5},{2,6},{3,7},{4,0},{5,1},{6,2},{7,3},{8,12},{9,13},{10,... | collective-permute-start | bytes 589832 | tf_op jit(solution)/shard_map/ppermute | solution.py:316
  20.1 0.0 collective-permute-done.2.refs_3_.refs_4_
  20.1 0.9 %merge_2.5 = (bf16[2,64,768]{2,1,0:T(8,128)(2,1)S(1)}, bf16[2,48,768]{2,1,0:T(8,128)(2,1)S(1)}) custom-call(f32[4,8,128]{2,1,0:T(8,128)S(1)} %get-tuple-element.33.refs_0_, bf16[4,256,768]{2,1,0:T(8,128)(2,1)S(1)} %get-tuple-element.34.refs_1_.refs_4_, bf16[2,64,1024]{2,1,0:T(8,128)(2,1)S(1)} %get-tuple-element.39.refs_6_.refs_2_, ...), custom_call_target="tpu_custom_call" | custom-call | flops 1207959552 | tf_op jit(solution)/shard_map/merge_2/pallas_call | solution.py:245
  21.0 2.7 %collective-permute-start.4 = (bf16[2,48,768]{2,1,0:T(8,128)(2,1)S(1)}, bf16[2,48,768]{2,1,0:T(8,128)(2,1)S(1)}, u32[]{:S(2)}, u32[]{:S(2)}) collective-permute-start(bf16[2,48,768]{2,1,0:T(8,128)(2,1)S(1)} %get-tuple-element.44), channel_id=1, source_target_pairs={{0,8},{1,9},{2,10},{3,11},{4,12},{5,13},{6,14},{7,15},{8,0},{9,1},... | collective-permute-start | bytes 442376 | tf_op jit(solution)/shard_map/ppermute | solution.py:316
  23.6 1.5 %collective-permute-done.5.refs_5_.refs_3_ = bf16[2,48,2048]{2,1,0:T(8,128)(2,1)S(1)} collective-permute-done((bf16[2,48,2048]{2,1,0:T(8,128)(2,1)S(1)}, bf16[2,48,2048]{2,1,0:T(8,128)(2,1)S(1)}, u32[]{:S(2)}, u32[]{:S(2)}) %collective-permute-start.5) | collective-permute-done | bytes 393248 | tf_op jit(solution)/shard_map/ppermute | solution.py:316
  25.1 0.8 %merge_1.7 = (bf16[2,64,768]{2,1,0:T(8,128)(2,1)S(1)}, bf16[2,48,768]{2,1,0:T(8,128)(2,1)S(1)}) custom-call(f32[4,8,128]{2,1,0:T(8,128)S(1)} %get-tuple-element.33.refs_0_, bf16[4,256,768]{2,1,0:T(8,128)(2,1)S(1)} %get-tuple-element.34.refs_1_.refs_4_, bf16[2,64,1024]{2,1,0:T(8,128)(2,1)S(1)} %get-tuple-element.37.refs_4_.refs_3_.refs_2_, ...), custom_call_target="tpu_custom_call" | custom-call | flops 1207959552 | tf_op jit(solution)/shard_map/merge_1/pallas_call | solution.py:245
  25.9 1.9 %collective-permute-start.8 = (bf16[2,48,768]{2,1,0:T(8,128)(2,1)S(1)}, bf16[2,48,768]{2,1,0:T(8,128)(2,1)S(1)}, u32[]{:S(2)}, u32[]{:S(2)}) collective-permute-start(bf16[2,48,768]{2,1,0:T(8,128)(2,1)S(1)} %get-tuple-element.51), channel_id=1, source_target_pairs={{0,4},{1,5},{2,6},{3,7},{4,0},{5,1},{6,2},{7,3},{8,12},{9,13},{10,... | collective-permute-start | bytes 442376 | tf_op jit(solution)/shard_map/ppermute | solution.py:316
  27.8 1.1 %merge_2.6 = (bf16[2,64,1024]{2,1,0:T(8,128)(2,1)S(1)}, bf16[2,48,1024]{2,1,0:T(8,128)(2,1)S(1)}) custom-call(f32[4,8,128]{2,1,0:T(8,128)S(1)} %get-tuple-element.33.refs_0_, bf16[4,256,768]{2,1,0:T(8,128)(2,1)S(1)} %get-tuple-element.34.refs_1_.refs_4_, bf16[2,64,1024]{2,1,0:T(8,128)(2,1)S(1)} %get-tuple-element.39.refs_6_.refs_2_, ...), custom_call_target="tpu_custom_call" | custom-call | flops 1610612736 | tf_op jit(solution)/shard_map/merge_2/pallas_call | solution.py:245
  28.9 2.7 %collective-permute-start.7 = (bf16[2,48,1024]{2,1,0:T(8,128)(2,1)S(1)}, bf16[2,48,1024]{2,1,0:T(8,128)(2,1)S(1)}, u32[]{:S(2)}, u32[]{:S(2)}) collective-permute-start(bf16[2,48,1024]{2,1,0:T(8,128)(2,1)S(1)} %get-tuple-element.50), channel_id=1, source_target_pairs={{0,8},{1,9},{2,10},{3,11},{4,12},{5,13},{6,14},{7,15},{8,0},{9,1},... | collective-permute-start | bytes 589832 | tf_op jit(solution)/shard_map/ppermute | solution.py:316
  31.6 0.9 %merge_1.8 = (bf16[2,64,768]{2,1,0:T(8,128)(2,1)S(1)}, bf16[2,48,768]{2,1,0:T(8,128)(2,1)S(1)}) custom-call(f32[4,8,128]{2,1,0:T(8,128)S(1)} %get-tuple-element.33.refs_0_, bf16[4,256,768]{2,1,0:T(8,128)(2,1)S(1)} %get-tuple-element.34.refs_1_.refs_4_, bf16[2,64,2048]{2,1,0:T(8,128)(2,1)S(1)} %get-tuple-element.38.refs_4_.refs_3_.refs_2_, ...), custom_call_target="tpu_custom_call" | custom-call | flops 1207959552 | tf_op jit(solution)/shard_map/merge_1/pallas_call | solution.py:245
  32.4 0.5 collective-permute-start.10
  32.9 0.8 %merge_3.5.refs_4_ = bf16[2,64,768]{2,1,0:T(8,128)(2,1)S(1)} custom-call(f32[4,8,128]{2,1,0:T(8,128)S(1)} %get-tuple-element.33.refs_0_, bf16[4,256,768]{2,1,0:T(8,128)(2,1)S(1)} %get-tuple-element.34.refs_1_.refs_4_, bf16[2,64,768]{2,1,0:T(8,128)(2,1)S(1)} %get-tuple-element.43.refs_6_.refs_2_, ...), custom_call_target="tpu_custom_call" | custom-call | flops 251658240 | tf_op jit(solution)/shard_map/merge_3/pallas_call | solution.py:245
  33.8 0.9 %merge_1.9 = (bf16[2,64,768]{2,1,0:T(8,128)(2,1)S(1)}, bf16[2,48,640]{2,1,0:T(8,128)(2,1)S(1)}) custom-call(f32[4,8,128]{2,1,0:T(8,128)S(1)} %get-tuple-element.33.refs_0_, bf16[4,256,768]{2,1,0:T(8,128)(2,1)S(1)} %get-tuple-element.34.refs_1_.refs_4_, bf16[2,64,2048]{2,1,0:T(8,128)(2,1)S(1)} %get-tuple-element.38.refs_4_.refs_3_.refs_2_, ...), custom_call_target="tpu_custom_call" | custom-call | flops 1006632960 | tf_op jit(solution)/shard_map/merge_1/pallas_call | solution.py:245
  34.7 1.7 %collective-permute-start.11 = (bf16[2,48,640]{2,1,0:T(8,128)(2,1)S(1)}, bf16[2,48,640]{2,1,0:T(8,128)(2,1)S(1)}, u32[]{:S(2)}, u32[]{:S(2)}) collective-permute-start(bf16[2,48,640]{2,1,0:T(8,128)(2,1)S(1)} %get-tuple-element.56), channel_id=1, source_target_pairs={{0,4},{1,5},{2,6},{3,7},{4,0},{5,1},{6,2},{7,3},{8,12},{9,13},{10,... | collective-permute-start | bytes 368648 | tf_op jit(solution)/shard_map/ppermute | solution.py:316
  36.3 0.9 %merge_2.7 = (bf16[2,64,768]{2,1,0:T(8,128)(2,1)S(1)}, bf16[2,48,768]{2,1,0:T(8,128)(2,1)S(1)}) custom-call(f32[4,8,128]{2,1,0:T(8,128)S(1)} %get-tuple-element.33.refs_0_, bf16[4,256,768]{2,1,0:T(8,128)(2,1)S(1)} %get-tuple-element.34.refs_1_.refs_4_, bf16[2,64,1024]{2,1,0:T(8,128)(2,1)S(1)} %get-tuple-element.42.refs_4_.refs_3_.refs_2_, ...), custom_call_target="tpu_custom_call" | custom-call | flops 1207959552 | tf_op jit(solution)/shard_map/merge_2/pallas_call | solution.py:245
  37.2 0.4 collective-permute-start.9
  37.6 3.7 %collective-permute-done.7.refs_5_.refs_4_ = bf16[2,48,1024]{2,1,0:T(8,128)(2,1)S(1)} collective-permute-done((bf16[2,48,1024]{2,1,0:T(8,128)(2,1)S(1)}, bf16[2,48,1024]{2,1,0:T(8,128)(2,1)S(1)}, u32[]{:S(2)}, u32[]{:S(2)}) %collective-permute-start.7) | collective-permute-done | bytes 196640 | tf_op jit(solution)/shard_map/ppermute | solution.py:316
  41.3 1.0 %merge_3.6.refs_6_ = bf16[2,64,1024]{2,1,0:T(8,128)(2,1)S(1)} custom-call(f32[4,8,128]{2,1,0:T(8,128)S(1)} %get-tuple-element.33.refs_0_, bf16[4,256,768]{2,1,0:T(8,128)(2,1)S(1)} %get-tuple-element.34.refs_1_.refs_4_, bf16[2,64,768]{2,1,0:T(8,128)(2,1)S(1)} %get-tuple-element.43.refs_6_.refs_2_, ...), custom_call_target="tpu_custom_call" | custom-call | flops 402653184 | tf_op jit(solution)/shard_map/merge_3/pallas_call | solution.py:245
  42.3 2.4 %collective-permute-done.10.refs_5_.refs_4_ = bf16[2,48,768]{2,1,0:T(8,128)(2,1)S(1)} collective-permute-done((bf16[2,48,768]{2,1,0:T(8,128)(2,1)S(1)}, bf16[2,48,768]{2,1,0:T(8,128)(2,1)S(1)}, u32[]{:S(2)}, u32[]{:S(2)}) %collective-permute-start.10) | collective-permute-done | bytes 147488 | tf_op jit(solution)/shard_map/ppermute | solution.py:316
  44.7 0.9 %merge_2.8 = (bf16[2,64,768]{2,1,0:T(8,128)(2,1)S(1)}, bf16[2,48,768]{2,1,0:T(8,128)(2,1)S(1)}) custom-call(f32[4,8,128]{2,1,0:T(8,128)S(1)} %get-tuple-element.33.refs_0_, bf16[4,256,768]{2,1,0:T(8,128)(2,1)S(1)} %get-tuple-element.34.refs_1_.refs_4_, bf16[2,64,768]{2,1,0:T(8,128)(2,1)S(1)} %get-tuple-element.47.refs_6_.refs_3_.refs_2_, ...), custom_call_target="tpu_custom_call" | custom-call | flops 1207959552 | tf_op jit(solution)/shard_map/merge_2/pallas_call | solution.py:245
  45.5 0.1 collective-permute-start.12
  45.6 0.7 %collective-permute-done.11.refs_5_ = bf16[2,48,640]{2,1,0:T(8,128)(2,1)S(1)} collective-permute-done((bf16[2,48,640]{2,1,0:T(8,128)(2,1)S(1)}, bf16[2,48,640]{2,1,0:T(8,128)(2,1)S(1)}, u32[]{:S(2)}, u32[]{:S(2)}) %collective-permute-start.11) | collective-permute-done | bytes 122912 | tf_op jit(solution)/shard_map/ppermute | solution.py:316
  46.3 0.9 %merge_2.9 = (bf16[2,64,768]{2,1,0:T(8,128)(2,1)S(1)}, bf16[2,48,768]{2,1,0:T(8,128)(2,1)S(1)}) custom-call(f32[4,8,128]{2,1,0:T(8,128)S(1)} %get-tuple-element.33.refs_0_, bf16[4,256,768]{2,1,0:T(8,128)(2,1)S(1)} %get-tuple-element.34.refs_1_.refs_4_, bf16[2,64,768]{2,1,0:T(8,128)(2,1)S(1)} %get-tuple-element.49.refs_4_.refs_3_.refs_2_, ...), custom_call_target="tpu_custom_call" | custom-call | flops 1207959552 | tf_op jit(solution)/shard_map/merge_2/pallas_call | solution.py:245
  47.2 2.3 %collective-permute-start.13 = (bf16[2,48,768]{2,1,0:T(8,128)(2,1)S(1)}, bf16[2,48,768]{2,1,0:T(8,128)(2,1)S(1)}, u32[]{:S(2)}, u32[]{:S(2)}) collective-permute-start(bf16[2,48,768]{2,1,0:T(8,128)(2,1)S(1)} %get-tuple-element.60), channel_id=1, source_target_pairs={{0,8},{1,9},{2,10},{3,11},{4,12},{5,13},{6,14},{7,15},{8,0},{9,1},... | collective-permute-start | bytes 442376 | tf_op jit(solution)/shard_map/ppermute | solution.py:316
  49.5 0.8 %merge_3.7.refs_6_ = bf16[2,64,768]{2,1,0:T(8,128)(2,1)S(1)} custom-call(f32[4,8,128]{2,1,0:T(8,128)S(1)} %get-tuple-element.33.refs_0_, bf16[4,256,768]{2,1,0:T(8,128)(2,1)S(1)} %get-tuple-element.34.refs_1_.refs_4_, bf16[2,64,1024]{2,1,0:T(8,128)(2,1)S(1)} %get-tuple-element.48.refs_4_.refs_3_.refs_2_, ...), custom_call_target="tpu_custom_call" | custom-call | flops 301989888 | tf_op jit(solution)/shard_map/merge_3/pallas_call | solution.py:245
  50.3 6.4 %collective-permute-done.12.refs_5_.refs_4_ = bf16[2,48,768]{2,1,0:T(8,128)(2,1)S(1)} collective-permute-done((bf16[2,48,768]{2,1,0:T(8,128)(2,1)S(1)}, bf16[2,48,768]{2,1,0:T(8,128)(2,1)S(1)}, u32[]{:S(2)}, u32[]{:S(2)}) %collective-permute-start.12) | collective-permute-done | bytes 147488 | tf_op jit(solution)/shard_map/ppermute | solution.py:316
  56.7 0.8 %merge_3.8.refs_6_ = bf16[2,64,768]{2,1,0:T(8,128)(2,1)S(1)} custom-call(f32[4,8,128]{2,1,0:T(8,128)S(1)} %get-tuple-element.33.refs_0_, bf16[4,256,768]{2,1,0:T(8,128)(2,1)S(1)} %get-tuple-element.34.refs_1_.refs_4_, bf16[2,64,768]{2,1,0:T(8,128)(2,1)S(1)} %get-tuple-element.53.refs_6_.refs_3_.refs_2_, ...), custom_call_target="tpu_custom_call" | custom-call | flops 301989888 | tf_op jit(solution)/shard_map/merge_3/pallas_call | solution.py:245
  57.5 0.0 copy-start.1
  57.6 1.7 %collective-permute-done.13.refs_5_ = bf16[2,48,768]{2,1,0:T(8,128)(2,1)S(1)} collective-permute-done((bf16[2,48,768]{2,1,0:T(8,128)(2,1)S(1)}, bf16[2,48,768]{2,1,0:T(8,128)(2,1)S(1)}, u32[]{:S(2)}, u32[]{:S(2)}) %collective-permute-start.13) | collective-permute-done | bytes 147488 | tf_op jit(solution)/shard_map/ppermute | solution.py:316
  59.3 1.0 %merge_3.9 = bf16[2,64,1024]{2,1,0:T(8,128)(2,1)S(1)} custom-call(f32[4,8,128]{2,1,0:T(8,128)S(1)} %get-tuple-element.33.refs_0_, bf16[4,256,768]{2,1,0:T(8,128)(2,1)S(1)} %get-tuple-element.34.refs_1_.refs_4_, bf16[2,64,768]{2,1,0:T(8,128)(2,1)S(1)} %get-tuple-element.57.refs_6_.refs_3_.refs_2_, bf16[2,64,768]{2,1,0:T(8,128)(2,1)S(1)} %get-tuple-element.58.refs_6_.refs_3_, ...), custom_call_target="tpu_custom_call" | custom-call | flops 352321536 | tf_op jit(solution)/shard_map/merge_3/pallas_call | solution.py:245
  60.3 0.7 %slice_dynamic-update-slice_fusion = bf16[2,64,4096]{2,1,0:T(8,128)(2,1)} fusion(bf16[2,64,4096]{2,1,0:T(8,128)(2,1)} %copy-done.1, bf16[2,64,1024]{2,1,0:T(8,128)(2,1)S(1)} %merge_3.9), kind=kLoop, calls=%fused_computation | loop fusion | bytes 458752 | tf_op jit(solution)/shard_map/concatenate | solution.py:342
  (10 shorter events, 0.1 us)
Async XLA Ops:
  0.0 3.0 %collective-permute-start = (bf16[2,64,4096]{2,1,0:T(8,128)(2,1)}, bf16[2,64,4096]{2,1,0:T(8,128)(2,1)S(1)}, u32[]{:S(2)}, u32[]{:S(2)}) collective-permute-start(bf16[2,64,4096]{2,1,0:T(8,128)(2,1)} %refs_2_.5), channel_id=1, source_target_pairs={{0,1},{1,0},{2,3},{3,2},{4,5},{5,4},{6,7},{7,6},{8,9},{9,8},{10,11... | collective-permute-start | bytes 3145736 | tf_op jit(solution)/shard_map/ppermute | solution.py:316
  2.0 1.2 %copy-start = (bf16[2,64,4096]{2,1,0:T(8,128)(2,1)S(1)}, bf16[2,64,4096]{2,1,0:T(8,128)(2,1)}, u32[]{:S(2)}) copy-start(bf16[2,64,4096]{2,1,0:T(8,128)(2,1)} %refs_2_.5) | copy-start | bytes 3145732
  4.3 8.4 %collective-permute-start.1 = (bf16[2,48,1024]{2,1,0:T(8,128)(2,1)S(1)}, bf16[2,48,1024]{2,1,0:T(8,128)(2,1)S(1)}, u32[]{:S(2)}, u32[]{:S(2)}) collective-permute-start(bf16[2,48,1024]{2,1,0:T(8,128)(2,1)S(1)} %get-tuple-element.36), channel_id=1, source_target_pairs={{0,2},{1,3},{2,0},{3,1},{4,6},{5,7},{6,4},{7,5},{8,10},{9,11},{10,... | collective-permute-start | bytes 589832 | tf_op jit(solution)/shard_map/ppermute | solution.py:316
  8.1 8.9 %collective-permute-start.3 = (bf16[2,48,1024]{2,1,0:T(8,128)(2,1)S(1)}, bf16[2,48,1024]{2,1,0:T(8,128)(2,1)S(1)}, u32[]{:S(2)}, u32[]{:S(2)}) collective-permute-start(bf16[2,48,1024]{2,1,0:T(8,128)(2,1)S(1)} %get-tuple-element.41), channel_id=1, source_target_pairs={{0,2},{1,3},{2,0},{3,1},{4,6},{5,7},{6,4},{7,5},{8,10},{9,11},{10,... | collective-permute-start | bytes 589832 | tf_op jit(solution)/shard_map/ppermute | solution.py:316
  10.6 14.5 %collective-permute-start.5 = (bf16[2,48,2048]{2,1,0:T(8,128)(2,1)S(1)}, bf16[2,48,2048]{2,1,0:T(8,128)(2,1)S(1)}, u32[]{:S(2)}, u32[]{:S(2)}) collective-permute-start(bf16[2,48,2048]{2,1,0:T(8,128)(2,1)S(1)} %get-tuple-element.45), channel_id=1, source_target_pairs={{0,2},{1,3},{2,0},{3,1},{4,6},{5,7},{6,4},{7,5},{8,10},{9,11},{10,... | collective-permute-start | bytes 1179656 | tf_op jit(solution)/shard_map/ppermute | solution.py:316
  13.8 6.3 %collective-permute-start.2 = (bf16[2,48,896]{2,1,0:T(8,128)(2,1)S(1)}, bf16[2,48,896]{2,1,0:T(8,128)(2,1)S(1)}, u32[]{:S(2)}, u32[]{:S(2)}) collective-permute-start(bf16[2,48,896]{2,1,0:T(8,128)(2,1)S(1)} %get-tuple-element.40), channel_id=1, source_target_pairs={{0,4},{1,5},{2,6},{3,7},{4,0},{5,1},{6,2},{7,3},{8,12},{9,13},{10,... | collective-permute-start | bytes 516104 | tf_op jit(solution)/shard_map/ppermute | solution.py:316
  18.0 9.8 %collective-permute-start.6 = (bf16[2,48,1024]{2,1,0:T(8,128)(2,1)S(1)}, bf16[2,48,1024]{2,1,0:T(8,128)(2,1)S(1)}, u32[]{:S(2)}, u32[]{:S(2)}) collective-permute-start(bf16[2,48,1024]{2,1,0:T(8,128)(2,1)S(1)} %get-tuple-element.46), channel_id=1, source_target_pairs={{0,4},{1,5},{2,6},{3,7},{4,0},{5,1},{6,2},{7,3},{8,12},{9,13},{10,... | collective-permute-start | bytes 589832 | tf_op jit(solution)/shard_map/ppermute | solution.py:316
  21.0 12.0 %collective-permute-start.4 = (bf16[2,48,768]{2,1,0:T(8,128)(2,1)S(1)}, bf16[2,48,768]{2,1,0:T(8,128)(2,1)S(1)}, u32[]{:S(2)}, u32[]{:S(2)}) collective-permute-start(bf16[2,48,768]{2,1,0:T(8,128)(2,1)S(1)} %get-tuple-element.44), channel_id=1, source_target_pairs={{0,8},{1,9},{2,10},{3,11},{4,12},{5,13},{6,14},{7,15},{8,0},{9,1},... | collective-permute-start | bytes 442376 | tf_op jit(solution)/shard_map/ppermute | solution.py:316
  25.9 10.4 %collective-permute-start.8 = (bf16[2,48,768]{2,1,0:T(8,128)(2,1)S(1)}, bf16[2,48,768]{2,1,0:T(8,128)(2,1)S(1)}, u32[]{:S(2)}, u32[]{:S(2)}) collective-permute-start(bf16[2,48,768]{2,1,0:T(8,128)(2,1)S(1)} %get-tuple-element.51), channel_id=1, source_target_pairs={{0,4},{1,5},{2,6},{3,7},{4,0},{5,1},{6,2},{7,3},{8,12},{9,13},{10,... | collective-permute-start | bytes 442376 | tf_op jit(solution)/shard_map/ppermute | solution.py:316
  28.9 12.3 %collective-permute-start.7 = (bf16[2,48,1024]{2,1,0:T(8,128)(2,1)S(1)}, bf16[2,48,1024]{2,1,0:T(8,128)(2,1)S(1)}, u32[]{:S(2)}, u32[]{:S(2)}) collective-permute-start(bf16[2,48,1024]{2,1,0:T(8,128)(2,1)S(1)} %get-tuple-element.50), channel_id=1, source_target_pairs={{0,8},{1,9},{2,10},{3,11},{4,12},{5,13},{6,14},{7,15},{8,0},{9,1},... | collective-permute-start | bytes 589832 | tf_op jit(solution)/shard_map/ppermute | solution.py:316
  32.4 12.2 %collective-permute-start.10 = (bf16[2,48,768]{2,1,0:T(8,128)(2,1)S(1)}, bf16[2,48,768]{2,1,0:T(8,128)(2,1)S(1)}, u32[]{:S(2)}, u32[]{:S(2)}) collective-permute-start(bf16[2,48,768]{2,1,0:T(8,128)(2,1)S(1)} %get-tuple-element.55), channel_id=1, source_target_pairs={{0,4},{1,5},{2,6},{3,7},{4,0},{5,1},{6,2},{7,3},{8,12},{9,13},{10,... | collective-permute-start | bytes 442376 | tf_op jit(solution)/shard_map/ppermute | solution.py:316
  34.7 11.6 %collective-permute-start.11 = (bf16[2,48,640]{2,1,0:T(8,128)(2,1)S(1)}, bf16[2,48,640]{2,1,0:T(8,128)(2,1)S(1)}, u32[]{:S(2)}, u32[]{:S(2)}) collective-permute-start(bf16[2,48,640]{2,1,0:T(8,128)(2,1)S(1)} %get-tuple-element.56), channel_id=1, source_target_pairs={{0,4},{1,5},{2,6},{3,7},{4,0},{5,1},{6,2},{7,3},{8,12},{9,13},{10,... | collective-permute-start | bytes 368648 | tf_op jit(solution)/shard_map/ppermute | solution.py:316
  37.2 12.3 %collective-permute-start.9 = (bf16[2,48,768]{2,1,0:T(8,128)(2,1)S(1)}, bf16[2,48,768]{2,1,0:T(8,128)(2,1)S(1)}, u32[]{:S(2)}, u32[]{:S(2)}) collective-permute-start(bf16[2,48,768]{2,1,0:T(8,128)(2,1)S(1)} %get-tuple-element.54), channel_id=1, source_target_pairs={{0,8},{1,9},{2,10},{3,11},{4,12},{5,13},{6,14},{7,15},{8,0},{9,1},... | collective-permute-start | bytes 442376 | tf_op jit(solution)/shard_map/ppermute | solution.py:316
  45.5 11.2 %collective-permute-start.12 = (bf16[2,48,768]{2,1,0:T(8,128)(2,1)S(1)}, bf16[2,48,768]{2,1,0:T(8,128)(2,1)S(1)}, u32[]{:S(2)}, u32[]{:S(2)}) collective-permute-start(bf16[2,48,768]{2,1,0:T(8,128)(2,1)S(1)} %get-tuple-element.59), channel_id=1, source_target_pairs={{0,8},{1,9},{2,10},{3,11},{4,12},{5,13},{6,14},{7,15},{8,0},{9,1},... | collective-permute-start | bytes 442376 | tf_op jit(solution)/shard_map/ppermute | solution.py:316
  47.2 12.1 %collective-permute-start.13 = (bf16[2,48,768]{2,1,0:T(8,128)(2,1)S(1)}, bf16[2,48,768]{2,1,0:T(8,128)(2,1)S(1)}, u32[]{:S(2)}, u32[]{:S(2)}) collective-permute-start(bf16[2,48,768]{2,1,0:T(8,128)(2,1)S(1)} %get-tuple-element.60), channel_id=1, source_target_pairs={{0,8},{1,9},{2,10},{3,11},{4,12},{5,13},{6,14},{7,15},{8,0},{9,1},... | collective-permute-start | bytes 442376 | tf_op jit(solution)/shard_map/ppermute | solution.py:316
  57.5 2.7 %copy-start.1 = (bf16[2,64,4096]{2,1,0:T(8,128)(2,1)}, bf16[2,64,4096]{2,1,0:T(8,128)(2,1)S(1)}, u32[]{:S(2)}) copy-start(bf16[2,64,4096]{2,1,0:T(8,128)(2,1)S(1)} %constant_dynamic-update-slice_fusion) | copy-start | bytes 3145732

commit v13 on v12

--- a/solution.py
+++ b/solution.py
@@ -273,9 +273,9 @@
 
 MARKS = (
     (8, 16),
-    (7, 15, 21, 27),
-    (6, 14, 20, 26),
-    (5, 13, 19, 25),
+    (7, 15, 21, 28),
+    (6, 14, 20, 27),
+    (5, 13, 19, 26),
 )
 ORDER = (
     (0, 0), (0, 1), (0, 2), (1, 0), (1, 1), (2, 0), (1, 2), (2, 1), (1, 3), (3, 0), (1, 4),

time: 61.2 us -> 61 us (level)
  waiting for transfers between devices: 17.5 us -> 16.4 us
    ppermute x14, waiting for transfers between devices: 17.5 us -> 16.4 us  [from_partner(): return lax.ppermute(value, 'pulse', pairs)]
    ppermute x14, starting transfers between devices: 21.6 us -> 22.2 us  [from_partner(): return lax.ppermute(value, 'pulse', pairs)]
  transfers between devices with their start and end apart: 14 -> 14, of which waited for: 8 -> 7; matrix products, arithmetic and copies ran while one was open for 3% -> 3% of each run, Pallas kernels for 28% -> 29%
where the time goes in v13:
time: 61 us; the launch traced here: 60.9 us
  starting transfers between devices  22.2 us (36%)
  Pallas kernels  19.4 us (32%)
  waiting for transfers between devices  16.4 us (27%)
  other arithmetic  1.54 us (3%)
  local copies, waits for them, and re-layouts  1.05 us (2%)
    ppermute x14, starting transfers between devices, from_partner(): return lax.ppermute(value, 'pulse', pairs)  22.2 us
    pallas_call x18, Pallas kernels, merge(): pl.pallas_call(functools.partial(merge_kernel, level, plan, start, stop,...  18.5 us
    ppermute x14, waiting for transfers between devices, from_partner(): return lax.ppermute(value, 'pulse', pairs)  16.4 us
    add x2, other arithmetic, stacked(): total = total + lax.pad(piece, zero, ((top, below, 0), (left, right, 0)))  1.54 us
  transfers between devices with their start and end apart: 14, of which 7 were waited for; matrix products, arithmetic and copies ran while one was open for 3% of the time, Pallas kernels for 29%

profile of v13, /device:TPU:0, one launch (start us, length us, event | category | flops | bytes accessed | tf_op | source)
XLA Modules:
  0.0 60.9 jit_solution(6671527479665444451)
XLA Ops:
  0.0 0.5 collective-permute-start
  0.5 0.7 %pad_add_fusion.real_ref = f32[14,128]{1,0:T(8,128)S(1)} fusion(f32[4,16]{1,0:T(4,128)} %bitcast.3, f32[8,128]{1,0:T(8,128)} %bitcast.2, bf16[2,32]{1,0:T(2,128)(2,1)} %param.8), kind=kLoop, calls=%fused_computation.5 | loop fusion | flops 5376 | bytes 11648 | tf_op jit(solution)/shard_map/add | solution.py:91
  1.2 0.8 %pad_add_fusion.1.whole_ref = s32[12,128]{1,0:T(8,128)S(1)} fusion(s32[4,64]{1,0:T(4,128)} %param.11, s32[4,16]{1,0:T(4,128)} %param.12, s32[4,16]{1,0:T(4,128)} %param.13), kind=kLoop, calls=%fused_computation.6 | loop fusion | flops 4608 | bytes 7680 | tf_op jit(solution)/shard_map/add | solution.py:91
  2.0 0.9 %mixing.1 = (bf16[4,256,768]{2,1,0:T(8,128)(2,1)S(1)}, f32[4,8,128]{2,1,0:T(8,128)S(1)}) custom-call(s32[12,128]{1,0:T(8,128)S(1)} %pad_add_fusion.1.whole_ref, f32[14,128]{1,0:T(8,128)S(1)} %pad_add_fusion.real_ref), custom_call_target="tpu_custom_call" | custom-call | flops 2000000000 | bytes 1572864 | tf_op jit(solution)/shard_map/mixing/pallas_call | solution.py:121
  2.9 0.1 collective-permute-done.refs_3_
  3.0 0.3 copy-done
  3.2 1.1 %merge_0.3 = (bf16[2,64,1024]{2,1,0:T(8,128)(2,1)S(1)}, bf16[2,48,1024]{2,1,0:T(8,128)(2,1)S(1)}) custom-call(f32[4,8,128]{2,1,0:T(8,128)S(1)} %get-tuple-element.33.refs_0_, bf16[4,256,768]{2,1,0:T(8,128)(2,1)S(1)} %get-tuple-element.34.refs_1_.refs_4_, bf16[2,64,4096]{2,1,0:T(8,128)(2,1)S(1)} %copy-done, ...), custom_call_target="tpu_custom_call" | custom-call | flops 1610612736 | tf_op jit(solution)/shard_map/merge_0/pallas_call | solution.py:245
  4.3 2.7 %collective-permute-start.1 = (bf16[2,48,1024]{2,1,0:T(8,128)(2,1)S(1)}, bf16[2,48,1024]{2,1,0:T(8,128)(2,1)S(1)}, u32[]{:S(2)}, u32[]{:S(2)}) collective-permute-start(bf16[2,48,1024]{2,1,0:T(8,128)(2,1)S(1)} %get-tuple-element.36), channel_id=1, source_target_pairs={{0,2},{1,3},{2,0},{3,1},{4,6},{5,7},{6,4},{7,5},{8,10},{9,11},{10,... | collective-permute-start | bytes 589832 | tf_op jit(solution)/shard_map/ppermute | solution.py:316
  7.0 1.1 %merge_0.4 = (bf16[2,64,1024]{2,1,0:T(8,128)(2,1)S(1)}, bf16[2,48,1024]{2,1,0:T(8,128)(2,1)S(1)}) custom-call(f32[4,8,128]{2,1,0:T(8,128)S(1)} %get-tuple-element.33.refs_0_, bf16[4,256,768]{2,1,0:T(8,128)(2,1)S(1)} %get-tuple-element.34.refs_1_.refs_4_, bf16[2,64,4096]{2,1,0:T(8,128)(2,1)S(1)} %copy-done, ...), custom_call_target="tpu_custom_call" | custom-call | flops 1610612736 | tf_op jit(solution)/shard_map/merge_0/pallas_call | solution.py:245
  8.0 0.1 collective-permute-start.3
  8.1 2.5 %merge_0.5 = (bf16[2,64,2048]{2,1,0:T(8,128)(2,1)S(1)}, bf16[2,48,2048]{2,1,0:T(8,128)(2,1)S(1)}) custom-call(f32[4,8,128]{2,1,0:T(8,128)S(1)} %get-tuple-element.33.refs_0_, bf16[4,256,768]{2,1,0:T(8,128)(2,1)S(1)} %get-tuple-element.34.refs_1_.refs_4_, bf16[2,64,4096]{2,1,0:T(8,128)(2,1)S(1)} %copy-done, ...), custom_call_target="tpu_custom_call" | custom-call | flops 3221225472 | tf_op jit(solution)/shard_map/merge_0/pallas_call | solution.py:245
  10.6 2.1 %collective-permute-start.5 = (bf16[2,48,2048]{2,1,0:T(8,128)(2,1)S(1)}, bf16[2,48,2048]{2,1,0:T(8,128)(2,1)S(1)}, u32[]{:S(2)}, u32[]{:S(2)}) collective-permute-start(bf16[2,48,2048]{2,1,0:T(8,128)(2,1)S(1)} %get-tuple-element.45), channel_id=1, source_target_pairs={{0,2},{1,3},{2,0},{3,1},{4,6},{5,7},{6,4},{7,5},{8,10},{9,11},{10,... | collective-permute-start | bytes 1179656 | tf_op jit(solution)/shard_map/ppermute | solution.py:316
  12.7 0.0 collective-permute-done.1.refs_3_.refs_4_
  12.7 1.0 %merge_1.5 = (bf16[2,64,1024]{2,1,0:T(8,128)(2,1)S(1)}, bf16[2,48,896]{2,1,0:T(8,128)(2,1)S(1)}) custom-call(f32[4,8,128]{2,1,0:T(8,128)S(1)} %get-tuple-element.33.refs_0_, bf16[4,256,768]{2,1,0:T(8,128)(2,1)S(1)} %get-tuple-element.34.refs_1_.refs_4_, bf16[2,64,1024]{2,1,0:T(8,128)(2,1)S(1)} %get-tuple-element.35.refs_4_.refs_2_, ...), custom_call_target="tpu_custom_call" | custom-call | flops 1409286144 | tf_op jit(solution)/shard_map/merge_1/pallas_call | solution.py:245
  13.8 2.1 %collective-permute-start.2 = (bf16[2,48,896]{2,1,0:T(8,128)(2,1)S(1)}, bf16[2,48,896]{2,1,0:T(8,128)(2,1)S(1)}, u32[]{:S(2)}, u32[]{:S(2)}) collective-permute-start(bf16[2,48,896]{2,1,0:T(8,128)(2,1)S(1)} %get-tuple-element.40), channel_id=1, source_target_pairs={{0,4},{1,5},{2,6},{3,7},{4,0},{5,1},{6,2},{7,3},{8,12},{9,13},{10,... | collective-permute-start | bytes 516104 | tf_op jit(solution)/shard_map/ppermute | solution.py:316
  15.9 1.1 %collective-permute-done.3.refs_5_.refs_4_ = bf16[2,48,1024]{2,1,0:T(8,128)(2,1)S(1)} collective-permute-done((bf16[2,48,1024]{2,1,0:T(8,128)(2,1)S(1)}, bf16[2,48,1024]{2,1,0:T(8,128)(2,1)S(1)}, u32[]{:S(2)}, u32[]{:S(2)}) %collective-permute-start.3) | collective-permute-done | bytes 196640 | tf_op jit(solution)/shard_map/ppermute | solution.py:316
  16.9 1.1 %merge_1.6 = (bf16[2,64,1024]{2,1,0:T(8,128)(2,1)S(1)}, bf16[2,48,1024]{2,1,0:T(8,128)(2,1)S(1)}) custom-call(f32[4,8,128]{2,1,0:T(8,128)S(1)} %get-tuple-element.33.refs_0_, bf16[4,256,768]{2,1,0:T(8,128)(2,1)S(1)} %get-tuple-element.34.refs_1_.refs_4_, bf16[2,64,1024]{2,1,0:T(8,128)(2,1)S(1)} %get-tuple-element.35.refs_4_.refs_2_, ...), custom_call_target="tpu_custom_call" | custom-call | flops 1610612736 | tf_op jit(solution)/shard_map/merge_1/pallas_call | solution.py:245
  18.0 2.1 %collective-permute-start.6 = (bf16[2,48,1024]{2,1,0:T(8,128)(2,1)S(1)}, bf16[2,48,1024]{2,1,0:T(8,128)(2,1)S(1)}, u32[]{:S(2)}, u32[]{:S(2)}) collective-permute-start(bf16[2,48,1024]{2,1,0:T(8,128)(2,1)S(1)} %get-tuple-element.46), channel_id=1, source_target_pairs={{0,4},{1,5},{2,6},{3,7},{4,0},{5,1},{6,2},{7,3},{8,12},{9,13},{10,... | collective-permute-start | bytes 589832 | tf_op jit(solution)/shard_map/ppermute | solution.py:316
  20.1 0.9 %merge_2.5 = (bf16[2,64,768]{2,1,0:T(8,128)(2,1)S(1)}, bf16[2,48,768]{2,1,0:T(8,128)(2,1)S(1)}) custom-call(f32[4,8,128]{2,1,0:T(8,128)S(1)} %get-tuple-element.33.refs_0_, bf16[4,256,768]{2,1,0:T(8,128)(2,1)S(1)} %get-tuple-element.34.refs_1_.refs_4_, bf16[2,64,1024]{2,1,0:T(8,128)(2,1)S(1)} %get-tuple-element.39.refs_6_.refs_2_, ...), custom_call_target="tpu_custom_call" | custom-call | flops 1207959552 | tf_op jit(solution)/shard_map/merge_2/pallas_call | solution.py:245
  21.0 2.7 %collective-permute-start.4 = (bf16[2,48,768]{2,1,0:T(8,128)(2,1)S(1)}, bf16[2,48,768]{2,1,0:T(8,128)(2,1)S(1)}, u32[]{:S(2)}, u32[]{:S(2)}) collective-permute-start(bf16[2,48,768]{2,1,0:T(8,128)(2,1)S(1)} %get-tuple-element.44), channel_id=1, source_target_pairs={{0,8},{1,9},{2,10},{3,11},{4,12},{5,13},{6,14},{7,15},{8,0},{9,1},... | collective-permute-start | bytes 442376 | tf_op jit(solution)/shard_map/ppermute | solution.py:316
  23.6 1.5 %collective-permute-done.5.refs_5_.refs_3_ = bf16[2,48,2048]{2,1,0:T(8,128)(2,1)S(1)} collective-permute-done((bf16[2,48,2048]{2,1,0:T(8,128)(2,1)S(1)}, bf16[2,48,2048]{2,1,0:T(8,128)(2,1)S(1)}, u32[]{:S(2)}, u32[]{:S(2)}) %collective-permute-start.5) | collective-permute-done | bytes 393248 | tf_op jit(solution)/shard_map/ppermute | solution.py:316
  25.1 0.8 %merge_1.7 = (bf16[2,64,768]{2,1,0:T(8,128)(2,1)S(1)}, bf16[2,48,768]{2,1,0:T(8,128)(2,1)S(1)}) custom-call(f32[4,8,128]{2,1,0:T(8,128)S(1)} %get-tuple-element.33.refs_0_, bf16[4,256,768]{2,1,0:T(8,128)(2,1)S(1)} %get-tuple-element.34.refs_1_.refs_4_, bf16[2,64,1024]{2,1,0:T(8,128)(2,1)S(1)} %get-tuple-element.37.refs_4_.refs_3_.refs_2_, ...), custom_call_target="tpu_custom_call" | custom-call | flops 1207959552 | tf_op jit(solution)/shard_map/merge_1/pallas_call | solution.py:245
  25.9 1.9 %collective-permute-start.8 = (bf16[2,48,768]{2,1,0:T(8,128)(2,1)S(1)}, bf16[2,48,768]{2,1,0:T(8,128)(2,1)S(1)}, u32[]{:S(2)}, u32[]{:S(2)}) collective-permute-start(bf16[2,48,768]{2,1,0:T(8,128)(2,1)S(1)} %get-tuple-element.51), channel_id=1, source_target_pairs={{0,4},{1,5},{2,6},{3,7},{4,0},{5,1},{6,2},{7,3},{8,12},{9,13},{10,... | collective-permute-start | bytes 442376 | tf_op jit(solution)/shard_map/ppermute | solution.py:316
  27.8 1.1 %merge_2.6 = (bf16[2,64,1024]{2,1,0:T(8,128)(2,1)S(1)}, bf16[2,48,1024]{2,1,0:T(8,128)(2,1)S(1)}) custom-call(f32[4,8,128]{2,1,0:T(8,128)S(1)} %get-tuple-element.33.refs_0_, bf16[4,256,768]{2,1,0:T(8,128)(2,1)S(1)} %get-tuple-element.34.refs_1_.refs_4_, bf16[2,64,1024]{2,1,0:T(8,128)(2,1)S(1)} %get-tuple-element.39.refs_6_.refs_2_, ...), custom_call_target="tpu_custom_call" | custom-call | flops 1610612736 | tf_op jit(solution)/shard_map/merge_2/pallas_call | solution.py:245
  28.9 2.7 %collective-permute-start.7 = (bf16[2,48,1024]{2,1,0:T(8,128)(2,1)S(1)}, bf16[2,48,1024]{2,1,0:T(8,128)(2,1)S(1)}, u32[]{:S(2)}, u32[]{:S(2)}) collective-permute-start(bf16[2,48,1024]{2,1,0:T(8,128)(2,1)S(1)} %get-tuple-element.50), channel_id=1, source_target_pairs={{0,8},{1,9},{2,10},{3,11},{4,12},{5,13},{6,14},{7,15},{8,0},{9,1},... | collective-permute-start | bytes 589832 | tf_op jit(solution)/shard_map/ppermute | solution.py:316
  31.6 1.1 %merge_1.8 = (bf16[2,64,1024]{2,1,0:T(8,128)(2,1)S(1)}, bf16[2,48,896]{2,1,0:T(8,128)(2,1)S(1)}) custom-call(f32[4,8,128]{2,1,0:T(8,128)S(1)} %get-tuple-element.33.refs_0_, bf16[4,256,768]{2,1,0:T(8,128)(2,1)S(1)} %get-tuple-element.34.refs_1_.refs_4_, bf16[2,64,2048]{2,1,0:T(8,128)(2,1)S(1)} %get-tuple-element.38.refs_4_.refs_3_.refs_2_, ...), custom_call_target="tpu_custom_call" | custom-call | flops 1409286144 | tf_op jit(solution)/shard_map/merge_1/pallas_call | solution.py:245
  32.6 0.5 collective-permute-start.10
  33.2 0.0 collective-permute-done.4.refs_3_.refs_4_
  33.2 0.8 %merge_3.5.refs_4_ = bf16[2,64,768]{2,1,0:T(8,128)(2,1)S(1)} custom-call(f32[4,8,128]{2,1,0:T(8,128)S(1)} %get-tuple-element.33.refs_0_, bf16[4,256,768]{2,1,0:T(8,128)(2,1)S(1)} %get-tuple-element.34.refs_1_.refs_4_, bf16[2,64,768]{2,1,0:T(8,128)(2,1)S(1)} %get-tuple-element.43.refs_6_.refs_2_, ...), custom_call_target="tpu_custom_call" | custom-call | flops 251658240 | tf_op jit(solution)/shard_map/merge_3/pallas_call | solution.py:245
  34.0 0.8 %merge_1.9 = (bf16[2,64,512]{2,1,0:T(8,128)(2,1)S(1)}, bf16[2,48,512]{2,1,0:T(8,128)(2,1)S(1)}) custom-call(f32[4,8,128]{2,1,0:T(8,128)S(1)} %get-tuple-element.33.refs_0_, bf16[4,256,768]{2,1,0:T(8,128)(2,1)S(1)} %get-tuple-element.34.refs_1_.refs_4_, bf16[2,64,2048]{2,1,0:T(8,128)(2,1)S(1)} %get-tuple-element.38.refs_4_.refs_3_.refs_2_, ...), custom_call_target="tpu_custom_call" | custom-call | flops 805306368 | tf_op jit(solution)/shard_map/merge_1/pallas_call | solution.py:245
  34.8 1.7 %collective-permute-start.11 = (bf16[2,48,512]{2,1,0:T(8,128)(2,1)S(1)}, bf16[2,48,512]{2,1,0:T(8,128)(2,1)S(1)}, u32[]{:S(2)}, u32[]{:S(2)}) collective-permute-start(bf16[2,48,512]{2,1,0:T(8,128)(2,1)S(1)} %get-tuple-element.56), channel_id=1, source_target_pairs={{0,4},{1,5},{2,6},{3,7},{4,0},{5,1},{6,2},{7,3},{8,12},{9,13},{10,... | collective-permute-start | bytes 294920 | tf_op jit(solution)/shard_map/ppermute | solution.py:316
  36.4 0.0 collective-permute-done.8.refs_5_.refs_4_
  36.4 0.8 %merge_2.7 = (bf16[2,64,768]{2,1,0:T(8,128)(2,1)S(1)}, bf16[2,48,768]{2,1,0:T(8,128)(2,1)S(1)}) custom-call(f32[4,8,128]{2,1,0:T(8,128)S(1)} %get-tuple-element.33.refs_0_, bf16[4,256,768]{2,1,0:T(8,128)(2,1)S(1)} %get-tuple-element.34.refs_1_.refs_4_, bf16[2,64,1024]{2,1,0:T(8,128)(2,1)S(1)} %get-tuple-element.42.refs_4_.refs_3_.refs_2_, ...), custom_call_target="tpu_custom_call" | custom-call | flops 1207959552 | tf_op jit(solution)/shard_map/merge_2/pallas_call | solution.py:245
  37.3 0.4 collective-permute-start.9
  37.7 3.5 %collective-permute-done.7.refs_5_.refs_4_ = bf16[2,48,1024]{2,1,0:T(8,128)(2,1)S(1)} collective-permute-done((bf16[2,48,1024]{2,1,0:T(8,128)(2,1)S(1)}, bf16[2,48,1024]{2,1,0:T(8,128)(2,1)S(1)}, u32[]{:S(2)}, u32[]{:S(2)}) %collective-permute-start.7) | collective-permute-done | bytes 196640 | tf_op jit(solution)/shard_map/ppermute | solution.py:316
  41.2 1.0 %merge_3.6.refs_6_ = bf16[2,64,1024]{2,1,0:T(8,128)(2,1)S(1)} custom-call(f32[4,8,128]{2,1,0:T(8,128)S(1)} %get-tuple-element.33.refs_0_, bf16[4,256,768]{2,1,0:T(8,128)(2,1)S(1)} %get-tuple-element.34.refs_1_.refs_4_, bf16[2,64,768]{2,1,0:T(8,128)(2,1)S(1)} %get-tuple-element.43.refs_6_.refs_2_, ...), custom_call_target="tpu_custom_call" | custom-call | flops 402653184 | tf_op jit(solution)/shard_map/merge_3/pallas_call | solution.py:245
  42.2 3.1 %collective-permute-done.10.refs_5_.refs_4_ = bf16[2,48,896]{2,1,0:T(8,128)(2,1)S(1)} collective-permute-done((bf16[2,48,896]{2,1,0:T(8,128)(2,1)S(1)}, bf16[2,48,896]{2,1,0:T(8,128)(2,1)S(1)}, u32[]{:S(2)}, u32[]{:S(2)}) %collective-permute-start.10) | collective-permute-done | bytes 172064 | tf_op jit(solution)/shard_map/ppermute | solution.py:316
  45.3 1.1 %merge_2.8 = (bf16[2,64,1024]{2,1,0:T(8,128)(2,1)S(1)}, bf16[2,48,896]{2,1,0:T(8,128)(2,1)S(1)}) custom-call(f32[4,8,128]{2,1,0:T(8,128)S(1)} %get-tuple-element.33.refs_0_, bf16[4,256,768]{2,1,0:T(8,128)(2,1)S(1)} %get-tuple-element.34.refs_1_.refs_4_, bf16[2,64,768]{2,1,0:T(8,128)(2,1)S(1)} %get-tuple-element.47.refs_6_.refs_3_.refs_2_, ...), custom_call_target="tpu_custom_call" | custom-call | flops 1409286144 | tf_op jit(solution)/shard_map/merge_2/pallas_call | solution.py:245
  46.4 0.1 collective-permute-start.12
  46.5 0.9 %merge_2.9 = (bf16[2,64,768]{2,1,0:T(8,128)(2,1)S(1)}, bf16[2,48,640]{2,1,0:T(8,128)(2,1)S(1)}) custom-call(f32[4,8,128]{2,1,0:T(8,128)S(1)} %get-tuple-element.33.refs_0_, bf16[4,256,768]{2,1,0:T(8,128)(2,1)S(1)} %get-tuple-element.34.refs_1_.refs_4_, bf16[2,64,1024]{2,1,0:T(8,128)(2,1)S(1)} %get-tuple-element.49.refs_4_.refs_3_.refs_2_, ...), custom_call_target="tpu_custom_call" | custom-call | flops 1006632960 | tf_op jit(solution)/shard_map/merge_2/pallas_call | solution.py:245
  47.3 3.0 %collective-permute-start.13 = (bf16[2,48,640]{2,1,0:T(8,128)(2,1)S(1)}, bf16[2,48,640]{2,1,0:T(8,128)(2,1)S(1)}, u32[]{:S(2)}, u32[]{:S(2)}) collective-permute-start(bf16[2,48,640]{2,1,0:T(8,128)(2,1)S(1)} %get-tuple-element.60), channel_id=1, source_target_pairs={{0,8},{1,9},{2,10},{3,11},{4,12},{5,13},{6,14},{7,15},{8,0},{9,1},... | collective-permute-start | bytes 368648 | tf_op jit(solution)/shard_map/ppermute | solution.py:316
  50.3 0.8 %merge_3.7.refs_6_ = bf16[2,64,768]{2,1,0:T(8,128)(2,1)S(1)} custom-call(f32[4,8,128]{2,1,0:T(8,128)S(1)} %get-tuple-element.33.refs_0_, bf16[4,256,768]{2,1,0:T(8,128)(2,1)S(1)} %get-tuple-element.34.refs_1_.refs_4_, bf16[2,64,1024]{2,1,0:T(8,128)(2,1)S(1)} %get-tuple-element.48.refs_4_.refs_3_.refs_2_, ...), custom_call_target="tpu_custom_call" | custom-call | flops 301989888 | tf_op jit(solution)/shard_map/merge_3/pallas_call | solution.py:245
  51.2 6.6 %collective-permute-done.12.refs_5_.refs_4_ = bf16[2,48,896]{2,1,0:T(8,128)(2,1)S(1)} collective-permute-done((bf16[2,48,896]{2,1,0:T(8,128)(2,1)S(1)}, bf16[2,48,896]{2,1,0:T(8,128)(2,1)S(1)}, u32[]{:S(2)}, u32[]{:S(2)}) %collective-permute-start.12) | collective-permute-done | bytes 172064 | tf_op jit(solution)/shard_map/ppermute | solution.py:316
  57.7 1.0 %merge_3.8.refs_6_ = bf16[2,64,1024]{2,1,0:T(8,128)(2,1)S(1)} custom-call(f32[4,8,128]{2,1,0:T(8,128)S(1)} %get-tuple-element.33.refs_0_, bf16[4,256,768]{2,1,0:T(8,128)(2,1)S(1)} %get-tuple-element.34.refs_1_.refs_4_, bf16[2,64,768]{2,1,0:T(8,128)(2,1)S(1)} %get-tuple-element.53.refs_6_.refs_3_.refs_2_, ...), custom_call_target="tpu_custom_call" | custom-call | flops 352321536 | tf_op jit(solution)/shard_map/merge_3/pallas_call | solution.py:245
  58.8 0.0 copy-start.1
  58.8 0.5 collective-permute-done.13.refs_5_
  59.3 0.8 %merge_3.9 = bf16[2,64,768]{2,1,0:T(8,128)(2,1)S(1)} custom-call(f32[4,8,128]{2,1,0:T(8,128)S(1)} %get-tuple-element.33.refs_0_, bf16[4,256,768]{2,1,0:T(8,128)(2,1)S(1)} %get-tuple-element.34.refs_1_.refs_4_, bf16[2,64,1024]{2,1,0:T(8,128)(2,1)S(1)} %get-tuple-element.57.refs_6_.refs_3_.refs_2_, bf16[2,64,768]{2,1,0:T(8,128)(2,1)S(1)} %get-tuple-element.58.refs_6_.refs_3_, ...), custom_call_target="tpu_custom_call" | custom-call | flops 301989888 | tf_op jit(solution)/shard_map/merge_3/pallas_call | solution.py:245
  60.2 0.7 %constant_dynamic-update-slice_fusion = bf16[2,64,4096]{2,1,0:T(8,128)(2,1)} fusion(bf16[2,64,4096]{2,1,0:T(8,128)(2,1)} %copy-done.1, bf16[2,64,768]{2,1,0:T(8,128)(2,1)S(1)} %merge_3.9), kind=kLoop, calls=%fused_computation.2 | loop fusion | bytes 393216 | tf_op jit(solution)/shard_map/concatenate | solution.py:342
  (10 shorter events, 0.1 us)
Async XLA Ops:
  0.0 3.0 %collective-permute-start = (bf16[2,64,4096]{2,1,0:T(8,128)(2,1)}, bf16[2,64,4096]{2,1,0:T(8,128)(2,1)S(1)}, u32[]{:S(2)}, u32[]{:S(2)}) collective-permute-start(bf16[2,64,4096]{2,1,0:T(8,128)(2,1)} %refs_2_.5), channel_id=1, source_target_pairs={{0,1},{1,0},{2,3},{3,2},{4,5},{5,4},{6,7},{7,6},{8,9},{9,8},{10,11... | collective-permute-start | bytes 3145736 | tf_op jit(solution)/shard_map/ppermute | solution.py:316
  2.0 1.2 %copy-start = (bf16[2,64,4096]{2,1,0:T(8,128)(2,1)S(1)}, bf16[2,64,4096]{2,1,0:T(8,128)(2,1)}, u32[]{:S(2)}) copy-start(bf16[2,64,4096]{2,1,0:T(8,128)(2,1)} %refs_2_.5) | copy-start | bytes 3145732
  4.3 8.4 %collective-permute-start.1 = (bf16[2,48,1024]{2,1,0:T(8,128)(2,1)S(1)}, bf16[2,48,1024]{2,1,0:T(8,128)(2,1)S(1)}, u32[]{:S(2)}, u32[]{:S(2)}) collective-permute-start(bf16[2,48,1024]{2,1,0:T(8,128)(2,1)S(1)} %get-tuple-element.36), channel_id=1, source_target_pairs={{0,2},{1,3},{2,0},{3,1},{4,6},{5,7},{6,4},{7,5},{8,10},{9,11},{10,... | collective-permute-start | bytes 589832 | tf_op jit(solution)/shard_map/ppermute | solution.py:316
  8.0 8.9 %collective-permute-start.3 = (bf16[2,48,1024]{2,1,0:T(8,128)(2,1)S(1)}, bf16[2,48,1024]{2,1,0:T(8,128)(2,1)S(1)}, u32[]{:S(2)}, u32[]{:S(2)}) collective-permute-start(bf16[2,48,1024]{2,1,0:T(8,128)(2,1)S(1)} %get-tuple-element.41), channel_id=1, source_target_pairs={{0,2},{1,3},{2,0},{3,1},{4,6},{5,7},{6,4},{7,5},{8,10},{9,11},{10,... | collective-permute-start | bytes 589832 | tf_op jit(solution)/shard_map/ppermute | solution.py:316
  10.6 14.5 %collective-permute-start.5 = (bf16[2,48,2048]{2,1,0:T(8,128)(2,1)S(1)}, bf16[2,48,2048]{2,1,0:T(8,128)(2,1)S(1)}, u32[]{:S(2)}, u32[]{:S(2)}) collective-permute-start(bf16[2,48,2048]{2,1,0:T(8,128)(2,1)S(1)} %get-tuple-element.45), channel_id=1, source_target_pairs={{0,2},{1,3},{2,0},{3,1},{4,6},{5,7},{6,4},{7,5},{8,10},{9,11},{10,... | collective-permute-start | bytes 1179656 | tf_op jit(solution)/shard_map/ppermute | solution.py:316
  13.8 6.3 %collective-permute-start.2 = (bf16[2,48,896]{2,1,0:T(8,128)(2,1)S(1)}, bf16[2,48,896]{2,1,0:T(8,128)(2,1)S(1)}, u32[]{:S(2)}, u32[]{:S(2)}) collective-permute-start(bf16[2,48,896]{2,1,0:T(8,128)(2,1)S(1)} %get-tuple-element.40), channel_id=1, source_target_pairs={{0,4},{1,5},{2,6},{3,7},{4,0},{5,1},{6,2},{7,3},{8,12},{9,13},{10,... | collective-permute-start | bytes 516104 | tf_op jit(solution)/shard_map/ppermute | solution.py:316
  18.0 9.8 %collective-permute-start.6 = (bf16[2,48,1024]{2,1,0:T(8,128)(2,1)S(1)}, bf16[2,48,1024]{2,1,0:T(8,128)(2,1)S(1)}, u32[]{:S(2)}, u32[]{:S(2)}) collective-permute-start(bf16[2,48,1024]{2,1,0:T(8,128)(2,1)S(1)} %get-tuple-element.46), channel_id=1, source_target_pairs={{0,4},{1,5},{2,6},{3,7},{4,0},{5,1},{6,2},{7,3},{8,12},{9,13},{10,... | collective-permute-start | bytes 589832 | tf_op jit(solution)/shard_map/ppermute | solution.py:316
  21.0 12.2 %collective-permute-start.4 = (bf16[2,48,768]{2,1,0:T(8,128)(2,1)S(1)}, bf16[2,48,768]{2,1,0:T(8,128)(2,1)S(1)}, u32[]{:S(2)}, u32[]{:S(2)}) collective-permute-start(bf16[2,48,768]{2,1,0:T(8,128)(2,1)S(1)} %get-tuple-element.44), channel_id=1, source_target_pairs={{0,8},{1,9},{2,10},{3,11},{4,12},{5,13},{6,14},{7,15},{8,0},{9,1},... | collective-permute-start | bytes 442376 | tf_op jit(solution)/shard_map/ppermute | solution.py:316
  25.9 10.5 %collective-permute-start.8 = (bf16[2,48,768]{2,1,0:T(8,128)(2,1)S(1)}, bf16[2,48,768]{2,1,0:T(8,128)(2,1)S(1)}, u32[]{:S(2)}, u32[]{:S(2)}) collective-permute-start(bf16[2,48,768]{2,1,0:T(8,128)(2,1)S(1)} %get-tuple-element.51), channel_id=1, source_target_pairs={{0,4},{1,5},{2,6},{3,7},{4,0},{5,1},{6,2},{7,3},{8,12},{9,13},{10,... | collective-permute-start | bytes 442376 | tf_op jit(solution)/shard_map/ppermute | solution.py:316
  28.9 12.3 %collective-permute-start.7 = (bf16[2,48,1024]{2,1,0:T(8,128)(2,1)S(1)}, bf16[2,48,1024]{2,1,0:T(8,128)(2,1)S(1)}, u32[]{:S(2)}, u32[]{:S(2)}) collective-permute-start(bf16[2,48,1024]{2,1,0:T(8,128)(2,1)S(1)} %get-tuple-element.50), channel_id=1, source_target_pairs={{0,8},{1,9},{2,10},{3,11},{4,12},{5,13},{6,14},{7,15},{8,0},{9,1},... | collective-permute-start | bytes 589832 | tf_op jit(solution)/shard_map/ppermute | solution.py:316
  32.6 12.6 %collective-permute-start.10 = (bf16[2,48,896]{2,1,0:T(8,128)(2,1)S(1)}, bf16[2,48,896]{2,1,0:T(8,128)(2,1)S(1)}, u32[]{:S(2)}, u32[]{:S(2)}) collective-permute-start(bf16[2,48,896]{2,1,0:T(8,128)(2,1)S(1)} %get-tuple-element.55), channel_id=1, source_target_pairs={{0,4},{1,5},{2,6},{3,7},{4,0},{5,1},{6,2},{7,3},{8,12},{9,13},{10,... | collective-permute-start | bytes 516104 | tf_op jit(solution)/shard_map/ppermute | solution.py:316
  34.8 11.7 %collective-permute-start.11 = (bf16[2,48,512]{2,1,0:T(8,128)(2,1)S(1)}, bf16[2,48,512]{2,1,0:T(8,128)(2,1)S(1)}, u32[]{:S(2)}, u32[]{:S(2)}) collective-permute-start(bf16[2,48,512]{2,1,0:T(8,128)(2,1)S(1)} %get-tuple-element.56), channel_id=1, source_target_pairs={{0,4},{1,5},{2,6},{3,7},{4,0},{5,1},{6,2},{7,3},{8,12},{9,13},{10,... | collective-permute-start | bytes 294920 | tf_op jit(solution)/shard_map/ppermute | solution.py:316
  37.3 13.0 %collective-permute-start.9 = (bf16[2,48,768]{2,1,0:T(8,128)(2,1)S(1)}, bf16[2,48,768]{2,1,0:T(8,128)(2,1)S(1)}, u32[]{:S(2)}, u32[]{:S(2)}) collective-permute-start(bf16[2,48,768]{2,1,0:T(8,128)(2,1)S(1)} %get-tuple-element.54), channel_id=1, source_target_pairs={{0,8},{1,9},{2,10},{3,11},{4,12},{5,13},{6,14},{7,15},{8,0},{9,1},... | collective-permute-start | bytes 442376 | tf_op jit(solution)/shard_map/ppermute | solution.py:316
  46.4 11.4 %collective-permute-start.12 = (bf16[2,48,896]{2,1,0:T(8,128)(2,1)S(1)}, bf16[2,48,896]{2,1,0:T(8,128)(2,1)S(1)}, u32[]{:S(2)}, u32[]{:S(2)}) collective-permute-start(bf16[2,48,896]{2,1,0:T(8,128)(2,1)S(1)} %get-tuple-element.59), channel_id=1, source_target_pairs={{0,8},{1,9},{2,10},{3,11},{4,12},{5,13},{6,14},{7,15},{8,0},{9,1},... | collective-permute-start | bytes 516104 | tf_op jit(solution)/shard_map/ppermute | solution.py:316
  47.3 12.0 %collective-permute-start.13 = (bf16[2,48,640]{2,1,0:T(8,128)(2,1)S(1)}, bf16[2,48,640]{2,1,0:T(8,128)(2,1)S(1)}, u32[]{:S(2)}, u32[]{:S(2)}) collective-permute-start(bf16[2,48,640]{2,1,0:T(8,128)(2,1)S(1)} %get-tuple-element.60), channel_id=1, source_target_pairs={{0,8},{1,9},{2,10},{3,11},{4,12},{5,13},{6,14},{7,15},{8,0},{9,1},... | collective-permute-start | bytes 368648 | tf_op jit(solution)/shard_map/ppermute | solution.py:316
  58.8 1.4 %copy-start.1 = (bf16[2,64,4096]{2,1,0:T(8,128)(2,1)}, bf16[2,64,4096]{2,1,0:T(8,128)(2,1)S(1)}, u32[]{:S(2)}) copy-start(bf16[2,64,4096]{2,1,0:T(8,128)(2,1)S(1)} %slice_dynamic-update-slice_fusion) | copy-start | bytes 3145732

commit v14 on v13

--- a/solution.py
+++ b/solution.py
@@ -166,7 +166,6 @@
     span = stop - start
     tiles = pl.cdiv(span, TILE)
     other = pl.ds(pl.multiple_of((1 - following) * (beams - window), 16), window)
-    inline = not last and span % TILE == 0
     lane = lax.broadcasted_iota(jnp.int32, (2 * window, LANES), 1).astype(jnp.int16)
     moves = []
     for child in range(2):
@@ -192,13 +191,13 @@
                 held = piece
             held_ref[number] = held
 
-    def multiply(stack_ref, step):
+    def multiply(stack_ref, step, width=TILE):
         column = pl.multiple_of(step * TILE, TILE)
         both = jnp.dot(mix_ref[level], stack_ref[...], preferred_element_type=jnp.float32)
         total = (both[:2 * beams] + both[2 * beams:]).astype(jnp.bfloat16)
         out_ref[:, :, pl.ds(column, TILE)] = total.reshape(2, beams, TILE)
-        if inline:
-            send_ref[:, :, pl.ds(column, TILE)] = out_ref[:, other, pl.ds(column, TILE)]
+        if not last:
+            send_ref[:, :, pl.ds(column, width)] = out_ref[:, other, pl.ds(column, width)]
 
     def two_tiles(pair, carry):
         build(odd_ref, 2 * pair + 1)
@@ -212,13 +211,11 @@
     build(even_ref, 0)
     lax.fori_loop(0, (tiles - 1) // 2, two_tiles, 0)
     if tiles % 2 == 1:
-        multiply(even_ref, tiles - 1)
+        multiply(even_ref, tiles - 1, span - (tiles - 1) * TILE)
     else:
         build(odd_ref, tiles - 1)
         multiply(even_ref, tiles - 2)
-        multiply(odd_ref, tiles - 1)
-    if not last and not inline:
-        send_ref[...] = out_ref[:, other, :span]
+        multiply(odd_ref, tiles - 1, span - (tiles - 1) * TILE)
 
 
 def pieces_of(bounds, start, stop):

time: 61 us -> 61 us (level)
  no operation moved by 1% of the time
where the time goes in v14:
time: 61 us; the launch traced here: 60.8 us
  starting transfers between devices  22.2 us (36%)
  Pallas kernels  19.4 us (32%)
  waiting for transfers between devices  16.3 us (27%)
  other arithmetic  1.54 us (3%)
  local copies, waits for them, and re-layouts  1.05 us (2%)
    ppermute x14, starting transfers between devices, from_partner(): return lax.ppermute(value, 'pulse', pairs)  22.2 us
    pallas_call x18, Pallas kernels, merge(): pl.pallas_call(functools.partial(merge_kernel, level, plan, start, stop,...  18.6 us
    ppermute x14, waiting for transfers between devices, from_partner(): return lax.ppermute(value, 'pulse', pairs)  16.3 us
    add x2, other arithmetic, stacked(): total = total + lax.pad(piece, zero, ((top, below, 0), (left, right, 0)))  1.54 us
  transfers between devices with their start and end apart: 14, of which 7 were waited for; matrix products, arithmetic and copies ran while one was open for 3% of the time, Pallas kernels for 29%

profile of v14, /device:TPU:0, one launch (start us, length us, event | category | flops | bytes accessed | tf_op | source)
XLA Modules:
  0.0 60.8 jit_solution(2290442242230628330)
XLA Ops:
  0.0 0.5 collective-permute-start
  0.5 0.7 %pad_add_fusion.real_ref = f32[14,128]{1,0:T(8,128)S(1)} fusion(f32[4,16]{1,0:T(4,128)} %bitcast.3, f32[8,128]{1,0:T(8,128)} %bitcast.2, bf16[2,32]{1,0:T(2,128)(2,1)} %param.8), kind=kLoop, calls=%fused_computation.5 | loop fusion | flops 5376 | bytes 11648 | tf_op jit(solution)/shard_map/add | solution.py:91
  1.2 0.8 %pad_add_fusion.1.whole_ref = s32[12,128]{1,0:T(8,128)S(1)} fusion(s32[4,64]{1,0:T(4,128)} %param.11, s32[4,16]{1,0:T(4,128)} %param.12, s32[4,16]{1,0:T(4,128)} %param.13), kind=kLoop, calls=%fused_computation.6 | loop fusion | flops 4608 | bytes 7680 | tf_op jit(solution)/shard_map/add | solution.py:91
  2.0 0.9 %mixing.1 = (bf16[4,256,768]{2,1,0:T(8,128)(2,1)S(1)}, f32[4,8,128]{2,1,0:T(8,128)S(1)}) custom-call(s32[12,128]{1,0:T(8,128)S(1)} %pad_add_fusion.1.whole_ref, f32[14,128]{1,0:T(8,128)S(1)} %pad_add_fusion.real_ref), custom_call_target="tpu_custom_call" | custom-call | flops 2000000000 | bytes 1572864 | tf_op jit(solution)/shard_map/mixing/pallas_call | solution.py:121
  2.9 0.1 collective-permute-done.refs_3_
  3.0 0.3 copy-done
  3.2 1.1 %merge_0.3 = (bf16[2,64,1024]{2,1,0:T(8,128)(2,1)S(1)}, bf16[2,48,1024]{2,1,0:T(8,128)(2,1)S(1)}) custom-call(f32[4,8,128]{2,1,0:T(8,128)S(1)} %get-tuple-element.33.refs_0_, bf16[4,256,768]{2,1,0:T(8,128)(2,1)S(1)} %get-tuple-element.34.refs_1_.refs_4_, bf16[2,64,4096]{2,1,0:T(8,128)(2,1)S(1)} %copy-done, ...), custom_call_target="tpu_custom_call" | custom-call | flops 1610612736 | tf_op jit(solution)/shard_map/merge_0/pallas_call | solution.py:242
  4.3 2.7 %collective-permute-start.1 = (bf16[2,48,1024]{2,1,0:T(8,128)(2,1)S(1)}, bf16[2,48,1024]{2,1,0:T(8,128)(2,1)S(1)}, u32[]{:S(2)}, u32[]{:S(2)}) collective-permute-start(bf16[2,48,1024]{2,1,0:T(8,128)(2,1)S(1)} %get-tuple-element.36), channel_id=1, source_target_pairs={{0,2},{1,3},{2,0},{3,1},{4,6},{5,7},{6,4},{7,5},{8,10},{9,11},{10,... | collective-permute-start | bytes 589832 | tf_op jit(solution)/shard_map/ppermute | solution.py:313
  7.0 1.1 %merge_0.4 = (bf16[2,64,1024]{2,1,0:T(8,128)(2,1)S(1)}, bf16[2,48,1024]{2,1,0:T(8,128)(2,1)S(1)}) custom-call(f32[4,8,128]{2,1,0:T(8,128)S(1)} %get-tuple-element.33.refs_0_, bf16[4,256,768]{2,1,0:T(8,128)(2,1)S(1)} %get-tuple-element.34.refs_1_.refs_4_, bf16[2,64,4096]{2,1,0:T(8,128)(2,1)S(1)} %copy-done, ...), custom_call_target="tpu_custom_call" | custom-call | flops 1610612736 | tf_op jit(solution)/shard_map/merge_0/pallas_call | solution.py:242
  8.1 0.1 collective-permute-start.3
  8.1 2.5 %merge_0.5 = (bf16[2,64,2048]{2,1,0:T(8,128)(2,1)S(1)}, bf16[2,48,2048]{2,1,0:T(8,128)(2,1)S(1)}) custom-call(f32[4,8,128]{2,1,0:T(8,128)S(1)} %get-tuple-element.33.refs_0_, bf16[4,256,768]{2,1,0:T(8,128)(2,1)S(1)} %get-tuple-element.34.refs_1_.refs_4_, bf16[2,64,4096]{2,1,0:T(8,128)(2,1)S(1)} %copy-done, ...), custom_call_target="tpu_custom_call" | custom-call | flops 3221225472 | tf_op jit(solution)/shard_map/merge_0/pallas_call | solution.py:242
  10.6 2.1 %collective-permute-start.5 = (bf16[2,48,2048]{2,1,0:T(8,128)(2,1)S(1)}, bf16[2,48,2048]{2,1,0:T(8,128)(2,1)S(1)}, u32[]{:S(2)}, u32[]{:S(2)}) collective-permute-start(bf16[2,48,2048]{2,1,0:T(8,128)(2,1)S(1)} %get-tuple-element.45), channel_id=1, source_target_pairs={{0,2},{1,3},{2,0},{3,1},{4,6},{5,7},{6,4},{7,5},{8,10},{9,11},{10,... | collective-permute-start | bytes 1179656 | tf_op jit(solution)/shard_map/ppermute | solution.py:313
  12.7 0.0 collective-permute-done.1.refs_3_.refs_4_
  12.7 1.1 %merge_1.5 = (bf16[2,64,1024]{2,1,0:T(8,128)(2,1)S(1)}, bf16[2,48,896]{2,1,0:T(8,128)(2,1)S(1)}) custom-call(f32[4,8,128]{2,1,0:T(8,128)S(1)} %get-tuple-element.33.refs_0_, bf16[4,256,768]{2,1,0:T(8,128)(2,1)S(1)} %get-tuple-element.34.refs_1_.refs_4_, bf16[2,64,1024]{2,1,0:T(8,128)(2,1)S(1)} %get-tuple-element.35.refs_4_.refs_2_, ...), custom_call_target="tpu_custom_call" | custom-call | flops 1409286144 | tf_op jit(solution)/shard_map/merge_1/pallas_call | solution.py:242
  13.8 2.1 %collective-permute-start.2 = (bf16[2,48,896]{2,1,0:T(8,128)(2,1)S(1)}, bf16[2,48,896]{2,1,0:T(8,128)(2,1)S(1)}, u32[]{:S(2)}, u32[]{:S(2)}) collective-permute-start(bf16[2,48,896]{2,1,0:T(8,128)(2,1)S(1)} %get-tuple-element.40), channel_id=1, source_target_pairs={{0,4},{1,5},{2,6},{3,7},{4,0},{5,1},{6,2},{7,3},{8,12},{9,13},{10,... | collective-permute-start | bytes 516104 | tf_op jit(solution)/shard_map/ppermute | solution.py:313
  15.9 1.0 %collective-permute-done.3.refs_5_.refs_4_ = bf16[2,48,1024]{2,1,0:T(8,128)(2,1)S(1)} collective-permute-done((bf16[2,48,1024]{2,1,0:T(8,128)(2,1)S(1)}, bf16[2,48,1024]{2,1,0:T(8,128)(2,1)S(1)}, u32[]{:S(2)}, u32[]{:S(2)}) %collective-permute-start.3) | collective-permute-done | bytes 196640 | tf_op jit(solution)/shard_map/ppermute | solution.py:313
  16.9 1.1 %merge_1.6 = (bf16[2,64,1024]{2,1,0:T(8,128)(2,1)S(1)}, bf16[2,48,1024]{2,1,0:T(8,128)(2,1)S(1)}) custom-call(f32[4,8,128]{2,1,0:T(8,128)S(1)} %get-tuple-element.33.refs_0_, bf16[4,256,768]{2,1,0:T(8,128)(2,1)S(1)} %get-tuple-element.34.refs_1_.refs_4_, bf16[2,64,1024]{2,1,0:T(8,128)(2,1)S(1)} %get-tuple-element.35.refs_4_.refs_2_, ...), custom_call_target="tpu_custom_call" | custom-call | flops 1610612736 | tf_op jit(solution)/shard_map/merge_1/pallas_call | solution.py:242
  18.0 2.1 %collective-permute-start.6 = (bf16[2,48,1024]{2,1,0:T(8,128)(2,1)S(1)}, bf16[2,48,1024]{2,1,0:T(8,128)(2,1)S(1)}, u32[]{:S(2)}, u32[]{:S(2)}) collective-permute-start(bf16[2,48,1024]{2,1,0:T(8,128)(2,1)S(1)} %get-tuple-element.46), channel_id=1, source_target_pairs={{0,4},{1,5},{2,6},{3,7},{4,0},{5,1},{6,2},{7,3},{8,12},{9,13},{10,... | collective-permute-start | bytes 589832 | tf_op jit(solution)/shard_map/ppermute | solution.py:313
  20.1 0.9 %merge_2.5 = (bf16[2,64,768]{2,1,0:T(8,128)(2,1)S(1)}, bf16[2,48,768]{2,1,0:T(8,128)(2,1)S(1)}) custom-call(f32[4,8,128]{2,1,0:T(8,128)S(1)} %get-tuple-element.33.refs_0_, bf16[4,256,768]{2,1,0:T(8,128)(2,1)S(1)} %get-tuple-element.34.refs_1_.refs_4_, bf16[2,64,1024]{2,1,0:T(8,128)(2,1)S(1)} %get-tuple-element.39.refs_6_.refs_2_, ...), custom_call_target="tpu_custom_call" | custom-call | flops 1207959552 | tf_op jit(solution)/shard_map/merge_2/pallas_call | solution.py:242
  21.0 2.6 %collective-permute-start.4 = (bf16[2,48,768]{2,1,0:T(8,128)(2,1)S(1)}, bf16[2,48,768]{2,1,0:T(8,128)(2,1)S(1)}, u32[]{:S(2)}, u32[]{:S(2)}) collective-permute-start(bf16[2,48,768]{2,1,0:T(8,128)(2,1)S(1)} %get-tuple-element.44), channel_id=1, source_target_pairs={{0,8},{1,9},{2,10},{3,11},{4,12},{5,13},{6,14},{7,15},{8,0},{9,1},... | collective-permute-start | bytes 442376 | tf_op jit(solution)/shard_map/ppermute | solution.py:313
  23.6 1.5 %collective-permute-done.5.refs_5_.refs_3_ = bf16[2,48,2048]{2,1,0:T(8,128)(2,1)S(1)} collective-permute-done((bf16[2,48,2048]{2,1,0:T(8,128)(2,1)S(1)}, bf16[2,48,2048]{2,1,0:T(8,128)(2,1)S(1)}, u32[]{:S(2)}, u32[]{:S(2)}) %collective-permute-start.5) | collective-permute-done | bytes 393248 | tf_op jit(solution)/shard_map/ppermute | solution.py:313
  25.1 0.9 %merge_1.7 = (bf16[2,64,768]{2,1,0:T(8,128)(2,1)S(1)}, bf16[2,48,768]{2,1,0:T(8,128)(2,1)S(1)}) custom-call(f32[4,8,128]{2,1,0:T(8,128)S(1)} %get-tuple-element.33.refs_0_, bf16[4,256,768]{2,1,0:T(8,128)(2,1)S(1)} %get-tuple-element.34.refs_1_.refs_4_, bf16[2,64,1024]{2,1,0:T(8,128)(2,1)S(1)} %get-tuple-element.37.refs_4_.refs_3_.refs_2_, ...), custom_call_target="tpu_custom_call" | custom-call | flops 1207959552 | tf_op jit(solution)/shard_map/merge_1/pallas_call | solution.py:242
  26.0 1.9 %collective-permute-start.8 = (bf16[2,48,768]{2,1,0:T(8,128)(2,1)S(1)}, bf16[2,48,768]{2,1,0:T(8,128)(2,1)S(1)}, u32[]{:S(2)}, u32[]{:S(2)}) collective-permute-start(bf16[2,48,768]{2,1,0:T(8,128)(2,1)S(1)} %get-tuple-element.51), channel_id=1, source_target_pairs={{0,4},{1,5},{2,6},{3,7},{4,0},{5,1},{6,2},{7,3},{8,12},{9,13},{10,... | collective-permute-start | bytes 442376 | tf_op jit(solution)/shard_map/ppermute | solution.py:313
  27.8 1.1 %merge_2.6 = (bf16[2,64,1024]{2,1,0:T(8,128)(2,1)S(1)}, bf16[2,48,1024]{2,1,0:T(8,128)(2,1)S(1)}) custom-call(f32[4,8,128]{2,1,0:T(8,128)S(1)} %get-tuple-element.33.refs_0_, bf16[4,256,768]{2,1,0:T(8,128)(2,1)S(1)} %get-tuple-element.34.refs_1_.refs_4_, bf16[2,64,1024]{2,1,0:T(8,128)(2,1)S(1)} %get-tuple-element.39.refs_6_.refs_2_, ...), custom_call_target="tpu_custom_call" | custom-call | flops 1610612736 | tf_op jit(solution)/shard_map/merge_2/pallas_call | solution.py:242
  28.9 2.7 %collective-permute-start.7 = (bf16[2,48,1024]{2,1,0:T(8,128)(2,1)S(1)}, bf16[2,48,1024]{2,1,0:T(8,128)(2,1)S(1)}, u32[]{:S(2)}, u32[]{:S(2)}) collective-permute-start(bf16[2,48,1024]{2,1,0:T(8,128)(2,1)S(1)} %get-tuple-element.50), channel_id=1, source_target_pairs={{0,8},{1,9},{2,10},{3,11},{4,12},{5,13},{6,14},{7,15},{8,0},{9,1},... | collective-permute-start | bytes 589832 | tf_op jit(solution)/shard_map/ppermute | solution.py:313
  31.6 1.1 %merge_1.8 = (bf16[2,64,1024]{2,1,0:T(8,128)(2,1)S(1)}, bf16[2,48,896]{2,1,0:T(8,128)(2,1)S(1)}) custom-call(f32[4,8,128]{2,1,0:T(8,128)S(1)} %get-tuple-element.33.refs_0_, bf16[4,256,768]{2,1,0:T(8,128)(2,1)S(1)} %get-tuple-element.34.refs_1_.refs_4_, bf16[2,64,2048]{2,1,0:T(8,128)(2,1)S(1)} %get-tuple-element.38.refs_4_.refs_3_.refs_2_, ...), custom_call_target="tpu_custom_call" | custom-call | flops 1409286144 | tf_op jit(solution)/shard_map/merge_1/pallas_call | solution.py:242
  32.6 0.5 collective-permute-start.10
  33.2 0.0 collective-permute-done.4.refs_3_.refs_4_
  33.2 0.8 %merge_3.5.refs_4_ = bf16[2,64,768]{2,1,0:T(8,128)(2,1)S(1)} custom-call(f32[4,8,128]{2,1,0:T(8,128)S(1)} %get-tuple-element.33.refs_0_, bf16[4,256,768]{2,1,0:T(8,128)(2,1)S(1)} %get-tuple-element.34.refs_1_.refs_4_, bf16[2,64,768]{2,1,0:T(8,128)(2,1)S(1)} %get-tuple-element.43.refs_6_.refs_2_, ...), custom_call_target="tpu_custom_call" | custom-call | flops 251658240 | tf_op jit(solution)/shard_map/merge_3/pallas_call | solution.py:242
  34.0 0.8 %merge_1.9 = (bf16[2,64,512]{2,1,0:T(8,128)(2,1)S(1)}, bf16[2,48,512]{2,1,0:T(8,128)(2,1)S(1)}) custom-call(f32[4,8,128]{2,1,0:T(8,128)S(1)} %get-tuple-element.33.refs_0_, bf16[4,256,768]{2,1,0:T(8,128)(2,1)S(1)} %get-tuple-element.34.refs_1_.refs_4_, bf16[2,64,2048]{2,1,0:T(8,128)(2,1)S(1)} %get-tuple-element.38.refs_4_.refs_3_.refs_2_, ...), custom_call_target="tpu_custom_call" | custom-call | flops 805306368 | tf_op jit(solution)/shard_map/merge_1/pallas_call | solution.py:242
  34.8 1.6 %collective-permute-start.11 = (bf16[2,48,512]{2,1,0:T(8,128)(2,1)S(1)}, bf16[2,48,512]{2,1,0:T(8,128)(2,1)S(1)}, u32[]{:S(2)}, u32[]{:S(2)}) collective-permute-start(bf16[2,48,512]{2,1,0:T(8,128)(2,1)S(1)} %get-tuple-element.56), channel_id=1, source_target_pairs={{0,4},{1,5},{2,6},{3,7},{4,0},{5,1},{6,2},{7,3},{8,12},{9,13},{10,... | collective-permute-start | bytes 294920 | tf_op jit(solution)/shard_map/ppermute | solution.py:313
  36.4 0.0 collective-permute-done.8.refs_5_.refs_4_
  36.4 0.8 %merge_2.7 = (bf16[2,64,768]{2,1,0:T(8,128)(2,1)S(1)}, bf16[2,48,768]{2,1,0:T(8,128)(2,1)S(1)}) custom-call(f32[4,8,128]{2,1,0:T(8,128)S(1)} %get-tuple-element.33.refs_0_, bf16[4,256,768]{2,1,0:T(8,128)(2,1)S(1)} %get-tuple-element.34.refs_1_.refs_4_, bf16[2,64,1024]{2,1,0:T(8,128)(2,1)S(1)} %get-tuple-element.42.refs_4_.refs_3_.refs_2_, ...), custom_call_target="tpu_custom_call" | custom-call | flops 1207959552 | tf_op jit(solution)/shard_map/merge_2/pallas_call | solution.py:242
  37.3 0.4 collective-permute-start.9
  37.7 3.4 %collective-permute-done.7.refs_5_.refs_4_ = bf16[2,48,1024]{2,1,0:T(8,128)(2,1)S(1)} collective-permute-done((bf16[2,48,1024]{2,1,0:T(8,128)(2,1)S(1)}, bf16[2,48,1024]{2,1,0:T(8,128)(2,1)S(1)}, u32[]{:S(2)}, u32[]{:S(2)}) %collective-permute-start.7) | collective-permute-done | bytes 196640 | tf_op jit(solution)/shard_map/ppermute | solution.py:313
  41.1 1.0 %merge_3.6.refs_6_ = bf16[2,64,1024]{2,1,0:T(8,128)(2,1)S(1)} custom-call(f32[4,8,128]{2,1,0:T(8,128)S(1)} %get-tuple-element.33.refs_0_, bf16[4,256,768]{2,1,0:T(8,128)(2,1)S(1)} %get-tuple-element.34.refs_1_.refs_4_, bf16[2,64,768]{2,1,0:T(8,128)(2,1)S(1)} %get-tuple-element.43.refs_6_.refs_2_, ...), custom_call_target="tpu_custom_call" | custom-call | flops 402653184 | tf_op jit(solution)/shard_map/merge_3/pallas_call | solution.py:242
  42.1 3.2 %collective-permute-done.10.refs_5_.refs_4_ = bf16[2,48,896]{2,1,0:T(8,128)(2,1)S(1)} collective-permute-done((bf16[2,48,896]{2,1,0:T(8,128)(2,1)S(1)}, bf16[2,48,896]{2,1,0:T(8,128)(2,1)S(1)}, u32[]{:S(2)}, u32[]{:S(2)}) %collective-permute-start.10) | collective-permute-done | bytes 172064 | tf_op jit(solution)/shard_map/ppermute | solution.py:313
  45.3 1.1 %merge_2.8 = (bf16[2,64,1024]{2,1,0:T(8,128)(2,1)S(1)}, bf16[2,48,896]{2,1,0:T(8,128)(2,1)S(1)}) custom-call(f32[4,8,128]{2,1,0:T(8,128)S(1)} %get-tuple-element.33.refs_0_, bf16[4,256,768]{2,1,0:T(8,128)(2,1)S(1)} %get-tuple-element.34.refs_1_.refs_4_, bf16[2,64,768]{2,1,0:T(8,128)(2,1)S(1)} %get-tuple-element.47.refs_6_.refs_3_.refs_2_, ...), custom_call_target="tpu_custom_call" | custom-call | flops 1409286144 | tf_op jit(solution)/shard_map/merge_2/pallas_call | solution.py:242
  46.4 0.1 collective-permute-start.12
  46.5 0.8 %merge_2.9 = (bf16[2,64,768]{2,1,0:T(8,128)(2,1)S(1)}, bf16[2,48,640]{2,1,0:T(8,128)(2,1)S(1)}) custom-call(f32[4,8,128]{2,1,0:T(8,128)S(1)} %get-tuple-element.33.refs_0_, bf16[4,256,768]{2,1,0:T(8,128)(2,1)S(1)} %get-tuple-element.34.refs_1_.refs_4_, bf16[2,64,1024]{2,1,0:T(8,128)(2,1)S(1)} %get-tuple-element.49.refs_4_.refs_3_.refs_2_, ...), custom_call_target="tpu_custom_call" | custom-call | flops 1006632960 | tf_op jit(solution)/shard_map/merge_2/pallas_call | solution.py:242
  47.4 3.0 %collective-permute-start.13 = (bf16[2,48,640]{2,1,0:T(8,128)(2,1)S(1)}, bf16[2,48,640]{2,1,0:T(8,128)(2,1)S(1)}, u32[]{:S(2)}, u32[]{:S(2)}) collective-permute-start(bf16[2,48,640]{2,1,0:T(8,128)(2,1)S(1)} %get-tuple-element.60), channel_id=1, source_target_pairs={{0,8},{1,9},{2,10},{3,11},{4,12},{5,13},{6,14},{7,15},{8,0},{9,1},... | collective-permute-start | bytes 368648 | tf_op jit(solution)/shard_map/ppermute | solution.py:313
  50.3 0.8 %merge_3.7.refs_6_ = bf16[2,64,768]{2,1,0:T(8,128)(2,1)S(1)} custom-call(f32[4,8,128]{2,1,0:T(8,128)S(1)} %get-tuple-element.33.refs_0_, bf16[4,256,768]{2,1,0:T(8,128)(2,1)S(1)} %get-tuple-element.34.refs_1_.refs_4_, bf16[2,64,1024]{2,1,0:T(8,128)(2,1)S(1)} %get-tuple-element.48.refs_4_.refs_3_.refs_2_, ...), custom_call_target="tpu_custom_call" | custom-call | flops 301989888 | tf_op jit(solution)/shard_map/merge_3/pallas_call | solution.py:242
  51.2 6.3 %collective-permute-done.12.refs_5_.refs_4_ = bf16[2,48,896]{2,1,0:T(8,128)(2,1)S(1)} collective-permute-done((bf16[2,48,896]{2,1,0:T(8,128)(2,1)S(1)}, bf16[2,48,896]{2,1,0:T(8,128)(2,1)S(1)}, u32[]{:S(2)}, u32[]{:S(2)}) %collective-permute-start.12) | collective-permute-done | bytes 172064 | tf_op jit(solution)/shard_map/ppermute | solution.py:313
  57.4 1.0 %merge_3.8.refs_6_ = bf16[2,64,1024]{2,1,0:T(8,128)(2,1)S(1)} custom-call(f32[4,8,128]{2,1,0:T(8,128)S(1)} %get-tuple-element.33.refs_0_, bf16[4,256,768]{2,1,0:T(8,128)(2,1)S(1)} %get-tuple-element.34.refs_1_.refs_4_, bf16[2,64,768]{2,1,0:T(8,128)(2,1)S(1)} %get-tuple-element.53.refs_6_.refs_3_.refs_2_, ...), custom_call_target="tpu_custom_call" | custom-call | flops 352321536 | tf_op jit(solution)/shard_map/merge_3/pallas_call | solution.py:242
  58.5 0.0 copy-start.1
  58.5 0.7 %collective-permute-done.13.refs_5_ = bf16[2,48,640]{2,1,0:T(8,128)(2,1)S(1)} collective-permute-done((bf16[2,48,640]{2,1,0:T(8,128)(2,1)S(1)}, bf16[2,48,640]{2,1,0:T(8,128)(2,1)S(1)}, u32[]{:S(2)}, u32[]{:S(2)}) %collective-permute-start.13) | collective-permute-done | bytes 122912 | tf_op jit(solution)/shard_map/ppermute | solution.py:313
  59.2 0.8 %merge_3.9 = bf16[2,64,768]{2,1,0:T(8,128)(2,1)S(1)} custom-call(f32[4,8,128]{2,1,0:T(8,128)S(1)} %get-tuple-element.33.refs_0_, bf16[4,256,768]{2,1,0:T(8,128)(2,1)S(1)} %get-tuple-element.34.refs_1_.refs_4_, bf16[2,64,1024]{2,1,0:T(8,128)(2,1)S(1)} %get-tuple-element.57.refs_6_.refs_3_.refs_2_, bf16[2,64,768]{2,1,0:T(8,128)(2,1)S(1)} %get-tuple-element.58.refs_6_.refs_3_, ...), custom_call_target="tpu_custom_call" | custom-call | flops 301989888 | tf_op jit(solution)/shard_map/merge_3/pallas_call | solution.py:242
  60.1 0.7 %constant_dynamic-update-slice_fusion = bf16[2,64,4096]{2,1,0:T(8,128)(2,1)} fusion(bf16[2,64,4096]{2,1,0:T(8,128)(2,1)} %copy-done.1, bf16[2,64,768]{2,1,0:T(8,128)(2,1)S(1)} %merge_3.9), kind=kLoop, calls=%fused_computation.2 | loop fusion | bytes 393216 | tf_op jit(solution)/shard_map/concatenate | solution.py:339
  (10 shorter events, 0.1 us)
Async XLA Ops:
  0.0 3.0 %collective-permute-start = (bf16[2,64,4096]{2,1,0:T(8,128)(2,1)}, bf16[2,64,4096]{2,1,0:T(8,128)(2,1)S(1)}, u32[]{:S(2)}, u32[]{:S(2)}) collective-permute-start(bf16[2,64,4096]{2,1,0:T(8,128)(2,1)} %refs_2_.5), channel_id=1, source_target_pairs={{0,1},{1,0},{2,3},{3,2},{4,5},{5,4},{6,7},{7,6},{8,9},{9,8},{10,11... | collective-permute-start | bytes 3145736 | tf_op jit(solution)/shard_map/ppermute | solution.py:313
  2.0 1.2 %copy-start = (bf16[2,64,4096]{2,1,0:T(8,128)(2,1)S(1)}, bf16[2,64,4096]{2,1,0:T(8,128)(2,1)}, u32[]{:S(2)}) copy-start(bf16[2,64,4096]{2,1,0:T(8,128)(2,1)} %refs_2_.5) | copy-start | bytes 3145732
  4.3 8.4 %collective-permute-start.1 = (bf16[2,48,1024]{2,1,0:T(8,128)(2,1)S(1)}, bf16[2,48,1024]{2,1,0:T(8,128)(2,1)S(1)}, u32[]{:S(2)}, u32[]{:S(2)}) collective-permute-start(bf16[2,48,1024]{2,1,0:T(8,128)(2,1)S(1)} %get-tuple-element.36), channel_id=1, source_target_pairs={{0,2},{1,3},{2,0},{3,1},{4,6},{5,7},{6,4},{7,5},{8,10},{9,11},{10,... | collective-permute-start | bytes 589832 | tf_op jit(solution)/shard_map/ppermute | solution.py:313
  8.1 8.9 %collective-permute-start.3 = (bf16[2,48,1024]{2,1,0:T(8,128)(2,1)S(1)}, bf16[2,48,1024]{2,1,0:T(8,128)(2,1)S(1)}, u32[]{:S(2)}, u32[]{:S(2)}) collective-permute-start(bf16[2,48,1024]{2,1,0:T(8,128)(2,1)S(1)} %get-tuple-element.41), channel_id=1, source_target_pairs={{0,2},{1,3},{2,0},{3,1},{4,6},{5,7},{6,4},{7,5},{8,10},{9,11},{10,... | collective-permute-start | bytes 589832 | tf_op jit(solution)/shard_map/ppermute | solution.py:313
  10.6 14.5 %collective-permute-start.5 = (bf16[2,48,2048]{2,1,0:T(8,128)(2,1)S(1)}, bf16[2,48,2048]{2,1,0:T(8,128)(2,1)S(1)}, u32[]{:S(2)}, u32[]{:S(2)}) collective-permute-start(bf16[2,48,2048]{2,1,0:T(8,128)(2,1)S(1)} %get-tuple-element.45), channel_id=1, source_target_pairs={{0,2},{1,3},{2,0},{3,1},{4,6},{5,7},{6,4},{7,5},{8,10},{9,11},{10,... | collective-permute-start | bytes 1179656 | tf_op jit(solution)/shard_map/ppermute | solution.py:313
  13.8 6.4 %collective-permute-start.2 = (bf16[2,48,896]{2,1,0:T(8,128)(2,1)S(1)}, bf16[2,48,896]{2,1,0:T(8,128)(2,1)S(1)}, u32[]{:S(2)}, u32[]{:S(2)}) collective-permute-start(bf16[2,48,896]{2,1,0:T(8,128)(2,1)S(1)} %get-tuple-element.40), channel_id=1, source_target_pairs={{0,4},{1,5},{2,6},{3,7},{4,0},{5,1},{6,2},{7,3},{8,12},{9,13},{10,... | collective-permute-start | bytes 516104 | tf_op jit(solution)/shard_map/ppermute | solution.py:313
  18.0 9.8 %collective-permute-start.6 = (bf16[2,48,1024]{2,1,0:T(8,128)(2,1)S(1)}, bf16[2,48,1024]{2,1,0:T(8,128)(2,1)S(1)}, u32[]{:S(2)}, u32[]{:S(2)}) collective-permute-start(bf16[2,48,1024]{2,1,0:T(8,128)(2,1)S(1)} %get-tuple-element.46), channel_id=1, source_target_pairs={{0,4},{1,5},{2,6},{3,7},{4,0},{5,1},{6,2},{7,3},{8,12},{9,13},{10,... | collective-permute-start | bytes 589832 | tf_op jit(solution)/shard_map/ppermute | solution.py:313
  21.0 12.2 %collective-permute-start.4 = (bf16[2,48,768]{2,1,0:T(8,128)(2,1)S(1)}, bf16[2,48,768]{2,1,0:T(8,128)(2,1)S(1)}, u32[]{:S(2)}, u32[]{:S(2)}) collective-permute-start(bf16[2,48,768]{2,1,0:T(8,128)(2,1)S(1)} %get-tuple-element.44), channel_id=1, source_target_pairs={{0,8},{1,9},{2,10},{3,11},{4,12},{5,13},{6,14},{7,15},{8,0},{9,1},... | collective-permute-start | bytes 442376 | tf_op jit(solution)/shard_map/ppermute | solution.py:313
  26.0 10.5 %collective-permute-start.8 = (bf16[2,48,768]{2,1,0:T(8,128)(2,1)S(1)}, bf16[2,48,768]{2,1,0:T(8,128)(2,1)S(1)}, u32[]{:S(2)}, u32[]{:S(2)}) collective-permute-start(bf16[2,48,768]{2,1,0:T(8,128)(2,1)S(1)} %get-tuple-element.51), channel_id=1, source_target_pairs={{0,4},{1,5},{2,6},{3,7},{4,0},{5,1},{6,2},{7,3},{8,12},{9,13},{10,... | collective-permute-start | bytes 442376 | tf_op jit(solution)/shard_map/ppermute | solution.py:313
  28.9 12.2 %collective-permute-start.7 = (bf16[2,48,1024]{2,1,0:T(8,128)(2,1)S(1)}, bf16[2,48,1024]{2,1,0:T(8,128)(2,1)S(1)}, u32[]{:S(2)}, u32[]{:S(2)}) collective-permute-start(bf16[2,48,1024]{2,1,0:T(8,128)(2,1)S(1)} %get-tuple-element.50), channel_id=1, source_target_pairs={{0,8},{1,9},{2,10},{3,11},{4,12},{5,13},{6,14},{7,15},{8,0},{9,1},... | collective-permute-start | bytes 589832 | tf_op jit(solution)/shard_map/ppermute | solution.py:313
  32.6 12.7 %collective-permute-start.10 = (bf16[2,48,896]{2,1,0:T(8,128)(2,1)S(1)}, bf16[2,48,896]{2,1,0:T(8,128)(2,1)S(1)}, u32[]{:S(2)}, u32[]{:S(2)}) collective-permute-start(bf16[2,48,896]{2,1,0:T(8,128)(2,1)S(1)} %get-tuple-element.55), channel_id=1, source_target_pairs={{0,4},{1,5},{2,6},{3,7},{4,0},{5,1},{6,2},{7,3},{8,12},{9,13},{10,... | collective-permute-start | bytes 516104 | tf_op jit(solution)/shard_map/ppermute | solution.py:313
  34.8 11.7 %collective-permute-start.11 = (bf16[2,48,512]{2,1,0:T(8,128)(2,1)S(1)}, bf16[2,48,512]{2,1,0:T(8,128)(2,1)S(1)}, u32[]{:S(2)}, u32[]{:S(2)}) collective-permute-start(bf16[2,48,512]{2,1,0:T(8,128)(2,1)S(1)} %get-tuple-element.56), channel_id=1, source_target_pairs={{0,4},{1,5},{2,6},{3,7},{4,0},{5,1},{6,2},{7,3},{8,12},{9,13},{10,... | collective-permute-start | bytes 294920 | tf_op jit(solution)/shard_map/ppermute | solution.py:313
  37.3 13.1 %collective-permute-start.9 = (bf16[2,48,768]{2,1,0:T(8,128)(2,1)S(1)}, bf16[2,48,768]{2,1,0:T(8,128)(2,1)S(1)}, u32[]{:S(2)}, u32[]{:S(2)}) collective-permute-start(bf16[2,48,768]{2,1,0:T(8,128)(2,1)S(1)} %get-tuple-element.54), channel_id=1, source_target_pairs={{0,8},{1,9},{2,10},{3,11},{4,12},{5,13},{6,14},{7,15},{8,0},{9,1},... | collective-permute-start | bytes 442376 | tf_op jit(solution)/shard_map/ppermute | solution.py:313
  46.4 11.1 %collective-permute-start.12 = (bf16[2,48,896]{2,1,0:T(8,128)(2,1)S(1)}, bf16[2,48,896]{2,1,0:T(8,128)(2,1)S(1)}, u32[]{:S(2)}, u32[]{:S(2)}) collective-permute-start(bf16[2,48,896]{2,1,0:T(8,128)(2,1)S(1)} %get-tuple-element.59), channel_id=1, source_target_pairs={{0,8},{1,9},{2,10},{3,11},{4,12},{5,13},{6,14},{7,15},{8,0},{9,1},... | collective-permute-start | bytes 516104 | tf_op jit(solution)/shard_map/ppermute | solution.py:313
  47.4 11.9 %collective-permute-start.13 = (bf16[2,48,640]{2,1,0:T(8,128)(2,1)S(1)}, bf16[2,48,640]{2,1,0:T(8,128)(2,1)S(1)}, u32[]{:S(2)}, u32[]{:S(2)}) collective-permute-start(bf16[2,48,640]{2,1,0:T(8,128)(2,1)S(1)} %get-tuple-element.60), channel_id=1, source_target_pairs={{0,8},{1,9},{2,10},{3,11},{4,12},{5,13},{6,14},{7,15},{8,0},{9,1},... | collective-permute-start | bytes 368648 | tf_op jit(solution)/shard_map/ppermute | solution.py:313
  58.5 1.6 %copy-start.1 = (bf16[2,64,4096]{2,1,0:T(8,128)(2,1)}, bf16[2,64,4096]{2,1,0:T(8,128)(2,1)S(1)}, u32[]{:S(2)}) copy-start(bf16[2,64,4096]{2,1,0:T(8,128)(2,1)S(1)} %slice_dynamic-update-slice_fusion) | copy-start | bytes 3145732
